TPU v7x, 32 devices: a whole 2x2x4 slice. The times are simulated.
32 devices in a mesh: fsdp: 8 (over z, y), ctx: 4 (over x, core).
Axes of the slice: x: 2, y: 2, z: 4, core: 2. Of those that a mesh axis runs over, the one named last changes fastest.
Arguments:
- token_ids: int32 [8, 512], P('fsdp', 'ctx'), may hold values from 0 to 511
- embedding: bfloat16 [512, 4096], replicated, may hold values from -15 to 15
- norm_gain: float32 [4096], replicated, may hold values from 0.5 to 1.5
- in_proj: bfloat16 [3, 4096, 4096], P(None, None, 'fsdp'), may hold values from -0.09375 to 0.09375
- short_taps: float32 [3, 3, 4096], P(None, None, 'fsdp'), may hold values from -3 to 3
- conv_taps: bfloat16 [256, 128], P('fsdp'), may hold values from -0.6 to 0.6
- out_proj: bfloat16 [4096, 4096], P('fsdp'), may hold values from -0.09375 to 0.09375
Outputs:
- output: bfloat16 [8, 512, 4096], P('fsdp', 'ctx')
All inputs are finite; a program needn't handle non-finite values.
Results may differ from a plain program's by a relative error of at most 0.02.
Values may be sent and summed in bfloat16 or wider, within the bound.
No kernel may reach another device: no remote copies, remote signals or barrier semaphores. Data moves between devices by JAX's collectives and lax.ppermute only.
A program may use at most 128 MiB of HBM per device.

v0:
```python
import jax
import jax.numpy as jnp
from jax import lax
from jax.sharding import PartitionSpec as P

GROUP = 16
TAPS = 128
SHORT = 3


def from_behind(x, axis, by):
    peers = lax.axis_size(axis)
    pairs = [(i, i + by) for i in range(peers) if 0 <= i + by < peers]
    return lax.ppermute(x, axis, pairs)


def normalize_rows(table_rows, norm_gain):
    values = table_rows.astype(jnp.float32)
    inverse_rms = lax.rsqrt(jnp.mean(values * values, axis=-1, keepdims=True) + 1e-06)
    return (values * inverse_rms * norm_gain).astype(jnp.bfloat16)


def per_device(token_ids, embedding, norm_gain, in_proj, short_taps, conv_taps, out_proj):
    tok_len = token_ids.shape[1]
    panel_width = out_proj.shape[0]
    short_reach = SHORT - 1
    long_reach = TAPS - 1
    all_ids = lax.all_gather(token_ids, "fsdp", axis=0, tiled=True)
    windows = all_ids.shape[0]
    normed = normalize_rows(jnp.take(embedding, all_ids, axis=0), norm_gain)
    projected = jnp.einsum(
        "wtd,idc->iwtc", normed, in_proj, preferred_element_type=jnp.float32
    ).astype(jnp.bfloat16)
    prior_rows = from_behind(projected[:, :, tok_len - short_reach :, :], "ctx", 1)
    extended = jnp.concatenate([prior_rows, projected], axis=2)
    featured = jnp.zeros(projected.shape, jnp.float32)
    for offset in range(SHORT):
        shifted = extended[:, :, short_reach - offset : short_reach - offset + tok_len, :].astype(
            jnp.float32
        )
        featured = featured + short_taps[offset][:, None, None, :] * shifted
    product = (featured[1] * featured[2]).astype(jnp.bfloat16)
    prior_products = from_behind(product[:, tok_len - long_reach :, :], "ctx", 1)
    with_rim = jnp.concatenate([prior_products, product], axis=1)
    lag_grid = jnp.arange(tok_len)[:, None] + long_reach - jnp.arange(tok_len + long_reach)[None, :]
    in_reach = (lag_grid >= 0) & (lag_grid < TAPS)
    toeplitz = jnp.where(
        in_reach[None],
        jnp.take(conv_taps, jnp.clip(lag_grid, 0, TAPS - 1), axis=1),
        jnp.zeros((), jnp.bfloat16),
    )
    groups_dev = conv_taps.shape[0]
    grouped = with_rim.reshape(windows, tok_len + long_reach, groups_dev, GROUP)
    filtered = jnp.einsum("gts,wsgc->wtgc", toeplitz, grouped, preferred_element_type=jnp.float32)
    filtered = filtered.reshape(windows, tok_len, panel_width)
    gated = (featured[0] * filtered).astype(jnp.bfloat16)
    summed = lax.psum_scatter(
        jnp.einsum("wtc,cd->wtd", gated, out_proj, preferred_element_type=jnp.float32).astype(
            jnp.bfloat16
        ),
        "fsdp",
        scatter_dimension=0,
        tiled=True,
    ).astype(jnp.float32)[0]
    residual = jnp.take(embedding, token_ids[0], axis=0).astype(jnp.float32)
    return (residual + summed).astype(jnp.bfloat16)[None]


def solution(mesh):
    return jax.shard_map(
        per_device,
        mesh=mesh,
        in_specs=(
            P("fsdp", "ctx"),
            P(),
            P(),
            P(None, None, "fsdp"),
            P(None, None, "fsdp"),
            P("fsdp", None),
            P("fsdp", None),
        ),
        out_specs=P("fsdp", "ctx", None),
        check_vma=False,
    )
```

profile of v0, /device:TPU:0, one launch (start us, length us, event | category | flops | bytes accessed | tf_op | source)
XLA Modules:
  0.0 339.4 jit_solution(4764492914570860073)
XLA Ops:
  6.5 22.3 %all-gather = s32[8,1,128]{2,1,0:T(1,128)S(1)} all-gather(s32[1,1,128]{2,1,0:T(1,128)} %bitcast.70), channel_id=1, replica_groups=mesh['fsdp'=8,'ctx'=4] {'fsdp'}, dimensions={0}, use_global_device_ids=true | all-gather | bytes 4608 | tf_op jit(solution)/shard_map/all_gather | solution.py:28
  28.9 17.8 %gather_fusion.1 = bf16[1024,4096]{1,0:T(8,128)(2,1)} fusion(bf16[512,4096]{1,0:T(8,128)(2,1)} %param.8, s32[1024]{0:T(1024)S(1)} %bitcast_clamp_fusion), kind=kCustom, calls=%fused_computation.1 | custom fusion | bytes 16781312 | tf_op jit(solution)/shard_map/jit(_take)/gather | solution.py:30
  46.7 5.9 %fusion = f32[8,128]{1,0:T(8,128)S(1)} fusion(bf16[8,128,4096]{2,1,0:T(8,128)(2,1)} %bitcast.64, pred[8,128]{1,0:T(8,128)(4,1)S(1)} %compare_and_fusion), kind=kLoop, calls=%fused_computation.5 | loop fusion | flops 16776192 | bytes 8393728 | tf_op jit(solution)/shard_map/reduce_sum | solution.py:19
  52.6 16.3 %convert_bitcast_fusion = bf16[3,8,128,512]{3,2,0,1:T(8,128)(2,1)S(1)} fusion(bf16[3,4096,512]{2,1,0:T(8,128)(2,1)} %param.10, f32[4096]{0:T(1024)S(1)} %copy-done.5, f32[8,128]{1,0:T(8,128)S(1)} %add_rsqrt_fusion, bf16[8,128,4096]{2,1,0:T(8,128)(2,1)S(1)} %bitcast.65, pred[8,128]{1,0:T(8,128)(4,1)S(1)} %compare_and_fusion), kind=kOutput, calls=%fused_computation.22 | convolution fusion | flops 12907446272 | bytes 24138752 | tf_op jit(solution)/shard_map/wtd,idc->iwtc/dot_general | solution.py:31
  69.0 0.1 slice.46
  69.0 1.5 collective-permute-start
  70.5 0.7 collective-permute-done
  71.2 2.4 multiply_add_fusion
  73.6 0.4 fusion.32
  73.9 0.2 slice.52
  74.2 2.1 copy.18
  76.3 0.2 copy-done.1
  76.5 5.4 %collective-permute-start.1 = (bf16[8,127,512]{2,0,1:T(8,128)(2,1)}, bf16[8,127,512]{2,0,1:T(8,128)(2,1)}, u32[]{:S(2)}, u32[]{:S(2)}) collective-permute-start(bf16[8,127,512]{2,0,1:T(8,128)(2,1)} %copy.18), channel_id=1, source_target_pairs={{0,1},{1,2},{2,3},{4,5},{5,6},{6,7},{8,9},{9,10},{10,11},{12,13},{... | collective-permute-start | bytes 3121160 | tf_op jit(solution)/shard_map/ppermute | solution.py:14
  81.9 0.1 copy.21
  82.1 0.1 compare_select_fusion
  82.2 0.3 reshape.192
  82.5 65.9 %gather_fusion.2 = bf16[32640,32]{1,0:T(8,128)(2,1)} fusion(bf16[32,128]{0,1:T(8,128)(2,1)S(1)} %copy.21, s32[32768]{0:T(1024)S(1)} %pad_clamp_fusion), kind=kCustom, calls=%fused_computation.2 | custom fusion | bytes 4308480 | tf_op jit(solution)/shard_map/jit(_take)/gather | solution.py:49
  148.4 6.9 %copy.22 = bf16[32640,32]{0,1:T(8,128)(2,1)S(1)} copy(bf16[32640,32]{1,0:T(8,128)(2,1)} %gather_fusion.2) | data formatting | bytes 4177920 | tf_op jit(solution)/shard_map/jit(_take)/gather | solution.py:49
  155.3 7.8 %reshape.195 = bf16[128,255,32]{1,0,2:T(8,128)(2,1)} reshape(bf16[32640,32]{0,1:T(8,128)(2,1)S(1)} %copy.22) | data formatting | bytes 4177920 | tf_op jit(solution)/shard_map/jit(_take)/gather | solution.py:49
  163.1 0.2 fusion.39
  163.3 1.5 copy.19
  164.8 0.3 pad_maximum_fusion.1
  165.1 2.4 copy.20
  167.5 2.9 fusion.26
  170.5 0.2 copy.24
  170.7 1.8 copy.25
  172.5 11.2 %convolution_convert_fusion = bf16[8,128,4096]{2,1,0:T(8,128)(2,1)} fusion(bf16[512,4096]{1,0:T(8,128)(2,1)} %param.13, f32[8,128,512]{2,1,0:T(8,128)} %copy.25, f32[3,8,128,512]{3,2,0,1:T(8,128)} %copy-done.1), kind=kOutput, calls=%fused_computation.14 | convolution fusion | flops 4300210176 | bytes 16777216 | tf_op jit(solution)/shard_map/wtc,cd->wtd/dot_general | solution.py:58
  183.7 0.0 reduce-scatter.2.cloned.1.call-update
  183.7 0.6 copy-done.4
  184.4 4.9 %gather_fusion = bf16[128,4096]{1,0:T(8,128)(2,1)S(1)} fusion(bf16[512,4096]{1,0:T(8,128)(2,1)} %param.8, s32[1024]{0:T(1024)S(1)} %pad_clamp_fusion.1), kind=kCustom, calls=%fused_computation | custom fusion | bytes 2097664 | tf_op jit(solution)/shard_map/jit(_take)/gather | solution.py:65
  189.3 140.6 %reduce-scatter.2.cloned.1.call-done = bf16[1,128,4096]{2,1,0:T(8,128)(2,1)} async-done(((bf16[8,128,4096]{2,1,0:T(8,128)(2,1)}), bf16[1,128,4096]{2,1,0:T(8,128)(2,1)}) %reduce-scatter.2.cloned.1.call-update) | async-done | bytes 1048592 | tf_op jit(solution)/shard_map/reduce_scatter | solution.py:57
  330.0 2.6 add_convert_fusion
  (21 shorter events, 0.1 us)
Async XLA Ops:
  6.5 323.4 %reduce-scatter.2.cloned.1.call-start = ((), (), s32[]{:S(2)}) async-start(), calls=%async_computation.1 | async-start | bytes 9437184 | tf_op jit(solution)/shard_map/reduce_scatter | solution.py:57
  28.9 23.7 %copy-start.5 = (f32[4096]{0:T(1024)S(1)}, f32[4096]{0:T(1024)}, u32[]{:S(2)}) copy-start(f32[4096]{0:T(1024)} %param.9) | copy-start | bytes 49156
  46.7 5.9 %copy-start = (bf16[1024,4096]{1,0:T(8,128)(2,1)S(1)}, bf16[1024,4096]{1,0:T(8,128)(2,1)}, u32[]{:S(2)}) copy-start(bf16[1024,4096]{1,0:T(8,128)(2,1)} %gather_fusion.1) | copy-start | bytes 25165828
  52.6 17.9 %copy-start.2 = (f32[3,3,512]{2,1,0:T(4,128)S(1)}, f32[3,3,512]{2,1,0:T(4,128)}, u32[]{:S(2)}) copy-start(f32[3,3,512]{2,1,0:T(4,128)} %param.11) | copy-start | bytes 55300
  69.0 2.2 collective-permute-start
  73.5 3.0 copy-start.1
  73.5 8.4 %copy-start.3 = (bf16[32,128]{1,0:T(8,128)(2,1)S(1)}, bf16[32,128]{1,0:T(8,128)(2,1)}, u32[]{:S(2)}) copy-start(bf16[32,128]{1,0:T(8,128)(2,1)} %param.12) | copy-start | bytes 24580
  76.5 86.7 %collective-permute-start.1 = (bf16[8,127,512]{2,0,1:T(8,128)(2,1)}, bf16[8,127,512]{2,0,1:T(8,128)(2,1)}, u32[]{:S(2)}, u32[]{:S(2)}) collective-permute-start(bf16[8,127,512]{2,0,1:T(8,128)(2,1)} %copy.18), channel_id=1, source_target_pairs={{0,1},{1,2},{2,3},{4,5},{5,6},{6,7},{8,9},{9,10},{10,11},{12,13},{... | collective-permute-start | bytes 3121160 | tf_op jit(solution)/shard_map/ppermute | solution.py:14
  183.7 0.7 copy-start.4
Sparse Core Ops, SparseCore 0:
  183.8 146.0 reduce-scatter.1
where the time goes:
time: 340 us; the launch traced here: 339 us
  waiting for transfers between devices  141 us (41%)
  local copies, waits for them, and re-layouts  113 us (33%)
  matrix products  30.5 us (9%)
  blocking collectives  22.3 us (7%)
  between operations  13.6 us (4%)
  other arithmetic  11.8 us (3%)
  starting transfers between devices  6.89 us (2%)
    reduce_scatter x1, waiting for transfers between devices, per_device(): lax.psum_scatter(jnp.einsum('wtc,cd->wtd', gated, out_proj, preferred_ele...  141 us
    gather x3, local copies, waits for them, and re-layouts, per_device(): jnp.take(conv_taps, jnp.clip(lag_grid, 0, TAPS - 1), axis=1)  80.5 us
    all_gather x1, blocking collectives, per_device(): all_ids = lax.all_gather(token_ids, 'fsdp', axis=0, tiled=True)  22.3 us
    gather x1, local copies, waits for them, and re-layouts, per_device(): normed = normalize_rows(jnp.take(embedding, all_ids, axis=0), norm_gain)  17.8 us
    dot_general x1, matrix products, per_device(): jnp.einsum('wtd,idc->iwtc', normed, in_proj, preferred_element_type=jnp.f...  16.3 us
    dot_general x1, matrix products, per_device(): jnp.einsum('wtc,cd->wtd', gated, out_proj, preferred_element_type=jnp.flo...  11.2 us
    ppermute x2, starting transfers between devices, from_behind(): return lax.ppermute(x, axis, pairs)  6.89 us
  transfers between devices with their start and end apart: 3, of which 2 were waited for; matrix products, arithmetic and copies ran while one was open for 25% of the time, Pallas kernels for 0%

commit v1 on v0

v1 whole, which is shorter than its diff:
```python
import functools

import jax
import jax.numpy as jnp
from jax import lax
from jax.experimental import pallas as pl
from jax.experimental.pallas import tpu as pltpu
from jax.sharding import PartitionSpec as P

GROUP = 16
TAPS = 128
SHORT = 3
LANES = 128
LEAD = 16


def from_behind(x, axis, by):
    peers = lax.axis_size(axis)
    return lax.ppermute(x, axis, [(i, i + by) for i in range(peers) if i + by < peers])


def swap(x, axis, mask):
    peers = lax.axis_size(axis)
    return lax.ppermute(x, axis, [(i, i ^ mask) for i in range(peers)])


def exchange_bits():
    peers = lax.axis_size("fsdp")
    return [1 << b for b in reversed(range(peers.bit_length() - 1))]


def normalize_rows(table_rows, norm_gain):
    values = table_rows.astype(jnp.float32)
    inverse_rms = lax.rsqrt(jnp.mean(values * values, axis=-1, keepdims=True) + 1e-06)
    return (values * inverse_rms * norm_gain).astype(jnp.bfloat16)


def gather_ids(token_ids):
    tok_len = token_ids.shape[1]
    place = lax.axis_index("ctx")
    one = from_behind(token_ids, "ctx", 1)
    two = from_behind(token_ids[:, tok_len - LEAD :], "ctx", 2)
    one = jnp.where(place >= 1, one, -1)
    two = jnp.where(place >= 2, two, -1)
    ids = jnp.concatenate([two, one, token_ids], axis=1)
    bits = exchange_bits()
    while bits:
        if len(bits) > 1:
            low, high = bits[:2]
            ids = jnp.concatenate([ids] + [swap(ids, "fsdp", mask) for mask in (low, high, low | high)], axis=0)
            bits = bits[2:]
        else:
            ids = jnp.concatenate([ids, swap(ids, "fsdp", bits[0])], axis=0)
            bits = []
    return ids


def mixer_kernel(ids_ref, table_ref, short_ref, base_ref, gated_ref, toeplitz, held):
    tok_len, panel = gated_ref.shape[1:]
    vocab = table_ref.shape[1]
    rows = ids_ref.shape[2]
    reach = 2 * tok_len
    tiles = panel // LANES
    per_tile = LANES // GROUP

    @pl.when(pl.program_id(0) == 0)
    def _():
        for tile in range(tiles):
            for k in range(per_tile):
                g = tile * per_tile + k
                wide = jnp.broadcast_to(base_ref[pl.ds(g, 1), :], (tok_len, reach))
                shifted = pltpu.roll(wide, 0, 1, stride=1, stride_axis=0)
                toeplitz[tile, pl.ds(k * tok_len, tok_len), :] = shifted.astype(jnp.bfloat16)

    names = lax.broadcasted_iota(jnp.int32, (vocab, rows), 0)
    lane_group = lax.broadcasted_iota(jnp.int32, (tok_len, 2 * LANES), 1) % LANES // GROUP
    for v in range(2):
        one_hot = (names == ids_ref[v]).astype(jnp.float32).astype(jnp.bfloat16)
        for i in range(3):
            held[v, i] = lax.dot_general(
                one_hot, table_ref[i], (((0,), (0,)), ((), ())), preferred_element_type=jnp.float32
            ).astype(jnp.bfloat16).astype(jnp.float32)

    def featured(v, i, first, count, cols):
        total = short_ref[0, i : i + 1, cols] * held[v, i, pl.ds(first, count), cols]
        for j in range(1, SHORT):
            total += short_ref[j, i : i + 1, cols] * held[v, i, pl.ds(first - j, count), cols]
        return total

    start = rows - reach
    for tile in range(tiles):
        cols = slice(tile * LANES, (tile + 1) * LANES)
        products = []
        for v in range(2):
            key = featured(v, 1, start, reach, cols)
            value = featured(v, 2, start, reach, cols)
            products.append((key * value).astype(jnp.bfloat16))
        both = jnp.concatenate(products, axis=1)
        filtered = None
        for k in range(per_tile):
            one = jnp.dot(
                toeplitz[tile, pl.ds(k * tok_len, tok_len), :], both, preferred_element_type=jnp.float32
            )
            filtered = one if k == 0 else jnp.where(lane_group == k, one, filtered)
        for v in range(2):
            query = featured(v, 0, rows - tok_len, tok_len, cols)
            gated_ref[v, :, cols] = (query * filtered[:, v * LANES : (v + 1) * LANES]).astype(jnp.bfloat16)


def mix(ids, table, short_taps, conv_taps, tok_len):
    windows, rows = ids.shape
    _, vocab, panel = table.shape
    groups = conv_taps.shape[0]
    reach = 2 * tok_len
    base = jnp.pad(conv_taps[:, ::-1].astype(jnp.float32), ((0, 0), (1, reach - TAPS - 1)))
    whole = lambda shape: pl.BlockSpec(shape, lambda p: (0,) * len(shape))
    return pl.pallas_call(
        mixer_kernel,
        grid=(windows // 2,),
        in_specs=[
            pl.BlockSpec((2, 1, rows), lambda p: (p, 0, 0)),
            whole((3, vocab, panel)),
            whole((SHORT, 3, panel)),
            whole((groups, reach)),
        ],
        out_specs=pl.BlockSpec((2, tok_len, panel), lambda p: (p, 0, 0)),
        out_shape=jax.ShapeDtypeStruct((windows, tok_len, panel), jnp.bfloat16),
        scratch_shapes=[
            pltpu.VMEM((panel // LANES, LANES // GROUP * tok_len, reach), jnp.bfloat16),
            pltpu.VMEM((2, 3, rows, panel), jnp.float32),
        ],
        compiler_params=pltpu.CompilerParams(vmem_limit_bytes=40 * 1024 * 1024),
        cost_estimate=pl.CostEstimate(flops=8_000_000_000, bytes_accessed=8_000_000, transcendentals=0),
    )(ids.reshape(windows, 1, rows), table, short_taps, base)


def per_device(token_ids, embedding, norm_gain, in_proj, short_taps, conv_taps, out_proj):
    tok_len = token_ids.shape[1]
    ids = gather_ids(token_ids)
    normed = normalize_rows(embedding, norm_gain)
    table = jnp.einsum("vd,idc->ivc", normed, in_proj, preferred_element_type=jnp.float32).astype(jnp.bfloat16)
    gated = mix(ids, table, short_taps, conv_taps, tok_len)
    partial = jnp.einsum("wtc,cd->wtd", gated, out_proj, preferred_element_type=jnp.float32).astype(jnp.bfloat16)
    for bit in reversed(exchange_bits()):
        half = partial.shape[0] // 2
        got = swap(partial[half:], "fsdp", bit)
        kind = jnp.bfloat16 if half > 1 else jnp.float32
        partial = (partial[:half].astype(jnp.float32) + got.astype(jnp.float32)).astype(kind)
    residual = jnp.take(embedding, token_ids[0], axis=0, mode="clip").astype(jnp.float32)
    return (residual + partial[0]).astype(jnp.bfloat16)[None]


def solution(mesh):
    return jax.shard_map(
        per_device,
        mesh=mesh,
        in_specs=(
            P("fsdp", "ctx"),
            P(),
            P(),
            P(None, None, "fsdp"),
            P(None, None, "fsdp"),
            P("fsdp", None),
            P("fsdp", None),
        ),
        out_specs=P("fsdp", "ctx", None),
        check_vma=False,
    )
```

time: 340 us -> 231 us (0.68)
  local copies, waits for them, and re-layouts: 113 us -> 7.55 us
  waiting for transfers between devices: 141 us -> 171 us
  blocking collectives: 22.3 us -> 0 us
  matrix products: 30.5 us -> 16 us
  between operations: 13.6 us -> 0.18 us
  starting transfers between devices: 6.89 us -> 17.4 us
  Pallas kernels: 0 us -> 9.26 us
    ppermute x2 -> x9, waiting for transfers between devices: 0.66 us -> 171 us  [the longest x7 171 us: swap(): return lax.ppermute(x, axis, [(i, i ^ mask) for i in range(peers)])]
    reduce_scatter x1 -> x0, waiting for transfers between devices: 141 us -> none  [per_device(): lax.psum_scatter(jnp.einsum('wtc,cd->wtd', gated, out_proj, preferred_ele...]
    gather x5 -> x1, local copies, waits for them, and re-layouts: 103 us -> 4.93 us  [per_device(): jnp.take(embedding, token_ids[0], axis=0, mode='clip').astype(jnp.float32)]
    all_gather x1 -> x0, blocking collectives: 22.3 us -> none  [per_device(): all_ids = lax.all_gather(token_ids, 'fsdp', axis=0, tiled=True)]
    ppermute x2 -> x9, starting transfers between devices: 6.89 us -> 17.4 us  [the longest x7 10.5 us: swap(): return lax.ppermute(x, axis, [(i, i ^ mask) for i in range(peers)])]
    pallas_call x0 -> x1, Pallas kernels: none -> 9.26 us  [mix(): pl.pallas_call(mixer_kernel, grid=(windows // 2,), in_specs=[pl.BlockSpec...]
    dot_general x2 -> x1, matrix products: 19.3 us -> 11 us  [per_device(): jnp.einsum('vd,idc->ivc', normed, in_proj, preferred_element_type=jnp.flo...]
    dot_general x1, matrix products: 11.2 us -> 4.96 us  [per_device(): jnp.einsum('wtc,cd->wtd', gated, out_proj, preferred_element_type=jnp.flo...]
  transfers between devices with their start and end apart: 3 -> 9, of which waited for: 2 -> 4; matrix products, arithmetic and copies ran while one was open for 25% -> 9% of each run, Pallas kernels for 0% -> 0%
where the time goes in v1:
time: 231 us; the launch traced here: 230 us
  waiting for transfers between devices  171 us (74%)
  starting transfers between devices  17.4 us (8%)
  matrix products  16 us (7%)
  Pallas kernels  9.26 us (4%)
  other arithmetic  8.73 us (4%)
  local copies, waits for them, and re-layouts  7.55 us (3%)
    ppermute x7, waiting for transfers between devices, swap(): return lax.ppermute(x, axis, [(i, i ^ mask) for i in range(peers)])  171 us
    dot_general x1, matrix products, per_device(): jnp.einsum('vd,idc->ivc', normed, in_proj, preferred_element_type=jnp.flo...  11 us
    ppermute x7, starting transfers between devices, swap(): return lax.ppermute(x, axis, [(i, i ^ mask) for i in range(peers)])  10.5 us
    pallas_call x1, Pallas kernels, mix(): pl.pallas_call(mixer_kernel, grid=(windows // 2,), in_specs=[pl.BlockSpec...  9.26 us
    ppermute x2, starting transfers between devices, from_behind(): lax.ppermute(x, axis, [(i, i + by) for i in range(peers) if i + by < peers])  6.87 us
    dot_general x1, matrix products, per_device(): jnp.einsum('wtc,cd->wtd', gated, out_proj, preferred_element_type=jnp.flo...  4.96 us
    gather x1, local copies, waits for them, and re-layouts, per_device(): jnp.take(embedding, token_ids[0], axis=0, mode='clip').astype(jnp.float32)  4.93 us
  transfers between devices with their start and end apart: 9, of which 4 were waited for; matrix products, arithmetic and copies ran while one was open for 9% of the time, Pallas kernels for 0%

profile of v1, /device:TPU:0, one launch (start us, length us, event | category | flops | bytes accessed | tf_op | source)
XLA Modules:
  0.0 230.4 jit_solution(162011789271864892)
XLA Ops:
  0.0 2.5 %collective-permute-start.1 = (s32[1,128]{1,0:T(1,128)}, s32[1,128]{1,0:T(1,128)S(1)}, u32[]{:S(2)}, u32[]{:S(2)}) collective-permute-start(s32[1,128]{1,0:T(1,128)} %param.7), channel_id=1, source_target_pairs={{0,1},{1,2},{2,3},{4,5},{5,6},{6,7},{8,9},{9,10},{10,11},{12,13},{... | collective-permute-start | bytes 1544 | tf_op jit(solution)/shard_map/ppermute | solution.py:19
  2.5 0.7 slice.21
  3.2 4.4 %collective-permute-start = (s32[1,16]{1,0:T(1,128)S(1)}, s32[1,16]{1,0:T(1,128)S(1)}, u32[]{:S(2)}, u32[]{:S(2)}) collective-permute-start(s32[1,16]{1,0:T(1,128)S(1)} %slice.21), channel_id=1, source_target_pairs={{0,2},{1,3},{4,6},{5,7},{8,10},{9,11},{12,14},{13,15},{16,18},{17,... | collective-permute-start | bytes 200 | tf_op jit(solution)/shard_map/ppermute | solution.py:19
  7.6 3.1 %fusion = f32[512]{0:T(512)S(1)} fusion(bf16[512,4096]{1,0:T(8,128)(2,1)} %param.8), kind=kLoop, calls=%fused_computation.3 | loop fusion | flops 6290944 | bytes 4196352 | tf_op jit(solution)/shard_map/reduce_sum | solution.py:34
  10.7 0.0 collective-permute-done
  10.8 0.1 pad_add_fusion.1
  10.9 2.6 %collective-permute-start.2 = (s32[1,272]{1,0:T(1,128)S(1)}, s32[1,272]{1,0:T(1,128)S(1)}, u32[]{:S(2)}, u32[]{:S(2)}) collective-permute-start(s32[1,272]{1,0:T(1,128)S(1)} %pad_add_fusion.1), channel_id=1, source_target_pairs={{0,16},{4,20},{8,24},{12,28},{16,0},{20,4},{24,8},{28,12},{1,17},{... | collective-permute-start | bytes 3272 | tf_op jit(solution)/shard_map/ppermute | solution.py:24
  13.5 1.6 collective-permute-start.3
  15.0 0.2 collective-permute-start.4
  15.3 11.0 %fusion.13.table_ref = bf16[3,512,512]{2,1,0:T(8,128)(2,1)S(1)} fusion(bf16[3,4096,512]{2,1,0:T(8,128)(2,1)} %param.10, bf16[512,4096]{1,0:T(8,128)(2,1)} %param.8, f32[4096]{0:T(1024)S(1)} %copy-done.4, f32[512]{0:T(512)S(1)} %add_rsqrt_fusion), kind=kOutput, calls=%fused_computation.17 | convolution fusion | flops 6451625984 | bytes 18368512 | tf_op jit(solution)/shard_map/vd,idc->ivc/dot_general | solution.py:141
  26.3 0.1 rev.3
  26.4 0.0 collective-permute-done.4
  26.4 0.1 pad_add_fusion
  26.5 1.5 collective-permute-start.5
  28.0 0.1 pad_convert_fusion.base_ref
  28.1 2.0 collective-permute-done.5
  30.2 0.0 copy-start.3
  30.2 9.3 %shard_map.73 = bf16[8,128,512]{2,1,0:T(8,128)(2,1)S(1)} custom-call(s32[8,1,272]{2,1,0:T(1,128)S(1)} %reshape.22.ids_ref, bf16[3,512,512]{2,1,0:T(8,128)(2,1)S(1)} %fusion.13.table_ref, f32[3,3,512]{2,1,0:T(4,128)S(1)} %copy-done, f32[32,256]{1,0:T(8,128)S(1)} %pad_convert_fusion.base_ref), custom_call_target="tpu_custom_call" | custom-call | flops 8000000000 | bytes 8000000 | tf_op jit(solution)/shard_map/pallas_call | solution.py:117
  39.5 5.0 %convolution_convert_fusion = bf16[8,128,4096]{2,1,0:T(8,128)(2,1)S(1)} fusion(bf16[8,128,512]{2,1,0:T(8,128)(2,1)S(1)} %shard_map.73, bf16[512,4096]{1,0:T(8,128)(2,1)S(1)} %copy-done.3), kind=kOutput, calls=%fused_computation.7 | convolution fusion | flops 4299161600 | bytes 13631488 | tf_op jit(solution)/shard_map/wtc,cd->wtd/dot_general | solution.py:143
  44.4 0.5 slice.31
  44.9 1.6 collective-permute-start.6
  46.5 88.5 %collective-permute-done.6 = bf16[4,128,4096]{2,1,0:T(8,128)(2,1)S(1)} collective-permute-done((bf16[4,128,4096]{2,1,0:T(8,128)(2,1)S(1)}, bf16[4,128,4096]{2,1,0:T(8,128)(2,1)S(1)}, u32[]{:S(2)}, u32[]{:S(2)}) %collective-permute-start.6) | collective-permute-done | bytes 4194336 | tf_op jit(solution)/shard_map/ppermute | solution.py:24
  135.0 1.8 add_convert_fusion
  136.8 0.2 slice.33
  137.0 0.7 collective-permute-start.7
  137.7 43.5 %collective-permute-done.7 = bf16[2,128,4096]{2,1,0:T(8,128)(2,1)S(1)} collective-permute-done((bf16[2,128,4096]{2,1,0:T(8,128)(2,1)S(1)}, bf16[2,128,4096]{2,1,0:T(8,128)(2,1)S(1)}, u32[]{:S(2)}, u32[]{:S(2)}) %collective-permute-start.7) | collective-permute-done | bytes 2097184 | tf_op jit(solution)/shard_map/ppermute | solution.py:24
  181.3 0.9 add_convert_fusion.1
  182.2 1.0 slice.35
  183.3 2.3 collective-permute-start.8
  185.6 4.9 %gather_fusion = bf16[128,4096]{1,0:T(8,128)(2,1)S(1)} fusion(bf16[512,4096]{1,0:T(8,128)(2,1)} %param.8, s32[1024]{0:T(1024)S(1)} %pad_clamp_fusion), kind=kCustom, calls=%fused_computation | custom fusion | bytes 2097664 | tf_op jit(solution)/shard_map/jit(_take)/gather | solution.py:149
  190.5 37.2 %collective-permute-done.8 = bf16[1,128,4096]{2,1,0:T(8,128)(2,1)} collective-permute-done((bf16[1,128,4096]{2,1,0:T(8,128)(2,1)}, bf16[1,128,4096]{2,1,0:T(8,128)(2,1)}, u32[]{:S(2)}, u32[]{:S(2)}) %collective-permute-start.8) | collective-permute-done | bytes 1048608 | tf_op jit(solution)/shard_map/ppermute | solution.py:24
  227.7 2.7 %fusion.9 = bf16[1,128,4096]{2,1,0:T(8,128)(2,1)} fusion(bf16[1,128,4096]{2,1,0:T(8,128)(2,1)} %collective-permute-done.8, bf16[2,128,4096]{2,1,0:T(8,128)(2,1)S(1)} %add_convert_fusion.1, bf16[128,4096]{1,0:T(8,128)(2,1)S(1)} %gather_fusion), kind=kLoop, calls=%fused_computation.15 | loop fusion | flops 3145728 | bytes 4194304 | tf_op jit(solution)/shard_map/convert_element_type | solution.py:150
  (18 shorter events, 0.1 us)
Async XLA Ops:
  0.0 10.8 %copy-start.2 = (s32[1,128]{1,0:T(1,128)S(1)}, s32[1,128]{1,0:T(1,128)}, u32[]{:S(2)}) copy-start(s32[1,128]{1,0:T(1,128)} %param.7) | copy-start | bytes 1540
  0.0 15.3 %copy-start.4 = (f32[4096]{0:T(1024)S(1)}, f32[4096]{0:T(1024)}, u32[]{:S(2)}) copy-start(f32[4096]{0:T(1024)} %param.9) | copy-start | bytes 49156
  0.0 10.7 %collective-permute-start.1 = (s32[1,128]{1,0:T(1,128)}, s32[1,128]{1,0:T(1,128)S(1)}, u32[]{:S(2)}, u32[]{:S(2)}) collective-permute-start(s32[1,128]{1,0:T(1,128)} %param.7), channel_id=1, source_target_pairs={{0,1},{1,2},{2,3},{4,5},{5,6},{6,7},{8,9},{9,10},{10,11},{12,13},{... | collective-permute-start | bytes 1544 | tf_op jit(solution)/shard_map/ppermute | solution.py:19
  3.2 7.5 %collective-permute-start = (s32[1,16]{1,0:T(1,128)S(1)}, s32[1,16]{1,0:T(1,128)S(1)}, u32[]{:S(2)}, u32[]{:S(2)}) collective-permute-start(s32[1,16]{1,0:T(1,128)S(1)} %slice.21), channel_id=1, source_target_pairs={{0,2},{1,3},{4,6},{5,7},{8,10},{9,11},{12,14},{13,15},{16,18},{17,... | collective-permute-start | bytes 200 | tf_op jit(solution)/shard_map/ppermute | solution.py:19
  10.8 15.4 %copy-start.1 = (bf16[32,128]{1,0:T(8,128)(2,1)S(1)}, bf16[32,128]{1,0:T(8,128)(2,1)}, u32[]{:S(2)}) copy-start(bf16[32,128]{1,0:T(8,128)(2,1)} %param.12) | copy-start | bytes 24580
  10.9 19.3 %copy-start = (f32[3,3,512]{2,1,0:T(4,128)S(1)}, f32[3,3,512]{2,1,0:T(4,128)}, u32[]{:S(2)}) copy-start(f32[3,3,512]{2,1,0:T(4,128)} %short_ref.1) | copy-start | bytes 55300
  10.9 15.5 %collective-permute-start.2 = (s32[1,272]{1,0:T(1,128)S(1)}, s32[1,272]{1,0:T(1,128)S(1)}, u32[]{:S(2)}, u32[]{:S(2)}) collective-permute-start(s32[1,272]{1,0:T(1,128)S(1)} %pad_add_fusion.1), channel_id=1, source_target_pairs={{0,16},{4,20},{8,24},{12,28},{16,0},{20,4},{24,8},{28,12},{1,17},{... | collective-permute-start | bytes 3272 | tf_op jit(solution)/shard_map/ppermute | solution.py:24
  13.5 12.9 %collective-permute-start.3 = (s32[1,272]{1,0:T(1,128)S(1)}, s32[1,272]{1,0:T(1,128)S(1)}, u32[]{:S(2)}, u32[]{:S(2)}) collective-permute-start(s32[1,272]{1,0:T(1,128)S(1)} %pad_add_fusion.1), channel_id=1, source_target_pairs={{0,8},{4,12},{8,0},{12,4},{16,24},{20,28},{24,16},{28,20},{1,9},{5... | collective-permute-start | bytes 3272 | tf_op jit(solution)/shard_map/ppermute | solution.py:24
  15.0 11.3 %collective-permute-start.4 = (s32[1,272]{1,0:T(1,128)S(1)}, s32[1,272]{1,0:T(1,128)S(1)}, u32[]{:S(2)}, u32[]{:S(2)}) collective-permute-start(s32[1,272]{1,0:T(1,128)S(1)} %pad_add_fusion.1), channel_id=1, source_target_pairs={{0,24},{4,28},{8,16},{12,20},{16,8},{20,12},{24,0},{28,4},{1,25},{... | collective-permute-start | bytes 3272 | tf_op jit(solution)/shard_map/ppermute | solution.py:24
  26.5 3.6 %collective-permute-start.5 = (s32[4,272]{1,0:T(4,128)S(1)}, s32[4,272]{1,0:T(4,128)S(1)}, u32[]{:S(2)}, u32[]{:S(2)}) collective-permute-start(s32[4,272]{1,0:T(4,128)S(1)} %pad_add_fusion), channel_id=1, source_target_pairs={{0,4},{4,0},{8,12},{12,8},{16,20},{20,16},{24,28},{28,24},{1,5},{5... | collective-permute-start | bytes 13064 | tf_op jit(solution)/shard_map/ppermute | solution.py:24
  30.2 9.3 %copy-start.3 = (bf16[512,4096]{1,0:T(8,128)(2,1)S(1)}, bf16[512,4096]{1,0:T(8,128)(2,1)}, u32[]{:S(2)}) copy-start(bf16[512,4096]{1,0:T(8,128)(2,1)} %param.13) | copy-start | bytes 12582916
  44.9 90.1 %collective-permute-start.6 = (bf16[4,128,4096]{2,1,0:T(8,128)(2,1)S(1)}, bf16[4,128,4096]{2,1,0:T(8,128)(2,1)S(1)}, u32[]{:S(2)}, u32[]{:S(2)}) collective-permute-start(bf16[4,128,4096]{2,1,0:T(8,128)(2,1)S(1)} %slice.31), channel_id=1, source_target_pairs={{0,4},{4,0},{8,12},{12,8},{16,20},{20,16},{24,28},{28,24},{1,5},{5... | collective-permute-start | bytes 12582920 | tf_op jit(solution)/shard_map/ppermute | solution.py:24
  137.0 44.2 %collective-permute-start.7 = (bf16[2,128,4096]{2,1,0:T(8,128)(2,1)S(1)}, bf16[2,128,4096]{2,1,0:T(8,128)(2,1)S(1)}, u32[]{:S(2)}, u32[]{:S(2)}) collective-permute-start(bf16[2,128,4096]{2,1,0:T(8,128)(2,1)S(1)} %slice.33), channel_id=1, source_target_pairs={{0,8},{4,12},{8,0},{12,4},{16,24},{20,28},{24,16},{28,20},{1,9},{5... | collective-permute-start | bytes 6291464 | tf_op jit(solution)/shard_map/ppermute | solution.py:24
  183.3 44.5 %collective-permute-start.8 = (bf16[1,128,4096]{2,1,0:T(8,128)(2,1)}, bf16[1,128,4096]{2,1,0:T(8,128)(2,1)}, u32[]{:S(2)}, u32[]{:S(2)}) collective-permute-start(bf16[1,128,4096]{2,1,0:T(8,128)(2,1)} %slice.35), channel_id=1, source_target_pairs={{0,16},{4,20},{8,24},{12,28},{16,0},{20,4},{24,8},{28,12},{1,17},{... | collective-permute-start | bytes 3145736 | tf_op jit(solution)/shard_map/ppermute | solution.py:24

commit v2 on v1

--- a/solution.py
+++ b/solution.py
@@ -12,6 +12,7 @@
 SHORT = 3
 LANES = 128
 LEAD = 16
+CHUNKS = 4
 
 
 def from_behind(x, axis, by):
@@ -55,23 +56,38 @@
     return ids
 
 
-def mixer_kernel(ids_ref, table_ref, short_ref, base_ref, gated_ref, toeplitz, held):
+def toeplitz_kernel(base_ref, out_ref):
+    per_tile = LANES // GROUP
+    tok_len = out_ref.shape[1] // per_tile
+    reach = out_ref.shape[2]
+    for k in range(per_tile):
+        wide = jnp.broadcast_to(base_ref[k : k + 1, :], (tok_len, reach))
+        shifted = pltpu.roll(wide, 0, 1, stride=1, stride_axis=0)
+        out_ref[0, pl.ds(k * tok_len, tok_len), :] = shifted.astype(jnp.bfloat16)
+
+
+def build_toeplitz(conv_taps, tok_len):
+    reach = 2 * tok_len
+    per_tile = LANES // GROUP
+    tiles = conv_taps.shape[0] // per_tile
+    base = jnp.pad(conv_taps[:, ::-1].astype(jnp.float32), ((0, 0), (1, reach - TAPS - 1)))
+    return pl.pallas_call(
+        toeplitz_kernel,
+        grid=(tiles,),
+        in_specs=[pl.BlockSpec((per_tile, reach), lambda i: (i, 0))],
+        out_specs=pl.BlockSpec((1, per_tile * tok_len, reach), lambda i: (i, 0, 0)),
+        out_shape=jax.ShapeDtypeStruct((tiles, per_tile * tok_len, reach), jnp.bfloat16),
+        cost_estimate=pl.CostEstimate(flops=0, bytes_accessed=4_000_000, transcendentals=0),
+    )(base)
+
+
+def mixer_kernel(ids_ref, table_ref, short_ref, toeplitz, gated_ref, held):
     tok_len, panel = gated_ref.shape[1:]
     vocab = table_ref.shape[1]
     rows = ids_ref.shape[2]
     reach = 2 * tok_len
     tiles = panel // LANES
     per_tile = LANES // GROUP
-
-    @pl.when(pl.program_id(0) == 0)
-    def _():
-        for tile in range(tiles):
-            for k in range(per_tile):
-                g = tile * per_tile + k
-                wide = jnp.broadcast_to(base_ref[pl.ds(g, 1), :], (tok_len, reach))
-                shifted = pltpu.roll(wide, 0, 1, stride=1, stride_axis=0)
-                toeplitz[tile, pl.ds(k * tok_len, tok_len), :] = shifted.astype(jnp.bfloat16)
-
     names = lax.broadcasted_iota(jnp.int32, (vocab, rows), 0)
     lane_group = lax.broadcasted_iota(jnp.int32, (tok_len, 2 * LANES), 1) % LANES // GROUP
     for v in range(2):
@@ -107,47 +123,129 @@
             gated_ref[v, :, cols] = (query * filtered[:, v * LANES : (v + 1) * LANES]).astype(jnp.bfloat16)
 
 
-def mix(ids, table, short_taps, conv_taps, tok_len):
+def mix(ids, table, short_taps, toeplitz, tok_len):
     windows, rows = ids.shape
     _, vocab, panel = table.shape
-    groups = conv_taps.shape[0]
-    reach = 2 * tok_len
-    base = jnp.pad(conv_taps[:, ::-1].astype(jnp.float32), ((0, 0), (1, reach - TAPS - 1)))
-    whole = lambda shape: pl.BlockSpec(shape, lambda p: (0,) * len(shape))
+    whole = lambda array: pl.BlockSpec(array.shape, lambda p: (0,) * array.ndim)
     return pl.pallas_call(
         mixer_kernel,
         grid=(windows // 2,),
         in_specs=[
             pl.BlockSpec((2, 1, rows), lambda p: (p, 0, 0)),
-            whole((3, vocab, panel)),
-            whole((SHORT, 3, panel)),
-            whole((groups, reach)),
+            whole(table),
+            whole(short_taps),
+            whole(toeplitz),
         ],
         out_specs=pl.BlockSpec((2, tok_len, panel), lambda p: (p, 0, 0)),
         out_shape=jax.ShapeDtypeStruct((windows, tok_len, panel), jnp.bfloat16),
-        scratch_shapes=[
-            pltpu.VMEM((panel // LANES, LANES // GROUP * tok_len, reach), jnp.bfloat16),
-            pltpu.VMEM((2, 3, rows, panel), jnp.float32),
-        ],
+        scratch_shapes=[pltpu.VMEM((2, 3, rows, panel), jnp.float32)],
         compiler_params=pltpu.CompilerParams(vmem_limit_bytes=40 * 1024 * 1024),
-        cost_estimate=pl.CostEstimate(flops=8_000_000_000, bytes_accessed=8_000_000, transcendentals=0),
-    )(ids.reshape(windows, 1, rows), table, short_taps, base)
+        cost_estimate=pl.CostEstimate(flops=4_000_000_000, bytes_accessed=4_000_000, transcendentals=0),
+    )(ids.reshape(windows, 1, rows), table, short_taps, toeplitz)
+
+
+def panel_kernel(place_ref, mine_ref, other_ref, w0, w1, w2, w3, even_ref, odd_ref, out_ref):
+    own = (w0, w1, w2, w3)
+    for k in range(4):
+        beside = (even_ref, odd_ref)[k % 2]
+        total = jnp.dot(mine_ref[...], own[k][...], preferred_element_type=jnp.float32)
+        total += jnp.dot(other_ref[...], beside[k // 2], preferred_element_type=jnp.float32)
+        out_ref[k] = total.astype(out_ref.dtype)
+
+
+def panel(place, mine, other, out_proj, even, odd, chunk):
+    count, tok_len, depth = mine.shape
+    rows = count * tok_len
+    quarter = even.shape[2]
+    whole = lambda shape: pl.BlockSpec(shape, lambda s, place: (0,) * len(shape))
+    at = lambda k: pl.BlockSpec((depth, quarter), lambda s, place: (0, chunk * 4 + (place[0] ^ k)))
+    return pl.pallas_call(
+        panel_kernel,
+        grid_spec=pltpu.PrefetchScalarGridSpec(
+            num_scalar_prefetch=1,
+            grid=(1,),
+            in_specs=[whole((rows, depth)), whole((rows, depth))]
+            + [at(k) for k in range(4)]
+            + [whole(even.shape), whole(odd.shape)],
+            out_specs=whole((4, rows, quarter)),
+        ),
+        out_shape=jax.ShapeDtypeStruct((4, rows, quarter), jnp.bfloat16),
+        compiler_params=pltpu.CompilerParams(vmem_limit_bytes=32 * 1024 * 1024),
+        cost_estimate=pl.CostEstimate(
+            flops=16 * rows * depth * quarter, bytes_accessed=16 * depth * quarter, transcendentals=0
+        ),
+    )(
+        place,
+        mine.reshape(rows, depth),
+        other.reshape(rows, depth),
+        *[out_proj] * 4,
+        even,
+        odd,
+    ).reshape(4, count, tok_len, quarter)
+
+
+def add(a, b):
+    return (a.astype(jnp.float32) + b.astype(jnp.float32)).astype(jnp.bfloat16)
+
+
+def place_kernel(place_ref, so_far_ref, near_ref, far_ref, out_ref):
+    total = near_ref[0, 0].astype(jnp.float32) + far_ref[0, 0].astype(jnp.float32)
+    out_ref[...] = (so_far_ref[...].astype(jnp.float32) + total).astype(jnp.bfloat16)
+
+
+def place_quarters(place, so_far, near, far, chunk):
+    _, _, tok_len, quarter = near.shape
+    at = pl.BlockSpec((tok_len, quarter), lambda k, place: (0, chunk * 4 + (place[0] ^ k)))
+    one = pl.BlockSpec((1, 1, tok_len, quarter), lambda k, place: (k, 0, 0, 0))
+    return pl.pallas_call(
+        place_kernel,
+        grid_spec=pltpu.PrefetchScalarGridSpec(
+            num_scalar_prefetch=1, grid=(4,), in_specs=[at, one, one], out_specs=at
+        ),
+        out_shape=jax.ShapeDtypeStruct(so_far.shape, so_far.dtype),
+        input_output_aliases={1: 0},
+        cost_estimate=pl.CostEstimate(flops=0, bytes_accessed=16 * tok_len * quarter, transcendentals=0),
+    )(place, so_far, near, far)
 
 
 def per_device(token_ids, embedding, norm_gain, in_proj, short_taps, conv_taps, out_proj):
     tok_len = token_ids.shape[1]
+    depth, width = out_proj.shape
+    place = lax.axis_index("ctx")
+    quarter = width // CHUNKS // 4
+    bits = exchange_bits()
+
+    beside = []
+    for j in range(CHUNKS):
+        piece = lax.dynamic_slice_in_dim(out_proj, (j * 4 + place) * quarter, quarter, axis=1)
+        piece = swap(piece, "fsdp", bits[-2])
+        even = jnp.stack([piece, swap(piece, "ctx", 2)])
+        beside.append((even, swap(even, "ctx", 1)))
+
     ids = gather_ids(token_ids)
+    toeplitz = build_toeplitz(conv_taps, tok_len)
     normed = normalize_rows(embedding, norm_gain)
     table = jnp.einsum("vd,idc->ivc", normed, in_proj, preferred_element_type=jnp.float32).astype(jnp.bfloat16)
-    gated = mix(ids, table, short_taps, conv_taps, tok_len)
-    partial = jnp.einsum("wtc,cd->wtd", gated, out_proj, preferred_element_type=jnp.float32).astype(jnp.bfloat16)
-    for bit in reversed(exchange_bits()):
-        half = partial.shape[0] // 2
-        got = swap(partial[half:], "fsdp", bit)
-        kind = jnp.bfloat16 if half > 1 else jnp.float32
-        partial = (partial[:half].astype(jnp.float32) + got.astype(jnp.float32)).astype(kind)
-    residual = jnp.take(embedding, token_ids[0], axis=0, mode="clip").astype(jnp.float32)
-    return (residual + partial[0]).astype(jnp.bfloat16)[None]
+
+    half = ids.shape[0] // 2
+    mine, other = [], []
+    for first in (half, 0):
+        gated = mix(ids[first : first + half], table, short_taps, toeplitz, tok_len)
+        mine.append(gated[: half // 2])
+        other.append(swap(gated[half // 2 :], "fsdp", bits[-2]))
+
+    at = place.reshape(1).astype(jnp.int32)
+    out = jnp.take(embedding, token_ids[0], axis=0, mode="clip")
+    for j in range(CHUNKS):
+        away = panel(at, mine[0], other[0], out_proj, *beside[j], j)
+        got = swap(away, "fsdp", bits[-1])
+        total = add(panel(at, mine[1], other[1], out_proj, *beside[j], j), got)
+        for bit in reversed(bits[:-2]):
+            half = total.shape[1] // 2
+            got = swap(total[:, half:], "fsdp", bit)
+            total = add(total[:, :half], got) if half > 1 else total[:, :half]
+        out = place_quarters(at, out, total, got, j)
+    return out[None]
 
 
 def solution(mesh):

time: 231 us -> 154 us (0.67)
  waiting for transfers between devices: 171 us -> 57 us
  Pallas kernels: 9.26 us -> 30.9 us
  starting transfers between devices: 17.4 us -> 34.5 us
  local copies, waits for them, and re-layouts: 7.55 us -> 15.6 us
  matrix products: 16 us -> 9.9 us
  other arithmetic: 8.73 us -> 4.93 us
    ppermute x7 -> x26, waiting for transfers between devices: 171 us -> 56.9 us  [swap(): return lax.ppermute(x, axis, [(i, i ^ mask) for i in range(peers)])]
    pallas_call x0 -> x13, Pallas kernels: none -> 21.7 us  [the longest x4 12.6 us: place_quarters(): pl.pallas_call(place_kernel, grid_spec=pltpu.PrefetchScalarGridSpec(num_s...]
    ppermute x7 -> x26, starting transfers between devices: 10.5 us -> 29.2 us  [swap(): return lax.ppermute(x, axis, [(i, i ^ mask) for i in range(peers)])]
    dot_general x1 -> x0, matrix products: 4.96 us -> none  [per_device(): jnp.einsum('wtc,cd->wtd', gated, out_proj, preferred_element_type=jnp.flo...]
    convert_element_type x3 -> x4, other arithmetic: 5.4 us -> 0.56 us  [add(): return (a.astype(jnp.float32) + b.astype(jnp.float32)).astype(jnp.bfloat16)]
    unnamed x10 -> x22, local copies, waits for them, and re-layouts: 0.02 us -> 4.61 us
    pallas_call x1 -> x2, Pallas kernels: 9.26 us -> 9.23 us  [mix(): pl.pallas_call(mixer_kernel, grid=(windows // 2,), in_specs=[pl.BlockSpec...]
  transfers between devices with their start and end apart: 9 -> 28, of which waited for: 4 -> 9; matrix products, arithmetic and copies ran while one was open for 9% -> 16% of each run, Pallas kernels for 0% -> 18%
where the time goes in v2:
time: 154 us; the launch traced here: 153 us
  waiting for transfers between devices  57 us (37%)
  starting transfers between devices  34.5 us (22%)
  Pallas kernels  30.9 us (20%)
  local copies, waits for them, and re-layouts  15.6 us (10%)
  matrix products  9.9 us (6%)
  other arithmetic  4.93 us (3%)
    ppermute x26, waiting for transfers between devices, swap(): return lax.ppermute(x, axis, [(i, i ^ mask) for i in range(peers)])  56.9 us
    ppermute x26, starting transfers between devices, swap(): return lax.ppermute(x, axis, [(i, i ^ mask) for i in range(peers)])  29.2 us
    pallas_call x4, Pallas kernels, place_quarters(): pl.pallas_call(place_kernel, grid_spec=pltpu.PrefetchScalarGridSpec(num_s...  12.6 us
    dot_general x1, matrix products, per_device(): jnp.einsum('vd,idc->ivc', normed, in_proj, preferred_element_type=jnp.flo...  9.9 us
    pallas_call x2, Pallas kernels, mix(): pl.pallas_call(mixer_kernel, grid=(windows // 2,), in_specs=[pl.BlockSpec...  9.23 us
    gather x1, local copies, waits for them, and re-layouts, per_device(): out = jnp.take(embedding, token_ids[0], axis=0, mode='clip')  5.9 us
    pallas_call x8, Pallas kernels, panel(): pl.pallas_call(panel_kernel, grid_spec=pltpu.PrefetchScalarGridSpec(num_s...  5.73 us
    ppermute x2, starting transfers between devices, from_behind(): lax.ppermute(x, axis, [(i, i + by) for i in range(peers) if i + by < peers])  5.29 us
  transfers between devices with their start and end apart: 28, of which 9 were waited for; matrix products, arithmetic and copies ran while one was open for 16% of the time, Pallas kernels for 18%

profile of v2, /device:TPU:0, one launch (start us, length us, event | category | flops | bytes accessed | tf_op | source)
XLA Modules:
  0.0 153.1 jit_solution(69167716126638236)
XLA Ops:
  1.3 3.1 %collective-permute-start.23 = (bf16[512,256]{1,0:T(8,128)(2,1)S(1)}, bf16[512,256]{1,0:T(8,128)(2,1)S(1)}, u32[]{:S(2)}, u32[]{:S(2)}) collective-permute-start(bf16[512,256]{1,0:T(8,128)(2,1)S(1)} %get-tuple-element.5), channel_id=1, source_target_pairs={{0,8},{4,12},{8,0},{12,4},{16,24},{20,28},{24,16},{28,20},{1,9},{5... | collective-permute-start | bytes 786440 | tf_op jit(solution)/shard_map/ppermute | solution.py:25
  6.6 3.8 %collective-permute-start = (s32[1,16]{1,0:T(1,128)S(1)}, s32[1,16]{1,0:T(1,128)S(1)}, u32[]{:S(2)}, u32[]{:S(2)}) collective-permute-start(s32[1,16]{1,0:T(1,128)S(1)} %slice.39), channel_id=1, source_target_pairs={{0,2},{1,3},{4,6},{5,7},{8,10},{9,11},{12,14},{13,15},{16,18},{17,... | collective-permute-start | bytes 200 | tf_op jit(solution)/shard_map/ppermute | solution.py:20
  10.9 3.2 %fusion = f32[512]{0:T(512)S(1)} fusion(bf16[512,4096]{1,0:T(8,128)(2,1)} %param.8), kind=kLoop, calls=%fused_computation.3 | loop fusion | flops 6290944 | bytes 4196352 | tf_op jit(solution)/shard_map/reduce_sum | solution.py:35
  14.4 9.9 %fusion.11.table_ref = bf16[3,512,512]{2,1,0:T(8,128)(2,1)S(1)} fusion(bf16[3,4096,512]{2,1,0:T(8,128)(2,1)} %param.10, bf16[512,4096]{1,0:T(8,128)(2,1)S(1)} %copy-done.3, f32[4096]{0:T(1024)S(1)} %copy-done.10, f32[512]{0:T(512)S(1)} %add_rsqrt_fusion), kind=kOutput, calls=%fused_computation.11 | convolution fusion | flops 6451625984 | bytes 18368512 | tf_op jit(solution)/shard_map/vd,idc->ivc/dot_general | solution.py:228
  24.5 2.6 %collective-permute-start.2 = (s32[1,272]{1,0:T(1,128)S(1)}, s32[1,272]{1,0:T(1,128)S(1)}, u32[]{:S(2)}, u32[]{:S(2)}) collective-permute-start(s32[1,272]{1,0:T(1,128)S(1)} %pad_add_fusion.1), channel_id=1, source_target_pairs={{0,16},{4,20},{8,24},{12,28},{16,0},{20,4},{24,8},{28,12},{1,17},{... | collective-permute-start | bytes 3272 | tf_op jit(solution)/shard_map/ppermute | solution.py:25
  27.1 1.6 %collective-permute-start.3 = (s32[1,272]{1,0:T(1,128)S(1)}, s32[1,272]{1,0:T(1,128)S(1)}, u32[]{:S(2)}, u32[]{:S(2)}) collective-permute-start(s32[1,272]{1,0:T(1,128)S(1)} %pad_add_fusion.1), channel_id=1, source_target_pairs={{0,8},{4,12},{8,0},{12,4},{16,24},{20,28},{24,16},{28,20},{1,9},{5... | collective-permute-start | bytes 3272 | tf_op jit(solution)/shard_map/ppermute | solution.py:25
  29.6 3.4 %shard_map.73.toeplitz = bf16[4,1024,256]{2,1,0:T(8,128)(2,1)} custom-call(f32[32,256]{1,0:T(8,128)} %pad_convert_fusion.base_ref), custom_call_target="tpu_custom_call" | custom-call | bytes 4000000 | tf_op jit(solution)/shard_map/pallas_call | solution.py:74
  35.1 1.5 collective-permute-start.9
  36.7 2.0 %collective-permute-done.9 = s32[4,272]{1,0:T(4,128)S(1)} collective-permute-done((s32[4,272]{1,0:T(4,128)S(1)}, s32[4,272]{1,0:T(4,128)S(1)}, u32[]{:S(2)}, u32[]{:S(2)}) %collective-permute-start.9) | collective-permute-done | bytes 4384 | tf_op jit(solution)/shard_map/ppermute | solution.py:25
  38.8 1.6 %copy-done.1 = bf16[4,1024,256]{2,1,0:T(8,128)(2,1)S(1)} copy-done((bf16[4,1024,256]{2,1,0:T(8,128)(2,1)S(1)}, bf16[4,1024,256]{2,1,0:T(8,128)(2,1)}, u32[]{:S(2)}) %copy-start.1) | copy-done | bytes 2097176
  40.4 4.5 %shard_map.76 = bf16[4,128,512]{2,1,0:T(8,128)(2,1)S(1)} custom-call(s32[4,1,272]{2,1,0:T(1,128)S(1)} %reshape.71.ids_ref, bf16[3,512,512]{2,1,0:T(8,128)(2,1)S(1)} %fusion.11.table_ref, f32[3,3,512]{2,1,0:T(4,128)S(1)} %copy-done.2, bf16[4,1024,256]{2,1,0:T(8,128)(2,1)S(1)} %copy-done.1), custom_call_target="tpu_custom_call" | custom-call | flops 4000000000 | bytes 4000000 | tf_op jit(solution)/shard_map/pallas_call | solution.py:130
  44.9 2.1 %collective-permute-start.19 = (bf16[512,256]{1,0:T(8,128)(2,1)S(1)}, bf16[512,256]{1,0:T(8,128)(2,1)S(1)}, u32[]{:S(2)}, u32[]{:S(2)}) collective-permute-start(bf16[512,256]{1,0:T(8,128)(2,1)S(1)} %collective-permute-done.18), channel_id=1, source_target_pairs={{0,2},{1,3},{2,0},{3,1},{4,6},{5,7},{6,4},{7,5},{8,10},{9,11},{10,... | collective-permute-start | bytes 786440 | tf_op jit(solution)/shard_map/ppermute | solution.py:25
  47.9 1.9 %collective-permute-start.7 = (bf16[512,256]{1,0:T(8,128)(2,1)S(1)}, bf16[512,256]{1,0:T(8,128)(2,1)S(1)}, u32[]{:S(2)}, u32[]{:S(2)}) collective-permute-start(bf16[512,256]{1,0:T(8,128)(2,1)S(1)} %collective-permute-done.6), channel_id=1, source_target_pairs={{0,2},{1,3},{2,0},{3,1},{4,6},{5,7},{6,4},{7,5},{8,10},{9,11},{10,... | collective-permute-start | bytes 786440 | tf_op jit(solution)/shard_map/ppermute | solution.py:25
  50.0 4.3 %collective-permute-done.19 = bf16[512,256]{1,0:T(8,128)(2,1)S(1)} collective-permute-done((bf16[512,256]{1,0:T(8,128)(2,1)S(1)}, bf16[512,256]{1,0:T(8,128)(2,1)S(1)}, u32[]{:S(2)}, u32[]{:S(2)}) %collective-permute-start.19) | collective-permute-done | bytes 262176 | tf_op jit(solution)/shard_map/ppermute | solution.py:25
  54.4 4.8 %collective-permute-done.14 = bf16[512,256]{1,0:T(8,128)(2,1)S(1)} collective-permute-done((bf16[512,256]{1,0:T(8,128)(2,1)S(1)}, bf16[512,256]{1,0:T(8,128)(2,1)S(1)}, u32[]{:S(2)}, u32[]{:S(2)}) %collective-permute-start.14) | collective-permute-done | bytes 262176 | tf_op jit(solution)/shard_map/ppermute | solution.py:25
  59.3 2.7 %collective-permute-done.7 = bf16[512,256]{1,0:T(8,128)(2,1)S(1)} collective-permute-done((bf16[512,256]{1,0:T(8,128)(2,1)S(1)}, bf16[512,256]{1,0:T(8,128)(2,1)S(1)}, u32[]{:S(2)}, u32[]{:S(2)}) %collective-permute-start.7) | collective-permute-done | bytes 262176 | tf_op jit(solution)/shard_map/ppermute | solution.py:25
  62.2 4.7 %shard_map.74 = bf16[4,128,512]{2,1,0:T(8,128)(2,1)S(1)} custom-call(s32[4,1,272]{2,1,0:T(1,128)S(1)} %copy.12.ids_ref, bf16[3,512,512]{2,1,0:T(8,128)(2,1)S(1)} %fusion.11.table_ref, f32[3,3,512]{2,1,0:T(4,128)S(1)} %copy-done.2, bf16[4,1024,256]{2,1,0:T(8,128)(2,1)S(1)} %copy-done.1), custom_call_target="tpu_custom_call" | custom-call | flops 4000000000 | bytes 4000000 | tf_op jit(solution)/shard_map/pallas_call | solution.py:130
  67.6 1.6 %collective-permute-start.21 = (bf16[4,2,128,256]{3,2,1,0:T(8,128)(2,1)S(1)}, bf16[4,2,128,256]{3,2,1,0:T(8,128)(2,1)S(1)}, u32[]{:S(2)}, u32[]{:S(2)}) collective-permute-start(bf16[4,2,128,256]{3,2,1,0:T(8,128)(2,1)S(1)} %bitcast.60), channel_id=1, source_target_pairs={{0,4},{4,0},{8,12},{12,8},{16,20},{20,16},{24,28},{28,24},{1,5},{5... | collective-permute-start | bytes 1572872 | tf_op jit(solution)/shard_map/ppermute | solution.py:25
  72.0 1.6 %collective-permute-start.16 = (bf16[4,2,128,256]{3,2,1,0:T(8,128)(2,1)S(1)}, bf16[4,2,128,256]{3,2,1,0:T(8,128)(2,1)S(1)}, u32[]{:S(2)}, u32[]{:S(2)}) collective-permute-start(bf16[4,2,128,256]{3,2,1,0:T(8,128)(2,1)S(1)} %bitcast.62), channel_id=1, source_target_pairs={{0,4},{4,0},{8,12},{12,8},{16,20},{20,16},{24,28},{28,24},{1,5},{5... | collective-permute-start | bytes 1572872 | tf_op jit(solution)/shard_map/ppermute | solution.py:25
  74.9 2.8 %collective-permute-done.5 = bf16[2,128,512]{2,1,0:T(8,128)(2,1)S(1)} collective-permute-done((bf16[2,128,512]{2,1,0:T(8,128)(2,1)S(1)}, bf16[2,128,512]{2,1,0:T(8,128)(2,1)S(1)}, u32[]{:S(2)}, u32[]{:S(2)}) %collective-permute-start.5) | collective-permute-done | bytes 262176 | tf_op jit(solution)/shard_map/ppermute | solution.py:25
  80.6 1.8 %collective-permute-done.21 = bf16[4,2,128,256]{3,2,1,0:T(8,128)(2,1)S(1)} collective-permute-done((bf16[4,2,128,256]{3,2,1,0:T(8,128)(2,1)S(1)}, bf16[4,2,128,256]{3,2,1,0:T(8,128)(2,1)S(1)}, u32[]{:S(2)}, u32[]{:S(2)}) %collective-permute-start.21) | collective-permute-done | bytes 524320 | tf_op jit(solution)/shard_map/ppermute | solution.py:25
  83.3 2.2 %collective-permute-start.22 = (bf16[4,1,128,256]{3,2,1,0:T(8,128)(2,1)S(1)}, bf16[4,1,128,256]{3,2,1,0:T(8,128)(2,1)S(1)}, u32[]{:S(2)}, u32[]{:S(2)}) collective-permute-start(bf16[4,1,128,256]{3,2,1,0:T(8,128)(2,1)S(1)} %get-tuple-element.11), channel_id=1, source_target_pairs={{0,16},{4,20},{8,24},{12,28},{16,0},{20,4},{24,8},{28,12},{1,17},{... | collective-permute-start | bytes 786440 | tf_op jit(solution)/shard_map/ppermute | solution.py:25
  85.5 19.4 %collective-permute-done.16 = bf16[4,2,128,256]{3,2,1,0:T(8,128)(2,1)S(1)} collective-permute-done((bf16[4,2,128,256]{3,2,1,0:T(8,128)(2,1)S(1)}, bf16[4,2,128,256]{3,2,1,0:T(8,128)(2,1)S(1)}, u32[]{:S(2)}, u32[]{:S(2)}) %collective-permute-start.16) | collective-permute-done | bytes 524320 | tf_op jit(solution)/shard_map/ppermute | solution.py:25
  105.8 2.2 %collective-permute-start.17 = (bf16[4,1,128,256]{3,2,1,0:T(8,128)(2,1)S(1)}, bf16[4,1,128,256]{3,2,1,0:T(8,128)(2,1)S(1)}, u32[]{:S(2)}, u32[]{:S(2)}) collective-permute-start(bf16[4,1,128,256]{3,2,1,0:T(8,128)(2,1)S(1)} %get-tuple-element.13), channel_id=1, source_target_pairs={{0,16},{4,20},{8,24},{12,28},{16,0},{20,4},{24,8},{28,12},{1,17},{... | collective-permute-start | bytes 786440 | tf_op jit(solution)/shard_map/ppermute | solution.py:25
  108.0 7.7 %collective-permute-done.11 = bf16[4,2,128,256]{3,2,1,0:T(8,128)(2,1)S(1)} collective-permute-done((bf16[4,2,128,256]{3,2,1,0:T(8,128)(2,1)S(1)}, bf16[4,2,128,256]{3,2,1,0:T(8,128)(2,1)S(1)}, u32[]{:S(2)}, u32[]{:S(2)}) %collective-permute-start.11) | collective-permute-done | bytes 524320 | tf_op jit(solution)/shard_map/ppermute | solution.py:25
  116.6 2.2 %collective-permute-start.12 = (bf16[4,1,128,256]{3,2,1,0:T(8,128)(2,1)S(1)}, bf16[4,1,128,256]{3,2,1,0:T(8,128)(2,1)S(1)}, u32[]{:S(2)}, u32[]{:S(2)}) collective-permute-start(bf16[4,1,128,256]{3,2,1,0:T(8,128)(2,1)S(1)} %get-tuple-element.15), channel_id=1, source_target_pairs={{0,16},{4,20},{8,24},{12,28},{16,0},{20,4},{24,8},{28,12},{1,17},{... | collective-permute-start | bytes 786440 | tf_op jit(solution)/shard_map/ppermute | solution.py:25
  120.4 5.9 %gather_fusion = bf16[128,4096]{1,0:T(8,128)(2,1)} fusion(bf16[512,4096]{1,0:T(8,128)(2,1)} %param.8, s32[1024]{0:T(1024)S(1)} %pad_clamp_fusion), kind=kCustom, calls=%fused_computation | custom fusion | bytes 2097664 | tf_op jit(solution)/shard_map/jit(_take)/gather | solution.py:238
  126.3 11.4 %collective-permute-done.12.far_ref = bf16[4,1,128,256]{3,2,1,0:T(8,128)(2,1)S(1)} collective-permute-done((bf16[4,1,128,256]{3,2,1,0:T(8,128)(2,1)S(1)}, bf16[4,1,128,256]{3,2,1,0:T(8,128)(2,1)S(1)}, u32[]{:S(2)}, u32[]{:S(2)}) %collective-permute-start.12) | collective-permute-done | bytes 262176 | tf_op jit(solution)/shard_map/ppermute | solution.py:25
  138.4 3.1 %shard_map.78.so_far_ref = bf16[128,4096]{1,0:T(8,128)(2,1)} custom-call(s32[1]{0:T(128)} %bitcast.place_ref, bf16[128,4096]{1,0:T(8,128)(2,1)} %gather_fusion, bf16[4,1,128,256]{3,2,1,0:T(8,128)(2,1)} %get-tuple-element.16.near_ref, bf16[4,1,128,256]{3,2,1,0:T(8,128)(2,1)} %copy-done.7), custom_call_target="tpu_custom_call", output_to_operand_aliasing={{}: (1, {})} | custom-call | bytes 524288 | tf_op jit(solution)/shard_map/pallas_call | solution.py:200
  142.3 3.1 %shard_map.81.so_far_ref = bf16[128,4096]{1,0:T(8,128)(2,1)} custom-call(s32[1]{0:T(128)} %bitcast.place_ref, bf16[128,4096]{1,0:T(8,128)(2,1)} %shard_map.78.so_far_ref, bf16[4,1,128,256]{3,2,1,0:T(8,128)(2,1)} %get-tuple-element.14.near_ref, bf16[4,1,128,256]{3,2,1,0:T(8,128)(2,1)} %copy-done.5), custom_call_target="tpu_custom_call", output_to_operand_aliasing={{}: (1, {})} | custom-call | bytes 524288 | tf_op jit(solution)/shard_map/pallas_call | solution.py:200
  146.1 3.1 %shard_map.84.so_far_ref = bf16[128,4096]{1,0:T(8,128)(2,1)} custom-call(s32[1]{0:T(128)} %bitcast.place_ref, bf16[128,4096]{1,0:T(8,128)(2,1)} %shard_map.81.so_far_ref, bf16[4,1,128,256]{3,2,1,0:T(8,128)(2,1)} %get-tuple-element.12.near_ref, bf16[4,1,128,256]{3,2,1,0:T(8,128)(2,1)} %copy-done.4), custom_call_target="tpu_custom_call", output_to_operand_aliasing={{}: (1, {})} | custom-call | bytes 524288 | tf_op jit(solution)/shard_map/pallas_call | solution.py:200
  150.0 3.1 %shard_map.87 = bf16[128,4096]{1,0:T(8,128)(2,1)} custom-call(s32[1]{0:T(128)} %bitcast.place_ref, bf16[128,4096]{1,0:T(8,128)(2,1)} %shard_map.84.so_far_ref, bf16[4,1,128,256]{3,2,1,0:T(8,128)(2,1)} %get-tuple-element.10.near_ref, bf16[4,1,128,256]{3,2,1,0:T(8,128)(2,1)} %copy-done.6), custom_call_target="tpu_custom_call", output_to_operand_aliasing={{}: (1, {})} | custom-call | bytes 524288 | tf_op jit(solution)/shard_map/pallas_call | solution.py:200
  (91 shorter events, 23.6 us)
Async XLA Ops:
  0.0 14.2 %copy-start.10 = (f32[4096]{0:T(1024)S(1)}, f32[4096]{0:T(1024)}, u32[]{:S(2)}) copy-start(f32[4096]{0:T(1024)} %param.9) | copy-start | bytes 49156
  1.3 37.4 %collective-permute-start.23 = (bf16[512,256]{1,0:T(8,128)(2,1)S(1)}, bf16[512,256]{1,0:T(8,128)(2,1)S(1)}, u32[]{:S(2)}, u32[]{:S(2)}) collective-permute-start(bf16[512,256]{1,0:T(8,128)(2,1)S(1)} %get-tuple-element.5), channel_id=1, source_target_pairs={{0,8},{4,12},{8,0},{12,4},{16,24},{20,28},{24,16},{28,20},{1,9},{5... | collective-permute-start | bytes 786440 | tf_op jit(solution)/shard_map/ppermute | solution.py:25
  4.4 20.0 %collective-permute-start.1 = (s32[1,128]{1,0:T(1,128)}, s32[1,128]{1,0:T(1,128)S(1)}, u32[]{:S(2)}, u32[]{:S(2)}) collective-permute-start(s32[1,128]{1,0:T(1,128)} %param.7), channel_id=1, source_target_pairs={{0,1},{1,2},{2,3},{4,5},{5,6},{6,7},{8,9},{9,10},{10,11},{12,13},{... | collective-permute-start | bytes 1544 | tf_op jit(solution)/shard_map/ppermute | solution.py:20
  6.6 17.8 %collective-permute-start = (s32[1,16]{1,0:T(1,128)S(1)}, s32[1,16]{1,0:T(1,128)S(1)}, u32[]{:S(2)}, u32[]{:S(2)}) collective-permute-start(s32[1,16]{1,0:T(1,128)S(1)} %slice.39), channel_id=1, source_target_pairs={{0,2},{1,3},{4,6},{5,7},{8,10},{9,11},{12,14},{13,15},{16,18},{17,... | collective-permute-start | bytes 200 | tf_op jit(solution)/shard_map/ppermute | solution.py:20
  10.4 34.5 %collective-permute-start.18 = (bf16[512,256]{1,0:T(8,128)(2,1)S(1)}, bf16[512,256]{1,0:T(8,128)(2,1)S(1)}, u32[]{:S(2)}, u32[]{:S(2)}) collective-permute-start(bf16[512,256]{1,0:T(8,128)(2,1)S(1)} %get-tuple-element.6), channel_id=1, source_target_pairs={{0,8},{4,12},{8,0},{12,4},{16,24},{20,28},{24,16},{28,20},{1,9},{5... | collective-permute-start | bytes 786440 | tf_op jit(solution)/shard_map/ppermute | solution.py:25
  14.4 9.9 %copy-start.9 = (bf16[32,128]{1,0:T(8,128)(2,1)S(1)}, bf16[32,128]{1,0:T(8,128)(2,1)}, u32[]{:S(2)}) copy-start(bf16[32,128]{1,0:T(8,128)(2,1)} %param.12) | copy-start | bytes 24580
  14.4 10.0 %copy-start.8 = (s32[1,128]{1,0:T(1,128)S(1)}, s32[1,128]{1,0:T(1,128)}, u32[]{:S(2)}) copy-start(s32[1,128]{1,0:T(1,128)} %param.7) | copy-start | bytes 1540
  14.4 24.4 %copy-start.2 = (f32[3,3,512]{2,1,0:T(4,128)S(1)}, f32[3,3,512]{2,1,0:T(4,128)}, u32[]{:S(2)}) copy-start(f32[3,3,512]{2,1,0:T(4,128)} %short_ref.3) | copy-start | bytes 55300
  24.5 8.5 %collective-permute-start.2 = (s32[1,272]{1,0:T(1,128)S(1)}, s32[1,272]{1,0:T(1,128)S(1)}, u32[]{:S(2)}, u32[]{:S(2)}) collective-permute-start(s32[1,272]{1,0:T(1,128)S(1)} %pad_add_fusion.1), channel_id=1, source_target_pairs={{0,16},{4,20},{8,24},{12,28},{16,0},{20,4},{24,8},{28,12},{1,17},{... | collective-permute-start | bytes 3272 | tf_op jit(solution)/shard_map/ppermute | solution.py:25
  27.1 6.5 %collective-permute-start.3 = (s32[1,272]{1,0:T(1,128)S(1)}, s32[1,272]{1,0:T(1,128)S(1)}, u32[]{:S(2)}, u32[]{:S(2)}) collective-permute-start(s32[1,272]{1,0:T(1,128)S(1)} %pad_add_fusion.1), channel_id=1, source_target_pairs={{0,8},{4,12},{8,0},{12,4},{16,24},{20,28},{24,16},{28,20},{1,9},{5... | collective-permute-start | bytes 3272 | tf_op jit(solution)/shard_map/ppermute | solution.py:25
  28.7 6.3 %collective-permute-start.4 = (s32[1,272]{1,0:T(1,128)S(1)}, s32[1,272]{1,0:T(1,128)S(1)}, u32[]{:S(2)}, u32[]{:S(2)}) collective-permute-start(s32[1,272]{1,0:T(1,128)S(1)} %pad_add_fusion.1), channel_id=1, source_target_pairs={{0,24},{4,28},{8,16},{12,20},{16,8},{20,12},{24,0},{28,4},{1,25},{... | collective-permute-start | bytes 3272 | tf_op jit(solution)/shard_map/ppermute | solution.py:25
  33.0 14.0 %collective-permute-start.13 = (bf16[512,256]{1,0:T(8,128)(2,1)S(1)}, bf16[512,256]{1,0:T(8,128)(2,1)S(1)}, u32[]{:S(2)}, u32[]{:S(2)}) collective-permute-start(bf16[512,256]{1,0:T(8,128)(2,1)S(1)} %get-tuple-element.7), channel_id=1, source_target_pairs={{0,8},{4,12},{8,0},{12,4},{16,24},{20,28},{24,16},{28,20},{1,9},{5... | collective-permute-start | bytes 786440 | tf_op jit(solution)/shard_map/ppermute | solution.py:25
  33.7 14.2 %collective-permute-start.6 = (bf16[512,256]{1,0:T(8,128)(2,1)S(1)}, bf16[512,256]{1,0:T(8,128)(2,1)S(1)}, u32[]{:S(2)}, u32[]{:S(2)}) collective-permute-start(bf16[512,256]{1,0:T(8,128)(2,1)S(1)} %get-tuple-element.8), channel_id=1, source_target_pairs={{0,8},{4,12},{8,0},{12,4},{16,24},{20,28},{24,16},{28,20},{1,9},{5... | collective-permute-start | bytes 786440 | tf_op jit(solution)/shard_map/ppermute | solution.py:25
  35.1 3.6 %collective-permute-start.9 = (s32[4,272]{1,0:T(4,128)S(1)}, s32[4,272]{1,0:T(4,128)S(1)}, u32[]{:S(2)}, u32[]{:S(2)}) collective-permute-start(s32[4,272]{1,0:T(4,128)S(1)} %pad_add_fusion), channel_id=1, source_target_pairs={{0,4},{4,0},{8,12},{12,8},{16,20},{20,16},{24,28},{28,24},{1,5},{5... | collective-permute-start | bytes 13064 | tf_op jit(solution)/shard_map/ppermute | solution.py:25
  38.7 11.1 %collective-permute-start.24 = (bf16[512,256]{1,0:T(8,128)(2,1)S(1)}, bf16[512,256]{1,0:T(8,128)(2,1)S(1)}, u32[]{:S(2)}, u32[]{:S(2)}) collective-permute-start(bf16[512,256]{1,0:T(8,128)(2,1)S(1)} %collective-permute-done.23), channel_id=1, source_target_pairs={{0,2},{1,3},{2,0},{3,1},{4,6},{5,7},{6,4},{7,5},{8,10},{9,11},{10,... | collective-permute-start | bytes 786440 | tf_op jit(solution)/shard_map/ppermute | solution.py:25
  44.9 9.3 %collective-permute-start.19 = (bf16[512,256]{1,0:T(8,128)(2,1)S(1)}, bf16[512,256]{1,0:T(8,128)(2,1)S(1)}, u32[]{:S(2)}, u32[]{:S(2)}) collective-permute-start(bf16[512,256]{1,0:T(8,128)(2,1)S(1)} %collective-permute-done.18), channel_id=1, source_target_pairs={{0,2},{1,3},{2,0},{3,1},{4,6},{5,7},{6,4},{7,5},{8,10},{9,11},{10,... | collective-permute-start | bytes 786440 | tf_op jit(solution)/shard_map/ppermute | solution.py:25
  47.0 12.2 %collective-permute-start.14 = (bf16[512,256]{1,0:T(8,128)(2,1)S(1)}, bf16[512,256]{1,0:T(8,128)(2,1)S(1)}, u32[]{:S(2)}, u32[]{:S(2)}) collective-permute-start(bf16[512,256]{1,0:T(8,128)(2,1)S(1)} %collective-permute-done.13), channel_id=1, source_target_pairs={{0,2},{1,3},{2,0},{3,1},{4,6},{5,7},{6,4},{7,5},{8,10},{9,11},{10,... | collective-permute-start | bytes 786440 | tf_op jit(solution)/shard_map/ppermute | solution.py:25
  47.1 19.7 %collective-permute-start.10 = (bf16[2,128,512]{2,1,0:T(8,128)(2,1)S(1)}, bf16[2,128,512]{2,1,0:T(8,128)(2,1)S(1)}, u32[]{:S(2)}, u32[]{:S(2)}) collective-permute-start(bf16[2,128,512]{2,1,0:T(8,128)(2,1)S(1)} %get-tuple-element.17), channel_id=1, source_target_pairs={{0,8},{4,12},{8,0},{12,4},{16,24},{20,28},{24,16},{28,20},{1,9},{5... | collective-permute-start | bytes 786440 | tf_op jit(solution)/shard_map/ppermute | solution.py:25
  47.9 14.1 %collective-permute-start.7 = (bf16[512,256]{1,0:T(8,128)(2,1)S(1)}, bf16[512,256]{1,0:T(8,128)(2,1)S(1)}, u32[]{:S(2)}, u32[]{:S(2)}) collective-permute-start(bf16[512,256]{1,0:T(8,128)(2,1)S(1)} %collective-permute-done.6), channel_id=1, source_target_pairs={{0,2},{1,3},{2,0},{3,1},{4,6},{5,7},{6,4},{7,5},{8,10},{9,11},{10,... | collective-permute-start | bytes 786440 | tf_op jit(solution)/shard_map/ppermute | solution.py:25
  49.9 20.1 %collective-permute-start.25 = (bf16[2,512,256]{2,1,0:T(8,128)(2,1)S(1)}, bf16[2,512,256]{2,1,0:T(8,128)(2,1)S(1)}, u32[]{:S(2)}, u32[]{:S(2)}) collective-permute-start(bf16[2,512,256]{2,1,0:T(8,128)(2,1)S(1)} %pad_maximum_fusion.3.even_ref), channel_id=1, source_target_pairs={{0,1},{1,0},{2,3},{3,2},{4,5},{5,4},{6,7},{7,6},{8,9},{9,8},{10,11... | collective-permute-start | bytes 1572872 | tf_op jit(solution)/shard_map/ppermute | solution.py:25
  54.3 12.6 %collective-permute-start.20 = (bf16[2,512,256]{2,1,0:T(8,128)(2,1)S(1)}, bf16[2,512,256]{2,1,0:T(8,128)(2,1)S(1)}, u32[]{:S(2)}, u32[]{:S(2)}) collective-permute-start(bf16[2,512,256]{2,1,0:T(8,128)(2,1)S(1)} %pad_maximum_fusion.2.even_ref), channel_id=1, source_target_pairs={{0,1},{1,0},{2,3},{3,2},{4,5},{5,4},{6,7},{7,6},{8,9},{9,8},{10,11... | collective-permute-start | bytes 1572872 | tf_op jit(solution)/shard_map/ppermute | solution.py:25
  59.3 12.0 %collective-permute-start.15 = (bf16[2,512,256]{2,1,0:T(8,128)(2,1)S(1)}, bf16[2,512,256]{2,1,0:T(8,128)(2,1)S(1)}, u32[]{:S(2)}, u32[]{:S(2)}) collective-permute-start(bf16[2,512,256]{2,1,0:T(8,128)(2,1)S(1)} %pad_maximum_fusion.1.even_ref), channel_id=1, source_target_pairs={{0,1},{1,0},{2,3},{3,2},{4,5},{5,4},{6,7},{7,6},{8,9},{9,8},{10,11... | collective-permute-start | bytes 1572872 | tf_op jit(solution)/shard_map/ppermute | solution.py:25
  62.1 11.5 %collective-permute-start.8 = (bf16[2,512,256]{2,1,0:T(8,128)(2,1)S(1)}, bf16[2,512,256]{2,1,0:T(8,128)(2,1)S(1)}, u32[]{:S(2)}, u32[]{:S(2)}) collective-permute-start(bf16[2,512,256]{2,1,0:T(8,128)(2,1)S(1)} %pad_maximum_fusion.even_ref), channel_id=1, source_target_pairs={{0,1},{1,0},{2,3},{3,2},{4,5},{5,4},{6,7},{7,6},{8,9},{9,8},{10,11... | collective-permute-start | bytes 1572872 | tf_op jit(solution)/shard_map/ppermute | solution.py:25
  67.6 14.8 %collective-permute-start.21 = (bf16[4,2,128,256]{3,2,1,0:T(8,128)(2,1)S(1)}, bf16[4,2,128,256]{3,2,1,0:T(8,128)(2,1)S(1)}, u32[]{:S(2)}, u32[]{:S(2)}) collective-permute-start(bf16[4,2,128,256]{3,2,1,0:T(8,128)(2,1)S(1)} %bitcast.60), channel_id=1, source_target_pairs={{0,4},{4,0},{8,12},{12,8},{16,20},{20,16},{24,28},{28,24},{1,5},{5... | collective-permute-start | bytes 1572872 | tf_op jit(solution)/shard_map/ppermute | solution.py:25
  69.3 8.5 %collective-permute-start.5 = (bf16[2,128,512]{2,1,0:T(8,128)(2,1)S(1)}, bf16[2,128,512]{2,1,0:T(8,128)(2,1)S(1)}, u32[]{:S(2)}, u32[]{:S(2)}) collective-permute-start(bf16[2,128,512]{2,1,0:T(8,128)(2,1)S(1)} %get-tuple-element.19), channel_id=1, source_target_pairs={{0,8},{4,12},{8,0},{12,4},{16,24},{20,28},{24,16},{28,20},{1,9},{5... | collective-permute-start | bytes 786440 | tf_op jit(solution)/shard_map/ppermute | solution.py:25
  70.7 48.1 %collective-permute-start.26 = (bf16[4,2,128,256]{3,2,1,0:T(8,128)(2,1)S(1)}, bf16[4,2,128,256]{3,2,1,0:T(8,128)(2,1)S(1)}, u32[]{:S(2)}, u32[]{:S(2)}) collective-permute-start(bf16[4,2,128,256]{3,2,1,0:T(8,128)(2,1)S(1)} %bitcast.59), channel_id=1, source_target_pairs={{0,4},{4,0},{8,12},{12,8},{16,20},{20,16},{24,28},{28,24},{1,5},{5... | collective-permute-start | bytes 1572872 | tf_op jit(solution)/shard_map/ppermute | solution.py:25
  72.0 32.9 %collective-permute-start.16 = (bf16[4,2,128,256]{3,2,1,0:T(8,128)(2,1)S(1)}, bf16[4,2,128,256]{3,2,1,0:T(8,128)(2,1)S(1)}, u32[]{:S(2)}, u32[]{:S(2)}) collective-permute-start(bf16[4,2,128,256]{3,2,1,0:T(8,128)(2,1)S(1)} %bitcast.62), channel_id=1, source_target_pairs={{0,4},{4,0},{8,12},{12,8},{16,20},{20,16},{24,28},{28,24},{1,5},{5... | collective-permute-start | bytes 1572872 | tf_op jit(solution)/shard_map/ppermute | solution.py:25
  74.3 41.4 %collective-permute-start.11 = (bf16[4,2,128,256]{3,2,1,0:T(8,128)(2,1)S(1)}, bf16[4,2,128,256]{3,2,1,0:T(8,128)(2,1)S(1)}, u32[]{:S(2)}, u32[]{:S(2)}) collective-permute-start(bf16[4,2,128,256]{3,2,1,0:T(8,128)(2,1)S(1)} %bitcast.61), channel_id=1, source_target_pairs={{0,4},{4,0},{8,12},{12,8},{16,20},{20,16},{24,28},{28,24},{1,5},{5... | collective-permute-start | bytes 1572872 | tf_op jit(solution)/shard_map/ppermute | solution.py:25
  83.3 62.1 %collective-permute-start.22 = (bf16[4,1,128,256]{3,2,1,0:T(8,128)(2,1)S(1)}, bf16[4,1,128,256]{3,2,1,0:T(8,128)(2,1)S(1)}, u32[]{:S(2)}, u32[]{:S(2)}) collective-permute-start(bf16[4,1,128,256]{3,2,1,0:T(8,128)(2,1)S(1)} %get-tuple-element.11), channel_id=1, source_target_pairs={{0,16},{4,20},{8,24},{12,28},{16,0},{20,4},{24,8},{28,12},{1,17},{... | collective-permute-start | bytes 786440 | tf_op jit(solution)/shard_map/ppermute | solution.py:25
  105.8 35.8 %collective-permute-start.17 = (bf16[4,1,128,256]{3,2,1,0:T(8,128)(2,1)S(1)}, bf16[4,1,128,256]{3,2,1,0:T(8,128)(2,1)S(1)}, u32[]{:S(2)}, u32[]{:S(2)}) collective-permute-start(bf16[4,1,128,256]{3,2,1,0:T(8,128)(2,1)S(1)} %get-tuple-element.13), channel_id=1, source_target_pairs={{0,16},{4,20},{8,24},{12,28},{16,0},{20,4},{24,8},{28,12},{1,17},{... | collective-permute-start | bytes 786440 | tf_op jit(solution)/shard_map/ppermute | solution.py:25
  116.6 21.1 %collective-permute-start.12 = (bf16[4,1,128,256]{3,2,1,0:T(8,128)(2,1)S(1)}, bf16[4,1,128,256]{3,2,1,0:T(8,128)(2,1)S(1)}, u32[]{:S(2)}, u32[]{:S(2)}) collective-permute-start(bf16[4,1,128,256]{3,2,1,0:T(8,128)(2,1)S(1)} %get-tuple-element.15), channel_id=1, source_target_pairs={{0,16},{4,20},{8,24},{12,28},{16,0},{20,4},{24,8},{28,12},{1,17},{... | collective-permute-start | bytes 786440 | tf_op jit(solution)/shard_map/ppermute | solution.py:25
  119.7 29.6 %collective-permute-start.27 = (bf16[4,1,128,256]{3,2,1,0:T(8,128)(2,1)S(1)}, bf16[4,1,128,256]{3,2,1,0:T(8,128)(2,1)S(1)}, u32[]{:S(2)}, u32[]{:S(2)}) collective-permute-start(bf16[4,1,128,256]{3,2,1,0:T(8,128)(2,1)S(1)} %get-tuple-element.9), channel_id=1, source_target_pairs={{0,16},{4,20},{8,24},{12,28},{16,0},{20,4},{24,8},{28,12},{1,17},{... | collective-permute-start | bytes 786440 | tf_op jit(solution)/shard_map/ppermute | solution.py:25
  (7 other events, 12.7 us)

commit v3 on v1

v3 whole, which is shorter than its diff:
```python
import functools

import jax
import jax.numpy as jnp
from jax import lax
from jax.experimental import pallas as pl
from jax.experimental.pallas import tpu as pltpu
from jax.sharding import PartitionSpec as P

GROUP = 16
TAPS = 128
SHORT = 3
LANES = 128
LEAD = 16
SPLITS = 2
STEPS = 2


def from_behind(x, axis, by):
    peers = lax.axis_size(axis)
    return lax.ppermute(x, axis, [(i, i + by) for i in range(peers) if i + by < peers])


def swap(x, axis, mask):
    peers = lax.axis_size(axis)
    return lax.ppermute(x, axis, [(i, i ^ mask) for i in range(peers)])


def exchange_bits():
    peers = lax.axis_size("fsdp")
    return [1 << b for b in reversed(range(peers.bit_length() - 1))]


def params(mib=40):
    return pltpu.CompilerParams(vmem_limit_bytes=mib * 1024 * 1024)


def cost(flops, bytes_accessed):
    return pl.CostEstimate(flops=flops, bytes_accessed=bytes_accessed, transcendentals=0)


def whole(array):
    return pl.BlockSpec(array.shape, lambda *_: (0,) * array.ndim)


def gather_ids(token_ids):
    tok_len = token_ids.shape[1]
    place = lax.axis_index("ctx")
    one = jnp.where(place >= 1, from_behind(token_ids, "ctx", 1), -1)
    two = jnp.where(place >= 2, from_behind(token_ids, "ctx", 2), -1)
    ids = jnp.concatenate([two[:, tok_len - LEAD :], one, token_ids], axis=1)
    bits = exchange_bits()
    while bits:
        if len(bits) > 1:
            low, high = bits[:2]
            ids = jnp.concatenate([ids] + [swap(ids, "fsdp", mask) for mask in (low, high, low | high)], axis=0)
            bits = bits[2:]
        else:
            ids = jnp.concatenate([ids, swap(ids, "fsdp", bits[0])], axis=0)
            bits = []
    return ids


def norm_kernel(rows_ref, gain_ref, base_ref, normed_ref, toeplitz_ref):
    values = rows_ref[...].astype(jnp.float32)
    inverse_rms = lax.rsqrt(jnp.mean(values * values, axis=-1, keepdims=True) + 1e-06)
    normed_ref[...] = (values * inverse_rms * gain_ref[...]).astype(jnp.bfloat16)
    per_tile, reach = base_ref.shape
    tok_len = toeplitz_ref.shape[1] // per_tile
    for k in range(per_tile):
        wide = jnp.broadcast_to(base_ref[k : k + 1, :], (tok_len, reach))
        shifted = pltpu.roll(wide, 0, 1, stride=1, stride_axis=0)
        toeplitz_ref[0, pl.ds(k * tok_len, tok_len), :] = shifted.astype(jnp.bfloat16)


def norm_and_toeplitz(embedding, norm_gain, conv_taps, tok_len):
    vocab, width = embedding.shape
    reach = 2 * tok_len
    per_tile = LANES // GROUP
    tiles = conv_taps.shape[0] // per_tile
    base = jnp.pad(conv_taps[:, ::-1].astype(jnp.float32), ((0, 0), (1, reach - TAPS - 1)))
    return pl.pallas_call(
        norm_kernel,
        grid=(tiles,),
        in_specs=[
            pl.BlockSpec((vocab // tiles, width), lambda i: (i, 0)),
            pl.BlockSpec((1, width), lambda i: (0, 0)),
            pl.BlockSpec((per_tile, reach), lambda i: (i, 0)),
        ],
        out_specs=[
            pl.BlockSpec((vocab // tiles, width), lambda i: (i, 0)),
            pl.BlockSpec((1, per_tile * tok_len, reach), lambda i: (i, 0, 0)),
        ],
        out_shape=[
            jax.ShapeDtypeStruct((vocab, width), jnp.bfloat16),
            jax.ShapeDtypeStruct((tiles, per_tile * tok_len, reach), jnp.bfloat16),
        ],
        compiler_params=params(),
        cost_estimate=cost(2_000_000_000, 10_000_000),
    )(embedding, norm_gain.reshape(1, width), base)


def table_kernel(normed_ref, weight_ref, out_ref):
    out_ref[0] = jnp.dot(normed_ref[...], weight_ref[0], preferred_element_type=jnp.float32).astype(jnp.bfloat16)


def project(normed, in_proj, first, count):
    vocab, width = normed.shape
    panel_width = in_proj.shape[2]
    cols = min(256, panel_width)
    per = panel_width // cols
    return pl.pallas_call(
        table_kernel,
        grid=(count * per,),
        in_specs=[
            whole(normed),
            pl.BlockSpec((1, width, cols), lambda s: (first + s // per, 0, s % per)),
        ],
        out_specs=pl.BlockSpec((1, vocab, cols), lambda s: (s // per, 0, s % per)),
        out_shape=jax.ShapeDtypeStruct((count, vocab, panel_width), jnp.bfloat16),
        compiler_params=params(),
        cost_estimate=cost(2 * vocab * width * panel_width * count, 2 * width * panel_width * count),
    )(normed, in_proj)


def mixer_kernel(ids_ref, query_ref, kv_ref, short_ref, toeplitz, gated_ref, held_query, held):
    tok_len, panel_width = gated_ref.shape[1:]
    vocab = kv_ref.shape[1]
    rows = ids_ref.shape[2]
    reach = 2 * tok_len
    lead = rows - reach
    tiles = panel_width // LANES
    per_tile = LANES // GROUP
    names = lax.broadcasted_iota(jnp.int32, (vocab, rows), 0)
    lane_group = lax.broadcasted_iota(jnp.int32, (tok_len, 2 * LANES), 1) % LANES // GROUP

    def look_up(one_hot, table):
        found = lax.dot_general(one_hot, table, (((0,), (0,)), ((), ())), preferred_element_type=jnp.float32)
        return found.astype(jnp.bfloat16).astype(jnp.float32)

    for v in range(2):
        one_hot = (names == ids_ref[v]).astype(jnp.float32).astype(jnp.bfloat16)
        held[v, 0] = look_up(one_hot, kv_ref[0])
        held[v, 1] = look_up(one_hot, kv_ref[1])
        held_query[v] = look_up(one_hot[:, rows - lead - tok_len :], query_ref[0])

    def featured(source, i, count, cols):
        total = short_ref[0, i : i + 1, cols] * source[pl.ds(lead, count), cols]
        for j in range(1, SHORT):
            total += short_ref[j, i : i + 1, cols] * source[pl.ds(lead - j, count), cols]
        return total

    for tile in range(tiles):
        cols = slice(tile * LANES, (tile + 1) * LANES)
        products = []
        for v in range(2):
            key = featured(held.at[v, 0], 1, reach, cols)
            value = featured(held.at[v, 1], 2, reach, cols)
            products.append((key * value).astype(jnp.bfloat16))
        both = jnp.concatenate(products, axis=1)
        filtered = None
        for k in range(per_tile):
            one = jnp.dot(
                toeplitz[tile, pl.ds(k * tok_len, tok_len), :], both, preferred_element_type=jnp.float32
            )
            filtered = one if k == 0 else jnp.where(lane_group == k, one, filtered)
        for v in range(2):
            query = featured(held_query.at[v], 0, tok_len, cols)
            gated_ref[v, :, cols] = (query * filtered[:, v * LANES : (v + 1) * LANES]).astype(jnp.bfloat16)


def mix(ids, query, key_value, short_taps, toeplitz, tok_len):
    windows, rows = ids.shape
    panel_width = query.shape[2]
    return pl.pallas_call(
        mixer_kernel,
        grid=(windows // 2,),
        in_specs=[pl.BlockSpec((2, 1, rows), lambda p: (p, 0, 0))]
        + [whole(array) for array in (query, key_value, short_taps, toeplitz)],
        out_specs=pl.BlockSpec((2, tok_len, panel_width), lambda p: (p, 0, 0)),
        out_shape=jax.ShapeDtypeStruct((windows, tok_len, panel_width), jnp.bfloat16),
        scratch_shapes=[
            pltpu.VMEM((2, LEAD + tok_len, panel_width), jnp.float32),
            pltpu.VMEM((2, 2, rows, panel_width), jnp.float32),
        ],
        compiler_params=params(),
        cost_estimate=cost(4_000_000_000, 4_000_000),
    )(ids.reshape(windows, 1, rows), query, key_value, short_taps, toeplitz)


def panel_kernel(place_ref, mine_ref, other_ref, w0, w1, w2, w3, even_ref, odd_ref, out_ref):
    own = (w0, w1, w2, w3)
    count, _, tok_len, _ = out_ref.shape
    for k in range(4):
        beside = (even_ref, odd_ref)[k % 2]
        total = jnp.dot(mine_ref[...], own[k][...], preferred_element_type=jnp.float32)
        total += jnp.dot(other_ref[...], beside[k // 2], preferred_element_type=jnp.float32)
        for w in range(count):
            out_ref[w, k] = total[w * tok_len : (w + 1) * tok_len].astype(out_ref.dtype)


def panel(place, mine, other, out_proj, even, odd, split, step):
    count, tok_len, depth = mine.shape
    rows = count * tok_len
    cols = even.shape[2] // STEPS
    fixed = lambda shape: pl.BlockSpec(shape, lambda s, place: (0,) * len(shape))
    at = lambda k: pl.BlockSpec((depth, cols), lambda s, place: (0, (split * 4 + (place[0] ^ k)) * STEPS + step))
    beside = pl.BlockSpec((2, depth, cols), lambda s, place: (0, 0, step))
    return pl.pallas_call(
        panel_kernel,
        grid_spec=pltpu.PrefetchScalarGridSpec(
            num_scalar_prefetch=1,
            grid=(1,),
            in_specs=[fixed((rows, depth))] * 2 + [at(k) for k in range(4)] + [beside] * 2,
            out_specs=fixed((count, 4, tok_len, cols)),
        ),
        out_shape=jax.ShapeDtypeStruct((count, 4, tok_len, cols), jnp.bfloat16),
        compiler_params=params(),
        cost_estimate=cost(16 * rows * depth * cols, 16 * depth * cols),
    )(place, mine.reshape(rows, depth), other.reshape(rows, depth), *[out_proj] * 4, even, odd)


def residual_kernel(ids_ref, rows_ref, out_ref):
    names = lax.broadcasted_iota(jnp.int32, (rows_ref.shape[0], ids_ref.shape[1]), 0)
    one_hot = (names == ids_ref[...]).astype(jnp.float32).astype(jnp.bfloat16)
    out_ref[...] = lax.dot_general(
        one_hot, rows_ref[...], (((0,), (0,)), ((), ())), preferred_element_type=jnp.float32
    ).astype(jnp.bfloat16)


def residual(token_ids, embedding):
    vocab, width = embedding.shape
    tok_len = token_ids.shape[1]
    cols = width // 4
    return pl.pallas_call(
        residual_kernel,
        grid=(4,),
        in_specs=[whole(token_ids), pl.BlockSpec((vocab, cols), lambda i: (0, i))],
        out_specs=pl.BlockSpec((tok_len, cols), lambda i: (0, i)),
        out_shape=jax.ShapeDtypeStruct((tok_len, width), jnp.bfloat16),
        cost_estimate=cost(2 * vocab * tok_len * width, 2 * vocab * width),
    )(token_ids, embedding)


def place_kernel(step, place_ref, so_far_ref, near_ref, far_ref, out_ref):
    tok_len, cols = near_ref.shape[2:]
    out_ref[...] = so_far_ref[...]
    for k in range(4):
        first = pl.multiple_of(((place_ref[0] ^ k) * STEPS + step) * cols, LANES)
        total = near_ref[0, k].astype(jnp.float32) + far_ref[0, k].astype(jnp.float32)
        at = pl.ds(first, cols)
        out_ref[:, at] = (so_far_ref[:, at].astype(jnp.float32) + total).astype(jnp.bfloat16)


def place_quarters(place, so_far, near, far, split, step):
    _, _, tok_len, cols = near.shape
    part = pl.BlockSpec((tok_len, 4 * STEPS * cols), lambda s, place: (0, split))
    one = pl.BlockSpec((1, 4, tok_len, cols), lambda s, place: (0, 0, 0, 0))
    return pl.pallas_call(
        functools.partial(place_kernel, step),
        grid_spec=pltpu.PrefetchScalarGridSpec(
            num_scalar_prefetch=1, grid=(1,), in_specs=[part, one, one], out_specs=part
        ),
        out_shape=jax.ShapeDtypeStruct(so_far.shape, so_far.dtype),
        input_output_aliases={1: 0},
        cost_estimate=cost(0, 16 * tok_len * cols * STEPS),
    )(place, so_far, near, far)


def add(a, b):
    return (a.astype(jnp.float32) + b.astype(jnp.float32)).astype(jnp.bfloat16)


def per_device(token_ids, embedding, norm_gain, in_proj, short_taps, conv_taps, out_proj):
    tok_len = token_ids.shape[1]
    width = out_proj.shape[1]
    place = lax.axis_index("ctx")
    quarter = width // SPLITS // 4
    bits = exchange_bits()

    beside = []
    for j in range(SPLITS):
        piece = lax.dynamic_slice_in_dim(out_proj, (j * 4 + place) * quarter, quarter, axis=1)
        piece = swap(piece, "fsdp", bits[-2])
        even = jnp.stack([piece, swap(piece, "ctx", 2)])
        beside.append((even, swap(even, "ctx", 1)))

    ids = gather_ids(token_ids)
    normed, toeplitz = norm_and_toeplitz(embedding, norm_gain, conv_taps, tok_len)
    key_value = project(normed, in_proj, 1, 2)
    query = project(normed, in_proj, 0, 1)

    half = ids.shape[0] // 2
    mine, other = [], []
    for first in (half, 0):
        gated = mix(ids[first : first + half], query, key_value, short_taps, toeplitz, tok_len)
        mine.append(gated[: half // 2])
        other.append(swap(gated[half // 2 :], "fsdp", bits[-2]))

    at = place.reshape(1).astype(jnp.int32)
    out = residual(token_ids, embedding)
    for j in range(SPLITS):
        for step in range(STEPS):
            away = panel(at, mine[0], other[0], out_proj, *beside[j], j, step)
            got = swap(away, "fsdp", bits[-1])
            total = add(panel(at, mine[1], other[1], out_proj, *beside[j], j, step), got)
            for bit in reversed(bits[:-2]):
                half = total.shape[0] // 2
                got = swap(total[half:], "fsdp", bit)
                total = add(total[:half], got) if half > 1 else total[:half]
            out = place_quarters(at, out, total, got, j, step)
    return out[None]


def solution(mesh):
    return jax.shard_map(
        per_device,
        mesh=mesh,
        in_specs=(
            P("fsdp", "ctx"),
            P(),
            P(),
            P(None, None, "fsdp"),
            P(None, None, "fsdp"),
            P("fsdp", None),
            P("fsdp", None),
        ),
        out_specs=P("fsdp", "ctx", None),
        check_vma=False,
    )
```

time: 231 us -> 129 us (0.56)
  waiting for transfers between devices: 171 us -> 34 us
  Pallas kernels: 9.26 us -> 41.4 us
  matrix products: 16 us -> 0 us
  starting transfers between devices: 17.4 us -> 33.2 us
  local copies, waits for them, and re-layouts: 7.55 us -> 16 us
  other arithmetic: 8.73 us -> 3.13 us
    ppermute x7 -> x20, waiting for transfers between devices: 171 us -> 34 us  [swap(): return lax.ppermute(x, axis, [(i, i ^ mask) for i in range(peers)])]
    pallas_call x0 -> x16, Pallas kernels: none -> 32.5 us  [the longest x2 11.4 us: project(): pl.pallas_call(table_kernel, grid=(count * per,), in_specs=[whole(normed)...]
    dot_general x2 -> x0, matrix products: 16 us -> none  [the longest x1 11 us: per_device(): jnp.einsum('vd,idc->ivc', normed, in_proj, preferred_element_type=jnp.flo...]
    ppermute x7 -> x20, starting transfers between devices: 10.5 us -> 26.5 us  [swap(): return lax.ppermute(x, axis, [(i, i ^ mask) for i in range(peers)])]
    unnamed x10 -> x22, local copies, waits for them, and re-layouts: 0.02 us -> 9.89 us
    gather x1 -> x0, local copies, waits for them, and re-layouts: 4.93 us -> none  [per_device(): jnp.take(embedding, token_ids[0], axis=0, mode='clip').astype(jnp.float32)]
    convert_element_type x3 -> x4, other arithmetic: 5.4 us -> 0.53 us  [add(): return (a.astype(jnp.float32) + b.astype(jnp.float32)).astype(jnp.bfloat16)]
    reduce_sum x1 -> x0, other arithmetic: 3.08 us -> none  [normalize_rows(): jnp.mean(values * values, axis=-1, keepdims=True) + 1e-06]
  transfers between devices with their start and end apart: 9 -> 22, of which waited for: 4 -> 7; matrix products, arithmetic and copies ran while one was open for 9% -> 7% of each run, Pallas kernels for 0% -> 31%
where the time goes in v3:
time: 129 us; the launch traced here: 128 us
  Pallas kernels  41.4 us (32%)
  waiting for transfers between devices  34 us (26%)
  starting transfers between devices  33.2 us (26%)
  local copies, waits for them, and re-layouts  16 us (12%)
  other arithmetic  3.13 us (2%)
    ppermute x20, waiting for transfers between devices, swap(): return lax.ppermute(x, axis, [(i, i ^ mask) for i in range(peers)])  34 us
    ppermute x20, starting transfers between devices, swap(): return lax.ppermute(x, axis, [(i, i ^ mask) for i in range(peers)])  26.5 us
    pallas_call x2, Pallas kernels, project(): pl.pallas_call(table_kernel, grid=(count * per,), in_specs=[whole(normed)...  11.4 us
    unnamed x22, local copies, waits for them, and re-layouts  9.89 us
    pallas_call x2, Pallas kernels, mix(): pl.pallas_call(mixer_kernel, grid=(windows // 2,), in_specs=[pl.BlockSpec...  8.84 us
    pallas_call x4, Pallas kernels, place_quarters(): pl.pallas_call(functools.partial(place_kernel, step), grid_spec=pltpu.Pre...  8.49 us
    ppermute x2, starting transfers between devices, from_behind(): lax.ppermute(x, axis, [(i, i + by) for i in range(peers) if i + by < peers])  6.76 us
    pallas_call x8, Pallas kernels, panel(): pl.pallas_call(panel_kernel, grid_spec=pltpu.PrefetchScalarGridSpec(num_s...  5.81 us
  transfers between devices with their start and end apart: 22, of which 7 were waited for; matrix products, arithmetic and copies ran while one was open for 7% of the time, Pallas kernels for 31%

profile of v3, /device:TPU:0, one launch (start us, length us, event | category | flops | bytes accessed | tf_op | source)
XLA Modules:
  0.0 128.1 jit_solution(2136712922502921096)
XLA Ops:
  0.0 2.3 %collective-permute-start.1 = (s32[1,128]{1,0:T(1,128)}, s32[1,128]{1,0:T(1,128)S(1)}, u32[]{:S(2)}, u32[]{:S(2)}) collective-permute-start(s32[1,128]{1,0:T(1,128)} %ids_ref.1), channel_id=1, source_target_pairs={{0,1},{1,2},{2,3},{4,5},{5,6},{6,7},{8,9},{9,10},{10,11},{12,13},{... | collective-permute-start | bytes 1544 | tf_op jit(solution)/shard_map/ppermute | solution.py:21
  2.4 4.4 %collective-permute-start = (s32[1,128]{1,0:T(1,128)}, s32[1,128]{1,0:T(1,128)S(1)}, u32[]{:S(2)}, u32[]{:S(2)}) collective-permute-start(s32[1,128]{1,0:T(1,128)} %ids_ref.1), channel_id=1, source_target_pairs={{0,2},{1,3},{4,6},{5,7},{8,10},{9,11},{12,14},{13,15},{16,18},{17,... | collective-permute-start | bytes 1544 | tf_op jit(solution)/shard_map/ppermute | solution.py:21
  6.8 2.2 %constant_dynamic-slice_fusion = (bf16[512,512]{1,0:T(8,128)(2,1)}, bf16[512,512]{1,0:T(8,128)(2,1)}) fusion(bf16[512,4096]{1,0:T(8,128)(2,1)} %w3.15, s32[]{:T(128)S(6)} %select_n.25, s32[]{:T(128)S(6)} %select_n.24), kind=kLoop, calls=%fused_computation.11 | loop fusion | bytes 2097160 | tf_op jit(solution)/shard_map/dynamic_slice | solution.py:283
  9.0 1.6 %collective-permute-start.6 = (bf16[512,512]{1,0:T(8,128)(2,1)}, bf16[512,512]{1,0:T(8,128)(2,1)}, u32[]{:S(2)}, u32[]{:S(2)}) collective-permute-start(bf16[512,512]{1,0:T(8,128)(2,1)} %get-tuple-element.10), channel_id=1, source_target_pairs={{0,8},{4,12},{8,0},{12,4},{16,24},{20,28},{24,16},{28,20},{1,9},{5... | collective-permute-start | bytes 1572872 | tf_op jit(solution)/shard_map/ppermute | solution.py:26
  11.9 2.2 %copy-done.3 = bf16[512,4096]{1,0:T(8,128)(2,1)S(1)} copy-done((bf16[512,4096]{1,0:T(8,128)(2,1)S(1)}, bf16[512,4096]{1,0:T(8,128)(2,1)}, u32[]{:S(2)}) %copy-start.3) | copy-done | bytes 4194328
  14.8 2.2 %shard_map.74 = (bf16[512,4096]{1,0:T(8,128)(2,1)S(1)}, bf16[4,1024,256]{2,1,0:T(8,128)(2,1)S(1)}) custom-call(bf16[512,4096]{1,0:T(8,128)(2,1)S(1)} %copy-done.3, f32[1,4096]{1,0:T(1,128)S(1)} %bitcast.29, f32[32,256]{1,0:T(8,128)S(1)} %pad_convert_fusion.base_ref), custom_call_target="tpu_custom_call" | custom-call | flops 2000000000 | bytes 10000000 | tf_op jit(solution)/shard_map/pallas_call | solution.py:82
  17.1 7.2 %shard_map.76.kv_ref = bf16[2,512,512]{2,1,0:T(8,128)(2,1)S(1)} custom-call(bf16[512,4096]{1,0:T(8,128)(2,1)S(1)} %get-tuple-element.7.normed_ref, bf16[3,4096,512]{2,1,0:T(8,128)(2,1)} %weight_ref.3), custom_call_target="tpu_custom_call" | custom-call | flops 4294967296 | bytes 8388608 | tf_op jit(solution)/shard_map/pallas_call | solution.py:112
  24.3 2.0 %copy-done.1 = bf16[512,4096]{1,0:T(8,128)(2,1)} copy-done((bf16[512,4096]{1,0:T(8,128)(2,1)}, bf16[512,4096]{1,0:T(8,128)(2,1)S(1)}, u32[]{:S(2)}) %copy-start.1) | copy-done | bytes 4194328
  26.4 3.6 %collective-permute-start.4 = (s32[1,272]{1,0:T(1,128)S(1)}, s32[1,272]{1,0:T(1,128)S(1)}, u32[]{:S(2)}, u32[]{:S(2)}) collective-permute-start(s32[1,272]{1,0:T(1,128)S(1)} %pad_add_fusion.1), channel_id=1, source_target_pairs={{0,24},{4,28},{8,16},{12,20},{16,8},{20,12},{24,0},{28,4},{1,25},{... | collective-permute-start | bytes 3272 | tf_op jit(solution)/shard_map/ppermute | solution.py:26
  30.8 2.2 %copy-done.2 = bf16[512,4096]{1,0:T(8,128)(2,1)S(1)} copy-done((bf16[512,4096]{1,0:T(8,128)(2,1)S(1)}, bf16[512,4096]{1,0:T(8,128)(2,1)}, u32[]{:S(2)}) %copy-start.2) | copy-done | bytes 4194328
  33.0 4.2 %shard_map.75.query_ref = bf16[1,512,512]{2,1,0:T(8,128)(2,1)S(1)} custom-call(bf16[512,4096]{1,0:T(8,128)(2,1)S(1)} %copy-done.2, bf16[3,4096,512]{2,1,0:T(8,128)(2,1)} %weight_ref.3), custom_call_target="tpu_custom_call" | custom-call | flops 2147483648 | bytes 4194304 | tf_op jit(solution)/shard_map/pallas_call | solution.py:112
  37.4 1.5 %collective-permute-start.9 = (s32[4,272]{1,0:T(4,128)S(1)}, s32[4,272]{1,0:T(4,128)S(1)}, u32[]{:S(2)}, u32[]{:S(2)}) collective-permute-start(s32[4,272]{1,0:T(4,128)S(1)} %pad_add_fusion), channel_id=1, source_target_pairs={{0,4},{4,0},{8,12},{12,8},{16,20},{20,16},{24,28},{28,24},{1,5},{5... | collective-permute-start | bytes 13064 | tf_op jit(solution)/shard_map/ppermute | solution.py:26
  38.9 2.0 %collective-permute-start.16 = (bf16[512,512]{1,0:T(8,128)(2,1)}, bf16[512,512]{1,0:T(8,128)(2,1)S(1)}, u32[]{:S(2)}, u32[]{:S(2)}) collective-permute-start(bf16[512,512]{1,0:T(8,128)(2,1)} %collective-permute-done.15), channel_id=1, source_target_pairs={{0,2},{1,3},{2,0},{3,1},{4,6},{5,7},{6,4},{7,5},{8,10},{9,11},{10,... | collective-permute-start | bytes 1572872 | tf_op jit(solution)/shard_map/ppermute | solution.py:26
  42.2 4.3 %shard_map.79 = bf16[4,128,512]{2,1,0:T(8,128)(2,1)S(1)} custom-call(s32[4,1,272]{2,1,0:T(1,128)S(1)} %reshape.41.ids_ref, bf16[1,512,512]{2,1,0:T(8,128)(2,1)S(1)} %shard_map.75.query_ref, bf16[2,512,512]{2,1,0:T(8,128)(2,1)S(1)} %shard_map.76.kv_ref, f32[3,3,512]{2,1,0:T(4,128)S(1)} %copy-done.4, bf16[4,1024,256]{2,1,0:T(8,128)(2,1)S(1)} %get-tuple-element.8.toeplitz), custom_call_target="tpu_custom_call" | custom-call | flops 4000000000 | bytes 4000000 | tf_op jit(solution)/shard_map/pallas_call | solution.py:175
  46.6 4.3 %collective-permute-done.16 = bf16[512,512]{1,0:T(8,128)(2,1)S(1)} collective-permute-done((bf16[512,512]{1,0:T(8,128)(2,1)}, bf16[512,512]{1,0:T(8,128)(2,1)S(1)}, u32[]{:S(2)}, u32[]{:S(2)}) %collective-permute-start.16) | collective-permute-done | bytes 524320 | tf_op jit(solution)/shard_map/ppermute | solution.py:26
  53.6 4.5 %shard_map.77 = bf16[4,128,512]{2,1,0:T(8,128)(2,1)S(1)} custom-call(s32[4,1,272]{2,1,0:T(1,128)S(1)} %copy.12.ids_ref, bf16[1,512,512]{2,1,0:T(8,128)(2,1)S(1)} %shard_map.75.query_ref, bf16[2,512,512]{2,1,0:T(8,128)(2,1)S(1)} %shard_map.76.kv_ref, f32[3,3,512]{2,1,0:T(4,128)S(1)} %copy-done.4, bf16[4,1024,256]{2,1,0:T(8,128)(2,1)S(1)} %get-tuple-element.8.toeplitz), custom_call_target="tpu_custom_call" | custom-call | flops 4000000000 | bytes 4000000 | tf_op jit(solution)/shard_map/pallas_call | solution.py:175
  58.1 2.8 %collective-permute-done.10 = bf16[2,128,512]{2,1,0:T(8,128)(2,1)S(1)} collective-permute-done((bf16[2,128,512]{2,1,0:T(8,128)(2,1)S(1)}, bf16[2,128,512]{2,1,0:T(8,128)(2,1)S(1)}, u32[]{:S(2)}, u32[]{:S(2)}) %collective-permute-start.10) | collective-permute-done | bytes 262176 | tf_op jit(solution)/shard_map/ppermute | solution.py:26
  63.0 1.6 %collective-permute-start.5 = (bf16[2,128,512]{2,1,0:T(8,128)(2,1)S(1)}, bf16[2,128,512]{2,1,0:T(8,128)(2,1)S(1)}, u32[]{:S(2)}, u32[]{:S(2)}) collective-permute-start(bf16[2,128,512]{2,1,0:T(8,128)(2,1)S(1)} %get-tuple-element.19), channel_id=1, source_target_pairs={{0,8},{4,12},{8,0},{12,4},{16,24},{20,28},{24,16},{28,20},{1,9},{5... | collective-permute-start | bytes 786440 | tf_op jit(solution)/shard_map/ppermute | solution.py:26
  66.8 1.5 %collective-permute-start.18 = (bf16[2,4,128,256]{3,2,1,0:T(8,128)(2,1)S(1)}, bf16[2,4,128,256]{3,2,1,0:T(8,128)(2,1)S(1)}, u32[]{:S(2)}, u32[]{:S(2)}) collective-permute-start(bf16[2,4,128,256]{3,2,1,0:T(8,128)(2,1)S(1)} %shard_map.86), channel_id=1, source_target_pairs={{0,4},{4,0},{8,12},{12,8},{16,20},{20,16},{24,28},{28,24},{1,5},{5... | collective-permute-start | bytes 1572872 | tf_op jit(solution)/shard_map/ppermute | solution.py:26
  73.6 2.9 %collective-permute-done.11 = bf16[2,4,128,256]{3,2,1,0:T(8,128)(2,1)S(1)} collective-permute-done((bf16[2,4,128,256]{3,2,1,0:T(8,128)(2,1)S(1)}, bf16[2,4,128,256]{3,2,1,0:T(8,128)(2,1)S(1)}, u32[]{:S(2)}, u32[]{:S(2)}) %collective-permute-start.11) | collective-permute-done | bytes 524320 | tf_op jit(solution)/shard_map/ppermute | solution.py:26
  77.4 2.3 %collective-permute-start.12 = (bf16[1,4,128,256]{3,2,1,0:T(8,128)(2,1)S(1)}, bf16[1,4,128,256]{3,2,1,0:T(8,128)(2,1)S(1)}, u32[]{:S(2)}, u32[]{:S(2)}) collective-permute-start(bf16[1,4,128,256]{3,2,1,0:T(8,128)(2,1)S(1)} %get-tuple-element.17), channel_id=1, source_target_pairs={{0,16},{4,20},{8,24},{12,28},{16,0},{20,4},{24,8},{28,12},{1,17},{... | collective-permute-start | bytes 786440 | tf_op jit(solution)/shard_map/ppermute | solution.py:26
  79.7 8.1 %collective-permute-done.13 = bf16[2,4,128,256]{3,2,1,0:T(8,128)(2,1)S(1)} collective-permute-done((bf16[2,4,128,256]{3,2,1,0:T(8,128)(2,1)S(1)}, bf16[2,4,128,256]{3,2,1,0:T(8,128)(2,1)S(1)}, u32[]{:S(2)}, u32[]{:S(2)}) %collective-permute-start.13) | collective-permute-done | bytes 524320 | tf_op jit(solution)/shard_map/ppermute | solution.py:26
  88.7 2.3 %collective-permute-start.14 = (bf16[1,4,128,256]{3,2,1,0:T(8,128)(2,1)S(1)}, bf16[1,4,128,256]{3,2,1,0:T(8,128)(2,1)S(1)}, u32[]{:S(2)}, u32[]{:S(2)}) collective-permute-start(bf16[1,4,128,256]{3,2,1,0:T(8,128)(2,1)S(1)} %get-tuple-element.15), channel_id=1, source_target_pairs={{0,16},{4,20},{8,24},{12,28},{16,0},{20,4},{24,8},{28,12},{1,17},{... | collective-permute-start | bytes 786440 | tf_op jit(solution)/shard_map/ppermute | solution.py:26
  91.0 8.1 %collective-permute-done.18 = bf16[2,4,128,256]{3,2,1,0:T(8,128)(2,1)S(1)} collective-permute-done((bf16[2,4,128,256]{3,2,1,0:T(8,128)(2,1)S(1)}, bf16[2,4,128,256]{3,2,1,0:T(8,128)(2,1)S(1)}, u32[]{:S(2)}, u32[]{:S(2)}) %collective-permute-start.18) | collective-permute-done | bytes 524320 | tf_op jit(solution)/shard_map/ppermute | solution.py:26
  99.9 2.3 %collective-permute-start.19 = (bf16[1,4,128,256]{3,2,1,0:T(8,128)(2,1)S(1)}, bf16[1,4,128,256]{3,2,1,0:T(8,128)(2,1)S(1)}, u32[]{:S(2)}, u32[]{:S(2)}) collective-permute-start(bf16[1,4,128,256]{3,2,1,0:T(8,128)(2,1)S(1)} %get-tuple-element.13), channel_id=1, source_target_pairs={{0,16},{4,20},{8,24},{12,28},{16,0},{20,4},{24,8},{28,12},{1,17},{... | collective-permute-start | bytes 786440 | tf_op jit(solution)/shard_map/ppermute | solution.py:26
  102.2 6.8 %collective-permute-done.20 = bf16[2,4,128,256]{3,2,1,0:T(8,128)(2,1)S(1)} collective-permute-done((bf16[2,4,128,256]{3,2,1,0:T(8,128)(2,1)S(1)}, bf16[2,4,128,256]{3,2,1,0:T(8,128)(2,1)S(1)}, u32[]{:S(2)}, u32[]{:S(2)}) %collective-permute-start.20) | collective-permute-done | bytes 524320 | tf_op jit(solution)/shard_map/ppermute | solution.py:26
  109.9 2.3 %collective-permute-start.21 = (bf16[1,4,128,256]{3,2,1,0:T(8,128)(2,1)S(1)}, bf16[1,4,128,256]{3,2,1,0:T(8,128)(2,1)S(1)}, u32[]{:S(2)}, u32[]{:S(2)}) collective-permute-start(bf16[1,4,128,256]{3,2,1,0:T(8,128)(2,1)S(1)} %get-tuple-element.11), channel_id=1, source_target_pairs={{0,16},{4,20},{8,24},{12,28},{16,0},{20,4},{24,8},{28,12},{1,17},{... | collective-permute-start | bytes 786440 | tf_op jit(solution)/shard_map/ppermute | solution.py:26
  112.1 4.6 %shard_map.73.so_far_ref = bf16[128,4096]{1,0:T(8,128)(2,1)} custom-call(s32[1,128]{1,0:T(1,128)} %ids_ref.1, bf16[512,4096]{1,0:T(8,128)(2,1)} %rows_ref.3), custom_call_target="tpu_custom_call" | custom-call | flops 536870912 | bytes 4194304 | tf_op jit(solution)/shard_map/pallas_call | solution.py:235
  117.5 2.1 %shard_map.81.so_far_ref = bf16[128,4096]{1,0:T(8,128)(2,1)} custom-call(s32[1]{0:T(128)} %bitcast.place_ref, bf16[128,4096]{1,0:T(8,128)(2,1)} %shard_map.73.so_far_ref, bf16[1,4,128,256]{3,2,1,0:T(8,128)(2,1)} %get-tuple-element.18.near_ref, bf16[1,4,128,256]{3,2,1,0:T(8,128)(2,1)} %copy-done.6), custom_call_target="tpu_custom_call", output_to_operand_aliasing={{}: (1, {})} | custom-call | bytes 1048576 | tf_op jit(solution)/shard_map/pallas_call | solution.py:259
  120.3 2.1 %shard_map.84.so_far_ref = bf16[128,4096]{1,0:T(8,128)(2,1)} custom-call(s32[1]{0:T(128)} %bitcast.place_ref, bf16[128,4096]{1,0:T(8,128)(2,1)} %shard_map.81.so_far_ref, bf16[1,4,128,256]{3,2,1,0:T(8,128)(2,1)} %get-tuple-element.16.near_ref, bf16[1,4,128,256]{3,2,1,0:T(8,128)(2,1)} %copy-done.7), custom_call_target="tpu_custom_call", output_to_operand_aliasing={{}: (1, {})} | custom-call | bytes 1048576 | tf_op jit(solution)/shard_map/pallas_call | solution.py:259
  123.1 2.1 %shard_map.87.so_far_ref = bf16[128,4096]{1,0:T(8,128)(2,1)} custom-call(s32[1]{0:T(128)} %bitcast.place_ref, bf16[128,4096]{1,0:T(8,128)(2,1)} %shard_map.84.so_far_ref, bf16[1,4,128,256]{3,2,1,0:T(8,128)(2,1)} %get-tuple-element.14.near_ref, bf16[1,4,128,256]{3,2,1,0:T(8,128)(2,1)} %copy-done.8), custom_call_target="tpu_custom_call", output_to_operand_aliasing={{}: (1, {})} | custom-call | bytes 1048576 | tf_op jit(solution)/shard_map/pallas_call | solution.py:259
  126.0 2.1 %shard_map.90 = bf16[128,4096]{1,0:T(8,128)(2,1)} custom-call(s32[1]{0:T(128)} %bitcast.place_ref, bf16[128,4096]{1,0:T(8,128)(2,1)} %shard_map.87.so_far_ref, bf16[1,4,128,256]{3,2,1,0:T(8,128)(2,1)} %get-tuple-element.12.near_ref, bf16[1,4,128,256]{3,2,1,0:T(8,128)(2,1)} %copy-done.9), custom_call_target="tpu_custom_call", output_to_operand_aliasing={{}: (1, {})} | custom-call | bytes 1048576 | tf_op jit(solution)/shard_map/pallas_call | solution.py:259
  (75 shorter events, 23.0 us)
Async XLA Ops:
  0.0 26.2 %collective-permute-start.1 = (s32[1,128]{1,0:T(1,128)}, s32[1,128]{1,0:T(1,128)S(1)}, u32[]{:S(2)}, u32[]{:S(2)}) collective-permute-start(s32[1,128]{1,0:T(1,128)} %ids_ref.1), channel_id=1, source_target_pairs={{0,1},{1,2},{2,3},{4,5},{5,6},{6,7},{8,9},{9,10},{10,11},{12,13},{... | collective-permute-start | bytes 1544 | tf_op jit(solution)/shard_map/ppermute | solution.py:21
  2.4 23.9 %collective-permute-start = (s32[1,128]{1,0:T(1,128)}, s32[1,128]{1,0:T(1,128)S(1)}, u32[]{:S(2)}, u32[]{:S(2)}) collective-permute-start(s32[1,128]{1,0:T(1,128)} %ids_ref.1), channel_id=1, source_target_pairs={{0,2},{1,3},{4,6},{5,7},{8,10},{9,11},{12,14},{13,15},{16,18},{17,... | collective-permute-start | bytes 1544 | tf_op jit(solution)/shard_map/ppermute | solution.py:21
  9.0 17.3 %collective-permute-start.6 = (bf16[512,512]{1,0:T(8,128)(2,1)}, bf16[512,512]{1,0:T(8,128)(2,1)}, u32[]{:S(2)}, u32[]{:S(2)}) collective-permute-start(bf16[512,512]{1,0:T(8,128)(2,1)} %get-tuple-element.10), channel_id=1, source_target_pairs={{0,8},{4,12},{8,0},{12,4},{16,24},{20,28},{24,16},{28,20},{1,9},{5... | collective-permute-start | bytes 1572872 | tf_op jit(solution)/shard_map/ppermute | solution.py:26
  10.6 28.3 %collective-permute-start.15 = (bf16[512,512]{1,0:T(8,128)(2,1)}, bf16[512,512]{1,0:T(8,128)(2,1)}, u32[]{:S(2)}, u32[]{:S(2)}) collective-permute-start(bf16[512,512]{1,0:T(8,128)(2,1)} %get-tuple-element.9), channel_id=1, source_target_pairs={{0,8},{4,12},{8,0},{12,4},{16,24},{20,28},{24,16},{28,20},{1,9},{5... | collective-permute-start | bytes 1572872 | tf_op jit(solution)/shard_map/ppermute | solution.py:26
  11.9 2.2 %copy-start.3 = (bf16[512,4096]{1,0:T(8,128)(2,1)S(1)}, bf16[512,4096]{1,0:T(8,128)(2,1)}, u32[]{:S(2)}) copy-start(bf16[512,4096]{1,0:T(8,128)(2,1)} %rows_ref.3) | copy-start | bytes 12582916
  14.1 0.7 copy-start.5
  17.0 9.3 %copy-start.10 = (s32[1,128]{1,0:T(1,128)S(1)}, s32[1,128]{1,0:T(1,128)}, u32[]{:S(2)}) copy-start(s32[1,128]{1,0:T(1,128)} %ids_ref.1) | copy-start | bytes 1540
  24.3 2.0 %copy-start.1 = (bf16[512,4096]{1,0:T(8,128)(2,1)}, bf16[512,4096]{1,0:T(8,128)(2,1)S(1)}, u32[]{:S(2)}) copy-start(bf16[512,4096]{1,0:T(8,128)(2,1)S(1)} %get-tuple-element.7.normed_ref) | copy-start | bytes 12582916
  26.3 14.7 %collective-permute-start.7 = (bf16[512,512]{1,0:T(8,128)(2,1)}, bf16[512,512]{1,0:T(8,128)(2,1)S(1)}, u32[]{:S(2)}, u32[]{:S(2)}) collective-permute-start(bf16[512,512]{1,0:T(8,128)(2,1)} %collective-permute-done.6), channel_id=1, source_target_pairs={{0,2},{1,3},{2,0},{3,1},{4,6},{5,7},{6,4},{7,5},{8,10},{9,11},{10,... | collective-permute-start | bytes 1572872 | tf_op jit(solution)/shard_map/ppermute | solution.py:26
  26.4 10.8 %collective-permute-start.4 = (s32[1,272]{1,0:T(1,128)S(1)}, s32[1,272]{1,0:T(1,128)S(1)}, u32[]{:S(2)}, u32[]{:S(2)}) collective-permute-start(s32[1,272]{1,0:T(1,128)S(1)} %pad_add_fusion.1), channel_id=1, source_target_pairs={{0,24},{4,28},{8,16},{12,20},{16,8},{20,12},{24,0},{28,4},{1,25},{... | collective-permute-start | bytes 3272 | tf_op jit(solution)/shard_map/ppermute | solution.py:26
  30.1 7.2 %collective-permute-start.3 = (s32[1,272]{1,0:T(1,128)S(1)}, s32[1,272]{1,0:T(1,128)S(1)}, u32[]{:S(2)}, u32[]{:S(2)}) collective-permute-start(s32[1,272]{1,0:T(1,128)S(1)} %pad_add_fusion.1), channel_id=1, source_target_pairs={{0,8},{4,12},{8,0},{12,4},{16,24},{20,28},{24,16},{28,20},{1,9},{5... | collective-permute-start | bytes 3272 | tf_op jit(solution)/shard_map/ppermute | solution.py:26
  30.1 7.2 %collective-permute-start.2 = (s32[1,272]{1,0:T(1,128)S(1)}, s32[1,272]{1,0:T(1,128)S(1)}, u32[]{:S(2)}, u32[]{:S(2)}) collective-permute-start(s32[1,272]{1,0:T(1,128)S(1)} %pad_add_fusion.1), channel_id=1, source_target_pairs={{0,16},{4,20},{8,24},{12,28},{16,0},{20,4},{24,8},{28,12},{1,17},{... | collective-permute-start | bytes 3272 | tf_op jit(solution)/shard_map/ppermute | solution.py:26
  30.8 2.2 %copy-start.2 = (bf16[512,4096]{1,0:T(8,128)(2,1)S(1)}, bf16[512,4096]{1,0:T(8,128)(2,1)}, u32[]{:S(2)}) copy-start(bf16[512,4096]{1,0:T(8,128)(2,1)} %copy-done.1) | copy-start | bytes 12582916
  33.0 9.2 %copy-start.4 = (f32[3,3,512]{2,1,0:T(4,128)S(1)}, f32[3,3,512]{2,1,0:T(4,128)}, u32[]{:S(2)}) copy-start(f32[3,3,512]{2,1,0:T(4,128)} %short_ref.3) | copy-start | bytes 55300
  37.4 3.6 %collective-permute-start.9 = (s32[4,272]{1,0:T(4,128)S(1)}, s32[4,272]{1,0:T(4,128)S(1)}, u32[]{:S(2)}, u32[]{:S(2)}) collective-permute-start(s32[4,272]{1,0:T(4,128)S(1)} %pad_add_fusion), channel_id=1, source_target_pairs={{0,4},{4,0},{8,12},{12,8},{16,20},{20,16},{24,28},{28,24},{1,5},{5... | collective-permute-start | bytes 13064 | tf_op jit(solution)/shard_map/ppermute | solution.py:26
  38.9 12.0 %collective-permute-start.16 = (bf16[512,512]{1,0:T(8,128)(2,1)}, bf16[512,512]{1,0:T(8,128)(2,1)S(1)}, u32[]{:S(2)}, u32[]{:S(2)}) collective-permute-start(bf16[512,512]{1,0:T(8,128)(2,1)} %collective-permute-done.15), channel_id=1, source_target_pairs={{0,2},{1,3},{2,0},{3,1},{4,6},{5,7},{6,4},{7,5},{8,10},{9,11},{10,... | collective-permute-start | bytes 1572872 | tf_op jit(solution)/shard_map/ppermute | solution.py:26
  42.2 18.8 %collective-permute-start.8 = (bf16[2,512,512]{2,1,0:T(8,128)(2,1)S(1)}, bf16[2,512,512]{2,1,0:T(8,128)(2,1)S(1)}, u32[]{:S(2)}, u32[]{:S(2)}) collective-permute-start(bf16[2,512,512]{2,1,0:T(8,128)(2,1)S(1)} %pad_maximum_fusion.even_ref), channel_id=1, source_target_pairs={{0,1},{1,0},{2,3},{3,2},{4,5},{5,4},{6,7},{7,6},{8,9},{9,8},{10,11... | collective-permute-start | bytes 3145736 | tf_op jit(solution)/shard_map/ppermute | solution.py:26
  52.0 14.0 %collective-permute-start.17 = (bf16[2,512,512]{2,1,0:T(8,128)(2,1)S(1)}, bf16[2,512,512]{2,1,0:T(8,128)(2,1)S(1)}, u32[]{:S(2)}, u32[]{:S(2)}) collective-permute-start(bf16[2,512,512]{2,1,0:T(8,128)(2,1)S(1)} %pad_maximum_fusion.1.even_ref), channel_id=1, source_target_pairs={{0,1},{1,0},{2,3},{3,2},{4,5},{5,4},{6,7},{7,6},{8,9},{9,8},{10,11... | collective-permute-start | bytes 3145736 | tf_op jit(solution)/shard_map/ppermute | solution.py:26
  52.1 8.8 %copy-start = (bf16[512,4096]{1,0:T(8,128)(2,1)S(1)}, bf16[512,4096]{1,0:T(8,128)(2,1)}, u32[]{:S(2)}) copy-start(bf16[512,4096]{1,0:T(8,128)(2,1)} %w3.15) | copy-start | bytes 12582916
  52.2 8.8 %collective-permute-start.10 = (bf16[2,128,512]{2,1,0:T(8,128)(2,1)S(1)}, bf16[2,128,512]{2,1,0:T(8,128)(2,1)S(1)}, u32[]{:S(2)}, u32[]{:S(2)}) collective-permute-start(bf16[2,128,512]{2,1,0:T(8,128)(2,1)S(1)} %get-tuple-element.21), channel_id=1, source_target_pairs={{0,8},{4,12},{8,0},{12,4},{16,24},{20,28},{24,16},{28,20},{1,9},{5... | collective-permute-start | bytes 786440 | tf_op jit(solution)/shard_map/ppermute | solution.py:26
  61.7 14.9 %collective-permute-start.11 = (bf16[2,4,128,256]{3,2,1,0:T(8,128)(2,1)S(1)}, bf16[2,4,128,256]{3,2,1,0:T(8,128)(2,1)S(1)}, u32[]{:S(2)}, u32[]{:S(2)}) collective-permute-start(bf16[2,4,128,256]{3,2,1,0:T(8,128)(2,1)S(1)} %shard_map.80), channel_id=1, source_target_pairs={{0,4},{4,0},{8,12},{12,8},{16,20},{20,16},{24,28},{28,24},{1,5},{5... | collective-permute-start | bytes 1572872 | tf_op jit(solution)/shard_map/ppermute | solution.py:26
  63.0 7.7 %collective-permute-start.5 = (bf16[2,128,512]{2,1,0:T(8,128)(2,1)S(1)}, bf16[2,128,512]{2,1,0:T(8,128)(2,1)S(1)}, u32[]{:S(2)}, u32[]{:S(2)}) collective-permute-start(bf16[2,128,512]{2,1,0:T(8,128)(2,1)S(1)} %get-tuple-element.19), channel_id=1, source_target_pairs={{0,8},{4,12},{8,0},{12,4},{16,24},{20,28},{24,16},{28,20},{1,9},{5... | collective-permute-start | bytes 786440 | tf_op jit(solution)/shard_map/ppermute | solution.py:26
  65.3 22.5 %collective-permute-start.13 = (bf16[2,4,128,256]{3,2,1,0:T(8,128)(2,1)S(1)}, bf16[2,4,128,256]{3,2,1,0:T(8,128)(2,1)S(1)}, u32[]{:S(2)}, u32[]{:S(2)}) collective-permute-start(bf16[2,4,128,256]{3,2,1,0:T(8,128)(2,1)S(1)} %shard_map.83), channel_id=1, source_target_pairs={{0,4},{4,0},{8,12},{12,8},{16,20},{20,16},{24,28},{28,24},{1,5},{5... | collective-permute-start | bytes 1572872 | tf_op jit(solution)/shard_map/ppermute | solution.py:26
  66.8 32.3 %collective-permute-start.18 = (bf16[2,4,128,256]{3,2,1,0:T(8,128)(2,1)S(1)}, bf16[2,4,128,256]{3,2,1,0:T(8,128)(2,1)S(1)}, u32[]{:S(2)}, u32[]{:S(2)}) collective-permute-start(bf16[2,4,128,256]{3,2,1,0:T(8,128)(2,1)S(1)} %shard_map.86), channel_id=1, source_target_pairs={{0,4},{4,0},{8,12},{12,8},{16,20},{20,16},{24,28},{28,24},{1,5},{5... | collective-permute-start | bytes 1572872 | tf_op jit(solution)/shard_map/ppermute | solution.py:26
  69.0 40.0 %collective-permute-start.20 = (bf16[2,4,128,256]{3,2,1,0:T(8,128)(2,1)S(1)}, bf16[2,4,128,256]{3,2,1,0:T(8,128)(2,1)S(1)}, u32[]{:S(2)}, u32[]{:S(2)}) collective-permute-start(bf16[2,4,128,256]{3,2,1,0:T(8,128)(2,1)S(1)} %shard_map.89), channel_id=1, source_target_pairs={{0,4},{4,0},{8,12},{12,8},{16,20},{20,16},{24,28},{28,24},{1,5},{5... | collective-permute-start | bytes 1572872 | tf_op jit(solution)/shard_map/ppermute | solution.py:26
  77.4 39.3 %collective-permute-start.12 = (bf16[1,4,128,256]{3,2,1,0:T(8,128)(2,1)S(1)}, bf16[1,4,128,256]{3,2,1,0:T(8,128)(2,1)S(1)}, u32[]{:S(2)}, u32[]{:S(2)}) collective-permute-start(bf16[1,4,128,256]{3,2,1,0:T(8,128)(2,1)S(1)} %get-tuple-element.17), channel_id=1, source_target_pairs={{0,16},{4,20},{8,24},{12,28},{16,0},{20,4},{24,8},{28,12},{1,17},{... | collective-permute-start | bytes 786440 | tf_op jit(solution)/shard_map/ppermute | solution.py:26
  88.7 30.9 %collective-permute-start.14 = (bf16[1,4,128,256]{3,2,1,0:T(8,128)(2,1)S(1)}, bf16[1,4,128,256]{3,2,1,0:T(8,128)(2,1)S(1)}, u32[]{:S(2)}, u32[]{:S(2)}) collective-permute-start(bf16[1,4,128,256]{3,2,1,0:T(8,128)(2,1)S(1)} %get-tuple-element.15), channel_id=1, source_target_pairs={{0,16},{4,20},{8,24},{12,28},{16,0},{20,4},{24,8},{28,12},{1,17},{... | collective-permute-start | bytes 786440 | tf_op jit(solution)/shard_map/ppermute | solution.py:26
  99.9 22.5 %collective-permute-start.19 = (bf16[1,4,128,256]{3,2,1,0:T(8,128)(2,1)S(1)}, bf16[1,4,128,256]{3,2,1,0:T(8,128)(2,1)S(1)}, u32[]{:S(2)}, u32[]{:S(2)}) collective-permute-start(bf16[1,4,128,256]{3,2,1,0:T(8,128)(2,1)S(1)} %get-tuple-element.13), channel_id=1, source_target_pairs={{0,16},{4,20},{8,24},{12,28},{16,0},{20,4},{24,8},{28,12},{1,17},{... | collective-permute-start | bytes 786440 | tf_op jit(solution)/shard_map/ppermute | solution.py:26
  109.9 15.4 %collective-permute-start.21 = (bf16[1,4,128,256]{3,2,1,0:T(8,128)(2,1)S(1)}, bf16[1,4,128,256]{3,2,1,0:T(8,128)(2,1)S(1)}, u32[]{:S(2)}, u32[]{:S(2)}) collective-permute-start(bf16[1,4,128,256]{3,2,1,0:T(8,128)(2,1)S(1)} %get-tuple-element.11), channel_id=1, source_target_pairs={{0,16},{4,20},{8,24},{12,28},{16,0},{20,4},{24,8},{28,12},{1,17},{... | collective-permute-start | bytes 786440 | tf_op jit(solution)/shard_map/ppermute | solution.py:26
  119.6 0.7 copy-start.7
  122.4 0.7 copy-start.8
  125.3 0.7 copy-start.9
  (1 other events, 0.7 us)

commit v4 on v3

v4 whole, which is shorter than its diff:
```python
import functools

import jax
import jax.numpy as jnp
from jax import lax
from jax.experimental import pallas as pl
from jax.experimental.pallas import tpu as pltpu
from jax.sharding import PartitionSpec as P

GROUP = 16
TAPS = 128
SHORT = 3
LANES = 128
LEAD = 16
SPLITS = ((0, 4, 2, ((0, 4),)), (4, 4, 4, ((0, 4),)), (8, 8, 2, ((0, 4), (4, 4))))
SIXTEENTHS = 16


def from_behind(x, axis, by):
    peers = lax.axis_size(axis)
    return lax.ppermute(x, axis, [(i, i + by) for i in range(peers) if i + by < peers])


def swap(x, axis, mask):
    peers = lax.axis_size(axis)
    return lax.ppermute(x, axis, [(i, i ^ mask) for i in range(peers)])


def exchange_bits():
    peers = lax.axis_size("fsdp")
    return [1 << b for b in reversed(range(peers.bit_length() - 1))]


def params(mib=24):
    return pltpu.CompilerParams(vmem_limit_bytes=mib * 1024 * 1024)


def cost(flops, bytes_accessed):
    return pl.CostEstimate(flops=flops, bytes_accessed=bytes_accessed, transcendentals=0)


def whole(array):
    return pl.BlockSpec(array.shape, lambda *_: (0,) * array.ndim)


def level_ids(ids, group):
    masks = [0]
    for bit in group:
        masks += [mask | bit for mask in masks]
    return jnp.concatenate([ids] + [swap(ids, "fsdp", mask) for mask in masks[1:]], axis=0)


def with_lead(ids):
    tok_len = ids.shape[1]
    place = lax.axis_index("ctx")
    one = jnp.where(place >= 1, from_behind(ids, "ctx", 1), -1)
    two = jnp.where(place >= 2, from_behind(ids, "ctx", 2), -1)
    return jnp.concatenate([two[:, tok_len - LEAD :], one, ids], axis=1)


def norm_kernel(rows_ref, gain_ref, normed_ref):
    values = rows_ref[...].astype(jnp.float32)
    inverse_rms = lax.rsqrt(jnp.mean(values * values, axis=-1, keepdims=True) + 1e-06)
    normed_ref[...] = (values * inverse_rms * gain_ref[...]).astype(jnp.bfloat16)


def normalize(embedding, norm_gain):
    vocab, width = embedding.shape
    rows = pl.BlockSpec((vocab // 4, width), lambda i: (i, 0))
    return pl.pallas_call(
        norm_kernel,
        grid=(4,),
        in_specs=[rows, pl.BlockSpec((1, width), lambda i: (0, 0))],
        out_specs=rows,
        out_shape=jax.ShapeDtypeStruct((vocab, width), jnp.bfloat16),
        compiler_params=params(),
        cost_estimate=cost(0, 2_000_000),
    )(embedding, norm_gain.reshape(1, width))


def table_kernel(normed_ref, weight_ref, out_ref):
    out_ref[0] = jnp.dot(normed_ref[...], weight_ref[0], preferred_element_type=jnp.float32).astype(jnp.bfloat16)


def project(normed, in_proj):
    vocab, width = normed.shape
    count, _, panel_width = in_proj.shape
    cols = min(256, panel_width)
    per = panel_width // cols
    return pl.pallas_call(
        table_kernel,
        grid=(count * per,),
        in_specs=[
            whole(normed),
            pl.BlockSpec((1, width, cols), lambda s: (s // per, 0, s % per)),
        ],
        out_specs=pl.BlockSpec((1, vocab, cols), lambda s: (s // per, 0, s % per)),
        out_shape=jax.ShapeDtypeStruct((count, vocab, panel_width), jnp.bfloat16),
        compiler_params=params(),
        cost_estimate=cost(3_000_000_000, 0),
    )(normed, in_proj)


def mixer_kernel(ids_ref, table_ref, short_ref, toeplitz, gated_ref, held_query, held):
    tok_len, panel_width = gated_ref.shape[1:]
    vocab = table_ref.shape[1]
    rows = ids_ref.shape[2]
    reach = 2 * tok_len
    lead = rows - reach
    tiles = panel_width // LANES
    per_tile = LANES // GROUP
    names = lax.broadcasted_iota(jnp.int32, (vocab, rows), 0)
    lane_group = lax.broadcasted_iota(jnp.int32, (tok_len, 2 * LANES), 1) % LANES // GROUP

    def look_up(one_hot, table):
        found = lax.dot_general(one_hot, table, (((0,), (0,)), ((), ())), preferred_element_type=jnp.float32)
        return found.astype(jnp.bfloat16).astype(jnp.float32)

    for v in range(2):
        one_hot = (names == ids_ref[v]).astype(jnp.float32).astype(jnp.bfloat16)
        held[v, 0] = look_up(one_hot, table_ref[1])
        held[v, 1] = look_up(one_hot, table_ref[2])
        held_query[v] = look_up(one_hot[:, rows - lead - tok_len :], table_ref[0])

    def featured(source, i, count, cols):
        total = short_ref[0, i : i + 1, cols] * source[pl.ds(lead, count), cols]
        for j in range(1, SHORT):
            total += short_ref[j, i : i + 1, cols] * source[pl.ds(lead - j, count), cols]
        return total

    for tile in range(tiles):
        cols = slice(tile * LANES, (tile + 1) * LANES)
        products = []
        for v in range(2):
            key = featured(held.at[v, 0], 1, reach, cols)
            value = featured(held.at[v, 1], 2, reach, cols)
            products.append((key * value).astype(jnp.bfloat16))
        both = jnp.concatenate(products, axis=1)
        filtered = None
        for k in range(per_tile):
            one = jnp.dot(
                toeplitz[tile, pl.ds(k * tok_len, tok_len), :], both, preferred_element_type=jnp.float32
            )
            filtered = one if k == 0 else jnp.where(lane_group == k, one, filtered)
        for v in range(2):
            query = featured(held_query.at[v], 0, tok_len, cols)
            gated_ref[v, :, cols] = (query * filtered[:, v * LANES : (v + 1) * LANES]).astype(jnp.bfloat16)


def mix(ids, table, short_taps, toeplitz, tok_len):
    windows, rows = ids.shape
    panel_width = table.shape[2]
    return pl.pallas_call(
        mixer_kernel,
        grid=(windows // 2,),
        in_specs=[pl.BlockSpec((2, 1, rows), lambda p: (p, 0, 0))]
        + [whole(array) for array in (table, short_taps, toeplitz)],
        out_specs=pl.BlockSpec((2, tok_len, panel_width), lambda p: (p, 0, 0)),
        out_shape=jax.ShapeDtypeStruct((windows, tok_len, panel_width), jnp.bfloat16),
        scratch_shapes=[
            pltpu.VMEM((2, LEAD + tok_len, panel_width), jnp.float32),
            pltpu.VMEM((2, 2, rows, panel_width), jnp.float32),
        ],
        compiler_params=params(),
        cost_estimate=cost(1_500_000_000, 0),
    )(ids.reshape(windows, 1, rows), table, short_taps, toeplitz)


def prepare_kernel(place_ref, base_ref, *refs):
    count = len(refs) // 2
    for source, piece in zip(refs[:count], refs[count:]):
        piece[...] = source[...]
    toeplitz_ref = refs[-1]
    tiles, stacked, reach = toeplitz_ref.shape
    per_tile = base_ref.shape[0] // tiles
    tok_len = stacked // per_tile
    for tile in range(tiles):
        for k in range(per_tile):
            g = tile * per_tile + k
            wide = jnp.broadcast_to(base_ref[g : g + 1, :], (tok_len, reach))
            shifted = pltpu.roll(wide, 0, 1, stride=1, stride_axis=0)
            toeplitz_ref[tile, pl.ds(k * tok_len, tok_len), :] = shifted.astype(jnp.bfloat16)


def prepare(place, out_proj, conv_taps, tok_len):
    depth, width = out_proj.shape
    unit = width // SIXTEENTHS
    reach = 2 * tok_len
    per_tile = LANES // GROUP
    tiles = conv_taps.shape[0] // per_tile
    base = jnp.pad(conv_taps[:, ::-1].astype(jnp.float32), ((0, 0), (1, reach - TAPS - 1)))
    ins, outs, shapes = [pl.BlockSpec(base.shape, lambda s, place: (0, 0))], [], []
    for first, extent, sharers, _ in SPLITS:
        cols = extent * unit // sharers
        start = first * unit // cols
        ins.append(pl.BlockSpec((depth, cols), lambda s, place, start=start, n=sharers: (0, start + place[0] % n)))
        outs.append(pl.BlockSpec((depth, cols), lambda s, place: (0, 0)))
        shapes.append(jax.ShapeDtypeStruct((depth, cols), out_proj.dtype))
    shapes.append(jax.ShapeDtypeStruct((tiles, per_tile * tok_len, reach), jnp.bfloat16))
    outs.append(pl.BlockSpec(shapes[-1].shape, lambda s, place: (0, 0, 0)))
    return pl.pallas_call(
        prepare_kernel,
        grid_spec=pltpu.PrefetchScalarGridSpec(num_scalar_prefetch=1, grid=(1,), in_specs=ins, out_specs=outs),
        out_shape=shapes,
        compiler_params=params(),
        cost_estimate=cost(0, 2_000_000),
    )(place, base, *[out_proj] * len(SPLITS))


def panel_kernel(place_ref, mine_ref, other_ref, *refs):
    out_ref = refs[-1]
    count, sharers, tok_len, _ = out_ref.shape
    beside = [ref.at[i] for ref in refs[sharers:-1] for i in range(ref.shape[0])]
    for k in range(sharers):
        total = jnp.dot(mine_ref[...], refs[k][...], preferred_element_type=jnp.float32)
        total += jnp.dot(other_ref[...], beside[k][...], preferred_element_type=jnp.float32)
        for w in range(count):
            out_ref[w, k] = total[w * tok_len : (w + 1) * tok_len].astype(out_ref.dtype)


def panel(place, mine, other, out_proj, beside, split, step):
    count, tok_len, depth = mine.shape
    rows = count * tok_len
    unit = out_proj.shape[1] // SIXTEENTHS
    base, extent, sharers, _ = split
    piece_cols = extent * unit // sharers
    offset, cols = (part * unit // sharers for part in step)
    order = range(sharers)
    fixed = lambda shape: pl.BlockSpec(shape, lambda s, place: (0,) * len(shape))

    def own(k):
        start, per = (base * unit + offset) // cols, piece_cols // cols
        return pl.BlockSpec((depth, cols), lambda s, place: (0, start + (place[0] % sharers ^ k) * per))

    near = lambda a: pl.BlockSpec((a.shape[0], depth, cols), lambda s, place: (0, 0, offset // cols))
    return pl.pallas_call(
        panel_kernel,
        grid_spec=pltpu.PrefetchScalarGridSpec(
            num_scalar_prefetch=1,
            grid=(1,),
            in_specs=[fixed((rows, depth))] * 2 + [own(k) for k in order] + [near(a) for a in beside],
            out_specs=fixed((count, sharers, tok_len, cols)),
        ),
        out_shape=jax.ShapeDtypeStruct((count, sharers, tok_len, cols), jnp.bfloat16),
        compiler_params=params(),
        cost_estimate=cost(400_000_000, 0),
    )(place, mine.reshape(rows, depth), other.reshape(rows, depth), *[out_proj] * sharers, *beside)


def residual_kernel(ids_ref, rows_ref, out_ref):
    names = lax.broadcasted_iota(jnp.int32, (rows_ref.shape[0], ids_ref.shape[1]), 0)
    one_hot = (names == ids_ref[...]).astype(jnp.float32).astype(jnp.bfloat16)
    out_ref[...] = lax.dot_general(
        one_hot, rows_ref[...], (((0,), (0,)), ((), ())), preferred_element_type=jnp.float32
    ).astype(jnp.bfloat16)


def residual(token_ids, embedding):
    vocab, width = embedding.shape
    tok_len = token_ids.shape[1]
    cols = width // 4
    return pl.pallas_call(
        residual_kernel,
        grid=(4,),
        in_specs=[whole(token_ids), pl.BlockSpec((vocab, cols), lambda i: (0, i))],
        out_specs=pl.BlockSpec((tok_len, cols), lambda i: (0, i)),
        out_shape=jax.ShapeDtypeStruct((tok_len, width), jnp.bfloat16),
        compiler_params=params(),
        cost_estimate=cost(400_000_000, 0),
    )(token_ids, embedding)


def place_kernel(split, step, place_ref, so_far_ref, near_ref, far_ref, out_ref):
    _, sharers, _, cols = near_ref.shape
    piece_cols = so_far_ref.shape[1] // sharers
    offset = step[0] * cols // step[1]
    out_ref[...] = so_far_ref[...]
    for k in range(sharers):
        first = (place_ref[0] % sharers ^ k) * piece_cols + offset
        total = near_ref[0, k].astype(jnp.float32) + far_ref[0, k].astype(jnp.float32)
        at = pl.ds(pl.multiple_of(first, LANES), cols)
        out_ref[:, at] = (so_far_ref[:, at].astype(jnp.float32) + total).astype(jnp.bfloat16)


def place_pieces(place, so_far, near, far, split, step):
    tok_len, width = so_far.shape
    base, extent, _, _ = split
    part = pl.BlockSpec((tok_len, extent * width // SIXTEENTHS), lambda s, place: (0, base // extent))
    one = pl.BlockSpec(near.shape, lambda s, place: (0, 0, 0, 0))
    return pl.pallas_call(
        functools.partial(place_kernel, split, step),
        grid_spec=pltpu.PrefetchScalarGridSpec(
            num_scalar_prefetch=1, grid=(1,), in_specs=[part, one, one], out_specs=part
        ),
        out_shape=jax.ShapeDtypeStruct(so_far.shape, so_far.dtype),
        input_output_aliases={1: 0},
        compiler_params=params(),
        cost_estimate=cost(0, 1_000_000),
    )(place, so_far, near, far)


def add(a, b):
    return (a.astype(jnp.float32) + b.astype(jnp.float32)).astype(jnp.bfloat16)


def per_device(token_ids, embedding, norm_gain, in_proj, short_taps, conv_taps, out_proj):
    tok_len = token_ids.shape[1]
    at = lax.axis_index("ctx").reshape(1).astype(jnp.int32)
    bits = exchange_bits()
    tie = lax.optimization_barrier

    *pieces, toeplitz = prepare(at, out_proj, conv_taps, tok_len)
    ids = level_ids(token_ids, bits[:2])
    ids, embedding_then, toeplitz = tie((ids, embedding, toeplitz))
    normed = normalize(embedding_then, norm_gain)
    for group in [bits[i : i + 2] for i in range(2, len(bits), 2)]:
        ids = level_ids(ids, group)
    normed, ids = tie((normed, ids))
    ids = with_lead(ids)
    table = project(normed, in_proj)
    pieces[:2] = [swap(piece, "fsdp", bits[-2]) for piece in pieces[:2]]
    table, pieces[0], pieces[2:] = tie((table, pieces[0], pieces[2:]))
    pieces[2:] = [swap(piece, "fsdp", bits[-2]) for piece in pieces[2:]]

    half = ids.shape[0] // 2
    mine, other = [], []
    for first in (half, 0):
        if first == 0:
            ids, pieces[1], mine[0] = tie((ids, pieces[1], mine[0]))
        gated = mix(ids[first : first + half], table, short_taps, toeplitz, tok_len)
        mine.append(gated[: half // 2])
        other.append(swap(gated[half // 2 :], "fsdp", bits[-2]) if first else None)

    def spread(piece):
        pair = jnp.concatenate([piece[None], swap(piece, "ctx", 1)[None]], axis=0)
        return pair, swap(pair, "ctx", 2)

    other[0], gated = tie((other[0], gated))
    other[1] = swap(gated[half // 2 :], "fsdp", bits[-2])
    beside = [(pieces[0][None], swap(pieces[0], "ctx", 1)[None]), spread(pieces[1])]
    steps = [(split, number, step) for number, split in enumerate(SPLITS) for step in split[3]]

    def send(number, then):
        split, shared, step = steps[number]
        ready, _ = tie((mine[0], then))
        return panel(at, ready, other[0], out_proj, beside[shared], split, step)

    away = [send(0, other[0]), send(1, other[0])]
    own_ids, other[1], away[1] = tie((token_ids, other[1], away[1]))
    out = residual(own_ids, embedding)
    behind = []
    for number, (split, shared, step) in enumerate(steps):
        got = swap(away[number], "fsdp", bits[-1])
        if number >= 2:
            out = place_pieces(at, out, *behind[number - 2])
            got, out = tie((got, out))
        total = panel(at, mine[1], other[1], out_proj, beside[shared], split, step)
        for bit in reversed(bits[:-2]):
            half = total.shape[0] // 2
            far = add(total[half:], got[half:])
            total, got = add(total[:half], got[:half]), swap(far, "fsdp", bit)
        behind.append((total, got, split, step))
        if number == 0:
            last, _ = tie((pieces[2], total))
            beside.append((last[None], swap(last, "ctx", 1)[None]))
        if number + 2 < len(steps):
            away.append(send(number + 2, total if number == 0 else (total, behind[number - 1][1])))
    behind = behind[-2:]
    for last in behind:
        out = place_pieces(at, out, *last)
    return out[None]


def solution(mesh):
    return jax.shard_map(
        per_device,
        mesh=mesh,
        in_specs=(
            P("fsdp", "ctx"),
            P(),
            P(),
            P(None, None, "fsdp"),
            P(None, None, "fsdp"),
            P("fsdp", None),
            P("fsdp", None),
        ),
        out_specs=P("fsdp", "ctx", None),
        check_vma=False,
    )
```

time: 129 us -> 148 us (1.15)
  waiting for transfers between devices: 34 us -> 68.8 us
  local copies, waits for them, and re-layouts: 16 us -> 10.9 us
  Pallas kernels: 41.4 us -> 36.6 us
  starting transfers between devices: 33.2 us -> 29.1 us
    ppermute x20 -> x21, waiting for transfers between devices: 34 us -> 68.8 us  [swap(): return lax.ppermute(x, axis, [(i, i ^ mask) for i in range(peers)])]
    slice x7 -> x5, local copies, waits for them, and re-layouts: 3.11 us -> 0.15 us  [the longest x1 0.07 us: with_lead(): return jnp.concatenate([two[:, tok_len - LEAD:], one, ids], axis=1)]
    pallas_call x2 -> x1, Pallas kernels: 11.4 us -> 8.66 us  [project(): pl.pallas_call(table_kernel, grid=(count * per,), in_specs=[whole(normed)...]
    ppermute x20 -> x21, starting transfers between devices: 26.5 us -> 23.8 us  [swap(): return lax.ppermute(x, axis, [(i, i ^ mask) for i in range(peers)])]
    another operation x2 -> x0, other arithmetic: 2.28 us -> none  [per_device(): even = jnp.stack([piece, swap(piece, 'ctx', 2)])]
    dynamic_slice x1 -> x0, local copies, waits for them, and re-layouts: 2.23 us -> none  [per_device(): lax.dynamic_slice_in_dim(out_proj, (j * 4 + place) * quarter, quarter, ax...]
    pallas_call x1, Pallas kernels: 4.62 us -> 2.65 us  [residual(): pl.pallas_call(residual_kernel, grid=(4,), in_specs=[whole(token_ids), pl...]
    pallas_call x5 -> x6, Pallas kernels: 10.7 us -> 10.5 us  [the longest x4 7.45 us: place_pieces(): pl.pallas_call(functools.partial(place_kernel, split, step), grid_spec=pl...]
  transfers between devices with their start and end apart: 22 -> 23, of which waited for: 7 -> 10; matrix products, arithmetic and copies ran while one was open for 7% -> 2% of each run, Pallas kernels for 31% -> 23%
where the time goes in v4:
time: 148 us; the launch traced here: 147 us
  waiting for transfers between devices  68.8 us (46%)
  Pallas kernels  36.6 us (25%)
  starting transfers between devices  29.1 us (20%)
  local copies, waits for them, and re-layouts  10.9 us (7%)
  other arithmetic  1.76 us (1%)
    ppermute x21, waiting for transfers between devices, swap(): return lax.ppermute(x, axis, [(i, i ^ mask) for i in range(peers)])  68.8 us
    ppermute x21, starting transfers between devices, swap(): return lax.ppermute(x, axis, [(i, i ^ mask) for i in range(peers)])  23.8 us
    unnamed x20, local copies, waits for them, and re-layouts  9.94 us
    pallas_call x2, Pallas kernels, mix(): pl.pallas_call(mixer_kernel, grid=(windows // 2,), in_specs=[pl.BlockSpec...  9.07 us
    pallas_call x1, Pallas kernels, project(): pl.pallas_call(table_kernel, grid=(count * per,), in_specs=[whole(normed)...  8.66 us
    pallas_call x4, Pallas kernels, place_pieces(): pl.pallas_call(functools.partial(place_kernel, split, step), grid_spec=pl...  7.45 us
    pallas_call x8, Pallas kernels, panel(): pl.pallas_call(panel_kernel, grid_spec=pltpu.PrefetchScalarGridSpec(num_s...  5.65 us
    ppermute x2, starting transfers between devices, from_behind(): lax.ppermute(x, axis, [(i, i + by) for i in range(peers) if i + by < peers])  5.31 us
  transfers between devices with their start and end apart: 23, of which 10 were waited for; matrix products, arithmetic and copies ran while one was open for 2% of the time, Pallas kernels for 23%

profile of v4, /device:TPU:0, one launch (start us, length us, event | category | flops | bytes accessed | tf_op | source)
XLA Modules:
  0.0 147.4 jit_solution(274151685231598522)
XLA Ops:
  0.0 5.0 %collective-permute-start.2 = (s32[1,128]{1,0:T(1,128)}, s32[1,128]{1,0:T(1,128)S(1)}, u32[]{:S(2)}, u32[]{:S(2)}) collective-permute-start(s32[1,128]{1,0:T(1,128)} %ids_ref), channel_id=1, source_target_pairs={{0,24},{4,28},{8,16},{12,20},{16,8},{20,12},{24,0},{28,4},{1,25},{... | collective-permute-start | bytes 1544 | tf_op jit(solution)/shard_map/ppermute | solution.py:26
  6.5 2.2 %copy-done = bf16[512,4096]{1,0:T(8,128)(2,1)S(1)} copy-done((bf16[512,4096]{1,0:T(8,128)(2,1)S(1)}, bf16[512,4096]{1,0:T(8,128)(2,1)}, u32[]{:S(2)}) %copy-start) | copy-done | bytes 4194328
  10.4 1.8 %collective-permute-start.3 = (s32[4,128]{1,0:T(4,128)S(1)}, s32[4,128]{1,0:T(4,128)S(1)}, u32[]{:S(2)}, u32[]{:S(2)}) collective-permute-start(s32[4,128]{1,0:T(4,128)S(1)} %pad_add_fusion.2), channel_id=1, source_target_pairs={{0,4},{4,0},{8,12},{12,8},{16,20},{20,16},{24,28},{28,24},{1,5},{5... | collective-permute-start | bytes 6152 | tf_op jit(solution)/shard_map/ppermute | solution.py:26
  12.2 1.2 collective-permute-start.6
  14.2 2.2 %copy-done.2 = bf16[512,4096]{1,0:T(8,128)(2,1)S(1)} copy-done((bf16[512,4096]{1,0:T(8,128)(2,1)S(1)}, bf16[512,4096]{1,0:T(8,128)(2,1)}, u32[]{:S(2)}) %copy-start.2) | copy-done | bytes 4194328
  16.4 2.4 %shard_map.74.normed_ref = bf16[512,4096]{1,0:T(8,128)(2,1)S(1)} custom-call(bf16[512,4096]{1,0:T(8,128)(2,1)S(1)} %copy-done.2, f32[1,4096]{1,0:T(1,128)S(1)} %bitcast.45), custom_call_target="tpu_custom_call" | custom-call | bytes 2000000 | tf_op jit(solution)/shard_map/pallas_call | solution.py:70
  18.8 1.3 collective-permute-start.5
  20.1 4.0 %collective-permute-start.4 = (s32[8,128]{1,0:T(8,128)S(1)}, s32[8,128]{1,0:T(8,128)S(1)}, u32[]{:S(2)}, u32[]{:S(2)}) collective-permute-start(s32[8,128]{1,0:T(8,128)S(1)} %pad_add_fusion.1), channel_id=1, source_target_pairs={{0,2},{1,3},{4,6},{5,7},{8,10},{9,11},{12,14},{13,15},{16,18},{17,... | collective-permute-start | bytes 12296 | tf_op jit(solution)/shard_map/ppermute | solution.py:21
  24.2 4.6 %copy-done.4 = bf16[3,4096,512]{2,1,0:T(8,128)(2,1)S(1)} copy-done((bf16[3,4096,512]{2,1,0:T(8,128)(2,1)S(1)}, bf16[3,4096,512]{2,1,0:T(8,128)(2,1)}, u32[]{:S(2)}) %copy-start.4) | copy-done | bytes 12582936
  28.7 8.7 %shard_map.75.table_ref = bf16[3,512,512]{2,1,0:T(8,128)(2,1)S(1)} custom-call(bf16[512,4096]{1,0:T(8,128)(2,1)S(1)} %shard_map.74.normed_ref, bf16[3,4096,512]{2,1,0:T(8,128)(2,1)S(1)} %copy-done.4), custom_call_target="tpu_custom_call" | custom-call | flops 3000000000 | tf_op jit(solution)/shard_map/pallas_call | solution.py:90
  37.6 4.5 %shard_map.76 = bf16[4,128,512]{2,1,0:T(8,128)(2,1)S(1)} custom-call(s32[4,1,272]{2,1,0:T(1,128)S(1)} %copy.12.ids_ref, bf16[3,512,512]{2,1,0:T(8,128)(2,1)S(1)} %shard_map.75.table_ref, f32[3,3,512]{2,1,0:T(4,128)S(1)} %copy-done.9, bf16[4,1024,256]{2,1,0:T(8,128)(2,1)S(1)} %get-tuple-element.42.toeplitz), custom_call_target="tpu_custom_call" | custom-call | flops 1500000000 | tf_op jit(solution)/shard_map/pallas_call | solution.py:153
  42.8 1.3 collective-permute-start.8
  46.0 4.5 %shard_map.77 = bf16[4,128,512]{2,1,0:T(8,128)(2,1)S(1)} custom-call(s32[4,1,272]{2,1,0:T(1,128)S(1)} %reshape.43.ids_ref, bf16[3,512,512]{2,1,0:T(8,128)(2,1)S(1)} %shard_map.75.table_ref, f32[3,3,512]{2,1,0:T(4,128)S(1)} %copy-done.9, bf16[4,1024,256]{2,1,0:T(8,128)(2,1)S(1)} %get-tuple-element.42.toeplitz), custom_call_target="tpu_custom_call" | custom-call | flops 1500000000 | tf_op jit(solution)/shard_map/pallas_call | solution.py:153
  50.6 1.5 %collective-permute-done.8 = bf16[2,128,512]{2,1,0:T(8,128)(2,1)S(1)} collective-permute-done((bf16[2,128,512]{2,1,0:T(8,128)(2,1)S(1)}, bf16[2,128,512]{2,1,0:T(8,128)(2,1)S(1)}, u32[]{:S(2)}, u32[]{:S(2)}) %collective-permute-start.8) | collective-permute-done | bytes 262176 | tf_op jit(solution)/shard_map/ppermute | solution.py:26
  53.4 1.3 collective-permute-start.9
  54.7 4.6 %collective-permute-done.11.refs_5_ = bf16[2,512,256]{2,1,0:T(8,128)(2,1)S(1)} collective-permute-done((bf16[2,512,256]{2,1,0:T(8,128)(2,1)S(1)}, bf16[2,512,256]{2,1,0:T(8,128)(2,1)S(1)}, u32[]{:S(2)}, u32[]{:S(2)}) %collective-permute-start.11) | collective-permute-done | bytes 524320 | tf_op jit(solution)/shard_map/ppermute | solution.py:26
  60.1 19.2 %collective-permute-done.9 = bf16[2,128,512]{2,1,0:T(8,128)(2,1)S(1)} collective-permute-done((bf16[2,128,512]{2,1,0:T(8,128)(2,1)S(1)}, bf16[2,128,512]{2,1,0:T(8,128)(2,1)S(1)}, u32[]{:S(2)}, u32[]{:S(2)}) %collective-permute-start.9) | collective-permute-done | bytes 262176 | tf_op jit(solution)/shard_map/ppermute | solution.py:26
  80.8 2.4 %collective-permute-start.15 = (bf16[1,2,128,512]{3,2,1,0:T(8,128)(2,1)S(1)}, bf16[1,2,128,512]{3,2,1,0:T(8,128)(2,1)S(1)}, u32[]{:S(2)}, u32[]{:S(2)}) collective-permute-start(bf16[1,2,128,512]{3,2,1,0:T(8,128)(2,1)S(1)} %get-tuple-element.68), channel_id=1, source_target_pairs={{0,16},{4,20},{8,24},{12,28},{16,0},{20,4},{24,8},{28,12},{1,17},{... | collective-permute-start | bytes 786440 | tf_op jit(solution)/shard_map/ppermute | solution.py:26
  84.0 10.6 %collective-permute-done.12 = bf16[2,4,128,256]{3,2,1,0:T(8,128)(2,1)S(1)} collective-permute-done((bf16[2,4,128,256]{3,2,1,0:T(8,128)(2,1)S(1)}, bf16[2,4,128,256]{3,2,1,0:T(8,128)(2,1)S(1)}, u32[]{:S(2)}, u32[]{:S(2)}) %collective-permute-start.12) | collective-permute-done | bytes 524320 | tf_op jit(solution)/shard_map/ppermute | solution.py:26
  96.4 1.6 %collective-permute-start.19 = (bf16[2,2,128,512]{3,2,1,0:T(8,128)(2,1)S(1)}, bf16[2,2,128,512]{3,2,1,0:T(8,128)(2,1)S(1)}, u32[]{:S(2)}, u32[]{:S(2)}) collective-permute-start(bf16[2,2,128,512]{3,2,1,0:T(8,128)(2,1)S(1)} %shard_map.83), channel_id=1, source_target_pairs={{0,4},{4,0},{8,12},{12,8},{16,20},{20,16},{24,28},{28,24},{1,5},{5... | collective-permute-start | bytes 1572872 | tf_op jit(solution)/shard_map/ppermute | solution.py:26
  99.3 1.5 %collective-permute-start.20 = (bf16[1,4,128,256]{3,2,1,0:T(8,128)(2,1)S(1)}, bf16[1,4,128,256]{3,2,1,0:T(8,128)(2,1)S(1)}, u32[]{:S(2)}, u32[]{:S(2)}) collective-permute-start(bf16[1,4,128,256]{3,2,1,0:T(8,128)(2,1)S(1)} %get-tuple-element.65), channel_id=1, source_target_pairs={{0,16},{4,20},{8,24},{12,28},{16,0},{20,4},{24,8},{28,12},{1,17},{... | collective-permute-start | bytes 786440 | tf_op jit(solution)/shard_map/ppermute | solution.py:26
  100.8 2.6 %shard_map.84.so_far_ref = bf16[128,4096]{1,0:T(8,128)(2,1)} custom-call(s32[1,128]{1,0:T(1,128)S(1)} %copy-done.6, bf16[512,4096]{1,0:T(8,128)(2,1)S(1)} %copy-done.3), custom_call_target="tpu_custom_call" | custom-call | flops 400000000 | tf_op jit(solution)/shard_map/pallas_call | solution.py:262
  103.4 1.8 %shard_map.85.so_far_ref = bf16[128,4096]{1,0:T(8,128)(2,1)} custom-call(s32[1]{0:T(128)} %bitcast.place_ref, bf16[128,4096]{1,0:T(8,128)(2,1)} %shard_map.84.so_far_ref, bf16[1,2,128,512]{3,2,1,0:T(8,128)(2,1)S(1)} %get-tuple-element.67.near_ref, bf16[1,2,128,512]{3,2,1,0:T(8,128)(2,1)S(1)} %collective-permute-done.15.far_ref), custom_call_target="tpu_custom_call", output_to_operand_aliasing={{}: (1, {})} | custom-call | bytes 1000000 | tf_op jit(solution)/shard_map/pallas_call | solution.py:290
  106.6 4.7 %collective-permute-done.19 = bf16[2,2,128,512]{3,2,1,0:T(8,128)(2,1)S(1)} collective-permute-done((bf16[2,2,128,512]{3,2,1,0:T(8,128)(2,1)S(1)}, bf16[2,2,128,512]{3,2,1,0:T(8,128)(2,1)S(1)}, u32[]{:S(2)}, u32[]{:S(2)}) %collective-permute-start.19) | collective-permute-done | bytes 524320 | tf_op jit(solution)/shard_map/ppermute | solution.py:26
  111.3 1.4 collective-permute-done.20.far_ref
  112.8 1.8 %shard_map.86.so_far_ref = bf16[128,4096]{1,0:T(8,128)(2,1)} custom-call(s32[1]{0:T(128)} %bitcast.place_ref, bf16[128,4096]{1,0:T(8,128)(2,1)} %shard_map.85.so_far_ref, bf16[1,4,128,256]{3,2,1,0:T(8,128)(2,1)S(1)} %get-tuple-element.66.near_ref, bf16[1,4,128,256]{3,2,1,0:T(8,128)(2,1)S(1)} %collective-permute-done.20.far_ref), custom_call_target="tpu_custom_call", output_to_operand_aliasing={{}: (1, {})} | custom-call | bytes 1000000 | tf_op jit(solution)/shard_map/pallas_call | solution.py:290
  114.6 6.3 %collective-permute-done.18 = bf16[2,2,128,512]{3,2,1,0:T(8,128)(2,1)S(1)} collective-permute-done((bf16[2,2,128,512]{3,2,1,0:T(8,128)(2,1)S(1)}, bf16[2,2,128,512]{3,2,1,0:T(8,128)(2,1)S(1)}, u32[]{:S(2)}, u32[]{:S(2)}) %collective-permute-start.18) | collective-permute-done | bytes 524320 | tf_op jit(solution)/shard_map/ppermute | solution.py:26
  121.0 1.9 %collective-permute-start.21 = (bf16[1,2,128,512]{3,2,1,0:T(8,128)(2,1)S(1)}, bf16[1,2,128,512]{3,2,1,0:T(8,128)(2,1)S(1)}, u32[]{:S(2)}, u32[]{:S(2)}) collective-permute-start(bf16[1,2,128,512]{3,2,1,0:T(8,128)(2,1)S(1)} %get-tuple-element.63), channel_id=1, source_target_pairs={{0,16},{4,20},{8,24},{12,28},{16,0},{20,4},{24,8},{28,12},{1,17},{... | collective-permute-start | bytes 786440 | tf_op jit(solution)/shard_map/ppermute | solution.py:26
  124.2 18.0 %collective-permute-done.21.far_ref = bf16[1,2,128,512]{3,2,1,0:T(8,128)(2,1)S(1)} collective-permute-done((bf16[1,2,128,512]{3,2,1,0:T(8,128)(2,1)S(1)}, bf16[1,2,128,512]{3,2,1,0:T(8,128)(2,1)S(1)}, u32[]{:S(2)}, u32[]{:S(2)}) %collective-permute-start.21) | collective-permute-done | bytes 262176 | tf_op jit(solution)/shard_map/ppermute | solution.py:26
  142.2 2.0 %shard_map.88.so_far_ref = bf16[128,4096]{1,0:T(8,128)(2,1)} custom-call(s32[1]{0:T(128)} %bitcast.place_ref, bf16[128,4096]{1,0:T(8,128)(2,1)} %shard_map.86.so_far_ref, bf16[1,2,128,512]{3,2,1,0:T(8,128)(2,1)S(1)} %get-tuple-element.64.near_ref, bf16[1,2,128,512]{3,2,1,0:T(8,128)(2,1)S(1)} %collective-permute-done.21.far_ref), custom_call_target="tpu_custom_call", output_to_operand_aliasing={{}: (1, {})} | custom-call | bytes 1000000 | tf_op jit(solution)/shard_map/pallas_call | solution.py:290
  144.1 1.3 collective-permute-done.22.far_ref
  145.5 2.0 %shard_map.90 = bf16[128,4096]{1,0:T(8,128)(2,1)} custom-call(s32[1]{0:T(128)} %bitcast.place_ref, bf16[128,4096]{1,0:T(8,128)(2,1)} %shard_map.88.so_far_ref, bf16[1,2,128,512]{3,2,1,0:T(8,128)(2,1)S(1)} %get-tuple-element.62.near_ref, bf16[1,2,128,512]{3,2,1,0:T(8,128)(2,1)S(1)} %collective-permute-done.22.far_ref), custom_call_target="tpu_custom_call", output_to_operand_aliasing={{}: (1, {})} | custom-call | bytes 1000000 | tf_op jit(solution)/shard_map/pallas_call | solution.py:290
  (72 shorter events, 16.8 us)
Async XLA Ops:
  0.0 10.3 %collective-permute-start.2 = (s32[1,128]{1,0:T(1,128)}, s32[1,128]{1,0:T(1,128)S(1)}, u32[]{:S(2)}, u32[]{:S(2)}) collective-permute-start(s32[1,128]{1,0:T(1,128)} %ids_ref), channel_id=1, source_target_pairs={{0,24},{4,28},{8,16},{12,20},{16,8},{20,12},{24,0},{28,4},{1,25},{... | collective-permute-start | bytes 1544 | tf_op jit(solution)/shard_map/ppermute | solution.py:26
  5.0 5.3 %collective-permute-start.1 = (s32[1,128]{1,0:T(1,128)}, s32[1,128]{1,0:T(1,128)S(1)}, u32[]{:S(2)}, u32[]{:S(2)}) collective-permute-start(s32[1,128]{1,0:T(1,128)} %ids_ref), channel_id=1, source_target_pairs={{0,8},{4,12},{8,0},{12,4},{16,24},{20,28},{24,16},{28,20},{1,9},{5... | collective-permute-start | bytes 1544 | tf_op jit(solution)/shard_map/ppermute | solution.py:26
  5.1 5.3 %collective-permute-start = (s32[1,128]{1,0:T(1,128)}, s32[1,128]{1,0:T(1,128)S(1)}, u32[]{:S(2)}, u32[]{:S(2)}) collective-permute-start(s32[1,128]{1,0:T(1,128)} %ids_ref), channel_id=1, source_target_pairs={{0,16},{4,20},{8,24},{12,28},{16,0},{20,4},{24,8},{28,12},{1,17},{... | collective-permute-start | bytes 1544 | tf_op jit(solution)/shard_map/ppermute | solution.py:26
  6.5 2.2 %copy-start = (bf16[512,4096]{1,0:T(8,128)(2,1)S(1)}, bf16[512,4096]{1,0:T(8,128)(2,1)}, u32[]{:S(2)}) copy-start(bf16[512,4096]{1,0:T(8,128)(2,1)} %refs_1_.17) | copy-start | bytes 12582916
  8.7 1.7 %copy-start.6 = (s32[1,128]{1,0:T(1,128)S(1)}, s32[1,128]{1,0:T(1,128)}, u32[]{:S(2)}) copy-start(s32[1,128]{1,0:T(1,128)} %ids_ref) | copy-start | bytes 1540
  8.7 5.5 %copy-start.5 = (f32[4096]{0:T(1024)S(1)}, f32[4096]{0:T(1024)}, u32[]{:S(2)}) copy-start(f32[4096]{0:T(1024)} %param.9) | copy-start | bytes 49156
  10.4 8.4 %collective-permute-start.3 = (s32[4,128]{1,0:T(4,128)S(1)}, s32[4,128]{1,0:T(4,128)S(1)}, u32[]{:S(2)}, u32[]{:S(2)}) collective-permute-start(s32[4,128]{1,0:T(4,128)S(1)} %pad_add_fusion.2), channel_id=1, source_target_pairs={{0,4},{4,0},{8,12},{12,8},{16,20},{20,16},{24,28},{28,24},{1,5},{5... | collective-permute-start | bytes 6152 | tf_op jit(solution)/shard_map/ppermute | solution.py:26
  12.2 30.1 %collective-permute-start.6 = (bf16[512,256]{1,0:T(8,128)(2,1)S(1)}, bf16[512,256]{1,0:T(8,128)(2,1)}, u32[]{:S(2)}, u32[]{:S(2)}) collective-permute-start(bf16[512,256]{1,0:T(8,128)(2,1)S(1)} %get-tuple-element.37), channel_id=1, source_target_pairs={{0,8},{4,12},{8,0},{12,4},{16,24},{20,28},{24,16},{28,20},{1,9},{5... | collective-permute-start | bytes 786440 | tf_op jit(solution)/shard_map/ppermute | solution.py:26
  13.4 24.2 %collective-permute-start.7 = (bf16[512,512]{1,0:T(8,128)(2,1)S(1)}, bf16[512,512]{1,0:T(8,128)(2,1)S(1)}, u32[]{:S(2)}, u32[]{:S(2)}) collective-permute-start(bf16[512,512]{1,0:T(8,128)(2,1)S(1)} %get-tuple-element.39), channel_id=1, source_target_pairs={{0,8},{4,12},{8,0},{12,4},{16,24},{20,28},{24,16},{28,20},{1,9},{5... | collective-permute-start | bytes 1572872 | tf_op jit(solution)/shard_map/ppermute | solution.py:26
  14.2 2.2 %copy-start.2 = (bf16[512,4096]{1,0:T(8,128)(2,1)S(1)}, bf16[512,4096]{1,0:T(8,128)(2,1)}, u32[]{:S(2)}) copy-start(bf16[512,4096]{1,0:T(8,128)(2,1)} %rows_ref.2) | copy-start | bytes 12582916
  18.8 18.7 %collective-permute-start.5 = (s32[8,128]{1,0:T(8,128)S(1)}, s32[8,128]{1,0:T(8,128)S(1)}, u32[]{:S(2)}, u32[]{:S(2)}) collective-permute-start(s32[8,128]{1,0:T(8,128)S(1)} %pad_add_fusion.1), channel_id=1, source_target_pairs={{0,1},{1,2},{2,3},{4,5},{5,6},{6,7},{8,9},{9,10},{10,11},{12,13},{... | collective-permute-start | bytes 12296 | tf_op jit(solution)/shard_map/ppermute | solution.py:21
  20.1 17.3 %collective-permute-start.4 = (s32[8,128]{1,0:T(8,128)S(1)}, s32[8,128]{1,0:T(8,128)S(1)}, u32[]{:S(2)}, u32[]{:S(2)}) collective-permute-start(s32[8,128]{1,0:T(8,128)S(1)} %pad_add_fusion.1), channel_id=1, source_target_pairs={{0,2},{1,3},{4,6},{5,7},{8,10},{9,11},{12,14},{13,15},{16,18},{17,... | collective-permute-start | bytes 12296 | tf_op jit(solution)/shard_map/ppermute | solution.py:21
  24.1 4.6 %copy-start.4 = (bf16[3,4096,512]{2,1,0:T(8,128)(2,1)S(1)}, bf16[3,4096,512]{2,1,0:T(8,128)(2,1)}, u32[]{:S(2)}) copy-start(bf16[3,4096,512]{2,1,0:T(8,128)(2,1)} %weight_ref.1) | copy-start | bytes 37748740
  28.7 8.9 %copy-start.9 = (f32[3,3,512]{2,1,0:T(4,128)S(1)}, f32[3,3,512]{2,1,0:T(4,128)}, u32[]{:S(2)}) copy-start(f32[3,3,512]{2,1,0:T(4,128)} %short_ref.3) | copy-start | bytes 55300
  37.4 6.8 %copy-start.8 = (bf16[512,1024]{1,0:T(8,128)(2,1)S(1)}, bf16[512,1024]{1,0:T(8,128)(2,1)}, u32[]{:S(2)}) copy-start(bf16[512,1024]{1,0:T(8,128)(2,1)} %copy-done.7) | copy-start | bytes 3145732
  42.2 9.9 %copy-start.1 = (bf16[512,4096]{1,0:T(8,128)(2,1)S(1)}, bf16[512,4096]{1,0:T(8,128)(2,1)}, u32[]{:S(2)}) copy-start(bf16[512,4096]{1,0:T(8,128)(2,1)} %refs_1_.17) | copy-start | bytes 12582916
  42.2 2.7 %collective-permute-start.10 = (bf16[512,256]{1,0:T(8,128)(2,1)}, bf16[512,256]{1,0:T(8,128)(2,1)S(1)}, u32[]{:S(2)}, u32[]{:S(2)}) collective-permute-start(bf16[512,256]{1,0:T(8,128)(2,1)} %collective-permute-done.6), channel_id=1, source_target_pairs={{0,1},{1,0},{2,3},{3,2},{4,5},{5,4},{6,7},{7,6},{8,9},{9,8},{10,11... | collective-permute-start | bytes 786440 | tf_op jit(solution)/shard_map/ppermute | solution.py:26
  42.3 9.7 %collective-permute-start.13 = (bf16[512,512]{1,0:T(8,128)(2,1)S(1)}, bf16[512,512]{1,0:T(8,128)(2,1)S(1)}, u32[]{:S(2)}, u32[]{:S(2)}) collective-permute-start(bf16[512,512]{1,0:T(8,128)(2,1)S(1)} %collective-permute-done.7), channel_id=1, source_target_pairs={{0,1},{1,0},{2,3},{3,2},{4,5},{5,4},{6,7},{7,6},{8,9},{9,8},{10,11... | collective-permute-start | bytes 1572872 | tf_op jit(solution)/shard_map/ppermute | solution.py:26
  42.8 9.2 %collective-permute-start.8 = (bf16[2,128,512]{2,1,0:T(8,128)(2,1)S(1)}, bf16[2,128,512]{2,1,0:T(8,128)(2,1)S(1)}, u32[]{:S(2)}, u32[]{:S(2)}) collective-permute-start(bf16[2,128,512]{2,1,0:T(8,128)(2,1)S(1)} %get-tuple-element.69), channel_id=1, source_target_pairs={{0,8},{4,12},{8,0},{12,4},{16,24},{20,28},{24,16},{28,20},{1,9},{5... | collective-permute-start | bytes 786440 | tf_op jit(solution)/shard_map/ppermute | solution.py:26
  44.1 36.0 %collective-permute-start.16 = (bf16[512,1024]{1,0:T(8,128)(2,1)S(1)}, bf16[512,1024]{1,0:T(8,128)(2,1)S(1)}, u32[]{:S(2)}, u32[]{:S(2)}) collective-permute-start(bf16[512,1024]{1,0:T(8,128)(2,1)S(1)} %copy-done.8), channel_id=1, source_target_pairs={{0,8},{4,12},{8,0},{12,4},{16,24},{20,28},{24,16},{28,20},{1,9},{5... | collective-permute-start | bytes 3145736 | tf_op jit(solution)/shard_map/ppermute | solution.py:26
  45.9 13.4 %collective-permute-start.11 = (bf16[2,512,256]{2,1,0:T(8,128)(2,1)S(1)}, bf16[2,512,256]{2,1,0:T(8,128)(2,1)S(1)}, u32[]{:S(2)}, u32[]{:S(2)}) collective-permute-start(bf16[2,512,256]{2,1,0:T(8,128)(2,1)S(1)} %pad_maximum_fusion.refs_4_), channel_id=1, source_target_pairs={{0,2},{1,3},{2,0},{3,1},{4,6},{5,7},{6,4},{7,5},{8,10},{9,11},{10,... | collective-permute-start | bytes 1572872 | tf_op jit(solution)/shard_map/ppermute | solution.py:26
  52.8 27.2 %collective-permute-start.14 = (bf16[2,2,128,512]{3,2,1,0:T(8,128)(2,1)S(1)}, bf16[2,2,128,512]{3,2,1,0:T(8,128)(2,1)S(1)}, u32[]{:S(2)}, u32[]{:S(2)}) collective-permute-start(bf16[2,2,128,512]{3,2,1,0:T(8,128)(2,1)S(1)} %shard_map.81), channel_id=1, source_target_pairs={{0,4},{4,0},{8,12},{12,8},{16,20},{20,16},{24,28},{28,24},{1,5},{5... | collective-permute-start | bytes 1572872 | tf_op jit(solution)/shard_map/ppermute | solution.py:26
  53.4 25.9 %collective-permute-start.9 = (bf16[2,128,512]{2,1,0:T(8,128)(2,1)S(1)}, bf16[2,128,512]{2,1,0:T(8,128)(2,1)S(1)}, u32[]{:S(2)}, u32[]{:S(2)}) collective-permute-start(bf16[2,128,512]{2,1,0:T(8,128)(2,1)S(1)} %slice.75), channel_id=1, source_target_pairs={{0,8},{4,12},{8,0},{12,4},{16,24},{20,28},{24,16},{28,20},{1,9},{5... | collective-permute-start | bytes 786440 | tf_op jit(solution)/shard_map/ppermute | solution.py:26
  80.2 15.5 %collective-permute-start.17 = (bf16[512,1024]{1,0:T(8,128)(2,1)S(1)}, bf16[512,1024]{1,0:T(8,128)(2,1)S(1)}, u32[]{:S(2)}, u32[]{:S(2)}) collective-permute-start(bf16[512,1024]{1,0:T(8,128)(2,1)S(1)} %collective-permute-done.16), channel_id=1, source_target_pairs={{0,1},{1,0},{2,3},{3,2},{4,5},{5,4},{6,7},{7,6},{8,9},{9,8},{10,11... | collective-permute-start | bytes 3145736 | tf_op jit(solution)/shard_map/ppermute | solution.py:26
  80.2 14.3 %collective-permute-start.12 = (bf16[2,4,128,256]{3,2,1,0:T(8,128)(2,1)S(1)}, bf16[2,4,128,256]{3,2,1,0:T(8,128)(2,1)S(1)}, u32[]{:S(2)}, u32[]{:S(2)}) collective-permute-start(bf16[2,4,128,256]{3,2,1,0:T(8,128)(2,1)S(1)} %shard_map.78), channel_id=1, source_target_pairs={{0,4},{4,0},{8,12},{12,8},{16,20},{20,16},{24,28},{28,24},{1,5},{5... | collective-permute-start | bytes 1572872 | tf_op jit(solution)/shard_map/ppermute | solution.py:26
  80.8 14.9 %collective-permute-start.15 = (bf16[1,2,128,512]{3,2,1,0:T(8,128)(2,1)S(1)}, bf16[1,2,128,512]{3,2,1,0:T(8,128)(2,1)S(1)}, u32[]{:S(2)}, u32[]{:S(2)}) collective-permute-start(bf16[1,2,128,512]{3,2,1,0:T(8,128)(2,1)S(1)} %get-tuple-element.68), channel_id=1, source_target_pairs={{0,16},{4,20},{8,24},{12,28},{16,0},{20,4},{24,8},{28,12},{1,17},{... | collective-permute-start | bytes 786440 | tf_op jit(solution)/shard_map/ppermute | solution.py:26
  96.4 14.9 %collective-permute-start.19 = (bf16[2,2,128,512]{3,2,1,0:T(8,128)(2,1)S(1)}, bf16[2,2,128,512]{3,2,1,0:T(8,128)(2,1)S(1)}, u32[]{:S(2)}, u32[]{:S(2)}) collective-permute-start(bf16[2,2,128,512]{3,2,1,0:T(8,128)(2,1)S(1)} %shard_map.83), channel_id=1, source_target_pairs={{0,4},{4,0},{8,12},{12,8},{16,20},{20,16},{24,28},{28,24},{1,5},{5... | collective-permute-start | bytes 1572872 | tf_op jit(solution)/shard_map/ppermute | solution.py:26
  98.0 2.8 %copy-start.3 = (bf16[512,4096]{1,0:T(8,128)(2,1)S(1)}, bf16[512,4096]{1,0:T(8,128)(2,1)}, u32[]{:S(2)}) copy-start(bf16[512,4096]{1,0:T(8,128)(2,1)} %rows_ref.2) | copy-start | bytes 12582916
  98.7 22.2 %collective-permute-start.18 = (bf16[2,2,128,512]{3,2,1,0:T(8,128)(2,1)S(1)}, bf16[2,2,128,512]{3,2,1,0:T(8,128)(2,1)S(1)}, u32[]{:S(2)}, u32[]{:S(2)}) collective-permute-start(bf16[2,2,128,512]{3,2,1,0:T(8,128)(2,1)S(1)} %shard_map.82), channel_id=1, source_target_pairs={{0,4},{4,0},{8,12},{12,8},{16,20},{20,16},{24,28},{28,24},{1,5},{5... | collective-permute-start | bytes 1572872 | tf_op jit(solution)/shard_map/ppermute | solution.py:26
  99.3 13.5 %collective-permute-start.20 = (bf16[1,4,128,256]{3,2,1,0:T(8,128)(2,1)S(1)}, bf16[1,4,128,256]{3,2,1,0:T(8,128)(2,1)S(1)}, u32[]{:S(2)}, u32[]{:S(2)}) collective-permute-start(bf16[1,4,128,256]{3,2,1,0:T(8,128)(2,1)S(1)} %get-tuple-element.65), channel_id=1, source_target_pairs={{0,16},{4,20},{8,24},{12,28},{16,0},{20,4},{24,8},{28,12},{1,17},{... | collective-permute-start | bytes 786440 | tf_op jit(solution)/shard_map/ppermute | solution.py:26
  121.0 21.2 %collective-permute-start.21 = (bf16[1,2,128,512]{3,2,1,0:T(8,128)(2,1)S(1)}, bf16[1,2,128,512]{3,2,1,0:T(8,128)(2,1)S(1)}, u32[]{:S(2)}, u32[]{:S(2)}) collective-permute-start(bf16[1,2,128,512]{3,2,1,0:T(8,128)(2,1)S(1)} %get-tuple-element.63), channel_id=1, source_target_pairs={{0,16},{4,20},{8,24},{12,28},{16,0},{20,4},{24,8},{28,12},{1,17},{... | collective-permute-start | bytes 786440 | tf_op jit(solution)/shard_map/ppermute | solution.py:26
  123.0 22.4 %collective-permute-start.22 = (bf16[1,2,128,512]{3,2,1,0:T(8,128)(2,1)S(1)}, bf16[1,2,128,512]{3,2,1,0:T(8,128)(2,1)S(1)}, u32[]{:S(2)}, u32[]{:S(2)}) collective-permute-start(bf16[1,2,128,512]{3,2,1,0:T(8,128)(2,1)S(1)} %get-tuple-element.61), channel_id=1, source_target_pairs={{0,16},{4,20},{8,24},{12,28},{16,0},{20,4},{24,8},{28,12},{1,17},{... | collective-permute-start | bytes 786440 | tf_op jit(solution)/shard_map/ppermute | solution.py:26
  (1 other events, 1.0 us)

commit v5 on v4

--- a/solution.py
+++ b/solution.py
@@ -12,8 +12,9 @@
 SHORT = 3
 LANES = 128
 LEAD = 16
-SPLITS = ((0, 4, 2, ((0, 4),)), (4, 4, 4, ((0, 4),)), (8, 8, 2, ((0, 4), (4, 4))))
+SPLITS = ((0, 4, 2, ((0, 4),)), (4, 4, 4, ((0, 4),)), (8, 8, 4, ((0, 4), (4, 4))))
 SIXTEENTHS = 16
+ORDER = {2: (0, 1), 4: (0, 2, 1, 3)}
 
 
 def from_behind(x, axis, by):
@@ -40,7 +41,7 @@
 
 
 def whole(array):
-    return pl.BlockSpec(array.shape, lambda *_: (0,) * array.ndim)
+    return pl.BlockSpec(array.shape, lambda *_: (0,) * len(array.shape))
 
 
 def level_ids(ids, group):
@@ -73,30 +74,43 @@
         in_specs=[rows, pl.BlockSpec((1, width), lambda i: (0, 0))],
         out_specs=rows,
         out_shape=jax.ShapeDtypeStruct((vocab, width), jnp.bfloat16),
-        compiler_params=params(),
+        compiler_params=params(60),
         cost_estimate=cost(0, 2_000_000),
     )(embedding, norm_gain.reshape(1, width))
 
 
-def table_kernel(normed_ref, weight_ref, out_ref):
-    out_ref[0] = jnp.dot(normed_ref[...], weight_ref[0], preferred_element_type=jnp.float32).astype(jnp.bfloat16)
+def table_kernel(normed_ref, weight_ref, out_ref, total_ref):
+    part = jnp.dot(normed_ref[...], weight_ref[0], preferred_element_type=jnp.float32)
+    step, last = pl.program_id(1), pl.num_programs(1) - 1
+
+    @pl.when(step == 0)
+    def _():
+        total_ref[...] = part
+
+    @pl.when((step > 0) & (step < last))
+    def _():
+        total_ref[...] += part
+
+    @pl.when(step == last)
+    def _():
+        out_ref[0] = (total_ref[...] + part).astype(jnp.bfloat16)
 
 
 def project(normed, in_proj):
     vocab, width = normed.shape
     count, _, panel_width = in_proj.shape
-    cols = min(256, panel_width)
-    per = panel_width // cols
+    deep = width // 4
     return pl.pallas_call(
         table_kernel,
-        grid=(count * per,),
+        grid=(count, width // deep),
         in_specs=[
-            whole(normed),
-            pl.BlockSpec((1, width, cols), lambda s: (s // per, 0, s % per)),
+            pl.BlockSpec((vocab, deep), lambda i, k: (0, k)),
+            pl.BlockSpec((1, deep, panel_width), lambda i, k: (i, k, 0)),
         ],
-        out_specs=pl.BlockSpec((1, vocab, cols), lambda s: (s // per, 0, s % per)),
+        out_specs=pl.BlockSpec((1, vocab, panel_width), lambda i, k: (i, 0, 0)),
         out_shape=jax.ShapeDtypeStruct((count, vocab, panel_width), jnp.bfloat16),
-        compiler_params=params(),
+        scratch_shapes=[pltpu.VMEM((vocab, panel_width), jnp.float32)],
+        compiler_params=params(60),
         cost_estimate=cost(3_000_000_000, 0),
     )(normed, in_proj)
 
@@ -166,11 +180,32 @@
     )(ids.reshape(windows, 1, rows), table, short_taps, toeplitz)
 
 
-def prepare_kernel(place_ref, base_ref, *refs):
+def cut_kernel(place_ref, *refs):
     count = len(refs) // 2
     for source, piece in zip(refs[:count], refs[count:]):
         piece[...] = source[...]
-    toeplitz_ref = refs[-1]
+
+
+def cut_pieces(place, out_proj):
+    depth, width = out_proj.shape
+    unit = width // SIXTEENTHS
+    ins, outs, shapes = [], [], []
+    for first, extent, sharers, _ in SPLITS:
+        cols = extent * unit // sharers
+        start = first * unit // cols
+        ins.append(pl.BlockSpec((depth, cols), lambda s, place, start=start, n=sharers: (0, start + place[0] % n)))
+        outs.append(pl.BlockSpec((depth, cols), lambda s, place: (0, 0)))
+        shapes.append(jax.ShapeDtypeStruct((depth, cols), out_proj.dtype))
+    return pl.pallas_call(
+        cut_kernel,
+        grid_spec=pltpu.PrefetchScalarGridSpec(num_scalar_prefetch=1, grid=(1,), in_specs=ins, out_specs=outs),
+        out_shape=shapes,
+        compiler_params=params(60),
+        cost_estimate=cost(0, 2_000_000),
+    )(place, *[out_proj] * len(SPLITS))
+
+
+def toeplitz_kernel(base_ref, toeplitz_ref):
     tiles, stacked, reach = toeplitz_ref.shape
     per_tile = base_ref.shape[0] // tiles
     tok_len = stacked // per_tile
@@ -182,29 +217,21 @@
             toeplitz_ref[tile, pl.ds(k * tok_len, tok_len), :] = shifted.astype(jnp.bfloat16)
 
 
-def prepare(place, out_proj, conv_taps, tok_len):
-    depth, width = out_proj.shape
-    unit = width // SIXTEENTHS
+def build_toeplitz(conv_taps, tok_len):
     reach = 2 * tok_len
     per_tile = LANES // GROUP
     tiles = conv_taps.shape[0] // per_tile
     base = jnp.pad(conv_taps[:, ::-1].astype(jnp.float32), ((0, 0), (1, reach - TAPS - 1)))
-    ins, outs, shapes = [pl.BlockSpec(base.shape, lambda s, place: (0, 0))], [], []
-    for first, extent, sharers, _ in SPLITS:
-        cols = extent * unit // sharers
-        start = first * unit // cols
-        ins.append(pl.BlockSpec((depth, cols), lambda s, place, start=start, n=sharers: (0, start + place[0] % n)))
-        outs.append(pl.BlockSpec((depth, cols), lambda s, place: (0, 0)))
-        shapes.append(jax.ShapeDtypeStruct((depth, cols), out_proj.dtype))
-    shapes.append(jax.ShapeDtypeStruct((tiles, per_tile * tok_len, reach), jnp.bfloat16))
-    outs.append(pl.BlockSpec(shapes[-1].shape, lambda s, place: (0, 0, 0)))
-    return pl.pallas_call(
-        prepare_kernel,
-        grid_spec=pltpu.PrefetchScalarGridSpec(num_scalar_prefetch=1, grid=(1,), in_specs=ins, out_specs=outs),
-        out_shape=shapes,
-        compiler_params=params(),
+    shape = jax.ShapeDtypeStruct((tiles, per_tile * tok_len, reach), jnp.bfloat16)
+    return pl.pallas_call(
+        toeplitz_kernel,
+        grid=(1,),
+        in_specs=[whole(base)],
+        out_specs=whole(shape),
+        out_shape=shape,
+        compiler_params=params(60),
         cost_estimate=cost(0, 2_000_000),
-    )(place, base, *[out_proj] * len(SPLITS))
+    )(base)
 
 
 def panel_kernel(place_ref, mine_ref, other_ref, *refs):
@@ -225,7 +252,7 @@
     base, extent, sharers, _ = split
     piece_cols = extent * unit // sharers
     offset, cols = (part * unit // sharers for part in step)
-    order = range(sharers)
+    order = ORDER[sharers]
     fixed = lambda shape: pl.BlockSpec(shape, lambda s, place: (0,) * len(shape))
 
     def own(k):
@@ -275,9 +302,9 @@
     piece_cols = so_far_ref.shape[1] // sharers
     offset = step[0] * cols // step[1]
     out_ref[...] = so_far_ref[...]
-    for k in range(sharers):
+    for i, k in enumerate(ORDER[sharers]):
         first = (place_ref[0] % sharers ^ k) * piece_cols + offset
-        total = near_ref[0, k].astype(jnp.float32) + far_ref[0, k].astype(jnp.float32)
+        total = near_ref[0, i].astype(jnp.float32) + far_ref[0, i].astype(jnp.float32)
         at = pl.ds(pl.multiple_of(first, LANES), cols)
         out_ref[:, at] = (so_far_ref[:, at].astype(jnp.float32) + total).astype(jnp.bfloat16)
 
@@ -308,8 +335,11 @@
     at = lax.axis_index("ctx").reshape(1).astype(jnp.int32)
     bits = exchange_bits()
     tie = lax.optimization_barrier
-
-    *pieces, toeplitz = prepare(at, out_proj, conv_taps, tok_len)
+    beside_bit = bits[-2]
+
+    pieces = list(cut_pieces(at, out_proj))
+    pieces[0], token_ids, conv_taps = tie((pieces[0], token_ids, conv_taps))
+    toeplitz = build_toeplitz(conv_taps, tok_len)
     ids = level_ids(token_ids, bits[:2])
     ids, embedding_then, toeplitz = tie((ids, embedding, toeplitz))
     normed = normalize(embedding_then, norm_gain)
@@ -318,55 +348,54 @@
     normed, ids = tie((normed, ids))
     ids = with_lead(ids)
     table = project(normed, in_proj)
-    pieces[:2] = [swap(piece, "fsdp", bits[-2]) for piece in pieces[:2]]
-    table, pieces[0], pieces[2:] = tie((table, pieces[0], pieces[2:]))
-    pieces[2:] = [swap(piece, "fsdp", bits[-2]) for piece in pieces[2:]]
+    pieces = [swap(piece, "fsdp", beside_bit) for piece in pieces]
+    table, pieces[:2] = tie((table, pieces[:2]))
+    across = [None, swap(pieces[1], "ctx", 2)]
 
     half = ids.shape[0] // 2
-    mine, other = [], []
-    for first in (half, 0):
-        if first == 0:
-            ids, pieces[1], mine[0] = tie((ids, pieces[1], mine[0]))
-        gated = mix(ids[first : first + half], table, short_taps, toeplitz, tok_len)
-        mine.append(gated[: half // 2])
-        other.append(swap(gated[half // 2 :], "fsdp", bits[-2]) if first else None)
-
-    def spread(piece):
-        pair = jnp.concatenate([piece[None], swap(piece, "ctx", 1)[None]], axis=0)
-        return pair, swap(pair, "ctx", 2)
-
-    other[0], gated = tie((other[0], gated))
-    other[1] = swap(gated[half // 2 :], "fsdp", bits[-2])
-    beside = [(pieces[0][None], swap(pieces[0], "ctx", 1)[None]), spread(pieces[1])]
+    gated = mix(ids[half:], table, short_taps, toeplitz, tok_len)
+    near = swap(pieces[0], "ctx", 1)
+    ids, gated, near = tie((ids, gated, near))
+    mine = [gated[: half // 2]]
+    other = [swap(gated[half // 2 :], "fsdp", beside_bit)]
+    gated = mix(ids[:half], table, short_taps, toeplitz, tok_len)
+    pieces[2], across[1], other[0], gated = tie((pieces[2], across[1], other[0], gated))
+    mine.append(gated[: half // 2])
+    other.append(swap(gated[half // 2 :], "fsdp", beside_bit))
+
+    second = jnp.stack([pieces[1], across[1]])
+    third = jnp.stack([pieces[2], swap(pieces[2], "ctx", 2)])
+    beside = [(pieces[0][None], near[None]), (second, swap(second, "ctx", 1)), None]
+    other[0], beside[1] = tie((other[0], beside[1]))
     steps = [(split, number, step) for number, split in enumerate(SPLITS) for step in split[3]]
-
-    def send(number, then):
-        split, shared, step = steps[number]
-        ready, _ = tie((mine[0], then))
-        return panel(at, ready, other[0], out_proj, beside[shared], split, step)
-
-    away = [send(0, other[0]), send(1, other[0])]
+    away = [panel(at, mine[0], other[0], out_proj, beside[n], split, step) for split, n, step in steps[:2]]
     own_ids, other[1], away[1] = tie((token_ids, other[1], away[1]))
     out = residual(own_ids, embedding)
+    own = [panel(at, mine[1], other[1], out_proj, beside[n], split, step) for split, n, step in steps[:2]]
+    arrived = [swap(away[0], "fsdp", bits[-1]), None]
+    third, arrived[0], own[0] = tie((third, arrived[0], own[0]))
+    beside[2] = (third, swap(third, "ctx", 1))
+    arrived[1] = swap(away[1], "fsdp", bits[-1])
+    away += [panel(at, mine[0], other[0], out_proj, beside[n], split, step) for split, n, step in steps[2:3]]
+    own += [panel(at, mine[1], other[1], out_proj, beside[n], split, step) for split, n, step in steps[2:]]
+
+    arrived.append(swap(away[2], "fsdp", bits[-1]))
     behind = []
-    for number, (split, shared, step) in enumerate(steps):
-        got = swap(away[number], "fsdp", bits[-1])
+    for number, (split, _, step) in enumerate(steps):
+        got, total = arrived[number], own[number]
         if number >= 2:
             out = place_pieces(at, out, *behind[number - 2])
             got, out = tie((got, out))
-        total = panel(at, mine[1], other[1], out_proj, beside[shared], split, step)
         for bit in reversed(bits[:-2]):
             half = total.shape[0] // 2
             far = add(total[half:], got[half:])
             total, got = add(total[:half], got[:half]), swap(far, "fsdp", bit)
         behind.append((total, got, split, step))
-        if number == 0:
-            last, _ = tie((pieces[2], total))
-            beside.append((last[None], swap(last, "ctx", 1)[None]))
-        if number + 2 < len(steps):
-            away.append(send(number + 2, total if number == 0 else (total, behind[number - 1][1])))
-    behind = behind[-2:]
-    for last in behind:
+        if number + 3 < len(steps):
+            split, n, step = steps[number + 3]
+            ready, _ = tie((mine[0], got))
+            arrived.append(swap(panel(at, ready, other[0], out_proj, beside[n], split, step), "fsdp", bits[-1]))
+    for last in behind[-2:]:
         out = place_pieces(at, out, *last)
     return out[None]
 

time: 148 us -> 144 us (0.973)
  Pallas kernels: 36.6 us -> 52.1 us
  waiting for transfers between devices: 68.8 us -> 57.7 us
  local copies, waits for them, and re-layouts: 10.9 us -> 2.91 us
    pallas_call x2 -> x3, Pallas kernels: 9.35 us -> 21.9 us  [the longest x1 16.7 us: project(): pl.pallas_call(table_kernel, grid=(count, width // deep), in_specs=[pl.Bl...]
    ppermute x21 -> x22, waiting for transfers between devices: 68.8 us -> 57.7 us  [swap(): return lax.ppermute(x, axis, [(i, i ^ mask) for i in range(peers)])]
    unnamed x20 -> x14, local copies, waits for them, and re-layouts: 9.94 us -> 2.65 us
    pallas_call x1, Pallas kernels: 2.38 us -> 5.81 us  [normalize(): pl.pallas_call(norm_kernel, grid=(4,), in_specs=[rows, pl.BlockSpec((1, w...]
    ppermute x21 -> x22, starting transfers between devices: 23.8 us -> 24 us  [swap(): return lax.ppermute(x, axis, [(i, i ^ mask) for i in range(peers)])]
  transfers between devices with their start and end apart: 23 -> 24, of which waited for: 10 -> 12; matrix products, arithmetic and copies ran while one was open for 2% -> 1% of each run, Pallas kernels for 23% -> 33%
where the time goes in v5:
time: 144 us; the launch traced here: 143 us
  waiting for transfers between devices  57.7 us (40%)
  Pallas kernels  52.1 us (36%)
  starting transfers between devices  28.8 us (20%)
  local copies, waits for them, and re-layouts  2.91 us (2%)
  other arithmetic  1.51 us (1%)
    ppermute x22, waiting for transfers between devices, swap(): return lax.ppermute(x, axis, [(i, i ^ mask) for i in range(peers)])  57.7 us
    ppermute x22, starting transfers between devices, swap(): return lax.ppermute(x, axis, [(i, i ^ mask) for i in range(peers)])  24 us
    pallas_call x1, Pallas kernels, project(): pl.pallas_call(table_kernel, grid=(count, width // deep), in_specs=[pl.Bl...  16.7 us
    pallas_call x2, Pallas kernels, mix(): pl.pallas_call(mixer_kernel, grid=(windows // 2,), in_specs=[pl.BlockSpec...  8.62 us
    pallas_call x4, Pallas kernels, place_pieces(): pl.pallas_call(functools.partial(place_kernel, split, step), grid_spec=pl...  7.5 us
    pallas_call x1, Pallas kernels, normalize(): pl.pallas_call(norm_kernel, grid=(4,), in_specs=[rows, pl.BlockSpec((1, w...  5.81 us
    pallas_call x8, Pallas kernels, panel(): pl.pallas_call(panel_kernel, grid_spec=pltpu.PrefetchScalarGridSpec(num_s...  5.67 us
    ppermute x2, starting transfers between devices, from_behind(): lax.ppermute(x, axis, [(i, i + by) for i in range(peers) if i + by < peers])  4.82 us
  transfers between devices with their start and end apart: 24, of which 12 were waited for; matrix products, arithmetic and copies ran while one was open for 1% of the time, Pallas kernels for 33%

profile of v5, /device:TPU:0, one launch (start us, length us, event | category | flops | bytes accessed | tf_op | source)
XLA Modules:
  0.0 143.4 jit_solution(7540927097543642069)
XLA Ops:
  0.0 2.4 %shard_map.73 = (bf16[512,512]{1,0:T(8,128)(2,1)}, bf16[512,256]{1,0:T(8,128)(2,1)}, bf16[512,512]{1,0:T(8,128)(2,1)}) custom-call(s32[1]{0:T(128)} %bitcast.place_ref, bf16[512,4096]{1,0:T(8,128)(2,1)} %refs_3_.11, bf16[512,4096]{1,0:T(8,128)(2,1)} %refs_3_.11, bf16[512,4096]{1,0:T(8,128)(2,1)} %refs_3_.11), custom_call_target="tpu_custom_call" | custom-call | bytes 2000000 | tf_op jit(solution)/shard_map/pallas_call | solution.py:199
  2.4 4.0 %collective-permute-start = (s32[1,128]{1,0:T(1,128)S(1)}, s32[1,128]{1,0:T(1,128)S(1)}, u32[]{:S(2)}, u32[]{:S(2)}) collective-permute-start(s32[1,128]{1,0:T(1,128)S(1)} %copy-done.4), channel_id=1, source_target_pairs={{0,16},{4,20},{8,24},{12,28},{16,0},{20,4},{24,8},{28,12},{1,17},{... | collective-permute-start | bytes 1544 | tf_op jit(solution)/shard_map/ppermute | solution.py:27
  8.8 2.7 %shard_map.74.toeplitz = bf16[4,1024,256]{2,1,0:T(8,128)(2,1)} custom-call(f32[32,256]{1,0:T(8,128)} %pad_convert_fusion.base_ref), custom_call_target="tpu_custom_call" | custom-call | bytes 2000000 | tf_op jit(solution)/shard_map/pallas_call | solution.py:226
  11.6 1.8 %collective-permute-done.2 = s32[1,128]{1,0:T(1,128)S(1)} collective-permute-done((s32[1,128]{1,0:T(1,128)S(1)}, s32[1,128]{1,0:T(1,128)S(1)}, u32[]{:S(2)}, u32[]{:S(2)}) %collective-permute-start.2) | collective-permute-done | bytes 544 | tf_op jit(solution)/shard_map/ppermute | solution.py:27
  13.4 1.6 %collective-permute-start.3 = (s32[4,128]{1,0:T(4,128)S(1)}, s32[4,128]{1,0:T(4,128)S(1)}, u32[]{:S(2)}, u32[]{:S(2)}) collective-permute-start(s32[4,128]{1,0:T(4,128)S(1)} %pad_add_fusion.2), channel_id=1, source_target_pairs={{0,4},{4,0},{8,12},{12,8},{16,20},{20,16},{24,28},{28,24},{1,5},{5... | collective-permute-start | bytes 6152 | tf_op jit(solution)/shard_map/ppermute | solution.py:27
  15.0 2.0 %collective-permute-start.7 = (bf16[512,256]{1,0:T(8,128)(2,1)}, bf16[512,256]{1,0:T(8,128)(2,1)S(1)}, u32[]{:S(2)}, u32[]{:S(2)}) collective-permute-start(bf16[512,256]{1,0:T(8,128)(2,1)} %get-tuple-element.48), channel_id=1, source_target_pairs={{0,8},{4,12},{8,0},{12,4},{16,24},{20,28},{24,16},{28,20},{1,9},{5... | collective-permute-start | bytes 786440 | tf_op jit(solution)/shard_map/ppermute | solution.py:27
  17.1 5.8 %shard_map.75.normed_ref = bf16[512,4096]{1,0:T(8,128)(2,1)} custom-call(bf16[512,4096]{1,0:T(8,128)(2,1)} %rows_ref.2, f32[1,4096]{1,0:T(1,128)} %bitcast.40), custom_call_target="tpu_custom_call" | custom-call | bytes 2000000 | tf_op jit(solution)/shard_map/pallas_call | solution.py:71
  22.9 3.5 %collective-permute-start.4 = (s32[8,128]{1,0:T(8,128)S(1)}, s32[8,128]{1,0:T(8,128)S(1)}, u32[]{:S(2)}, u32[]{:S(2)}) collective-permute-start(s32[8,128]{1,0:T(8,128)S(1)} %pad_add_fusion.1), channel_id=1, source_target_pairs={{0,2},{1,3},{4,6},{5,7},{8,10},{9,11},{12,14},{13,15},{16,18},{17,... | collective-permute-start | bytes 12296 | tf_op jit(solution)/shard_map/ppermute | solution.py:22
  27.7 16.7 %shard_map.76.table_ref = bf16[3,512,512]{2,1,0:T(8,128)(2,1)} custom-call(bf16[512,4096]{1,0:T(8,128)(2,1)} %shard_map.75.normed_ref, bf16[3,4096,512]{2,1,0:T(8,128)(2,1)} %weight_ref.1), custom_call_target="tpu_custom_call" | custom-call | flops 3000000000 | tf_op jit(solution)/shard_map/pallas_call | solution.py:103
  46.3 4.3 %shard_map.77 = bf16[4,128,512]{2,1,0:T(8,128)(2,1)S(1)} custom-call(s32[4,1,272]{2,1,0:T(1,128)S(1)} %copy.12.ids_ref, bf16[3,512,512]{2,1,0:T(8,128)(2,1)S(1)} %copy-done.3, f32[3,3,512]{2,1,0:T(4,128)S(1)} %copy-done.5, bf16[4,1024,256]{2,1,0:T(8,128)(2,1)S(1)} %copy-done.2), custom_call_target="tpu_custom_call" | custom-call | flops 1500000000 | tf_op jit(solution)/shard_map/pallas_call | solution.py:167
  50.7 2.1 %collective-permute-start.11 = (bf16[2,128,512]{2,1,0:T(8,128)(2,1)S(1)}, bf16[2,128,512]{2,1,0:T(8,128)(2,1)S(1)}, u32[]{:S(2)}, u32[]{:S(2)}) collective-permute-start(bf16[2,128,512]{2,1,0:T(8,128)(2,1)S(1)} %get-tuple-element.85), channel_id=1, source_target_pairs={{0,8},{4,12},{8,0},{12,4},{16,24},{20,28},{24,16},{28,20},{1,9},{5... | collective-permute-start | bytes 786440 | tf_op jit(solution)/shard_map/ppermute | solution.py:27
  52.8 4.3 %shard_map.78 = bf16[4,128,512]{2,1,0:T(8,128)(2,1)S(1)} custom-call(s32[4,1,272]{2,1,0:T(1,128)S(1)} %reshape.41.ids_ref, bf16[3,512,512]{2,1,0:T(8,128)(2,1)S(1)} %copy-done.3, f32[3,3,512]{2,1,0:T(4,128)S(1)} %copy-done.5, bf16[4,1024,256]{2,1,0:T(8,128)(2,1)S(1)} %copy-done.2), custom_call_target="tpu_custom_call" | custom-call | flops 1500000000 | tf_op jit(solution)/shard_map/pallas_call | solution.py:167
  57.1 2.5 %collective-permute-done.11 = bf16[2,128,512]{2,1,0:T(8,128)(2,1)S(1)} collective-permute-done((bf16[2,128,512]{2,1,0:T(8,128)(2,1)S(1)}, bf16[2,128,512]{2,1,0:T(8,128)(2,1)S(1)}, u32[]{:S(2)}, u32[]{:S(2)}) %collective-permute-start.11) | collective-permute-done | bytes 262176 | tf_op jit(solution)/shard_map/ppermute | solution.py:27
  59.8 1.8 %collective-permute-start.12 = (bf16[512,512]{1,0:T(8,128)(2,1)S(1)}, bf16[512,512]{1,0:T(8,128)(2,1)S(1)}, u32[]{:S(2)}, u32[]{:S(2)}) collective-permute-start(bf16[512,512]{1,0:T(8,128)(2,1)S(1)} %collective-permute-done.9), channel_id=1, source_target_pairs={{0,2},{1,3},{2,0},{3,1},{4,6},{5,7},{6,4},{7,5},{8,10},{9,11},{10,... | collective-permute-start | bytes 1572872 | tf_op jit(solution)/shard_map/ppermute | solution.py:27
  63.0 1.8 %collective-permute-start.15 = (bf16[2,128,512]{2,1,0:T(8,128)(2,1)S(1)}, bf16[2,128,512]{2,1,0:T(8,128)(2,1)S(1)}, u32[]{:S(2)}, u32[]{:S(2)}) collective-permute-start(bf16[2,128,512]{2,1,0:T(8,128)(2,1)S(1)} %get-tuple-element.83), channel_id=1, source_target_pairs={{0,8},{4,12},{8,0},{12,4},{16,24},{20,28},{24,16},{28,20},{1,9},{5... | collective-permute-start | bytes 786440 | tf_op jit(solution)/shard_map/ppermute | solution.py:27
  65.5 5.6 %collective-permute-done.15 = bf16[2,128,512]{2,1,0:T(8,128)(2,1)S(1)} collective-permute-done((bf16[2,128,512]{2,1,0:T(8,128)(2,1)S(1)}, bf16[2,128,512]{2,1,0:T(8,128)(2,1)S(1)}, u32[]{:S(2)}, u32[]{:S(2)}) %collective-permute-start.15) | collective-permute-done | bytes 262176 | tf_op jit(solution)/shard_map/ppermute | solution.py:27
  71.8 2.3 %collective-permute-done.12 = bf16[512,512]{1,0:T(8,128)(2,1)S(1)} collective-permute-done((bf16[512,512]{1,0:T(8,128)(2,1)S(1)}, bf16[512,512]{1,0:T(8,128)(2,1)S(1)}, u32[]{:S(2)}, u32[]{:S(2)}) %collective-permute-start.12) | collective-permute-done | bytes 524320 | tf_op jit(solution)/shard_map/ppermute | solution.py:27
  74.2 2.2 %collective-permute-done.14 = bf16[2,2,128,512]{3,2,1,0:T(8,128)(2,1)S(1)} collective-permute-done((bf16[2,2,128,512]{3,2,1,0:T(8,128)(2,1)S(1)}, bf16[2,2,128,512]{3,2,1,0:T(8,128)(2,1)S(1)}, u32[]{:S(2)}, u32[]{:S(2)}) %collective-permute-start.14) | collective-permute-done | bytes 524320 | tf_op jit(solution)/shard_map/ppermute | solution.py:27
  77.1 2.4 %collective-permute-start.16 = (bf16[1,2,128,512]{3,2,1,0:T(8,128)(2,1)S(1)}, bf16[1,2,128,512]{3,2,1,0:T(8,128)(2,1)S(1)}, u32[]{:S(2)}, u32[]{:S(2)}) collective-permute-start(bf16[1,2,128,512]{3,2,1,0:T(8,128)(2,1)S(1)} %get-tuple-element.82), channel_id=1, source_target_pairs={{0,16},{4,20},{8,24},{12,28},{16,0},{20,4},{24,8},{28,12},{1,17},{... | collective-permute-start | bytes 786440 | tf_op jit(solution)/shard_map/ppermute | solution.py:27
  79.4 12.7 %collective-permute-done.16.far_ref = bf16[1,2,128,512]{3,2,1,0:T(8,128)(2,1)S(1)} collective-permute-done((bf16[1,2,128,512]{3,2,1,0:T(8,128)(2,1)S(1)}, bf16[1,2,128,512]{3,2,1,0:T(8,128)(2,1)S(1)}, u32[]{:S(2)}, u32[]{:S(2)}) %collective-permute-start.16) | collective-permute-done | bytes 262176 | tf_op jit(solution)/shard_map/ppermute | solution.py:27
  92.8 1.6 %collective-permute-start.19 = (bf16[2,4,128,256]{3,2,1,0:T(8,128)(2,1)S(1)}, bf16[2,4,128,256]{3,2,1,0:T(8,128)(2,1)S(1)}, u32[]{:S(2)}, u32[]{:S(2)}) collective-permute-start(bf16[2,4,128,256]{3,2,1,0:T(8,128)(2,1)S(1)} %shard_map.83), channel_id=1, source_target_pairs={{0,4},{4,0},{8,12},{12,8},{16,20},{20,16},{24,28},{28,24},{1,5},{5... | collective-permute-start | bytes 1572872 | tf_op jit(solution)/shard_map/ppermute | solution.py:27
  97.9 2.6 %shard_map.84.so_far_ref = bf16[128,4096]{1,0:T(8,128)(2,1)} custom-call(s32[1,128]{1,0:T(1,128)S(1)} %copy-done.4, bf16[512,4096]{1,0:T(8,128)(2,1)S(1)} %copy-done.1), custom_call_target="tpu_custom_call" | custom-call | flops 400000000 | tf_op jit(solution)/shard_map/pallas_call | solution.py:289
  100.5 1.8 %shard_map.85.so_far_ref = bf16[128,4096]{1,0:T(8,128)(2,1)} custom-call(s32[1]{0:T(128)} %bitcast.place_ref, bf16[128,4096]{1,0:T(8,128)(2,1)} %shard_map.84.so_far_ref, bf16[1,2,128,512]{3,2,1,0:T(8,128)(2,1)S(1)} %get-tuple-element.81.near_ref, bf16[1,2,128,512]{3,2,1,0:T(8,128)(2,1)S(1)} %collective-permute-done.16.far_ref), custom_call_target="tpu_custom_call", output_to_operand_aliasing={{}: (1, {})} | custom-call | bytes 1000000 | tf_op jit(solution)/shard_map/pallas_call | solution.py:317
  103.7 4.0 %collective-permute-done.19 = bf16[2,4,128,256]{3,2,1,0:T(8,128)(2,1)S(1)} collective-permute-done((bf16[2,4,128,256]{3,2,1,0:T(8,128)(2,1)S(1)}, bf16[2,4,128,256]{3,2,1,0:T(8,128)(2,1)S(1)}, u32[]{:S(2)}, u32[]{:S(2)}) %collective-permute-start.19) | collective-permute-done | bytes 524320 | tf_op jit(solution)/shard_map/ppermute | solution.py:27
  107.7 1.9 %collective-permute-done.21.far_ref = bf16[1,4,128,256]{3,2,1,0:T(8,128)(2,1)S(1)} collective-permute-done((bf16[1,4,128,256]{3,2,1,0:T(8,128)(2,1)S(1)}, bf16[1,4,128,256]{3,2,1,0:T(8,128)(2,1)S(1)}, u32[]{:S(2)}, u32[]{:S(2)}) %collective-permute-start.21) | collective-permute-done | bytes 262176 | tf_op jit(solution)/shard_map/ppermute | solution.py:27
  109.6 1.8 %shard_map.87.so_far_ref = bf16[128,4096]{1,0:T(8,128)(2,1)} custom-call(s32[1]{0:T(128)} %bitcast.place_ref, bf16[128,4096]{1,0:T(8,128)(2,1)} %shard_map.85.so_far_ref, bf16[1,4,128,256]{3,2,1,0:T(8,128)(2,1)S(1)} %get-tuple-element.80.near_ref, bf16[1,4,128,256]{3,2,1,0:T(8,128)(2,1)S(1)} %collective-permute-done.21.far_ref), custom_call_target="tpu_custom_call", output_to_operand_aliasing={{}: (1, {})} | custom-call | bytes 1000000 | tf_op jit(solution)/shard_map/pallas_call | solution.py:317
  111.4 6.0 %collective-permute-done.18 = bf16[2,4,128,256]{3,2,1,0:T(8,128)(2,1)S(1)} collective-permute-done((bf16[2,4,128,256]{3,2,1,0:T(8,128)(2,1)S(1)}, bf16[2,4,128,256]{3,2,1,0:T(8,128)(2,1)S(1)}, u32[]{:S(2)}, u32[]{:S(2)}) %collective-permute-start.18) | collective-permute-done | bytes 524320 | tf_op jit(solution)/shard_map/ppermute | solution.py:27
  117.7 3.0 %collective-permute-start.23 = (bf16[1,4,128,256]{3,2,1,0:T(8,128)(2,1)S(1)}, bf16[1,4,128,256]{3,2,1,0:T(8,128)(2,1)S(1)}, u32[]{:S(2)}, u32[]{:S(2)}) collective-permute-start(bf16[1,4,128,256]{3,2,1,0:T(8,128)(2,1)S(1)} %get-tuple-element.75), channel_id=1, source_target_pairs={{0,16},{4,20},{8,24},{12,28},{16,0},{20,4},{24,8},{28,12},{1,17},{... | collective-permute-start | bytes 786440 | tf_op jit(solution)/shard_map/ppermute | solution.py:27
  120.7 15.2 %collective-permute-done.22.far_ref = bf16[1,4,128,256]{3,2,1,0:T(8,128)(2,1)S(1)} collective-permute-done((bf16[1,4,128,256]{3,2,1,0:T(8,128)(2,1)S(1)}, bf16[1,4,128,256]{3,2,1,0:T(8,128)(2,1)S(1)}, u32[]{:S(2)}, u32[]{:S(2)}) %collective-permute-start.22) | collective-permute-done | bytes 262176 | tf_op jit(solution)/shard_map/ppermute | solution.py:27
  135.9 2.0 %shard_map.89.so_far_ref = bf16[128,4096]{1,0:T(8,128)(2,1)} custom-call(s32[1]{0:T(128)} %bitcast.place_ref, bf16[128,4096]{1,0:T(8,128)(2,1)} %shard_map.87.so_far_ref, bf16[1,4,128,256]{3,2,1,0:T(8,128)(2,1)S(1)} %get-tuple-element.78.near_ref, bf16[1,4,128,256]{3,2,1,0:T(8,128)(2,1)S(1)} %collective-permute-done.22.far_ref), custom_call_target="tpu_custom_call", output_to_operand_aliasing={{}: (1, {})} | custom-call | bytes 1000000 | tf_op jit(solution)/shard_map/pallas_call | solution.py:317
  137.8 3.5 %collective-permute-done.23.far_ref = bf16[1,4,128,256]{3,2,1,0:T(8,128)(2,1)S(1)} collective-permute-done((bf16[1,4,128,256]{3,2,1,0:T(8,128)(2,1)S(1)}, bf16[1,4,128,256]{3,2,1,0:T(8,128)(2,1)S(1)}, u32[]{:S(2)}, u32[]{:S(2)}) %collective-permute-start.23) | collective-permute-done | bytes 262176 | tf_op jit(solution)/shard_map/ppermute | solution.py:27
  141.4 2.0 %shard_map.91 = bf16[128,4096]{1,0:T(8,128)(2,1)} custom-call(s32[1]{0:T(128)} %bitcast.place_ref, bf16[128,4096]{1,0:T(8,128)(2,1)} %shard_map.89.so_far_ref, bf16[1,4,128,256]{3,2,1,0:T(8,128)(2,1)S(1)} %get-tuple-element.76.near_ref, bf16[1,4,128,256]{3,2,1,0:T(8,128)(2,1)S(1)} %collective-permute-done.23.far_ref), custom_call_target="tpu_custom_call", output_to_operand_aliasing={{}: (1, {})} | custom-call | bytes 1000000 | tf_op jit(solution)/shard_map/pallas_call | solution.py:317
  (69 shorter events, 15.3 us)
Async XLA Ops:
  0.0 2.4 %copy-start.4 = (s32[1,128]{1,0:T(1,128)S(1)}, s32[1,128]{1,0:T(1,128)}, u32[]{:S(2)}) copy-start(s32[1,128]{1,0:T(1,128)} %ids_ref) | copy-start | bytes 1540
  0.0 8.0 %copy-start.6 = (bf16[32,128]{1,0:T(8,128)(2,1)S(1)}, bf16[32,128]{1,0:T(8,128)(2,1)}, u32[]{:S(2)}) copy-start(bf16[32,128]{1,0:T(8,128)(2,1)} %param.12) | copy-start | bytes 24580
  2.4 9.2 %collective-permute-start = (s32[1,128]{1,0:T(1,128)S(1)}, s32[1,128]{1,0:T(1,128)S(1)}, u32[]{:S(2)}, u32[]{:S(2)}) collective-permute-start(s32[1,128]{1,0:T(1,128)S(1)} %copy-done.4), channel_id=1, source_target_pairs={{0,16},{4,20},{8,24},{12,28},{16,0},{20,4},{24,8},{28,12},{1,17},{... | collective-permute-start | bytes 1544 | tf_op jit(solution)/shard_map/ppermute | solution.py:27
  6.5 5.1 %collective-permute-start.1 = (s32[1,128]{1,0:T(1,128)S(1)}, s32[1,128]{1,0:T(1,128)S(1)}, u32[]{:S(2)}, u32[]{:S(2)}) collective-permute-start(s32[1,128]{1,0:T(1,128)S(1)} %copy-done.4), channel_id=1, source_target_pairs={{0,8},{4,12},{8,0},{12,4},{16,24},{20,28},{24,16},{28,20},{1,9},{5... | collective-permute-start | bytes 1544 | tf_op jit(solution)/shard_map/ppermute | solution.py:27
  8.0 5.3 %collective-permute-start.2 = (s32[1,128]{1,0:T(1,128)S(1)}, s32[1,128]{1,0:T(1,128)S(1)}, u32[]{:S(2)}, u32[]{:S(2)}) collective-permute-start(s32[1,128]{1,0:T(1,128)S(1)} %copy-done.4), channel_id=1, source_target_pairs={{0,24},{4,28},{8,16},{12,20},{16,8},{20,12},{24,0},{28,4},{1,25},{... | collective-permute-start | bytes 1544 | tf_op jit(solution)/shard_map/ppermute | solution.py:27
  13.4 9.5 %collective-permute-start.3 = (s32[4,128]{1,0:T(4,128)S(1)}, s32[4,128]{1,0:T(4,128)S(1)}, u32[]{:S(2)}, u32[]{:S(2)}) collective-permute-start(s32[4,128]{1,0:T(4,128)S(1)} %pad_add_fusion.2), channel_id=1, source_target_pairs={{0,4},{4,0},{8,12},{12,8},{16,20},{20,16},{24,28},{28,24},{1,5},{5... | collective-permute-start | bytes 6152 | tf_op jit(solution)/shard_map/ppermute | solution.py:27
  15.0 29.5 %collective-permute-start.6 = (bf16[512,512]{1,0:T(8,128)(2,1)}, bf16[512,512]{1,0:T(8,128)(2,1)S(1)}, u32[]{:S(2)}, u32[]{:S(2)}) collective-permute-start(bf16[512,512]{1,0:T(8,128)(2,1)} %get-tuple-element.47), channel_id=1, source_target_pairs={{0,8},{4,12},{8,0},{12,4},{16,24},{20,28},{24,16},{28,20},{1,9},{5... | collective-permute-start | bytes 1572872 | tf_op jit(solution)/shard_map/ppermute | solution.py:27
  15.0 29.5 %collective-permute-start.7 = (bf16[512,256]{1,0:T(8,128)(2,1)}, bf16[512,256]{1,0:T(8,128)(2,1)S(1)}, u32[]{:S(2)}, u32[]{:S(2)}) collective-permute-start(bf16[512,256]{1,0:T(8,128)(2,1)} %get-tuple-element.48), channel_id=1, source_target_pairs={{0,8},{4,12},{8,0},{12,4},{16,24},{20,28},{24,16},{28,20},{1,9},{5... | collective-permute-start | bytes 786440 | tf_op jit(solution)/shard_map/ppermute | solution.py:27
  17.0 40.1 %collective-permute-start.9 = (bf16[512,512]{1,0:T(8,128)(2,1)}, bf16[512,512]{1,0:T(8,128)(2,1)S(1)}, u32[]{:S(2)}, u32[]{:S(2)}) collective-permute-start(bf16[512,512]{1,0:T(8,128)(2,1)} %get-tuple-element.53), channel_id=1, source_target_pairs={{0,8},{4,12},{8,0},{12,4},{16,24},{20,28},{24,16},{28,20},{1,9},{5... | collective-permute-start | bytes 1572872 | tf_op jit(solution)/shard_map/ppermute | solution.py:27
  22.9 22.0 %copy-start.2 = (bf16[4,1024,256]{2,1,0:T(8,128)(2,1)S(1)}, bf16[4,1024,256]{2,1,0:T(8,128)(2,1)}, u32[]{:S(2)}) copy-start(bf16[4,1024,256]{2,1,0:T(8,128)(2,1)} %shard_map.74.toeplitz) | copy-start | bytes 6291460
  22.9 22.0 %copy-start.5 = (f32[3,3,512]{2,1,0:T(4,128)S(1)}, f32[3,3,512]{2,1,0:T(4,128)}, u32[]{:S(2)}) copy-start(f32[3,3,512]{2,1,0:T(4,128)} %short_ref.3) | copy-start | bytes 55300
  22.9 21.5 %collective-permute-start.4 = (s32[8,128]{1,0:T(8,128)S(1)}, s32[8,128]{1,0:T(8,128)S(1)}, u32[]{:S(2)}, u32[]{:S(2)}) collective-permute-start(s32[8,128]{1,0:T(8,128)S(1)} %pad_add_fusion.1), channel_id=1, source_target_pairs={{0,2},{1,3},{4,6},{5,7},{8,10},{9,11},{12,14},{13,15},{16,18},{17,... | collective-permute-start | bytes 12296 | tf_op jit(solution)/shard_map/ppermute | solution.py:22
  26.4 18.2 %collective-permute-start.5 = (s32[8,128]{1,0:T(8,128)S(1)}, s32[8,128]{1,0:T(8,128)S(1)}, u32[]{:S(2)}, u32[]{:S(2)}) collective-permute-start(s32[8,128]{1,0:T(8,128)S(1)} %pad_add_fusion.1), channel_id=1, source_target_pairs={{0,1},{1,2},{2,3},{4,5},{5,6},{6,7},{8,9},{9,10},{10,11},{12,13},{... | collective-permute-start | bytes 12296 | tf_op jit(solution)/shard_map/ppermute | solution.py:22
  44.5 6.2 %collective-permute-start.8 = (bf16[512,512]{1,0:T(8,128)(2,1)S(1)}, bf16[512,512]{1,0:T(8,128)(2,1)S(1)}, u32[]{:S(2)}, u32[]{:S(2)}) collective-permute-start(bf16[512,512]{1,0:T(8,128)(2,1)S(1)} %collective-permute-done.6), channel_id=1, source_target_pairs={{0,1},{1,0},{2,3},{3,2},{4,5},{5,4},{6,7},{7,6},{8,9},{9,8},{10,11... | collective-permute-start | bytes 1572872 | tf_op jit(solution)/shard_map/ppermute | solution.py:27
  44.8 12.3 %collective-permute-start.10 = (bf16[512,256]{1,0:T(8,128)(2,1)S(1)}, bf16[512,256]{1,0:T(8,128)(2,1)S(1)}, u32[]{:S(2)}, u32[]{:S(2)}) collective-permute-start(bf16[512,256]{1,0:T(8,128)(2,1)S(1)} %collective-permute-done.7), channel_id=1, source_target_pairs={{0,2},{1,3},{2,0},{3,1},{4,6},{5,7},{6,4},{7,5},{8,10},{9,11},{10,... | collective-permute-start | bytes 786440 | tf_op jit(solution)/shard_map/ppermute | solution.py:27
  44.9 1.4 copy-start.3
  50.6 11.0 %copy-start = (bf16[512,4096]{1,0:T(8,128)(2,1)S(1)}, bf16[512,4096]{1,0:T(8,128)(2,1)}, u32[]{:S(2)}) copy-start(bf16[512,4096]{1,0:T(8,128)(2,1)} %refs_3_.11) | copy-start | bytes 12582916
  50.7 8.9 %collective-permute-start.11 = (bf16[2,128,512]{2,1,0:T(8,128)(2,1)S(1)}, bf16[2,128,512]{2,1,0:T(8,128)(2,1)S(1)}, u32[]{:S(2)}, u32[]{:S(2)}) collective-permute-start(bf16[2,128,512]{2,1,0:T(8,128)(2,1)S(1)} %get-tuple-element.85), channel_id=1, source_target_pairs={{0,8},{4,12},{8,0},{12,4},{16,24},{20,28},{24,16},{28,20},{1,9},{5... | collective-permute-start | bytes 786440 | tf_op jit(solution)/shard_map/ppermute | solution.py:27
  59.7 2.0 %collective-permute-start.13 = (bf16[2,512,256]{2,1,0:T(8,128)(2,1)S(1)}, bf16[2,512,256]{2,1,0:T(8,128)(2,1)S(1)}, u32[]{:S(2)}, u32[]{:S(2)}) collective-permute-start(bf16[2,512,256]{2,1,0:T(8,128)(2,1)S(1)} %pad_maximum_fusion.1.refs_4_), channel_id=1, source_target_pairs={{0,1},{1,0},{2,3},{3,2},{4,5},{5,4},{6,7},{7,6},{8,9},{9,8},{10,11... | collective-permute-start | bytes 1572872 | tf_op jit(solution)/shard_map/ppermute | solution.py:27
  59.8 14.3 %collective-permute-start.12 = (bf16[512,512]{1,0:T(8,128)(2,1)S(1)}, bf16[512,512]{1,0:T(8,128)(2,1)S(1)}, u32[]{:S(2)}, u32[]{:S(2)}) collective-permute-start(bf16[512,512]{1,0:T(8,128)(2,1)S(1)} %collective-permute-done.9), channel_id=1, source_target_pairs={{0,2},{1,3},{2,0},{3,1},{4,6},{5,7},{6,4},{7,5},{8,10},{9,11},{10,... | collective-permute-start | bytes 1572872 | tf_op jit(solution)/shard_map/ppermute | solution.py:27
  62.4 14.0 %collective-permute-start.14 = (bf16[2,2,128,512]{3,2,1,0:T(8,128)(2,1)S(1)}, bf16[2,2,128,512]{3,2,1,0:T(8,128)(2,1)S(1)}, u32[]{:S(2)}, u32[]{:S(2)}) collective-permute-start(bf16[2,2,128,512]{3,2,1,0:T(8,128)(2,1)S(1)} %shard_map.79), channel_id=1, source_target_pairs={{0,4},{4,0},{8,12},{12,8},{16,20},{20,16},{24,28},{28,24},{1,5},{5... | collective-permute-start | bytes 1572872 | tf_op jit(solution)/shard_map/ppermute | solution.py:27
  63.0 8.1 %collective-permute-start.15 = (bf16[2,128,512]{2,1,0:T(8,128)(2,1)S(1)}, bf16[2,128,512]{2,1,0:T(8,128)(2,1)S(1)}, u32[]{:S(2)}, u32[]{:S(2)}) collective-permute-start(bf16[2,128,512]{2,1,0:T(8,128)(2,1)S(1)} %get-tuple-element.83), channel_id=1, source_target_pairs={{0,8},{4,12},{8,0},{12,4},{16,24},{20,28},{24,16},{28,20},{1,9},{5... | collective-permute-start | bytes 786440 | tf_op jit(solution)/shard_map/ppermute | solution.py:27
  76.4 15.7 %collective-permute-start.17 = (bf16[2,512,512]{2,1,0:T(8,128)(2,1)S(1)}, bf16[2,512,512]{2,1,0:T(8,128)(2,1)S(1)}, u32[]{:S(2)}, u32[]{:S(2)}) collective-permute-start(bf16[2,512,512]{2,1,0:T(8,128)(2,1)S(1)} %pad_maximum_fusion.refs_4_), channel_id=1, source_target_pairs={{0,1},{1,0},{2,3},{3,2},{4,5},{5,4},{6,7},{7,6},{8,9},{9,8},{10,11... | collective-permute-start | bytes 3145736 | tf_op jit(solution)/shard_map/ppermute | solution.py:27
  76.4 20.0 %collective-permute-start.20 = (bf16[2,4,128,256]{3,2,1,0:T(8,128)(2,1)S(1)}, bf16[2,4,128,256]{3,2,1,0:T(8,128)(2,1)S(1)}, u32[]{:S(2)}, u32[]{:S(2)}) collective-permute-start(bf16[2,4,128,256]{3,2,1,0:T(8,128)(2,1)S(1)} %shard_map.80), channel_id=1, source_target_pairs={{0,4},{4,0},{8,12},{12,8},{16,20},{20,16},{24,28},{28,24},{1,5},{5... | collective-permute-start | bytes 1572872 | tf_op jit(solution)/shard_map/ppermute | solution.py:27
  77.1 15.0 %collective-permute-start.16 = (bf16[1,2,128,512]{3,2,1,0:T(8,128)(2,1)S(1)}, bf16[1,2,128,512]{3,2,1,0:T(8,128)(2,1)S(1)}, u32[]{:S(2)}, u32[]{:S(2)}) collective-permute-start(bf16[1,2,128,512]{3,2,1,0:T(8,128)(2,1)S(1)} %get-tuple-element.82), channel_id=1, source_target_pairs={{0,16},{4,20},{8,24},{12,28},{16,0},{20,4},{24,8},{28,12},{1,17},{... | collective-permute-start | bytes 786440 | tf_op jit(solution)/shard_map/ppermute | solution.py:27
  92.8 14.9 %collective-permute-start.19 = (bf16[2,4,128,256]{3,2,1,0:T(8,128)(2,1)S(1)}, bf16[2,4,128,256]{3,2,1,0:T(8,128)(2,1)S(1)}, u32[]{:S(2)}, u32[]{:S(2)}) collective-permute-start(bf16[2,4,128,256]{3,2,1,0:T(8,128)(2,1)S(1)} %shard_map.83), channel_id=1, source_target_pairs={{0,4},{4,0},{8,12},{12,8},{16,20},{20,16},{24,28},{28,24},{1,5},{5... | collective-permute-start | bytes 1572872 | tf_op jit(solution)/shard_map/ppermute | solution.py:27
  95.1 22.2 %collective-permute-start.18 = (bf16[2,4,128,256]{3,2,1,0:T(8,128)(2,1)S(1)}, bf16[2,4,128,256]{3,2,1,0:T(8,128)(2,1)S(1)}, u32[]{:S(2)}, u32[]{:S(2)}) collective-permute-start(bf16[2,4,128,256]{3,2,1,0:T(8,128)(2,1)S(1)} %shard_map.82), channel_id=1, source_target_pairs={{0,4},{4,0},{8,12},{12,8},{16,20},{20,16},{24,28},{28,24},{1,5},{5... | collective-permute-start | bytes 1572872 | tf_op jit(solution)/shard_map/ppermute | solution.py:27
  95.7 2.2 %copy-start.1 = (bf16[512,4096]{1,0:T(8,128)(2,1)S(1)}, bf16[512,4096]{1,0:T(8,128)(2,1)}, u32[]{:S(2)}) copy-start(bf16[512,4096]{1,0:T(8,128)(2,1)} %rows_ref.2) | copy-start | bytes 12582916
  96.6 13.1 %collective-permute-start.21 = (bf16[1,4,128,256]{3,2,1,0:T(8,128)(2,1)S(1)}, bf16[1,4,128,256]{3,2,1,0:T(8,128)(2,1)S(1)}, u32[]{:S(2)}, u32[]{:S(2)}) collective-permute-start(bf16[1,4,128,256]{3,2,1,0:T(8,128)(2,1)S(1)} %get-tuple-element.79), channel_id=1, source_target_pairs={{0,16},{4,20},{8,24},{12,28},{16,0},{20,4},{24,8},{28,12},{1,17},{... | collective-permute-start | bytes 786440 | tf_op jit(solution)/shard_map/ppermute | solution.py:27
  117.5 18.4 %collective-permute-start.22 = (bf16[1,4,128,256]{3,2,1,0:T(8,128)(2,1)S(1)}, bf16[1,4,128,256]{3,2,1,0:T(8,128)(2,1)S(1)}, u32[]{:S(2)}, u32[]{:S(2)}) collective-permute-start(bf16[1,4,128,256]{3,2,1,0:T(8,128)(2,1)S(1)} %get-tuple-element.77), channel_id=1, source_target_pairs={{0,16},{4,20},{8,24},{12,28},{16,0},{20,4},{24,8},{28,12},{1,17},{... | collective-permute-start | bytes 786440 | tf_op jit(solution)/shard_map/ppermute | solution.py:27
  117.7 23.7 %collective-permute-start.23 = (bf16[1,4,128,256]{3,2,1,0:T(8,128)(2,1)S(1)}, bf16[1,4,128,256]{3,2,1,0:T(8,128)(2,1)S(1)}, u32[]{:S(2)}, u32[]{:S(2)}) collective-permute-start(bf16[1,4,128,256]{3,2,1,0:T(8,128)(2,1)S(1)} %get-tuple-element.75), channel_id=1, source_target_pairs={{0,16},{4,20},{8,24},{12,28},{16,0},{20,4},{24,8},{28,12},{1,17},{... | collective-permute-start | bytes 786440 | tf_op jit(solution)/shard_map/ppermute | solution.py:27

commit v6 on v5

--- a/solution.py
+++ b/solution.py
@@ -12,7 +12,7 @@
 SHORT = 3
 LANES = 128
 LEAD = 16
-SPLITS = ((0, 4, 2, ((0, 4),)), (4, 4, 4, ((0, 4),)), (8, 8, 4, ((0, 4), (4, 4))))
+SPLITS = ((0, 8, 4, ((0, 4), (4, 4))), (8, 8, 4, ((0, 4), (4, 4))))
 SIXTEENTHS = 16
 ORDER = {2: (0, 1), 4: (0, 2, 1, 3)}
 
@@ -59,60 +59,61 @@
     return jnp.concatenate([two[:, tok_len - LEAD :], one, ids], axis=1)
 
 
-def norm_kernel(rows_ref, gain_ref, normed_ref):
-    values = rows_ref[...].astype(jnp.float32)
-    inverse_rms = lax.rsqrt(jnp.mean(values * values, axis=-1, keepdims=True) + 1e-06)
-    normed_ref[...] = (values * inverse_rms * gain_ref[...]).astype(jnp.bfloat16)
-
-
-def normalize(embedding, norm_gain):
+def table_kernel(rows_hbm, weight_hbm, gain_ref, table_ref, rows, weight, row_sems, weight_sems):
+    count, width, panel_width = weight.shape
+    parts, blocks = row_sems.shape[0], weight_sems.shape[1]
+    each, deep = rows.shape[0] // parts, width // blocks
+    row_copies = [
+        pltpu.make_async_copy(rows_hbm.at[pl.ds(r * each, each)], rows.at[pl.ds(r * each, each)], row_sems.at[r])
+        for r in range(parts)
+    ]
+    weight_copies = [
+        [
+            pltpu.make_async_copy(
+                weight_hbm.at[i, pl.ds(k * deep, deep)], weight.at[i, pl.ds(k * deep, deep)], weight_sems.at[i, k]
+            )
+            for k in range(blocks)
+        ]
+        for i in range(count)
+    ]
+    for copy in row_copies + sum(weight_copies, []):
+        copy.start()
+    for r in range(parts):
+        row_copies[r].wait()
+        at = pl.ds(r * each, each)
+        values = rows[at, :].astype(jnp.float32)
+        inverse_rms = lax.rsqrt(jnp.mean(values * values, axis=-1, keepdims=True) + 1e-06)
+        rows[at, :] = (values * inverse_rms * gain_ref[...]).astype(jnp.bfloat16)
+    cols = min(256, panel_width)
+    for i in range(count):
+        for copy in weight_copies[i]:
+            copy.wait()
+        for first in range(0, panel_width, cols):
+            at = slice(first, first + cols)
+            part = jnp.dot(rows[...], weight[i, :, at], preferred_element_type=jnp.float32)
+            table_ref[i, :, at] = part.astype(jnp.bfloat16)
+
+
+def project(embedding, norm_gain, in_proj):
     vocab, width = embedding.shape
-    rows = pl.BlockSpec((vocab // 4, width), lambda i: (i, 0))
-    return pl.pallas_call(
-        norm_kernel,
-        grid=(4,),
-        in_specs=[rows, pl.BlockSpec((1, width), lambda i: (0, 0))],
-        out_specs=rows,
-        out_shape=jax.ShapeDtypeStruct((vocab, width), jnp.bfloat16),
-        compiler_params=params(60),
-        cost_estimate=cost(0, 2_000_000),
-    )(embedding, norm_gain.reshape(1, width))
-
-
-def table_kernel(normed_ref, weight_ref, out_ref, total_ref):
-    part = jnp.dot(normed_ref[...], weight_ref[0], preferred_element_type=jnp.float32)
-    step, last = pl.program_id(1), pl.num_programs(1) - 1
-
-    @pl.when(step == 0)
-    def _():
-        total_ref[...] = part
-
-    @pl.when((step > 0) & (step < last))
-    def _():
-        total_ref[...] += part
-
-    @pl.when(step == last)
-    def _():
-        out_ref[0] = (total_ref[...] + part).astype(jnp.bfloat16)
-
-
-def project(normed, in_proj):
-    vocab, width = normed.shape
     count, _, panel_width = in_proj.shape
-    deep = width // 4
+    hbm = pl.BlockSpec(memory_space=pltpu.HBM)
+    shape = jax.ShapeDtypeStruct((count, vocab, panel_width), jnp.bfloat16)
     return pl.pallas_call(
         table_kernel,
-        grid=(count, width // deep),
-        in_specs=[
-            pl.BlockSpec((vocab, deep), lambda i, k: (0, k)),
-            pl.BlockSpec((1, deep, panel_width), lambda i, k: (i, k, 0)),
+        grid=(1,),
+        in_specs=[hbm, hbm, pl.BlockSpec((1, width), lambda s: (0, 0))],
+        out_specs=whole(shape),
+        out_shape=shape,
+        scratch_shapes=[
+            pltpu.VMEM(embedding.shape, jnp.bfloat16),
+            pltpu.VMEM(in_proj.shape, jnp.bfloat16),
+            pltpu.SemaphoreType.DMA((8,)),
+            pltpu.SemaphoreType.DMA((count, 4)),
         ],
-        out_specs=pl.BlockSpec((1, vocab, panel_width), lambda i, k: (i, 0, 0)),
-        out_shape=jax.ShapeDtypeStruct((count, vocab, panel_width), jnp.bfloat16),
-        scratch_shapes=[pltpu.VMEM((vocab, panel_width), jnp.float32)],
-        compiler_params=params(60),
+        compiler_params=params(40),
         cost_estimate=cost(3_000_000_000, 0),
-    )(normed, in_proj)
+    )(embedding, in_proj, norm_gain.reshape(1, width))
 
 
 def mixer_kernel(ids_ref, table_ref, short_ref, toeplitz, gated_ref, held_query, held):
@@ -180,29 +181,35 @@
     )(ids.reshape(windows, 1, rows), table, short_taps, toeplitz)
 
 
-def cut_kernel(place_ref, *refs):
-    count = len(refs) // 2
-    for source, piece in zip(refs[:count], refs[count:]):
-        piece[...] = source[...]
+def cut_kernel(place_ref, source, *refs):
+    pieces, sems = refs[:-1], refs[-1]
+    unit = source.shape[1] // SIXTEENTHS
+    copies = []
+    for n, ((base, _, sharers, _), piece) in enumerate(zip(SPLITS, pieces)):
+        cols = piece.shape[1]
+        first = pl.multiple_of(base * unit + place_ref[0] % sharers * cols, LANES)
+        copies.append(pltpu.make_async_copy(source.at[:, pl.ds(first, cols)], piece, sems.at[n]))
+    for copy in copies:
+        copy.start()
+    for copy in copies:
+        copy.wait()
 
 
 def cut_pieces(place, out_proj):
     depth, width = out_proj.shape
-    unit = width // SIXTEENTHS
-    ins, outs, shapes = [], [], []
-    for first, extent, sharers, _ in SPLITS:
-        cols = extent * unit // sharers
-        start = first * unit // cols
-        ins.append(pl.BlockSpec((depth, cols), lambda s, place, start=start, n=sharers: (0, start + place[0] % n)))
-        outs.append(pl.BlockSpec((depth, cols), lambda s, place: (0, 0)))
-        shapes.append(jax.ShapeDtypeStruct((depth, cols), out_proj.dtype))
+    hbm = pl.BlockSpec(memory_space=pltpu.HBM)
+    shapes = [
+        jax.ShapeDtypeStruct((depth, extent * width // SIXTEENTHS // sharers), out_proj.dtype)
+        for _, extent, sharers, _ in SPLITS
+    ]
     return pl.pallas_call(
         cut_kernel,
-        grid_spec=pltpu.PrefetchScalarGridSpec(num_scalar_prefetch=1, grid=(1,), in_specs=ins, out_specs=outs),
+        in_specs=[pl.BlockSpec(memory_space=pltpu.SMEM), hbm],
+        out_specs=[hbm] * len(shapes),
         out_shape=shapes,
-        compiler_params=params(60),
+        scratch_shapes=[pltpu.SemaphoreType.DMA((len(shapes),))],
         cost_estimate=cost(0, 2_000_000),
-    )(place, *[out_proj] * len(SPLITS))
+    )(place, out_proj)
 
 
 def toeplitz_kernel(base_ref, toeplitz_ref):
@@ -229,7 +236,7 @@
         in_specs=[whole(base)],
         out_specs=whole(shape),
         out_shape=shape,
-        compiler_params=params(60),
+        compiler_params=params(8),
         cost_estimate=cost(0, 2_000_000),
     )(base)
 
@@ -337,65 +344,51 @@
     tie = lax.optimization_barrier
     beside_bit = bits[-2]
 
-    pieces = list(cut_pieces(at, out_proj))
-    pieces[0], token_ids, conv_taps = tie((pieces[0], token_ids, conv_taps))
+    early, late = cut_pieces(at, out_proj)
+    early, late, token_ids, conv_taps = tie((early, late, token_ids, conv_taps))
     toeplitz = build_toeplitz(conv_taps, tok_len)
     ids = level_ids(token_ids, bits[:2])
-    ids, embedding_then, toeplitz = tie((ids, embedding, toeplitz))
-    normed = normalize(embedding_then, norm_gain)
+    ids, toeplitz = tie((ids, toeplitz))
     for group in [bits[i : i + 2] for i in range(2, len(bits), 2)]:
         ids = level_ids(ids, group)
-    normed, ids = tie((normed, ids))
+    early, late = swap(early, "fsdp", beside_bit), swap(late, "fsdp", beside_bit)
+    ids, embedding_then, early = tie((ids, embedding, early))
     ids = with_lead(ids)
-    table = project(normed, in_proj)
-    pieces = [swap(piece, "fsdp", beside_bit) for piece in pieces]
-    table, pieces[:2] = tie((table, pieces[:2]))
-    across = [None, swap(pieces[1], "ctx", 2)]
+    early_across = swap(early, "ctx", 2)
+    table = project(embedding_then, norm_gain, in_proj)
+    table, late = tie((table, late))
+    late_across = swap(late, "ctx", 2)
 
     half = ids.shape[0] // 2
     gated = mix(ids[half:], table, short_taps, toeplitz, tok_len)
-    near = swap(pieces[0], "ctx", 1)
-    ids, gated, near = tie((ids, gated, near))
+    ids, gated, early, early_across = tie((ids, gated, early, early_across))
+    pair = jnp.stack([early, early_across])
+    beside = [(pair, swap(pair, "ctx", 1))]
     mine = [gated[: half // 2]]
     other = [swap(gated[half // 2 :], "fsdp", beside_bit)]
     gated = mix(ids[:half], table, short_taps, toeplitz, tok_len)
-    pieces[2], across[1], other[0], gated = tie((pieces[2], across[1], other[0], gated))
+    late, late_across, other[0], gated = tie((late, late_across, other[0], gated))
+    pair = jnp.stack([late, late_across])
+    beside.append((pair, swap(pair, "ctx", 1)))
     mine.append(gated[: half // 2])
     other.append(swap(gated[half // 2 :], "fsdp", beside_bit))
 
-    second = jnp.stack([pieces[1], across[1]])
-    third = jnp.stack([pieces[2], swap(pieces[2], "ctx", 2)])
-    beside = [(pieces[0][None], near[None]), (second, swap(second, "ctx", 1)), None]
-    other[0], beside[1] = tie((other[0], beside[1]))
-    steps = [(split, number, step) for number, split in enumerate(SPLITS) for step in split[3]]
-    away = [panel(at, mine[0], other[0], out_proj, beside[n], split, step) for split, n, step in steps[:2]]
-    own_ids, other[1], away[1] = tie((token_ids, other[1], away[1]))
-    out = residual(own_ids, embedding)
-    own = [panel(at, mine[1], other[1], out_proj, beside[n], split, step) for split, n, step in steps[:2]]
-    arrived = [swap(away[0], "fsdp", bits[-1]), None]
-    third, arrived[0], own[0] = tie((third, arrived[0], own[0]))
-    beside[2] = (third, swap(third, "ctx", 1))
-    arrived[1] = swap(away[1], "fsdp", bits[-1])
-    away += [panel(at, mine[0], other[0], out_proj, beside[n], split, step) for split, n, step in steps[2:3]]
-    own += [panel(at, mine[1], other[1], out_proj, beside[n], split, step) for split, n, step in steps[2:]]
-
-    arrived.append(swap(away[2], "fsdp", bits[-1]))
+    out = residual(token_ids, embedding)
     behind = []
-    for number, (split, _, step) in enumerate(steps):
-        got, total = arrived[number], own[number]
-        if number >= 2:
-            out = place_pieces(at, out, *behind[number - 2])
-            got, out = tie((got, out))
-        for bit in reversed(bits[:-2]):
-            half = total.shape[0] // 2
-            far = add(total[half:], got[half:])
-            total, got = add(total[:half], got[:half]), swap(far, "fsdp", bit)
-        behind.append((total, got, split, step))
-        if number + 3 < len(steps):
-            split, n, step = steps[number + 3]
-            ready, _ = tie((mine[0], got))
-            arrived.append(swap(panel(at, ready, other[0], out_proj, beside[n], split, step), "fsdp", bits[-1]))
-    for last in behind[-2:]:
+    for split, shared in zip(SPLITS, beside):
+        for step in split[3]:
+            away = panel(at, mine[0], other[0], out_proj, shared, split, step)
+            away, mine[0] = tie((away, mine[0]))
+            got = swap(away, "fsdp", bits[-1])
+            total = panel(at, mine[1], other[1], out_proj, shared, split, step)
+            if not behind:
+                total, out = tie((total, out))
+            for bit in reversed(bits[:-2]):
+                half = total.shape[0] // 2
+                far = add(total[half:], got[half:])
+                total, got = add(total[:half], got[:half]), swap(far, "fsdp", bit)
+            behind.append((total, got, split, step))
+    for last in behind:
         out = place_pieces(at, out, *last)
     return out[None]
 

time: 144 us -> 173 us (1.20)
  waiting for transfers between devices: 57.7 us -> 75.9 us
  Pallas kernels: 52.1 us -> 68 us
  starting transfers between devices: 28.8 us -> 25.3 us
    ppermute x22 -> x20, waiting for transfers between devices: 57.7 us -> 75.9 us  [swap(): return lax.ppermute(x, axis, [(i, i ^ mask) for i in range(peers)])]
    pallas_call x3 -> x2, Pallas kernels: 24.9 us -> 42.6 us  [the longest x1 32.9 us: cut_pieces(): pl.pallas_call(cut_kernel, in_specs=[pl.BlockSpec(memory_space=pltpu.SMEM...]
    ppermute x22 -> x20, starting transfers between devices: 24 us -> 20 us  [swap(): return lax.ppermute(x, axis, [(i, i ^ mask) for i in range(peers)])]
    pallas_call x1, Pallas kernels: 2.75 us -> 0.61 us  [build_toeplitz(): pl.pallas_call(toeplitz_kernel, grid=(1,), in_specs=[whole(base)], out_sp...]
  transfers between devices with their start and end apart: 24 -> 22, of which waited for: 12 -> 10; matrix products, arithmetic and copies ran while one was open for 1% -> 1% of each run, Pallas kernels for 33% -> 19%
where the time goes in v6:
time: 173 us
  waiting for transfers between devices  75.9 us (44%)
  Pallas kernels  68 us (39%)
  starting transfers between devices  25.3 us (15%)
  local copies, waits for them, and re-layouts  2.46 us (1%)
    ppermute x20, waiting for transfers between devices, swap(): return lax.ppermute(x, axis, [(i, i ^ mask) for i in range(peers)])  75.9 us
    pallas_call x1, Pallas kernels, cut_pieces(): pl.pallas_call(cut_kernel, in_specs=[pl.BlockSpec(memory_space=pltpu.SMEM...  32.9 us
    ppermute x20, starting transfers between devices, swap(): return lax.ppermute(x, axis, [(i, i ^ mask) for i in range(peers)])  20 us
    pallas_call x1, Pallas kernels, project(): pl.pallas_call(table_kernel, grid=(1,), in_specs=[hbm, hbm, pl.BlockSpec(...  9.69 us
    pallas_call x2, Pallas kernels, mix(): pl.pallas_call(mixer_kernel, grid=(windows // 2,), in_specs=[pl.BlockSpec...  8.58 us
    pallas_call x4, Pallas kernels, place_pieces(): pl.pallas_call(functools.partial(place_kernel, split, step), grid_spec=pl...  7.92 us
    pallas_call x8, Pallas kernels, panel(): pl.pallas_call(panel_kernel, grid_spec=pltpu.PrefetchScalarGridSpec(num_s...  5.67 us
    ppermute x2, starting transfers between devices, from_behind(): lax.ppermute(x, axis, [(i, i + by) for i in range(peers) if i + by < peers])  5.32 us
  transfers between devices with their start and end apart: 22, of which 10 were waited for; matrix products, arithmetic and copies ran while one was open for 1% of the time, Pallas kernels for 19%

profile of v6, /device:TPU:0, one launch (start us, length us, event | category | flops | bytes accessed | tf_op | source)
XLA Modules:
  0.0 172.9 jit_solution(3465783064231644753)
XLA Ops:
  0.0 32.9 %shard_map.73 = (bf16[512,512]{1,0:T(8,128)(2,1)}, bf16[512,512]{1,0:T(8,128)(2,1)}) custom-call(s32[1]{0:T(128)} %bitcast.place_ref, bf16[512,4096]{1,0:T(8,128)(2,1)} %refs_3_.15), custom_call_target="tpu_custom_call" | custom-call | bytes 2000000 | tf_op jit(solution)/shard_map/pallas_call | solution.py:205
  32.9 3.1 %collective-permute-start.4 = (bf16[512,512]{1,0:T(8,128)(2,1)}, bf16[512,512]{1,0:T(8,128)(2,1)S(1)}, u32[]{:S(2)}, u32[]{:S(2)}) collective-permute-start(bf16[512,512]{1,0:T(8,128)(2,1)} %get-tuple-element.40), channel_id=1, source_target_pairs={{0,8},{4,12},{8,0},{12,4},{16,24},{20,28},{24,16},{28,20},{1,9},{5... | collective-permute-start | bytes 1572872 | tf_op jit(solution)/shard_map/ppermute | solution.py:27
  36.0 2.5 %collective-permute-start.2 = (s32[1,128]{1,0:T(1,128)S(1)}, s32[1,128]{1,0:T(1,128)S(1)}, u32[]{:S(2)}, u32[]{:S(2)}) collective-permute-start(s32[1,128]{1,0:T(1,128)S(1)} %copy-done.3), channel_id=1, source_target_pairs={{0,24},{4,28},{8,16},{12,20},{16,8},{20,12},{24,0},{28,4},{1,25},{... | collective-permute-start | bytes 1544 | tf_op jit(solution)/shard_map/ppermute | solution.py:27
  39.2 1.2 collective-permute-start
  41.4 10.0 %collective-permute-done.2 = s32[1,128]{1,0:T(1,128)S(1)} collective-permute-done((s32[1,128]{1,0:T(1,128)S(1)}, s32[1,128]{1,0:T(1,128)S(1)}, u32[]{:S(2)}, u32[]{:S(2)}) %collective-permute-start.2) | collective-permute-done | bytes 544 | tf_op jit(solution)/shard_map/ppermute | solution.py:27
  51.5 1.6 collective-permute-start.3
  53.1 2.1 %collective-permute-done.3 = s32[4,128]{1,0:T(4,128)S(1)} collective-permute-done((s32[4,128]{1,0:T(4,128)S(1)}, s32[4,128]{1,0:T(4,128)S(1)}, u32[]{:S(2)}, u32[]{:S(2)}) %collective-permute-start.3) | collective-permute-done | bytes 2080 | tf_op jit(solution)/shard_map/ppermute | solution.py:27
  55.1 1.3 collective-permute-start.8
  56.4 4.0 %collective-permute-start.7 = (s32[8,128]{1,0:T(8,128)S(1)}, s32[8,128]{1,0:T(8,128)S(1)}, u32[]{:S(2)}, u32[]{:S(2)}) collective-permute-start(s32[8,128]{1,0:T(8,128)S(1)} %pad_add_fusion.1), channel_id=1, source_target_pairs={{0,2},{1,3},{4,6},{5,7},{8,10},{9,11},{12,14},{13,15},{16,18},{17,... | collective-permute-start | bytes 12296 | tf_op jit(solution)/shard_map/ppermute | solution.py:22
  60.5 2.2 %copy-done.1 = bf16[512,4096]{1,0:T(8,128)(2,1)S(1)} copy-done((bf16[512,4096]{1,0:T(8,128)(2,1)S(1)}, bf16[512,4096]{1,0:T(8,128)(2,1)}, u32[]{:S(2)}) %copy-start.1) | copy-done | bytes 4194328
  62.7 9.7 %shard_map.75.table_ref = bf16[3,512,512]{2,1,0:T(8,128)(2,1)S(1)} custom-call(bf16[512,4096]{1,0:T(8,128)(2,1)S(1)} %copy-done.1, bf16[3,4096,512]{2,1,0:T(8,128)(2,1)} %weight_hbm.1, f32[1,4096]{1,0:T(1,128)S(1)} %bitcast.32), custom_call_target="tpu_custom_call" | custom-call | flops 3000000000 | tf_op jit(solution)/shard_map/pallas_call | solution.py:102
  72.5 2.0 %collective-permute-start.9 = (bf16[512,512]{1,0:T(8,128)(2,1)S(1)}, bf16[512,512]{1,0:T(8,128)(2,1)S(1)}, u32[]{:S(2)}, u32[]{:S(2)}) collective-permute-start(bf16[512,512]{1,0:T(8,128)(2,1)S(1)} %collective-permute-done.4), channel_id=1, source_target_pairs={{0,2},{1,3},{2,0},{3,1},{4,6},{5,7},{6,4},{7,5},{8,10},{9,11},{10,... | collective-permute-start | bytes 1572872 | tf_op jit(solution)/shard_map/ppermute | solution.py:27
  74.7 4.3 %shard_map.76 = bf16[4,128,512]{2,1,0:T(8,128)(2,1)S(1)} custom-call(s32[4,1,272]{2,1,0:T(1,128)S(1)} %copy.12.ids_ref, bf16[3,512,512]{2,1,0:T(8,128)(2,1)S(1)} %shard_map.75.table_ref, f32[3,3,512]{2,1,0:T(4,128)S(1)} %copy-done.4, bf16[4,1024,256]{2,1,0:T(8,128)(2,1)S(1)} %shard_map.74.toeplitz), custom_call_target="tpu_custom_call" | custom-call | flops 1500000000 | tf_op jit(solution)/shard_map/pallas_call | solution.py:168
  79.0 18.0 %collective-permute-done.9 = bf16[512,512]{1,0:T(8,128)(2,1)S(1)} collective-permute-done((bf16[512,512]{1,0:T(8,128)(2,1)S(1)}, bf16[512,512]{1,0:T(8,128)(2,1)S(1)}, u32[]{:S(2)}, u32[]{:S(2)}) %collective-permute-start.9) | collective-permute-done | bytes 524320 | tf_op jit(solution)/shard_map/ppermute | solution.py:27
  97.9 4.3 %shard_map.77 = bf16[4,128,512]{2,1,0:T(8,128)(2,1)S(1)} custom-call(s32[4,1,272]{2,1,0:T(1,128)S(1)} %reshape.45.ids_ref, bf16[3,512,512]{2,1,0:T(8,128)(2,1)S(1)} %shard_map.75.table_ref, f32[3,3,512]{2,1,0:T(4,128)S(1)} %copy-done.4, bf16[4,1024,256]{2,1,0:T(8,128)(2,1)S(1)} %shard_map.74.toeplitz), custom_call_target="tpu_custom_call" | custom-call | flops 1500000000 | tf_op jit(solution)/shard_map/pallas_call | solution.py:168
  102.2 3.8 %collective-permute-done.10 = bf16[2,128,512]{2,1,0:T(8,128)(2,1)S(1)} collective-permute-done((bf16[2,128,512]{2,1,0:T(8,128)(2,1)S(1)}, bf16[2,128,512]{2,1,0:T(8,128)(2,1)S(1)}, u32[]{:S(2)}, u32[]{:S(2)}) %collective-permute-start.10) | collective-permute-done | bytes 262176 | tf_op jit(solution)/shard_map/ppermute | solution.py:27
  106.9 1.6 collective-permute-start.13
  110.5 2.6 %shard_map.79.so_far_ref = bf16[128,4096]{1,0:T(8,128)(2,1)} custom-call(s32[1,128]{1,0:T(1,128)S(1)} %copy-done.3, bf16[512,4096]{1,0:T(8,128)(2,1)S(1)} %copy-done.1), custom_call_target="tpu_custom_call" | custom-call | flops 400000000 | tf_op jit(solution)/shard_map/pallas_call | solution.py:296
  113.1 3.9 %collective-permute-done.11 = bf16[2,128,512]{2,1,0:T(8,128)(2,1)S(1)} collective-permute-done((bf16[2,128,512]{2,1,0:T(8,128)(2,1)S(1)}, bf16[2,128,512]{2,1,0:T(8,128)(2,1)S(1)}, u32[]{:S(2)}, u32[]{:S(2)}) %collective-permute-start.11) | collective-permute-done | bytes 262176 | tf_op jit(solution)/shard_map/ppermute | solution.py:27
  120.5 1.6 collective-permute-start.20
  124.4 8.6 %collective-permute-done.15 = bf16[2,4,128,256]{3,2,1,0:T(8,128)(2,1)S(1)} collective-permute-done((bf16[2,4,128,256]{3,2,1,0:T(8,128)(2,1)S(1)}, bf16[2,4,128,256]{3,2,1,0:T(8,128)(2,1)S(1)}, u32[]{:S(2)}, u32[]{:S(2)}) %collective-permute-start.15) | collective-permute-done | bytes 524320 | tf_op jit(solution)/shard_map/ppermute | solution.py:27
  133.1 0.7 collective-permute-start.16
  133.8 10.4 %collective-permute-done.18 = bf16[2,4,128,256]{3,2,1,0:T(8,128)(2,1)S(1)} collective-permute-done((bf16[2,4,128,256]{3,2,1,0:T(8,128)(2,1)S(1)}, bf16[2,4,128,256]{3,2,1,0:T(8,128)(2,1)S(1)}, u32[]{:S(2)}, u32[]{:S(2)}) %collective-permute-start.18) | collective-permute-done | bytes 524320 | tf_op jit(solution)/shard_map/ppermute | solution.py:27
  144.3 0.7 collective-permute-start.19
  145.1 10.0 %collective-permute-done.20 = bf16[2,4,128,256]{3,2,1,0:T(8,128)(2,1)S(1)} collective-permute-done((bf16[2,4,128,256]{3,2,1,0:T(8,128)(2,1)S(1)}, bf16[2,4,128,256]{3,2,1,0:T(8,128)(2,1)S(1)}, u32[]{:S(2)}, u32[]{:S(2)}) %collective-permute-start.20) | collective-permute-done | bytes 524320 | tf_op jit(solution)/shard_map/ppermute | solution.py:27
  155.2 0.7 collective-permute-start.21
  155.9 2.0 %shard_map.81.so_far_ref = bf16[128,4096]{1,0:T(8,128)(2,1)} custom-call(s32[1]{0:T(128)} %bitcast.place_ref, bf16[128,4096]{1,0:T(8,128)(2,1)} %shard_map.79.so_far_ref, bf16[1,4,128,256]{3,2,1,0:T(8,128)(2,1)S(1)} %get-tuple-element.72.near_ref, bf16[1,4,128,256]{3,2,1,0:T(8,128)(2,1)S(1)} %collective-permute-done.14.far_ref), custom_call_target="tpu_custom_call", output_to_operand_aliasing={{}: (1, {})} | custom-call | bytes 1000000 | tf_op jit(solution)/shard_map/pallas_call | solution.py:324
  157.9 2.0 %shard_map.84.so_far_ref = bf16[128,4096]{1,0:T(8,128)(2,1)} custom-call(s32[1]{0:T(128)} %bitcast.place_ref, bf16[128,4096]{1,0:T(8,128)(2,1)} %shard_map.81.so_far_ref, bf16[1,4,128,256]{3,2,1,0:T(8,128)(2,1)S(1)} %get-tuple-element.70.near_ref, bf16[1,4,128,256]{3,2,1,0:T(8,128)(2,1)S(1)} %collective-permute-done.16.far_ref), custom_call_target="tpu_custom_call", output_to_operand_aliasing={{}: (1, {})} | custom-call | bytes 1000000 | tf_op jit(solution)/shard_map/pallas_call | solution.py:324
  159.8 5.6 %collective-permute-done.19.far_ref = bf16[1,4,128,256]{3,2,1,0:T(8,128)(2,1)S(1)} collective-permute-done((bf16[1,4,128,256]{3,2,1,0:T(8,128)(2,1)S(1)}, bf16[1,4,128,256]{3,2,1,0:T(8,128)(2,1)S(1)}, u32[]{:S(2)}, u32[]{:S(2)}) %collective-permute-start.19) | collective-permute-done | bytes 262176 | tf_op jit(solution)/shard_map/ppermute | solution.py:27
  165.5 2.0 %shard_map.87.so_far_ref = bf16[128,4096]{1,0:T(8,128)(2,1)} custom-call(s32[1]{0:T(128)} %bitcast.place_ref, bf16[128,4096]{1,0:T(8,128)(2,1)} %shard_map.84.so_far_ref, bf16[1,4,128,256]{3,2,1,0:T(8,128)(2,1)S(1)} %get-tuple-element.68.near_ref, bf16[1,4,128,256]{3,2,1,0:T(8,128)(2,1)S(1)} %collective-permute-done.19.far_ref), custom_call_target="tpu_custom_call", output_to_operand_aliasing={{}: (1, {})} | custom-call | bytes 1000000 | tf_op jit(solution)/shard_map/pallas_call | solution.py:324
  167.4 3.5 %collective-permute-done.21.far_ref = bf16[1,4,128,256]{3,2,1,0:T(8,128)(2,1)S(1)} collective-permute-done((bf16[1,4,128,256]{3,2,1,0:T(8,128)(2,1)S(1)}, bf16[1,4,128,256]{3,2,1,0:T(8,128)(2,1)S(1)}, u32[]{:S(2)}, u32[]{:S(2)}) %collective-permute-start.21) | collective-permute-done | bytes 262176 | tf_op jit(solution)/shard_map/ppermute | solution.py:27
  171.0 2.0 %shard_map.90 = bf16[128,4096]{1,0:T(8,128)(2,1)} custom-call(s32[1]{0:T(128)} %bitcast.place_ref, bf16[128,4096]{1,0:T(8,128)(2,1)} %shard_map.87.so_far_ref, bf16[1,4,128,256]{3,2,1,0:T(8,128)(2,1)S(1)} %get-tuple-element.66.near_ref, bf16[1,4,128,256]{3,2,1,0:T(8,128)(2,1)S(1)} %collective-permute-done.21.far_ref), custom_call_target="tpu_custom_call", output_to_operand_aliasing={{}: (1, {})} | custom-call | bytes 1000000 | tf_op jit(solution)/shard_map/pallas_call | solution.py:324
  (62 shorter events, 11.8 us)
Async XLA Ops:
  0.0 36.0 %copy-start.3 = (s32[1,128]{1,0:T(1,128)S(1)}, s32[1,128]{1,0:T(1,128)}, u32[]{:S(2)}) copy-start(s32[1,128]{1,0:T(1,128)} %ids_ref) | copy-start | bytes 1540
  0.0 40.6 %copy-start.5 = (bf16[32,128]{1,0:T(8,128)(2,1)S(1)}, bf16[32,128]{1,0:T(8,128)(2,1)}, u32[]{:S(2)}) copy-start(bf16[32,128]{1,0:T(8,128)(2,1)} %param.12) | copy-start | bytes 24580
  0.0 60.5 %copy-start.2 = (f32[4096]{0:T(1024)S(1)}, f32[4096]{0:T(1024)}, u32[]{:S(2)}) copy-start(f32[4096]{0:T(1024)} %param.9) | copy-start | bytes 49156
  32.9 22.2 %collective-permute-start.4 = (bf16[512,512]{1,0:T(8,128)(2,1)}, bf16[512,512]{1,0:T(8,128)(2,1)S(1)}, u32[]{:S(2)}, u32[]{:S(2)}) collective-permute-start(bf16[512,512]{1,0:T(8,128)(2,1)} %get-tuple-element.40), channel_id=1, source_target_pairs={{0,8},{4,12},{8,0},{12,4},{16,24},{20,28},{24,16},{28,20},{1,9},{5... | collective-permute-start | bytes 1572872 | tf_op jit(solution)/shard_map/ppermute | solution.py:27
  36.0 15.5 %collective-permute-start.2 = (s32[1,128]{1,0:T(1,128)S(1)}, s32[1,128]{1,0:T(1,128)S(1)}, u32[]{:S(2)}, u32[]{:S(2)}) collective-permute-start(s32[1,128]{1,0:T(1,128)S(1)} %copy-done.3), channel_id=1, source_target_pairs={{0,24},{4,28},{8,16},{12,20},{16,8},{20,12},{24,0},{28,4},{1,25},{... | collective-permute-start | bytes 1544 | tf_op jit(solution)/shard_map/ppermute | solution.py:27
  38.5 13.0 %collective-permute-start.1 = (s32[1,128]{1,0:T(1,128)S(1)}, s32[1,128]{1,0:T(1,128)S(1)}, u32[]{:S(2)}, u32[]{:S(2)}) collective-permute-start(s32[1,128]{1,0:T(1,128)S(1)} %copy-done.3), channel_id=1, source_target_pairs={{0,8},{4,12},{8,0},{12,4},{16,24},{20,28},{24,16},{28,20},{1,9},{5... | collective-permute-start | bytes 1544 | tf_op jit(solution)/shard_map/ppermute | solution.py:27
  39.2 12.3 %collective-permute-start = (s32[1,128]{1,0:T(1,128)S(1)}, s32[1,128]{1,0:T(1,128)S(1)}, u32[]{:S(2)}, u32[]{:S(2)}) collective-permute-start(s32[1,128]{1,0:T(1,128)S(1)} %copy-done.3), channel_id=1, source_target_pairs={{0,16},{4,20},{8,24},{12,28},{16,0},{20,4},{24,8},{28,12},{1,17},{... | collective-permute-start | bytes 1544 | tf_op jit(solution)/shard_map/ppermute | solution.py:27
  40.4 32.0 %collective-permute-start.5 = (bf16[512,512]{1,0:T(8,128)(2,1)}, bf16[512,512]{1,0:T(8,128)(2,1)S(1)}, u32[]{:S(2)}, u32[]{:S(2)}) collective-permute-start(bf16[512,512]{1,0:T(8,128)(2,1)} %get-tuple-element.42), channel_id=1, source_target_pairs={{0,8},{4,12},{8,0},{12,4},{16,24},{20,28},{24,16},{28,20},{1,9},{5... | collective-permute-start | bytes 1572872 | tf_op jit(solution)/shard_map/ppermute | solution.py:27
  51.5 3.7 %collective-permute-start.3 = (s32[4,128]{1,0:T(4,128)S(1)}, s32[4,128]{1,0:T(4,128)S(1)}, u32[]{:S(2)}, u32[]{:S(2)}) collective-permute-start(s32[4,128]{1,0:T(4,128)S(1)} %pad_add_fusion.2), channel_id=1, source_target_pairs={{0,4},{4,0},{8,12},{12,8},{16,20},{20,16},{24,28},{28,24},{1,5},{5... | collective-permute-start | bytes 6152 | tf_op jit(solution)/shard_map/ppermute | solution.py:27
  55.1 19.3 %collective-permute-start.8 = (s32[8,128]{1,0:T(8,128)S(1)}, s32[8,128]{1,0:T(8,128)S(1)}, u32[]{:S(2)}, u32[]{:S(2)}) collective-permute-start(s32[8,128]{1,0:T(8,128)S(1)} %pad_add_fusion.1), channel_id=1, source_target_pairs={{0,1},{1,2},{2,3},{4,5},{5,6},{6,7},{8,9},{9,10},{10,11},{12,13},{... | collective-permute-start | bytes 12296 | tf_op jit(solution)/shard_map/ppermute | solution.py:22
  56.4 18.0 %collective-permute-start.7 = (s32[8,128]{1,0:T(8,128)S(1)}, s32[8,128]{1,0:T(8,128)S(1)}, u32[]{:S(2)}, u32[]{:S(2)}) collective-permute-start(s32[8,128]{1,0:T(8,128)S(1)} %pad_add_fusion.1), channel_id=1, source_target_pairs={{0,2},{1,3},{4,6},{5,7},{8,10},{9,11},{12,14},{13,15},{16,18},{17,... | collective-permute-start | bytes 12296 | tf_op jit(solution)/shard_map/ppermute | solution.py:22
  60.5 2.2 %copy-start.1 = (bf16[512,4096]{1,0:T(8,128)(2,1)S(1)}, bf16[512,4096]{1,0:T(8,128)(2,1)}, u32[]{:S(2)}) copy-start(bf16[512,4096]{1,0:T(8,128)(2,1)} %rows_ref.1) | copy-start | bytes 12582916
  62.7 12.0 %copy-start.4 = (f32[3,3,512]{2,1,0:T(4,128)S(1)}, f32[3,3,512]{2,1,0:T(4,128)}, u32[]{:S(2)}) copy-start(f32[3,3,512]{2,1,0:T(4,128)} %short_ref.3) | copy-start | bytes 55300
  72.4 29.8 %collective-permute-start.6 = (bf16[512,512]{1,0:T(8,128)(2,1)S(1)}, bf16[512,512]{1,0:T(8,128)(2,1)S(1)}, u32[]{:S(2)}, u32[]{:S(2)}) collective-permute-start(bf16[512,512]{1,0:T(8,128)(2,1)S(1)} %collective-permute-done.5), channel_id=1, source_target_pairs={{0,2},{1,3},{2,0},{3,1},{4,6},{5,7},{6,4},{7,5},{8,10},{9,11},{10,... | collective-permute-start | bytes 1572872 | tf_op jit(solution)/shard_map/ppermute | solution.py:27
  72.5 24.5 %collective-permute-start.9 = (bf16[512,512]{1,0:T(8,128)(2,1)S(1)}, bf16[512,512]{1,0:T(8,128)(2,1)S(1)}, u32[]{:S(2)}, u32[]{:S(2)}) collective-permute-start(bf16[512,512]{1,0:T(8,128)(2,1)S(1)} %collective-permute-done.4), channel_id=1, source_target_pairs={{0,2},{1,3},{2,0},{3,1},{4,6},{5,7},{6,4},{7,5},{8,10},{9,11},{10,... | collective-permute-start | bytes 1572872 | tf_op jit(solution)/shard_map/ppermute | solution.py:27
  97.1 9.1 %copy-start = (bf16[512,4096]{1,0:T(8,128)(2,1)S(1)}, bf16[512,4096]{1,0:T(8,128)(2,1)}, u32[]{:S(2)}) copy-start(bf16[512,4096]{1,0:T(8,128)(2,1)} %refs_3_.15) | copy-start | bytes 12582916
  97.1 9.1 %collective-permute-start.12 = (bf16[2,512,512]{2,1,0:T(8,128)(2,1)S(1)}, bf16[2,512,512]{2,1,0:T(8,128)(2,1)S(1)}, u32[]{:S(2)}, u32[]{:S(2)}) collective-permute-start(bf16[2,512,512]{2,1,0:T(8,128)(2,1)S(1)} %pad_maximum_fusion.refs_4_), channel_id=1, source_target_pairs={{0,1},{1,0},{2,3},{3,2},{4,5},{5,4},{6,7},{7,6},{8,9},{9,8},{10,11... | collective-permute-start | bytes 3145736 | tf_op jit(solution)/shard_map/ppermute | solution.py:27
  97.2 8.8 %collective-permute-start.10 = (bf16[2,128,512]{2,1,0:T(8,128)(2,1)S(1)}, bf16[2,128,512]{2,1,0:T(8,128)(2,1)S(1)}, u32[]{:S(2)}, u32[]{:S(2)}) collective-permute-start(bf16[2,128,512]{2,1,0:T(8,128)(2,1)S(1)} %get-tuple-element.74), channel_id=1, source_target_pairs={{0,8},{4,12},{8,0},{12,4},{16,24},{20,28},{24,16},{28,20},{1,9},{5... | collective-permute-start | bytes 786440 | tf_op jit(solution)/shard_map/ppermute | solution.py:27
  106.1 12.4 %collective-permute-start.17 = (bf16[2,512,512]{2,1,0:T(8,128)(2,1)S(1)}, bf16[2,512,512]{2,1,0:T(8,128)(2,1)S(1)}, u32[]{:S(2)}, u32[]{:S(2)}) collective-permute-start(bf16[2,512,512]{2,1,0:T(8,128)(2,1)S(1)} %pad_maximum_fusion.1.refs_4_), channel_id=1, source_target_pairs={{0,1},{1,0},{2,3},{3,2},{4,5},{5,4},{6,7},{7,6},{8,9},{9,8},{10,11... | collective-permute-start | bytes 3145736 | tf_op jit(solution)/shard_map/ppermute | solution.py:27
  106.9 16.6 %collective-permute-start.13 = (bf16[2,4,128,256]{3,2,1,0:T(8,128)(2,1)S(1)}, bf16[2,4,128,256]{3,2,1,0:T(8,128)(2,1)S(1)}, u32[]{:S(2)}, u32[]{:S(2)}) collective-permute-start(bf16[2,4,128,256]{3,2,1,0:T(8,128)(2,1)S(1)} %shard_map.80), channel_id=1, source_target_pairs={{0,4},{4,0},{8,12},{12,8},{16,20},{20,16},{24,28},{28,24},{1,5},{5... | collective-permute-start | bytes 1572872 | tf_op jit(solution)/shard_map/ppermute | solution.py:27
  108.5 8.5 %collective-permute-start.11 = (bf16[2,128,512]{2,1,0:T(8,128)(2,1)S(1)}, bf16[2,128,512]{2,1,0:T(8,128)(2,1)S(1)}, u32[]{:S(2)}, u32[]{:S(2)}) collective-permute-start(bf16[2,128,512]{2,1,0:T(8,128)(2,1)S(1)} %get-tuple-element.75), channel_id=1, source_target_pairs={{0,8},{4,12},{8,0},{12,4},{16,24},{20,28},{24,16},{28,20},{1,9},{5... | collective-permute-start | bytes 786440 | tf_op jit(solution)/shard_map/ppermute | solution.py:27
  109.9 23.0 %collective-permute-start.15 = (bf16[2,4,128,256]{3,2,1,0:T(8,128)(2,1)S(1)}, bf16[2,4,128,256]{3,2,1,0:T(8,128)(2,1)S(1)}, u32[]{:S(2)}, u32[]{:S(2)}) collective-permute-start(bf16[2,4,128,256]{3,2,1,0:T(8,128)(2,1)S(1)} %shard_map.83), channel_id=1, source_target_pairs={{0,4},{4,0},{8,12},{12,8},{16,20},{20,16},{24,28},{28,24},{1,5},{5... | collective-permute-start | bytes 1572872 | tf_op jit(solution)/shard_map/ppermute | solution.py:27
  119.2 25.0 %collective-permute-start.18 = (bf16[2,4,128,256]{3,2,1,0:T(8,128)(2,1)S(1)}, bf16[2,4,128,256]{3,2,1,0:T(8,128)(2,1)S(1)}, u32[]{:S(2)}, u32[]{:S(2)}) collective-permute-start(bf16[2,4,128,256]{3,2,1,0:T(8,128)(2,1)S(1)} %shard_map.86), channel_id=1, source_target_pairs={{0,4},{4,0},{8,12},{12,8},{16,20},{20,16},{24,28},{28,24},{1,5},{5... | collective-permute-start | bytes 1572872 | tf_op jit(solution)/shard_map/ppermute | solution.py:27
  120.5 34.5 %collective-permute-start.20 = (bf16[2,4,128,256]{3,2,1,0:T(8,128)(2,1)S(1)}, bf16[2,4,128,256]{3,2,1,0:T(8,128)(2,1)S(1)}, u32[]{:S(2)}, u32[]{:S(2)}) collective-permute-start(bf16[2,4,128,256]{3,2,1,0:T(8,128)(2,1)S(1)} %shard_map.89), channel_id=1, source_target_pairs={{0,4},{4,0},{8,12},{12,8},{16,20},{20,16},{24,28},{28,24},{1,5},{5... | collective-permute-start | bytes 1572872 | tf_op jit(solution)/shard_map/ppermute | solution.py:27
  123.7 32.2 %collective-permute-start.14 = (bf16[1,4,128,256]{3,2,1,0:T(8,128)(2,1)S(1)}, bf16[1,4,128,256]{3,2,1,0:T(8,128)(2,1)S(1)}, u32[]{:S(2)}, u32[]{:S(2)}) collective-permute-start(bf16[1,4,128,256]{3,2,1,0:T(8,128)(2,1)S(1)} %get-tuple-element.71), channel_id=1, source_target_pairs={{0,16},{4,20},{8,24},{12,28},{16,0},{20,4},{24,8},{28,12},{1,17},{... | collective-permute-start | bytes 786440 | tf_op jit(solution)/shard_map/ppermute | solution.py:27
  133.1 24.8 %collective-permute-start.16 = (bf16[1,4,128,256]{3,2,1,0:T(8,128)(2,1)S(1)}, bf16[1,4,128,256]{3,2,1,0:T(8,128)(2,1)S(1)}, u32[]{:S(2)}, u32[]{:S(2)}) collective-permute-start(bf16[1,4,128,256]{3,2,1,0:T(8,128)(2,1)S(1)} %get-tuple-element.69), channel_id=1, source_target_pairs={{0,16},{4,20},{8,24},{12,28},{16,0},{20,4},{24,8},{28,12},{1,17},{... | collective-permute-start | bytes 786440 | tf_op jit(solution)/shard_map/ppermute | solution.py:27
  144.3 21.1 %collective-permute-start.19 = (bf16[1,4,128,256]{3,2,1,0:T(8,128)(2,1)S(1)}, bf16[1,4,128,256]{3,2,1,0:T(8,128)(2,1)S(1)}, u32[]{:S(2)}, u32[]{:S(2)}) collective-permute-start(bf16[1,4,128,256]{3,2,1,0:T(8,128)(2,1)S(1)} %get-tuple-element.67), channel_id=1, source_target_pairs={{0,16},{4,20},{8,24},{12,28},{16,0},{20,4},{24,8},{28,12},{1,17},{... | collective-permute-start | bytes 786440 | tf_op jit(solution)/shard_map/ppermute | solution.py:27
  155.2 15.8 %collective-permute-start.21 = (bf16[1,4,128,256]{3,2,1,0:T(8,128)(2,1)S(1)}, bf16[1,4,128,256]{3,2,1,0:T(8,128)(2,1)S(1)}, u32[]{:S(2)}, u32[]{:S(2)}) collective-permute-start(bf16[1,4,128,256]{3,2,1,0:T(8,128)(2,1)S(1)} %get-tuple-element.65), channel_id=1, source_target_pairs={{0,16},{4,20},{8,24},{12,28},{16,0},{20,4},{24,8},{28,12},{1,17},{... | collective-permute-start | bytes 786440 | tf_op jit(solution)/shard_map/ppermute | solution.py:27

commit v7 on v6

--- a/solution.py
+++ b/solution.py
@@ -12,9 +12,8 @@
 SHORT = 3
 LANES = 128
 LEAD = 16
-SPLITS = ((0, 8, 4, ((0, 4), (4, 4))), (8, 8, 4, ((0, 4), (4, 4))))
+SPLITS = ((0, 8, (0, 2, 1, 3), ((0, 2), (2, 2), (4, 4))), (8, 8, (0, 1, 2, 3), ((0, 4), (4, 2), (6, 2))))
 SIXTEENTHS = 16
-ORDER = {2: (0, 1), 4: (0, 2, 1, 3)}
 
 
 def from_behind(x, axis, by):
@@ -181,35 +180,30 @@
     )(ids.reshape(windows, 1, rows), table, short_taps, toeplitz)
 
 
-def cut_kernel(place_ref, source, *refs):
-    pieces, sems = refs[:-1], refs[-1]
-    unit = source.shape[1] // SIXTEENTHS
-    copies = []
-    for n, ((base, _, sharers, _), piece) in enumerate(zip(SPLITS, pieces)):
-        cols = piece.shape[1]
-        first = pl.multiple_of(base * unit + place_ref[0] % sharers * cols, LANES)
-        copies.append(pltpu.make_async_copy(source.at[:, pl.ds(first, cols)], piece, sems.at[n]))
-    for copy in copies:
-        copy.start()
-    for copy in copies:
-        copy.wait()
+def cut_kernel(place_ref, *refs):
+    count = len(refs) // 2
+    for source, piece in zip(refs[:count], refs[count:]):
+        piece[...] = source[...]
 
 
 def cut_pieces(place, out_proj):
     depth, width = out_proj.shape
-    hbm = pl.BlockSpec(memory_space=pltpu.HBM)
-    shapes = [
-        jax.ShapeDtypeStruct((depth, extent * width // SIXTEENTHS // sharers), out_proj.dtype)
-        for _, extent, sharers, _ in SPLITS
-    ]
+    unit = width // SIXTEENTHS
+    ins, outs, shapes = [], [], []
+    for first, extent, order, _ in SPLITS:
+        sharers = len(order)
+        cols = extent * unit // sharers
+        start = first * unit // cols
+        ins.append(pl.BlockSpec((depth, cols), lambda s, place, start=start, n=sharers: (0, start + place[0] % n)))
+        outs.append(pl.BlockSpec((depth, cols), lambda s, place: (0, 0)))
+        shapes.append(jax.ShapeDtypeStruct((depth, cols), out_proj.dtype))
     return pl.pallas_call(
         cut_kernel,
-        in_specs=[pl.BlockSpec(memory_space=pltpu.SMEM), hbm],
-        out_specs=[hbm] * len(shapes),
+        grid_spec=pltpu.PrefetchScalarGridSpec(num_scalar_prefetch=1, grid=(1,), in_specs=ins, out_specs=outs),
         out_shape=shapes,
-        scratch_shapes=[pltpu.SemaphoreType.DMA((len(shapes),))],
+        compiler_params=params(60),
         cost_estimate=cost(0, 2_000_000),
-    )(place, out_proj)
+    )(place, *[out_proj] * len(SPLITS))
 
 
 def toeplitz_kernel(base_ref, toeplitz_ref):
@@ -256,10 +250,10 @@
     count, tok_len, depth = mine.shape
     rows = count * tok_len
     unit = out_proj.shape[1] // SIXTEENTHS
-    base, extent, sharers, _ = split
+    base, extent, order, _ = split
+    sharers = len(order)
     piece_cols = extent * unit // sharers
     offset, cols = (part * unit // sharers for part in step)
-    order = ORDER[sharers]
     fixed = lambda shape: pl.BlockSpec(shape, lambda s, place: (0,) * len(shape))
 
     def own(k):
@@ -309,7 +303,7 @@
     piece_cols = so_far_ref.shape[1] // sharers
     offset = step[0] * cols // step[1]
     out_ref[...] = so_far_ref[...]
-    for i, k in enumerate(ORDER[sharers]):
+    for i, k in enumerate(split[2]):
         first = (place_ref[0] % sharers ^ k) * piece_cols + offset
         total = near_ref[0, i].astype(jnp.float32) + far_ref[0, i].astype(jnp.float32)
         at = pl.ds(pl.multiple_of(first, LANES), cols)
@@ -345,51 +339,67 @@
     beside_bit = bits[-2]
 
     early, late = cut_pieces(at, out_proj)
-    early, late, token_ids, conv_taps = tie((early, late, token_ids, conv_taps))
+    ids = level_ids(token_ids, bits[:2])
+    ids, early, late, conv_taps = tie((ids, early, late, conv_taps))
     toeplitz = build_toeplitz(conv_taps, tok_len)
-    ids = level_ids(token_ids, bits[:2])
-    ids, toeplitz = tie((ids, toeplitz))
     for group in [bits[i : i + 2] for i in range(2, len(bits), 2)]:
         ids = level_ids(ids, group)
+    ids, toeplitz = tie((ids, toeplitz))
     early, late = swap(early, "fsdp", beside_bit), swap(late, "fsdp", beside_bit)
-    ids, embedding_then, early = tie((ids, embedding, early))
+    ids, embedding_then = tie((ids, embedding))
     ids = with_lead(ids)
+    table = project(embedding_then, norm_gain, in_proj)
+    table, early = tie((table, early))
     early_across = swap(early, "ctx", 2)
-    table = project(embedding_then, norm_gain, in_proj)
-    table, late = tie((table, late))
-    late_across = swap(late, "ctx", 2)
-
-    half = ids.shape[0] // 2
-    gated = mix(ids[half:], table, short_taps, toeplitz, tok_len)
-    ids, gated, early, early_across = tie((ids, gated, early, early_across))
+
+    part = ids.shape[0] // 4
+    sent = mix(ids[3 * part :], table, short_taps, toeplitz, tok_len)
+    ids, sent = tie((ids, sent))
+    other = [swap(sent, "fsdp", beside_bit)]
+    gated = mix(ids[: 3 * part], table, short_taps, toeplitz, tok_len)
+    gated, other[0], early, early_across, late = tie((gated, other[0], early, early_across, late))
+    mine = [gated[2 * part :], gated[:part]]
+    other.append(swap(gated[part : 2 * part], "fsdp", beside_bit))
     pair = jnp.stack([early, early_across])
     beside = [(pair, swap(pair, "ctx", 1))]
-    mine = [gated[: half // 2]]
-    other = [swap(gated[half // 2 :], "fsdp", beside_bit)]
-    gated = mix(ids[:half], table, short_taps, toeplitz, tok_len)
-    late, late_across, other[0], gated = tie((late, late_across, other[0], gated))
-    pair = jnp.stack([late, late_across])
-    beside.append((pair, swap(pair, "ctx", 1)))
-    mine.append(gated[: half // 2])
-    other.append(swap(gated[half // 2 :], "fsdp", beside_bit))
+    pair = jnp.stack([late, swap(late, "ctx", 1)])
+    beside.append((pair, swap(pair, "ctx", 2)))
 
     out = residual(token_ids, embedding)
-    behind = []
-    for split, shared in zip(SPLITS, beside):
-        for step in split[3]:
-            away = panel(at, mine[0], other[0], out_proj, shared, split, step)
-            away, mine[0] = tie((away, mine[0]))
-            got = swap(away, "fsdp", bits[-1])
-            total = panel(at, mine[1], other[1], out_proj, shared, split, step)
-            if not behind:
-                total, out = tie((total, out))
-            for bit in reversed(bits[:-2]):
-                half = total.shape[0] // 2
-                far = add(total[half:], got[half:])
-                total, got = add(total[:half], got[:half]), swap(far, "fsdp", bit)
-            behind.append((total, got, split, step))
+    away, arrived, behind = [], [], []
+
+    def send(number, step):
+        part = panel(at, mine[0], other[0], out_proj, beside[number], SPLITS[number], step)
+        part, mine[0] = tie((part, mine[0]))
+        away.append(part)
+        arrived.append(swap(part, "fsdp", bits[-1]))
+
+    def sum_up(number, step):
+        got, total = arrived[len(behind)], panel(at, mine[1], other[1], out_proj, beside[number], SPLITS[number], step)
+        if behind:
+            got, _ = tie((got, behind[-1][-1]))
+        for bit in reversed(bits[:-2]):
+            half = total.shape[0] // 2
+            far = add(total[half:], got[half:])
+            total, got = add(total[:half], got[:half]), swap(far, "fsdp", bit)
+        behind.append((total, got, SPLITS[number], step, far))
+
+    first, second, *rest = SPLITS[0][3]
+    send(0, first)
+    send(0, second)
+    other[1], out, _ = tie((other[1], out, away[1]))
+    mine[0], arrived[0] = tie((mine[0], arrived[0]))
+    for step in rest:
+        send(0, step)
+    for step in SPLITS[0][3]:
+        sum_up(0, step)
+    beside[1], _ = tie((beside[1], (behind[0][1], behind[1][1])))
+    for step in SPLITS[1][3]:
+        send(1, step)
+    for step in SPLITS[1][3]:
+        sum_up(1, step)
     for last in behind:
-        out = place_pieces(at, out, *last)
+        out = place_pieces(at, out, *last[:-1])
     return out[None]
 
 

time: 173 us -> 121 us (0.70)
  waiting for transfers between devices: 75.9 us -> 42 us
  Pallas kernels: 68 us -> 44.5 us
  starting transfers between devices: 25.3 us -> 30.7 us
    ppermute x20 -> x24, waiting for transfers between devices: 75.9 us -> 42 us  [swap(): return lax.ppermute(x, axis, [(i, i ^ mask) for i in range(peers)])]
    pallas_call x1, Pallas kernels: 32.9 us -> 2.24 us  [cut_pieces(): pl.pallas_call(cut_kernel, grid_spec=pltpu.PrefetchScalarGridSpec(num_sca...]
    ppermute x20 -> x24, starting transfers between devices: 20 us -> 25.4 us  [swap(): return lax.ppermute(x, axis, [(i, i ^ mask) for i in range(peers)])]
    pallas_call x4 -> x6, Pallas kernels: 7.92 us -> 11.7 us  [place_pieces(): pl.pallas_call(functools.partial(place_kernel, split, step), grid_spec=pl...]
    pallas_call x8 -> x12, Pallas kernels: 5.67 us -> 9.08 us  [panel(): pl.pallas_call(panel_kernel, grid_spec=pltpu.PrefetchScalarGridSpec(num_s...]
  transfers between devices with their start and end apart: 22 -> 26, of which waited for: 10 -> 15; matrix products, arithmetic and copies ran while one was open for 1% -> 1% of each run, Pallas kernels for 19% -> 35%
where the time goes in v7:
time: 121 us
  Pallas kernels  44.5 us (37%)
  waiting for transfers between devices  42 us (35%)
  starting transfers between devices  30.7 us (25%)
  local copies, waits for them, and re-layouts  2.45 us (2%)
    ppermute x24, waiting for transfers between devices, swap(): return lax.ppermute(x, axis, [(i, i ^ mask) for i in range(peers)])  42 us
    ppermute x24, starting transfers between devices, swap(): return lax.ppermute(x, axis, [(i, i ^ mask) for i in range(peers)])  25.4 us
    pallas_call x6, Pallas kernels, place_pieces(): pl.pallas_call(functools.partial(place_kernel, split, step), grid_spec=pl...  11.7 us
    pallas_call x1, Pallas kernels, project(): pl.pallas_call(table_kernel, grid=(1,), in_specs=[hbm, hbm, pl.BlockSpec(...  9.69 us
    pallas_call x12, Pallas kernels, panel(): pl.pallas_call(panel_kernel, grid_spec=pltpu.PrefetchScalarGridSpec(num_s...  9.08 us
    pallas_call x2, Pallas kernels, mix(): pl.pallas_call(mixer_kernel, grid=(windows // 2,), in_specs=[pl.BlockSpec...  8.52 us
    ppermute x2, starting transfers between devices, from_behind(): lax.ppermute(x, axis, [(i, i + by) for i in range(peers) if i + by < peers])  5.32 us
    pallas_call x1, Pallas kernels, residual(): pl.pallas_call(residual_kernel, grid=(4,), in_specs=[whole(token_ids), pl...  2.65 us
  transfers between devices with their start and end apart: 26, of which 15 were waited for; matrix products, arithmetic and copies ran while one was open for 1% of the time, Pallas kernels for 35%

profile of v7, /device:TPU:0, one launch (start us, length us, event | category | flops | bytes accessed | tf_op | source)
XLA Modules:
  0.0 120.9 jit_solution(1581988550148125762)
XLA Ops:
  0.0 5.0 %collective-permute-start.2 = (s32[1,128]{1,0:T(1,128)}, s32[1,128]{1,0:T(1,128)S(1)}, u32[]{:S(2)}, u32[]{:S(2)}) collective-permute-start(s32[1,128]{1,0:T(1,128)} %ids_ref.1), channel_id=1, source_target_pairs={{0,24},{4,28},{8,16},{12,20},{16,8},{20,12},{24,0},{28,4},{1,25},{... | collective-permute-start | bytes 1544 | tf_op jit(solution)/shard_map/ppermute | solution.py:26
  5.6 2.2 %shard_map.73 = (bf16[512,512]{1,0:T(8,128)(2,1)}, bf16[512,512]{1,0:T(8,128)(2,1)}) custom-call(s32[1]{0:T(128)} %bitcast.place_ref, bf16[512,4096]{1,0:T(8,128)(2,1)} %refs_3_.23, bf16[512,4096]{1,0:T(8,128)(2,1)} %refs_3_.23), custom_call_target="tpu_custom_call" | custom-call | bytes 2000000 | tf_op jit(solution)/shard_map/pallas_call | solution.py:200
  9.6 1.6 %collective-permute-start.3 = (s32[4,128]{1,0:T(4,128)S(1)}, s32[4,128]{1,0:T(4,128)S(1)}, u32[]{:S(2)}, u32[]{:S(2)}) collective-permute-start(s32[4,128]{1,0:T(4,128)S(1)} %pad_add_fusion.2), channel_id=1, source_target_pairs={{0,4},{4,0},{8,12},{12,8},{16,20},{20,16},{24,28},{28,24},{1,5},{5... | collective-permute-start | bytes 6152 | tf_op jit(solution)/shard_map/ppermute | solution.py:26
  12.0 2.1 %collective-permute-start.6 = (bf16[512,512]{1,0:T(8,128)(2,1)}, bf16[512,512]{1,0:T(8,128)(2,1)S(1)}, u32[]{:S(2)}, u32[]{:S(2)}) collective-permute-start(bf16[512,512]{1,0:T(8,128)(2,1)} %get-tuple-element.53), channel_id=1, source_target_pairs={{0,8},{4,12},{8,0},{12,4},{16,24},{20,28},{24,16},{28,20},{1,9},{5... | collective-permute-start | bytes 1572872 | tf_op jit(solution)/shard_map/ppermute | solution.py:26
  14.2 1.3 %collective-permute-start.5 = (s32[8,128]{1,0:T(8,128)S(1)}, s32[8,128]{1,0:T(8,128)S(1)}, u32[]{:S(2)}, u32[]{:S(2)}) collective-permute-start(s32[8,128]{1,0:T(8,128)S(1)} %pad_add_fusion.1), channel_id=1, source_target_pairs={{0,1},{1,2},{2,3},{4,5},{5,6},{6,7},{8,9},{9,10},{10,11},{12,13},{... | collective-permute-start | bytes 12296 | tf_op jit(solution)/shard_map/ppermute | solution.py:21
  15.5 4.0 %collective-permute-start.4 = (s32[8,128]{1,0:T(8,128)S(1)}, s32[8,128]{1,0:T(8,128)S(1)}, u32[]{:S(2)}, u32[]{:S(2)}) collective-permute-start(s32[8,128]{1,0:T(8,128)S(1)} %pad_add_fusion.1), channel_id=1, source_target_pairs={{0,2},{1,3},{4,6},{5,7},{8,10},{9,11},{12,14},{13,15},{16,18},{17,... | collective-permute-start | bytes 12296 | tf_op jit(solution)/shard_map/ppermute | solution.py:21
  19.5 2.2 %copy-done.1 = bf16[512,4096]{1,0:T(8,128)(2,1)S(1)} copy-done((bf16[512,4096]{1,0:T(8,128)(2,1)S(1)}, bf16[512,4096]{1,0:T(8,128)(2,1)}, u32[]{:S(2)}) %copy-start.1) | copy-done | bytes 4194328
  21.7 9.7 %shard_map.75.table_ref = bf16[3,512,512]{2,1,0:T(8,128)(2,1)S(1)} custom-call(bf16[512,4096]{1,0:T(8,128)(2,1)S(1)} %copy-done.1, bf16[3,4096,512]{2,1,0:T(8,128)(2,1)} %weight_hbm.1, f32[1,4096]{1,0:T(1,128)S(1)} %bitcast.43), custom_call_target="tpu_custom_call" | custom-call | flops 3000000000 | tf_op jit(solution)/shard_map/pallas_call | solution.py:101
  31.7 2.1 %shard_map.76 = bf16[2,128,512]{2,1,0:T(8,128)(2,1)S(1)} custom-call(s32[2,1,272]{2,1,0:T(1,128)S(1)} %copy.14.ids_ref, bf16[3,512,512]{2,1,0:T(8,128)(2,1)S(1)} %shard_map.75.table_ref, f32[3,3,512]{2,1,0:T(4,128)S(1)} %copy-done.4, bf16[4,1024,256]{2,1,0:T(8,128)(2,1)S(1)} %shard_map.74.toeplitz), custom_call_target="tpu_custom_call" | custom-call | flops 1500000000 | tf_op jit(solution)/shard_map/pallas_call | solution.py:167
  33.8 2.0 %collective-permute-start.7 = (bf16[2,128,512]{2,1,0:T(8,128)(2,1)S(1)}, bf16[2,128,512]{2,1,0:T(8,128)(2,1)S(1)}, u32[]{:S(2)}, u32[]{:S(2)}) collective-permute-start(bf16[2,128,512]{2,1,0:T(8,128)(2,1)S(1)} %shard_map.76), channel_id=1, source_target_pairs={{0,8},{4,12},{8,0},{12,4},{16,24},{20,28},{24,16},{28,20},{1,9},{5... | collective-permute-start | bytes 786440 | tf_op jit(solution)/shard_map/ppermute | solution.py:26
  35.8 6.4 %shard_map.77 = bf16[6,128,512]{2,1,0:T(8,128)(2,1)S(1)} custom-call(s32[6,1,272]{2,1,0:T(1,128)S(1)} %reshape.57.ids_ref, bf16[3,512,512]{2,1,0:T(8,128)(2,1)S(1)} %shard_map.75.table_ref, f32[3,3,512]{2,1,0:T(4,128)S(1)} %copy-done.4, bf16[4,1024,256]{2,1,0:T(8,128)(2,1)S(1)} %shard_map.74.toeplitz), custom_call_target="tpu_custom_call" | custom-call | flops 1500000000 | tf_op jit(solution)/shard_map/pallas_call | solution.py:167
  42.3 2.7 %collective-permute-done.8 = bf16[512,512]{1,0:T(8,128)(2,1)S(1)} collective-permute-done((bf16[512,512]{1,0:T(8,128)(2,1)S(1)}, bf16[512,512]{1,0:T(8,128)(2,1)S(1)}, u32[]{:S(2)}, u32[]{:S(2)}) %collective-permute-start.8) | collective-permute-done | bytes 524320 | tf_op jit(solution)/shard_map/ppermute | solution.py:26
  45.6 2.9 %collective-permute-done.18 = bf16[512,512]{1,0:T(8,128)(2,1)S(1)} collective-permute-done((bf16[512,512]{1,0:T(8,128)(2,1)S(1)}, bf16[512,512]{1,0:T(8,128)(2,1)S(1)}, u32[]{:S(2)}, u32[]{:S(2)}) %collective-permute-start.18) | collective-permute-done | bytes 524320 | tf_op jit(solution)/shard_map/ppermute | solution.py:26
  49.1 2.0 %collective-permute-start.10 = (bf16[2,128,512]{2,1,0:T(8,128)(2,1)S(1)}, bf16[2,128,512]{2,1,0:T(8,128)(2,1)S(1)}, u32[]{:S(2)}, u32[]{:S(2)}) collective-permute-start(bf16[2,128,512]{2,1,0:T(8,128)(2,1)S(1)} %get-tuple-element.93), channel_id=1, source_target_pairs={{0,8},{4,12},{8,0},{12,4},{16,24},{20,28},{24,16},{28,20},{1,9},{5... | collective-permute-start | bytes 786440 | tf_op jit(solution)/shard_map/ppermute | solution.py:26
  52.6 2.6 %shard_map.78.so_far_ref = bf16[128,4096]{1,0:T(8,128)(2,1)} custom-call(s32[1,128]{1,0:T(1,128)S(1)} %copy-done.3, bf16[512,4096]{1,0:T(8,128)(2,1)S(1)} %copy-done.1), custom_call_target="tpu_custom_call" | custom-call | flops 400000000 | tf_op jit(solution)/shard_map/pallas_call | solution.py:290
  56.0 1.4 %collective-permute-start.14 = (bf16[2,4,128,128]{3,2,1,0:T(8,128)(2,1)S(1)}, bf16[2,4,128,128]{3,2,1,0:T(8,128)(2,1)S(1)}, u32[]{:S(2)}, u32[]{:S(2)}) collective-permute-start(bf16[2,4,128,128]{3,2,1,0:T(8,128)(2,1)S(1)} %shard_map.80), channel_id=1, source_target_pairs={{0,4},{4,0},{8,12},{12,8},{16,20},{20,16},{24,28},{28,24},{1,5},{5... | collective-permute-start | bytes 786440 | tf_op jit(solution)/shard_map/ppermute | solution.py:26
  59.0 2.1 %collective-permute-done.12 = bf16[2,4,128,128]{3,2,1,0:T(8,128)(2,1)S(1)} collective-permute-done((bf16[2,4,128,128]{3,2,1,0:T(8,128)(2,1)S(1)}, bf16[2,4,128,128]{3,2,1,0:T(8,128)(2,1)S(1)}, u32[]{:S(2)}, u32[]{:S(2)}) %collective-permute-start.12) | collective-permute-done | bytes 262176 | tf_op jit(solution)/shard_map/ppermute | solution.py:26
  61.9 3.4 %collective-permute-done.14 = bf16[2,4,128,128]{3,2,1,0:T(8,128)(2,1)S(1)} collective-permute-done((bf16[2,4,128,128]{3,2,1,0:T(8,128)(2,1)S(1)}, bf16[2,4,128,128]{3,2,1,0:T(8,128)(2,1)S(1)}, u32[]{:S(2)}, u32[]{:S(2)}) %collective-permute-start.14) | collective-permute-done | bytes 262176 | tf_op jit(solution)/shard_map/ppermute | solution.py:26
  68.0 6.6 %collective-permute-done.15.far_ref = bf16[1,4,128,128]{3,2,1,0:T(8,128)(2,1)S(1)} collective-permute-done((bf16[1,4,128,128]{3,2,1,0:T(8,128)(2,1)S(1)}, bf16[1,4,128,128]{3,2,1,0:T(8,128)(2,1)S(1)}, u32[]{:S(2)}, u32[]{:S(2)}) %collective-permute-start.15) | collective-permute-done | bytes 131104 | tf_op jit(solution)/shard_map/ppermute | solution.py:26
  83.6 7.6 %collective-permute-done.20 = bf16[2,4,128,256]{3,2,1,0:T(8,128)(2,1)S(1)} collective-permute-done((bf16[2,4,128,256]{3,2,1,0:T(8,128)(2,1)S(1)}, bf16[2,4,128,256]{3,2,1,0:T(8,128)(2,1)S(1)}, u32[]{:S(2)}, u32[]{:S(2)}) %collective-permute-start.20) | collective-permute-done | bytes 524320 | tf_op jit(solution)/shard_map/ppermute | solution.py:26
  91.3 1.3 %collective-permute-start.21 = (bf16[1,4,128,256]{3,2,1,0:T(8,128)(2,1)S(1)}, bf16[1,4,128,256]{3,2,1,0:T(8,128)(2,1)S(1)}, u32[]{:S(2)}, u32[]{:S(2)}) collective-permute-start(bf16[1,4,128,256]{3,2,1,0:T(8,128)(2,1)S(1)} %get-tuple-element.87), channel_id=1, source_target_pairs={{0,16},{4,20},{8,24},{12,28},{16,0},{20,4},{24,8},{28,12},{1,17},{... | collective-permute-start | bytes 786440 | tf_op jit(solution)/shard_map/ppermute | solution.py:26
  92.6 4.2 %collective-permute-done.22 = bf16[2,4,128,128]{3,2,1,0:T(8,128)(2,1)S(1)} collective-permute-done((bf16[2,4,128,128]{3,2,1,0:T(8,128)(2,1)S(1)}, bf16[2,4,128,128]{3,2,1,0:T(8,128)(2,1)S(1)}, u32[]{:S(2)}, u32[]{:S(2)}) %collective-permute-start.22) | collective-permute-done | bytes 262176 | tf_op jit(solution)/shard_map/ppermute | solution.py:26
  96.9 1.3 %collective-permute-start.23 = (bf16[1,4,128,128]{3,2,1,0:T(8,128)(2,1)S(1)}, bf16[1,4,128,128]{3,2,1,0:T(8,128)(2,1)S(1)}, u32[]{:S(2)}, u32[]{:S(2)}) collective-permute-start(bf16[1,4,128,128]{3,2,1,0:T(8,128)(2,1)S(1)} %get-tuple-element.96), channel_id=1, source_target_pairs={{0,16},{4,20},{8,24},{12,28},{16,0},{20,4},{24,8},{28,12},{1,17},{... | collective-permute-start | bytes 393224 | tf_op jit(solution)/shard_map/ppermute | solution.py:26
  98.2 2.9 %collective-permute-done.24 = bf16[2,4,128,128]{3,2,1,0:T(8,128)(2,1)S(1)} collective-permute-done((bf16[2,4,128,128]{3,2,1,0:T(8,128)(2,1)S(1)}, bf16[2,4,128,128]{3,2,1,0:T(8,128)(2,1)S(1)}, u32[]{:S(2)}, u32[]{:S(2)}) %collective-permute-start.24) | collective-permute-done | bytes 262176 | tf_op jit(solution)/shard_map/ppermute | solution.py:26
  101.9 1.9 %shard_map.82.so_far_ref = bf16[128,4096]{1,0:T(8,128)(2,1)} custom-call(s32[1]{0:T(128)} %bitcast.place_ref, bf16[128,4096]{1,0:T(8,128)(2,1)} %shard_map.78.so_far_ref, bf16[1,4,128,128]{3,2,1,0:T(8,128)(2,1)S(1)} %get-tuple-element.101.near_ref, bf16[1,4,128,128]{3,2,1,0:T(8,128)(2,1)S(1)} %collective-permute-done.13.far_ref), custom_call_target="tpu_custom_call", output_to_operand_aliasing={{}: (1, {})} | custom-call | bytes 1000000 | tf_op jit(solution)/shard_map/pallas_call | solution.py:318
  103.8 1.9 %shard_map.84.so_far_ref = bf16[128,4096]{1,0:T(8,128)(2,1)} custom-call(s32[1]{0:T(128)} %bitcast.place_ref, bf16[128,4096]{1,0:T(8,128)(2,1)} %shard_map.82.so_far_ref, bf16[1,4,128,128]{3,2,1,0:T(8,128)(2,1)S(1)} %get-tuple-element.99.near_ref, bf16[1,4,128,128]{3,2,1,0:T(8,128)(2,1)S(1)} %collective-permute-done.15.far_ref), custom_call_target="tpu_custom_call", output_to_operand_aliasing={{}: (1, {})} | custom-call | bytes 1000000 | tf_op jit(solution)/shard_map/pallas_call | solution.py:318
  105.7 2.6 %collective-permute-done.17.far_ref = bf16[1,4,128,256]{3,2,1,0:T(8,128)(2,1)S(1)} collective-permute-done((bf16[1,4,128,256]{3,2,1,0:T(8,128)(2,1)S(1)}, bf16[1,4,128,256]{3,2,1,0:T(8,128)(2,1)S(1)}, u32[]{:S(2)}, u32[]{:S(2)}) %collective-permute-start.17) | collective-permute-done | bytes 262176 | tf_op jit(solution)/shard_map/ppermute | solution.py:26
  108.3 2.0 %shard_map.87.so_far_ref = bf16[128,4096]{1,0:T(8,128)(2,1)} custom-call(s32[1]{0:T(128)} %bitcast.place_ref, bf16[128,4096]{1,0:T(8,128)(2,1)} %shard_map.84.so_far_ref, bf16[1,4,128,256]{3,2,1,0:T(8,128)(2,1)S(1)} %get-tuple-element.90.near_ref, bf16[1,4,128,256]{3,2,1,0:T(8,128)(2,1)S(1)} %collective-permute-done.17.far_ref), custom_call_target="tpu_custom_call", output_to_operand_aliasing={{}: (1, {})} | custom-call | bytes 1000000 | tf_op jit(solution)/shard_map/pallas_call | solution.py:318
  110.3 3.6 %collective-permute-done.21.far_ref = bf16[1,4,128,256]{3,2,1,0:T(8,128)(2,1)S(1)} collective-permute-done((bf16[1,4,128,256]{3,2,1,0:T(8,128)(2,1)S(1)}, bf16[1,4,128,256]{3,2,1,0:T(8,128)(2,1)S(1)}, u32[]{:S(2)}, u32[]{:S(2)}) %collective-permute-start.21) | collective-permute-done | bytes 262176 | tf_op jit(solution)/shard_map/ppermute | solution.py:26
  113.9 2.0 %shard_map.90.so_far_ref = bf16[128,4096]{1,0:T(8,128)(2,1)} custom-call(s32[1]{0:T(128)} %bitcast.place_ref, bf16[128,4096]{1,0:T(8,128)(2,1)} %shard_map.87.so_far_ref, bf16[1,4,128,256]{3,2,1,0:T(8,128)(2,1)S(1)} %get-tuple-element.88.near_ref, bf16[1,4,128,256]{3,2,1,0:T(8,128)(2,1)S(1)} %collective-permute-done.21.far_ref), custom_call_target="tpu_custom_call", output_to_operand_aliasing={{}: (1, {})} | custom-call | bytes 1000000 | tf_op jit(solution)/shard_map/pallas_call | solution.py:318
  116.7 1.9 %shard_map.93.so_far_ref = bf16[128,4096]{1,0:T(8,128)(2,1)} custom-call(s32[1]{0:T(128)} %bitcast.place_ref, bf16[128,4096]{1,0:T(8,128)(2,1)} %shard_map.90.so_far_ref, bf16[1,4,128,128]{3,2,1,0:T(8,128)(2,1)S(1)} %get-tuple-element.97.near_ref, bf16[1,4,128,128]{3,2,1,0:T(8,128)(2,1)S(1)} %collective-permute-done.23.far_ref), custom_call_target="tpu_custom_call", output_to_operand_aliasing={{}: (1, {})} | custom-call | bytes 1000000 | tf_op jit(solution)/shard_map/pallas_call | solution.py:318
  119.0 1.9 %shard_map.96 = bf16[128,4096]{1,0:T(8,128)(2,1)} custom-call(s32[1]{0:T(128)} %bitcast.place_ref, bf16[128,4096]{1,0:T(8,128)(2,1)} %shard_map.93.so_far_ref, bf16[1,4,128,128]{3,2,1,0:T(8,128)(2,1)S(1)} %get-tuple-element.95.near_ref, bf16[1,4,128,128]{3,2,1,0:T(8,128)(2,1)S(1)} %collective-permute-done.25.far_ref), custom_call_target="tpu_custom_call", output_to_operand_aliasing={{}: (1, {})} | custom-call | bytes 1000000 | tf_op jit(solution)/shard_map/pallas_call | solution.py:318
  (76 shorter events, 22.9 us)
Async XLA Ops:
  0.0 7.9 %collective-permute-start.2 = (s32[1,128]{1,0:T(1,128)}, s32[1,128]{1,0:T(1,128)S(1)}, u32[]{:S(2)}, u32[]{:S(2)}) collective-permute-start(s32[1,128]{1,0:T(1,128)} %ids_ref.1), channel_id=1, source_target_pairs={{0,24},{4,28},{8,16},{12,20},{16,8},{20,12},{24,0},{28,4},{1,25},{... | collective-permute-start | bytes 1544 | tf_op jit(solution)/shard_map/ppermute | solution.py:26
  5.0 3.7 %collective-permute-start.1 = (s32[1,128]{1,0:T(1,128)}, s32[1,128]{1,0:T(1,128)S(1)}, u32[]{:S(2)}, u32[]{:S(2)}) collective-permute-start(s32[1,128]{1,0:T(1,128)} %ids_ref.1), channel_id=1, source_target_pairs={{0,8},{4,12},{8,0},{12,4},{16,24},{20,28},{24,16},{28,20},{1,9},{5... | collective-permute-start | bytes 1544 | tf_op jit(solution)/shard_map/ppermute | solution.py:26
  5.1 4.6 %collective-permute-start = (s32[1,128]{1,0:T(1,128)}, s32[1,128]{1,0:T(1,128)S(1)}, u32[]{:S(2)}, u32[]{:S(2)}) collective-permute-start(s32[1,128]{1,0:T(1,128)} %ids_ref.1), channel_id=1, source_target_pairs={{0,16},{4,20},{8,24},{12,28},{16,0},{20,4},{24,8},{28,12},{1,17},{... | collective-permute-start | bytes 1544 | tf_op jit(solution)/shard_map/ppermute | solution.py:26
  5.6 4.0 %copy-start.3 = (s32[1,128]{1,0:T(1,128)S(1)}, s32[1,128]{1,0:T(1,128)}, u32[]{:S(2)}) copy-start(s32[1,128]{1,0:T(1,128)} %ids_ref.1) | copy-start | bytes 1540
  5.6 5.6 %copy-start.5 = (bf16[32,128]{1,0:T(8,128)(2,1)S(1)}, bf16[32,128]{1,0:T(8,128)(2,1)}, u32[]{:S(2)}) copy-start(bf16[32,128]{1,0:T(8,128)(2,1)} %param.12) | copy-start | bytes 24580
  5.6 13.9 %copy-start.2 = (f32[4096]{0:T(1024)S(1)}, f32[4096]{0:T(1024)}, u32[]{:S(2)}) copy-start(f32[4096]{0:T(1024)} %param.9) | copy-start | bytes 49156
  9.6 4.5 %collective-permute-start.3 = (s32[4,128]{1,0:T(4,128)S(1)}, s32[4,128]{1,0:T(4,128)S(1)}, u32[]{:S(2)}, u32[]{:S(2)}) collective-permute-start(s32[4,128]{1,0:T(4,128)S(1)} %pad_add_fusion.2), channel_id=1, source_target_pairs={{0,4},{4,0},{8,12},{12,8},{16,20},{20,16},{24,28},{28,24},{1,5},{5... | collective-permute-start | bytes 6152 | tf_op jit(solution)/shard_map/ppermute | solution.py:26
  12.0 19.6 %collective-permute-start.6 = (bf16[512,512]{1,0:T(8,128)(2,1)}, bf16[512,512]{1,0:T(8,128)(2,1)S(1)}, u32[]{:S(2)}, u32[]{:S(2)}) collective-permute-start(bf16[512,512]{1,0:T(8,128)(2,1)} %get-tuple-element.53), channel_id=1, source_target_pairs={{0,8},{4,12},{8,0},{12,4},{16,24},{20,28},{24,16},{28,20},{1,9},{5... | collective-permute-start | bytes 1572872 | tf_op jit(solution)/shard_map/ppermute | solution.py:26
  14.1 28.1 %collective-permute-start.9 = (bf16[512,512]{1,0:T(8,128)(2,1)}, bf16[512,512]{1,0:T(8,128)(2,1)S(1)}, u32[]{:S(2)}, u32[]{:S(2)}) collective-permute-start(bf16[512,512]{1,0:T(8,128)(2,1)} %get-tuple-element.59), channel_id=1, source_target_pairs={{0,8},{4,12},{8,0},{12,4},{16,24},{20,28},{24,16},{28,20},{1,9},{5... | collective-permute-start | bytes 1572872 | tf_op jit(solution)/shard_map/ppermute | solution.py:26
  14.2 17.3 %collective-permute-start.5 = (s32[8,128]{1,0:T(8,128)S(1)}, s32[8,128]{1,0:T(8,128)S(1)}, u32[]{:S(2)}, u32[]{:S(2)}) collective-permute-start(s32[8,128]{1,0:T(8,128)S(1)} %pad_add_fusion.1), channel_id=1, source_target_pairs={{0,1},{1,2},{2,3},{4,5},{5,6},{6,7},{8,9},{9,10},{10,11},{12,13},{... | collective-permute-start | bytes 12296 | tf_op jit(solution)/shard_map/ppermute | solution.py:21
  15.5 15.9 %collective-permute-start.4 = (s32[8,128]{1,0:T(8,128)S(1)}, s32[8,128]{1,0:T(8,128)S(1)}, u32[]{:S(2)}, u32[]{:S(2)}) collective-permute-start(s32[8,128]{1,0:T(8,128)S(1)} %pad_add_fusion.1), channel_id=1, source_target_pairs={{0,2},{1,3},{4,6},{5,7},{8,10},{9,11},{12,14},{13,15},{16,18},{17,... | collective-permute-start | bytes 12296 | tf_op jit(solution)/shard_map/ppermute | solution.py:21
  19.5 2.2 %copy-start.1 = (bf16[512,4096]{1,0:T(8,128)(2,1)S(1)}, bf16[512,4096]{1,0:T(8,128)(2,1)}, u32[]{:S(2)}) copy-start(bf16[512,4096]{1,0:T(8,128)(2,1)} %rows_ref.1) | copy-start | bytes 12582916
  21.7 9.9 %copy-start.4 = (f32[3,3,512]{2,1,0:T(4,128)S(1)}, f32[3,3,512]{2,1,0:T(4,128)}, u32[]{:S(2)}) copy-start(f32[3,3,512]{2,1,0:T(4,128)} %short_ref.3) | copy-start | bytes 55300
  31.6 13.3 %collective-permute-start.8 = (bf16[512,512]{1,0:T(8,128)(2,1)S(1)}, bf16[512,512]{1,0:T(8,128)(2,1)S(1)}, u32[]{:S(2)}, u32[]{:S(2)}) collective-permute-start(bf16[512,512]{1,0:T(8,128)(2,1)S(1)} %collective-permute-done.6), channel_id=1, source_target_pairs={{0,2},{1,3},{2,0},{3,1},{4,6},{5,7},{6,4},{7,5},{8,10},{9,11},{10,... | collective-permute-start | bytes 1572872 | tf_op jit(solution)/shard_map/ppermute | solution.py:26
  33.8 8.5 %collective-permute-start.7 = (bf16[2,128,512]{2,1,0:T(8,128)(2,1)S(1)}, bf16[2,128,512]{2,1,0:T(8,128)(2,1)S(1)}, u32[]{:S(2)}, u32[]{:S(2)}) collective-permute-start(bf16[2,128,512]{2,1,0:T(8,128)(2,1)S(1)} %shard_map.76), channel_id=1, source_target_pairs={{0,8},{4,12},{8,0},{12,4},{16,24},{20,28},{24,16},{28,20},{1,9},{5... | collective-permute-start | bytes 786440 | tf_op jit(solution)/shard_map/ppermute | solution.py:26
  42.2 8.8 %copy-start = (bf16[512,4096]{1,0:T(8,128)(2,1)S(1)}, bf16[512,4096]{1,0:T(8,128)(2,1)}, u32[]{:S(2)}) copy-start(bf16[512,4096]{1,0:T(8,128)(2,1)} %refs_3_.23) | copy-start | bytes 12582916
  45.0 6.0 %collective-permute-start.11 = (bf16[2,512,512]{2,1,0:T(8,128)(2,1)S(1)}, bf16[2,512,512]{2,1,0:T(8,128)(2,1)S(1)}, u32[]{:S(2)}, u32[]{:S(2)}) collective-permute-start(bf16[2,512,512]{2,1,0:T(8,128)(2,1)S(1)} %pad_maximum_fusion.refs_4_), channel_id=1, source_target_pairs={{0,1},{1,0},{2,3},{3,2},{4,5},{5,4},{6,7},{7,6},{8,9},{9,8},{10,11... | collective-permute-start | bytes 3145736 | tf_op jit(solution)/shard_map/ppermute | solution.py:26
  45.1 3.4 %collective-permute-start.18 = (bf16[512,512]{1,0:T(8,128)(2,1)S(1)}, bf16[512,512]{1,0:T(8,128)(2,1)S(1)}, u32[]{:S(2)}, u32[]{:S(2)}) collective-permute-start(bf16[512,512]{1,0:T(8,128)(2,1)S(1)} %collective-permute-done.9), channel_id=1, source_target_pairs={{0,1},{1,0},{2,3},{3,2},{4,5},{5,4},{6,7},{7,6},{8,9},{9,8},{10,11... | collective-permute-start | bytes 1572872 | tf_op jit(solution)/shard_map/ppermute | solution.py:26
  48.6 26.0 %collective-permute-start.19 = (bf16[2,512,512]{2,1,0:T(8,128)(2,1)S(1)}, bf16[2,512,512]{2,1,0:T(8,128)(2,1)S(1)}, u32[]{:S(2)}, u32[]{:S(2)}) collective-permute-start(bf16[2,512,512]{2,1,0:T(8,128)(2,1)S(1)} %pad_maximum_fusion.1.refs_4_), channel_id=1, source_target_pairs={{0,2},{1,3},{2,0},{3,1},{4,6},{5,7},{6,4},{7,5},{8,10},{9,11},{10,... | collective-permute-start | bytes 3145736 | tf_op jit(solution)/shard_map/ppermute | solution.py:26
  49.1 8.4 %collective-permute-start.10 = (bf16[2,128,512]{2,1,0:T(8,128)(2,1)S(1)}, bf16[2,128,512]{2,1,0:T(8,128)(2,1)S(1)}, u32[]{:S(2)}, u32[]{:S(2)}) collective-permute-start(bf16[2,128,512]{2,1,0:T(8,128)(2,1)S(1)} %get-tuple-element.93), channel_id=1, source_target_pairs={{0,8},{4,12},{8,0},{12,4},{16,24},{20,28},{24,16},{28,20},{1,9},{5... | collective-permute-start | bytes 786440 | tf_op jit(solution)/shard_map/ppermute | solution.py:26
  51.9 9.3 %collective-permute-start.12 = (bf16[2,4,128,128]{3,2,1,0:T(8,128)(2,1)S(1)}, bf16[2,4,128,128]{3,2,1,0:T(8,128)(2,1)S(1)}, u32[]{:S(2)}, u32[]{:S(2)}) collective-permute-start(bf16[2,4,128,128]{3,2,1,0:T(8,128)(2,1)S(1)} %shard_map.79), channel_id=1, source_target_pairs={{0,4},{4,0},{8,12},{12,8},{16,20},{20,16},{24,28},{28,24},{1,5},{5... | collective-permute-start | bytes 786440 | tf_op jit(solution)/shard_map/ppermute | solution.py:26
  56.0 9.3 %collective-permute-start.14 = (bf16[2,4,128,128]{3,2,1,0:T(8,128)(2,1)S(1)}, bf16[2,4,128,128]{3,2,1,0:T(8,128)(2,1)S(1)}, u32[]{:S(2)}, u32[]{:S(2)}) collective-permute-start(bf16[2,4,128,128]{3,2,1,0:T(8,128)(2,1)S(1)} %shard_map.80), channel_id=1, source_target_pairs={{0,4},{4,0},{8,12},{12,8},{16,20},{20,16},{24,28},{28,24},{1,5},{5... | collective-permute-start | bytes 786440 | tf_op jit(solution)/shard_map/ppermute | solution.py:26
  61.2 6.8 %collective-permute-start.13 = (bf16[1,4,128,128]{3,2,1,0:T(8,128)(2,1)S(1)}, bf16[1,4,128,128]{3,2,1,0:T(8,128)(2,1)S(1)}, u32[]{:S(2)}, u32[]{:S(2)}) collective-permute-start(bf16[1,4,128,128]{3,2,1,0:T(8,128)(2,1)S(1)} %get-tuple-element.100), channel_id=1, source_target_pairs={{0,16},{4,20},{8,24},{12,28},{16,0},{20,4},{24,8},{28,12},{1,17},{... | collective-permute-start | bytes 393224 | tf_op jit(solution)/shard_map/ppermute | solution.py:26
  66.1 17.3 %collective-permute-start.16 = (bf16[2,4,128,256]{3,2,1,0:T(8,128)(2,1)S(1)}, bf16[2,4,128,256]{3,2,1,0:T(8,128)(2,1)S(1)}, u32[]{:S(2)}, u32[]{:S(2)}) collective-permute-start(bf16[2,4,128,256]{3,2,1,0:T(8,128)(2,1)S(1)} %shard_map.86), channel_id=1, source_target_pairs={{0,4},{4,0},{8,12},{12,8},{16,20},{20,16},{24,28},{28,24},{1,5},{5... | collective-permute-start | bytes 1572872 | tf_op jit(solution)/shard_map/ppermute | solution.py:26
  66.9 7.8 %collective-permute-start.15 = (bf16[1,4,128,128]{3,2,1,0:T(8,128)(2,1)S(1)}, bf16[1,4,128,128]{3,2,1,0:T(8,128)(2,1)S(1)}, u32[]{:S(2)}, u32[]{:S(2)}) collective-permute-start(bf16[1,4,128,128]{3,2,1,0:T(8,128)(2,1)S(1)} %get-tuple-element.98), channel_id=1, source_target_pairs={{0,16},{4,20},{8,24},{12,28},{16,0},{20,4},{24,8},{28,12},{1,17},{... | collective-permute-start | bytes 393224 | tf_op jit(solution)/shard_map/ppermute | solution.py:26
  75.4 15.8 %collective-permute-start.20 = (bf16[2,4,128,256]{3,2,1,0:T(8,128)(2,1)S(1)}, bf16[2,4,128,256]{3,2,1,0:T(8,128)(2,1)S(1)}, u32[]{:S(2)}, u32[]{:S(2)}) collective-permute-start(bf16[2,4,128,256]{3,2,1,0:T(8,128)(2,1)S(1)} %shard_map.89), channel_id=1, source_target_pairs={{0,4},{4,0},{8,12},{12,8},{16,20},{20,16},{24,28},{28,24},{1,5},{5... | collective-permute-start | bytes 1572872 | tf_op jit(solution)/shard_map/ppermute | solution.py:26
  78.1 18.7 %collective-permute-start.22 = (bf16[2,4,128,128]{3,2,1,0:T(8,128)(2,1)S(1)}, bf16[2,4,128,128]{3,2,1,0:T(8,128)(2,1)S(1)}, u32[]{:S(2)}, u32[]{:S(2)}) collective-permute-start(bf16[2,4,128,128]{3,2,1,0:T(8,128)(2,1)S(1)} %shard_map.92), channel_id=1, source_target_pairs={{0,4},{4,0},{8,12},{12,8},{16,20},{20,16},{24,28},{28,24},{1,5},{5... | collective-permute-start | bytes 786440 | tf_op jit(solution)/shard_map/ppermute | solution.py:26
  79.8 21.3 %collective-permute-start.24 = (bf16[2,4,128,128]{3,2,1,0:T(8,128)(2,1)S(1)}, bf16[2,4,128,128]{3,2,1,0:T(8,128)(2,1)S(1)}, u32[]{:S(2)}, u32[]{:S(2)}) collective-permute-start(bf16[2,4,128,128]{3,2,1,0:T(8,128)(2,1)S(1)} %shard_map.95), channel_id=1, source_target_pairs={{0,4},{4,0},{8,12},{12,8},{16,20},{20,16},{24,28},{28,24},{1,5},{5... | collective-permute-start | bytes 786440 | tf_op jit(solution)/shard_map/ppermute | solution.py:26
  83.5 24.8 %collective-permute-start.17 = (bf16[1,4,128,256]{3,2,1,0:T(8,128)(2,1)S(1)}, bf16[1,4,128,256]{3,2,1,0:T(8,128)(2,1)S(1)}, u32[]{:S(2)}, u32[]{:S(2)}) collective-permute-start(bf16[1,4,128,256]{3,2,1,0:T(8,128)(2,1)S(1)} %get-tuple-element.89), channel_id=1, source_target_pairs={{0,16},{4,20},{8,24},{12,28},{16,0},{20,4},{24,8},{28,12},{1,17},{... | collective-permute-start | bytes 786440 | tf_op jit(solution)/shard_map/ppermute | solution.py:26
  91.3 22.6 %collective-permute-start.21 = (bf16[1,4,128,256]{3,2,1,0:T(8,128)(2,1)S(1)}, bf16[1,4,128,256]{3,2,1,0:T(8,128)(2,1)S(1)}, u32[]{:S(2)}, u32[]{:S(2)}) collective-permute-start(bf16[1,4,128,256]{3,2,1,0:T(8,128)(2,1)S(1)} %get-tuple-element.87), channel_id=1, source_target_pairs={{0,16},{4,20},{8,24},{12,28},{16,0},{20,4},{24,8},{28,12},{1,17},{... | collective-permute-start | bytes 786440 | tf_op jit(solution)/shard_map/ppermute | solution.py:26
  96.9 19.9 %collective-permute-start.23 = (bf16[1,4,128,128]{3,2,1,0:T(8,128)(2,1)S(1)}, bf16[1,4,128,128]{3,2,1,0:T(8,128)(2,1)S(1)}, u32[]{:S(2)}, u32[]{:S(2)}) collective-permute-start(bf16[1,4,128,128]{3,2,1,0:T(8,128)(2,1)S(1)} %get-tuple-element.96), channel_id=1, source_target_pairs={{0,16},{4,20},{8,24},{12,28},{16,0},{20,4},{24,8},{28,12},{1,17},{... | collective-permute-start | bytes 393224 | tf_op jit(solution)/shard_map/ppermute | solution.py:26
  101.2 17.8 %collective-permute-start.25 = (bf16[1,4,128,128]{3,2,1,0:T(8,128)(2,1)S(1)}, bf16[1,4,128,128]{3,2,1,0:T(8,128)(2,1)S(1)}, u32[]{:S(2)}, u32[]{:S(2)}) collective-permute-start(bf16[1,4,128,128]{3,2,1,0:T(8,128)(2,1)S(1)} %get-tuple-element.94), channel_id=1, source_target_pairs={{0,16},{4,20},{8,24},{12,28},{16,0},{20,4},{24,8},{28,12},{1,17},{... | collective-permute-start | bytes 393224 | tf_op jit(solution)/shard_map/ppermute | solution.py:26

commit v8 on v7

--- a/solution.py
+++ b/solution.py
@@ -12,13 +12,13 @@
 SHORT = 3
 LANES = 128
 LEAD = 16
-SPLITS = ((0, 8, (0, 2, 1, 3), ((0, 2), (2, 2), (4, 4))), (8, 8, (0, 1, 2, 3), ((0, 4), (4, 2), (6, 2))))
+SPLITS = ((0, 8, (0, 2, 1, 3), ((0, 4), (4, 4))), (8, 8, (0, 1, 2, 3), ((0, 4), (4, 2), (6, 2))))
 SIXTEENTHS = 16
 
 
 def from_behind(x, axis, by):
     peers = lax.axis_size(axis)
-    return lax.ppermute(x, axis, [(i, i + by) for i in range(peers) if i + by < peers])
+    return lax.ppermute(x, axis, [(i, (i + by) % peers) for i in range(peers)])
 
 
 def swap(x, axis, mask):
@@ -110,7 +110,7 @@
             pltpu.SemaphoreType.DMA((8,)),
             pltpu.SemaphoreType.DMA((count, 4)),
         ],
-        compiler_params=params(40),
+        compiler_params=params(59),
         cost_estimate=cost(3_000_000_000, 0),
     )(embedding, in_proj, norm_gain.reshape(1, width))
 
@@ -246,7 +246,7 @@
             out_ref[w, k] = total[w * tok_len : (w + 1) * tok_len].astype(out_ref.dtype)
 
 
-def panel(place, mine, other, out_proj, beside, split, step):
+def panel(place, mine, other, out_proj, beside, split, step, begin=0):
     count, tok_len, depth = mine.shape
     rows = count * tok_len
     unit = out_proj.shape[1] // SIXTEENTHS
@@ -260,7 +260,7 @@
         start, per = (base * unit + offset) // cols, piece_cols // cols
         return pl.BlockSpec((depth, cols), lambda s, place: (0, start + (place[0] % sharers ^ k) * per))
 
-    near = lambda a: pl.BlockSpec((a.shape[0], depth, cols), lambda s, place: (0, 0, offset // cols))
+    near = lambda a: pl.BlockSpec((a.shape[0], depth, cols), lambda s, place: (0, 0, offset // cols - begin * unit // sharers // cols))
     return pl.pallas_call(
         panel_kernel,
         grid_spec=pltpu.PrefetchScalarGridSpec(
@@ -339,12 +339,12 @@
     beside_bit = bits[-2]
 
     early, late = cut_pieces(at, out_proj)
+    early, late, conv_taps = tie((early, late, conv_taps))
+    toeplitz = build_toeplitz(conv_taps, tok_len)
     ids = level_ids(token_ids, bits[:2])
-    ids, early, late, conv_taps = tie((ids, early, late, conv_taps))
-    toeplitz = build_toeplitz(conv_taps, tok_len)
+    ids, toeplitz = tie((ids, toeplitz))
     for group in [bits[i : i + 2] for i in range(2, len(bits), 2)]:
         ids = level_ids(ids, group)
-    ids, toeplitz = tie((ids, toeplitz))
     early, late = swap(early, "fsdp", beside_bit), swap(late, "fsdp", beside_bit)
     ids, embedding_then = tie((ids, embedding))
     ids = with_lead(ids)
@@ -359,23 +359,21 @@
     gated = mix(ids[: 3 * part], table, short_taps, toeplitz, tok_len)
     gated, other[0], early, early_across, late = tie((gated, other[0], early, early_across, late))
     mine = [gated[2 * part :], gated[:part]]
-    other.append(swap(gated[part : 2 * part], "fsdp", beside_bit))
+    sent = gated[part : 2 * part]
     pair = jnp.stack([early, early_across])
     beside = [(pair, swap(pair, "ctx", 1))]
-    pair = jnp.stack([late, swap(late, "ctx", 1)])
-    beside.append((pair, swap(pair, "ctx", 2)))
 
     out = residual(token_ids, embedding)
     away, arrived, behind = [], [], []
 
-    def send(number, step):
-        part = panel(at, mine[0], other[0], out_proj, beside[number], SPLITS[number], step)
+    def send(shared, number, step, begin=0):
+        part = panel(at, mine[0], other[0], out_proj, shared, SPLITS[number], step, begin)
         part, mine[0] = tie((part, mine[0]))
         away.append(part)
         arrived.append(swap(part, "fsdp", bits[-1]))
 
-    def sum_up(number, step):
-        got, total = arrived[len(behind)], panel(at, mine[1], other[1], out_proj, beside[number], SPLITS[number], step)
+    def sum_up(shared, number, step, begin=0):
+        got, total = arrived[len(behind)], panel(at, mine[1], other[1], out_proj, shared, SPLITS[number], step, begin)
         if behind:
             got, _ = tie((got, behind[-1][-1]))
         for bit in reversed(bits[:-2]):
@@ -384,20 +382,24 @@
             total, got = add(total[:half], got[:half]), swap(far, "fsdp", bit)
         behind.append((total, got, SPLITS[number], step, far))
 
-    first, second, *rest = SPLITS[0][3]
-    send(0, first)
-    send(0, second)
+    first, second = SPLITS[0][3]
+    send(beside[0], 0, first)
+    sent, late, out, _ = tie((sent, late, out, away[0]))
+    other.append(swap(sent, "fsdp", beside_bit))
+    pair = jnp.stack([late, swap(late, "ctx", 1)])
+    middle = pair.shape[2] // 2
+    send(beside[0], 0, second)
     other[1], out, _ = tie((other[1], out, away[1]))
-    mine[0], arrived[0] = tie((mine[0], arrived[0]))
-    for step in rest:
-        send(0, step)
-    for step in SPLITS[0][3]:
-        sum_up(0, step)
-    beside[1], _ = tie((beside[1], (behind[0][1], behind[1][1])))
-    for step in SPLITS[1][3]:
-        send(1, step)
-    for step in SPLITS[1][3]:
-        sum_up(1, step)
+    sum_up(beside[0], 0, first)
+    sum_up(beside[0], 0, second)
+    third, *rest = SPLITS[1][3]
+    for columns, steps, begin in ((pair[:, :, :middle], [third], 0), (pair[:, :, middle:], rest, third[1])):
+        shared = (columns, swap(columns, "ctx", 2))
+        shared, _ = tie((shared, behind[0][-1] if begin == 0 else behind[0][1]))
+        for step in steps:
+            send(shared, 1, step, begin)
+        for step in steps:
+            sum_up(shared, 1, step, begin)
     for last in behind:
         out = place_pieces(at, out, *last[:-1])
     return out[None]

time: 121 us -> 118 us (0.975)
  starting transfers between devices: 30.7 us -> 26.4 us
  Pallas kernels: 44.5 us -> 46.4 us
    pallas_call x1, Pallas kernels: 9.69 us -> 14.8 us  [project(): pl.pallas_call(table_kernel, grid=(1,), in_specs=[hbm, hbm, pl.BlockSpec(...]
    ppermute x2, starting transfers between devices: 5.32 us -> 1.61 us  [from_behind(): return lax.ppermute(x, axis, [(i, (i + by) % peers) for i in range(peers)])]
    pallas_call x6 -> x5, Pallas kernels: 11.7 us -> 9.8 us  [place_pieces(): pl.pallas_call(functools.partial(place_kernel, split, step), grid_spec=pl...]
    pallas_call x12 -> x10, Pallas kernels: 9.08 us -> 7.27 us  [panel(): pl.pallas_call(panel_kernel, grid_spec=pltpu.PrefetchScalarGridSpec(num_s...]
    ppermute x24 -> x23, starting transfers between devices: 25.4 us -> 24.8 us  [swap(): return lax.ppermute(x, axis, [(i, i ^ mask) for i in range(peers)])]
    ppermute x24 -> x23, waiting for transfers between devices: 42 us -> 41.9 us  [swap(): return lax.ppermute(x, axis, [(i, i ^ mask) for i in range(peers)])]
  transfers between devices with their start and end apart: 26 -> 25, of which waited for: 15 -> 13; matrix products, arithmetic and copies ran while one was open for 1% -> 1% of each run, Pallas kernels for 35% -> 37%
where the time goes in v8:
time: 118 us; the launch traced here: 117 us
  Pallas kernels  46.4 us (39%)
  waiting for transfers between devices  41.9 us (36%)
  starting transfers between devices  26.4 us (22%)
  local copies, waits for them, and re-layouts  1.67 us (1%)
    ppermute x23, waiting for transfers between devices, swap(): return lax.ppermute(x, axis, [(i, i ^ mask) for i in range(peers)])  41.9 us
    ppermute x23, starting transfers between devices, swap(): return lax.ppermute(x, axis, [(i, i ^ mask) for i in range(peers)])  24.8 us
    pallas_call x1, Pallas kernels, project(): pl.pallas_call(table_kernel, grid=(1,), in_specs=[hbm, hbm, pl.BlockSpec(...  14.8 us
    pallas_call x5, Pallas kernels, place_pieces(): pl.pallas_call(functools.partial(place_kernel, split, step), grid_spec=pl...  9.8 us
    pallas_call x2, Pallas kernels, mix(): pl.pallas_call(mixer_kernel, grid=(windows // 2,), in_specs=[pl.BlockSpec...  8.96 us
    pallas_call x10, Pallas kernels, panel(): pl.pallas_call(panel_kernel, grid_spec=pltpu.PrefetchScalarGridSpec(num_s...  7.27 us
    pallas_call x1, Pallas kernels, residual(): pl.pallas_call(residual_kernel, grid=(4,), in_specs=[whole(token_ids), pl...  2.66 us
  transfers between devices with their start and end apart: 25, of which 13 were waited for; matrix products, arithmetic and copies ran while one was open for 1% of the time, Pallas kernels for 37%

profile of v8, /device:TPU:0, one launch (start us, length us, event | category | flops | bytes accessed | tf_op | source)
XLA Modules:
  0.0 117.5 jit_solution(17140594809724213309)
XLA Ops:
  0.0 5.0 %collective-permute-start.2 = (s32[1,128]{1,0:T(1,128)}, s32[1,128]{1,0:T(1,128)S(1)}, u32[]{:S(2)}, u32[]{:S(2)}) collective-permute-start(s32[1,128]{1,0:T(1,128)} %ids_ref.1), channel_id=1, source_target_pairs={{0,24},{4,28},{8,16},{12,20},{16,8},{20,12},{24,0},{28,4},{1,25},{... | collective-permute-start | bytes 1544 | tf_op jit(solution)/shard_map/ppermute | solution.py:26
  5.6 2.2 %shard_map.73 = (bf16[512,512]{1,0:T(8,128)(2,1)}, bf16[512,512]{1,0:T(8,128)(2,1)}) custom-call(s32[1]{0:T(128)} %bitcast.place_ref, bf16[512,4096]{1,0:T(8,128)(2,1)} %refs_3_.19, bf16[512,4096]{1,0:T(8,128)(2,1)} %refs_3_.19), custom_call_target="tpu_custom_call" | custom-call | bytes 2000000 | tf_op jit(solution)/shard_map/pallas_call | solution.py:200
  9.6 1.6 %collective-permute-start.3 = (s32[4,128]{1,0:T(4,128)S(1)}, s32[4,128]{1,0:T(4,128)S(1)}, u32[]{:S(2)}, u32[]{:S(2)}) collective-permute-start(s32[4,128]{1,0:T(4,128)S(1)} %pad_add_fusion.2), channel_id=1, source_target_pairs={{0,4},{4,0},{8,12},{12,8},{16,20},{20,16},{24,28},{28,24},{1,5},{5... | collective-permute-start | bytes 6152 | tf_op jit(solution)/shard_map/ppermute | solution.py:26
  11.2 2.0 %collective-permute-start.6 = (bf16[512,512]{1,0:T(8,128)(2,1)}, bf16[512,512]{1,0:T(8,128)(2,1)S(1)}, u32[]{:S(2)}, u32[]{:S(2)}) collective-permute-start(bf16[512,512]{1,0:T(8,128)(2,1)} %get-tuple-element.51), channel_id=1, source_target_pairs={{0,8},{4,12},{8,0},{12,4},{16,24},{20,28},{24,16},{28,20},{1,9},{5... | collective-permute-start | bytes 1572872 | tf_op jit(solution)/shard_map/ppermute | solution.py:26
  13.4 1.6 %collective-permute-start.4 = (s32[8,128]{1,0:T(8,128)S(1)}, s32[8,128]{1,0:T(8,128)S(1)}, u32[]{:S(2)}, u32[]{:S(2)}) collective-permute-start(s32[8,128]{1,0:T(8,128)S(1)} %pad_add_fusion.1), channel_id=1, source_target_pairs={{0,2},{1,3},{2,0},{3,1},{4,6},{5,7},{6,4},{7,5},{8,10},{9,11},{10,... | collective-permute-start | bytes 12296 | tf_op jit(solution)/shard_map/ppermute | solution.py:21
  14.9 14.8 %shard_map.75.table_ref = bf16[3,512,512]{2,1,0:T(8,128)(2,1)} custom-call(bf16[512,4096]{1,0:T(8,128)(2,1)} %rows_ref.1, bf16[3,4096,512]{2,1,0:T(8,128)(2,1)} %weight_hbm.1, f32[1,4096]{1,0:T(1,128)} %bitcast.43), custom_call_target="tpu_custom_call" | custom-call | flops 3000000000 | tf_op jit(solution)/shard_map/pallas_call | solution.py:101
  30.5 1.4 %copy-done.2 = bf16[3,512,512]{2,1,0:T(8,128)(2,1)S(1)} copy-done((bf16[3,512,512]{2,1,0:T(8,128)(2,1)S(1)}, bf16[3,512,512]{2,1,0:T(8,128)(2,1)}, u32[]{:S(2)}) %copy-start.2) | copy-done | bytes 1572888
  31.9 2.2 %shard_map.76 = bf16[2,128,512]{2,1,0:T(8,128)(2,1)S(1)} custom-call(s32[2,1,272]{2,1,0:T(1,128)S(1)} %copy.13.ids_ref, bf16[3,512,512]{2,1,0:T(8,128)(2,1)S(1)} %copy-done.2, f32[3,3,512]{2,1,0:T(4,128)S(1)} %copy-done.4, bf16[4,1024,256]{2,1,0:T(8,128)(2,1)S(1)} %shard_map.74.toeplitz), custom_call_target="tpu_custom_call" | custom-call | flops 1500000000 | tf_op jit(solution)/shard_map/pallas_call | solution.py:167
  34.1 2.1 %collective-permute-start.7 = (bf16[2,128,512]{2,1,0:T(8,128)(2,1)S(1)}, bf16[2,128,512]{2,1,0:T(8,128)(2,1)S(1)}, u32[]{:S(2)}, u32[]{:S(2)}) collective-permute-start(bf16[2,128,512]{2,1,0:T(8,128)(2,1)S(1)} %shard_map.76), channel_id=1, source_target_pairs={{0,8},{4,12},{8,0},{12,4},{16,24},{20,28},{24,16},{28,20},{1,9},{5... | collective-permute-start | bytes 786440 | tf_op jit(solution)/shard_map/ppermute | solution.py:26
  36.2 6.8 %shard_map.77 = bf16[6,128,512]{2,1,0:T(8,128)(2,1)S(1)} custom-call(s32[6,1,272]{2,1,0:T(1,128)S(1)} %reshape.51.ids_ref, bf16[3,512,512]{2,1,0:T(8,128)(2,1)S(1)} %copy-done.2, f32[3,3,512]{2,1,0:T(4,128)S(1)} %copy-done.4, bf16[4,1024,256]{2,1,0:T(8,128)(2,1)S(1)} %shard_map.74.toeplitz), custom_call_target="tpu_custom_call" | custom-call | flops 1500000000 | tf_op jit(solution)/shard_map/pallas_call | solution.py:167
  43.1 1.0 collective-permute-done.8
  44.3 2.7 %shard_map.78.so_far_ref = bf16[128,4096]{1,0:T(8,128)(2,1)} custom-call(s32[1,128]{1,0:T(1,128)S(1)} %copy-done.3, bf16[512,4096]{1,0:T(8,128)(2,1)S(1)} %copy-done.1), custom_call_target="tpu_custom_call" | custom-call | flops 400000000 | tf_op jit(solution)/shard_map/pallas_call | solution.py:290
  48.3 1.5 %collective-permute-start.12 = (bf16[2,4,128,256]{3,2,1,0:T(8,128)(2,1)S(1)}, bf16[2,4,128,256]{3,2,1,0:T(8,128)(2,1)S(1)}, u32[]{:S(2)}, u32[]{:S(2)}) collective-permute-start(bf16[2,4,128,256]{3,2,1,0:T(8,128)(2,1)S(1)} %shard_map.79), channel_id=1, source_target_pairs={{0,4},{4,0},{8,12},{12,8},{16,20},{20,16},{24,28},{28,24},{1,5},{5... | collective-permute-start | bytes 1572872 | tf_op jit(solution)/shard_map/ppermute | solution.py:26
  49.7 2.0 %collective-permute-start.11 = (bf16[2,128,512]{2,1,0:T(8,128)(2,1)S(1)}, bf16[2,128,512]{2,1,0:T(8,128)(2,1)S(1)}, u32[]{:S(2)}, u32[]{:S(2)}) collective-permute-start(bf16[2,128,512]{2,1,0:T(8,128)(2,1)S(1)} %get-tuple-element.64), channel_id=1, source_target_pairs={{0,8},{4,12},{8,0},{12,4},{16,24},{20,28},{24,16},{28,20},{1,9},{5... | collective-permute-start | bytes 786440 | tf_op jit(solution)/shard_map/ppermute | solution.py:26
  51.8 1.0 collective-permute-start.17
  54.2 3.9 %collective-permute-done.11 = bf16[2,128,512]{2,1,0:T(8,128)(2,1)S(1)} collective-permute-done((bf16[2,128,512]{2,1,0:T(8,128)(2,1)S(1)}, bf16[2,128,512]{2,1,0:T(8,128)(2,1)S(1)}, u32[]{:S(2)}, u32[]{:S(2)}) %collective-permute-start.11) | collective-permute-done | bytes 262176 | tf_op jit(solution)/shard_map/ppermute | solution.py:26
  58.8 1.0 collective-permute-start.20
  59.8 3.3 %collective-permute-done.12 = bf16[2,4,128,256]{3,2,1,0:T(8,128)(2,1)S(1)} collective-permute-done((bf16[2,4,128,256]{3,2,1,0:T(8,128)(2,1)S(1)}, bf16[2,4,128,256]{3,2,1,0:T(8,128)(2,1)S(1)}, u32[]{:S(2)}, u32[]{:S(2)}) %collective-permute-start.12) | collective-permute-done | bytes 524320 | tf_op jit(solution)/shard_map/ppermute | solution.py:26
  63.2 3.6 %collective-permute-done.17.refs_5_ = bf16[2,512,256]{2,1,0:T(8,128)(2,1)S(1)} collective-permute-done((bf16[2,512,256]{2,1,0:T(8,128)(2,1)S(1)}, bf16[2,512,256]{2,1,0:T(8,128)(2,1)S(1)}, u32[]{:S(2)}, u32[]{:S(2)}) %collective-permute-start.17) | collective-permute-done | bytes 524320 | tf_op jit(solution)/shard_map/ppermute | solution.py:26
  68.1 1.4 %collective-permute-start.13 = (bf16[1,4,128,256]{3,2,1,0:T(8,128)(2,1)S(1)}, bf16[1,4,128,256]{3,2,1,0:T(8,128)(2,1)S(1)}, u32[]{:S(2)}, u32[]{:S(2)}) collective-permute-start(bf16[1,4,128,256]{3,2,1,0:T(8,128)(2,1)S(1)} %get-tuple-element.91), channel_id=1, source_target_pairs={{0,16},{4,20},{8,24},{12,28},{16,0},{20,4},{24,8},{28,12},{1,17},{... | collective-permute-start | bytes 786440 | tf_op jit(solution)/shard_map/ppermute | solution.py:26
  70.2 4.1 %collective-permute-done.14 = bf16[2,4,128,256]{3,2,1,0:T(8,128)(2,1)S(1)} collective-permute-done((bf16[2,4,128,256]{3,2,1,0:T(8,128)(2,1)S(1)}, bf16[2,4,128,256]{3,2,1,0:T(8,128)(2,1)S(1)}, u32[]{:S(2)}, u32[]{:S(2)}) %collective-permute-start.14) | collective-permute-done | bytes 524320 | tf_op jit(solution)/shard_map/ppermute | solution.py:26
  74.4 1.5 %collective-permute-start.15 = (bf16[1,4,128,256]{3,2,1,0:T(8,128)(2,1)S(1)}, bf16[1,4,128,256]{3,2,1,0:T(8,128)(2,1)S(1)}, u32[]{:S(2)}, u32[]{:S(2)}) collective-permute-start(bf16[1,4,128,256]{3,2,1,0:T(8,128)(2,1)S(1)} %get-tuple-element.89), channel_id=1, source_target_pairs={{0,16},{4,20},{8,24},{12,28},{16,0},{20,4},{24,8},{28,12},{1,17},{... | collective-permute-start | bytes 786440 | tf_op jit(solution)/shard_map/ppermute | solution.py:26
  75.9 11.7 %collective-permute-done.13.far_ref = bf16[1,4,128,256]{3,2,1,0:T(8,128)(2,1)S(1)} collective-permute-done((bf16[1,4,128,256]{3,2,1,0:T(8,128)(2,1)S(1)}, bf16[1,4,128,256]{3,2,1,0:T(8,128)(2,1)S(1)}, u32[]{:S(2)}, u32[]{:S(2)}) %collective-permute-start.13) | collective-permute-done | bytes 262176 | tf_op jit(solution)/shard_map/ppermute | solution.py:26
  92.0 1.6 %collective-permute-start.23 = (bf16[2,4,128,128]{3,2,1,0:T(8,128)(2,1)S(1)}, bf16[2,4,128,128]{3,2,1,0:T(8,128)(2,1)S(1)}, u32[]{:S(2)}, u32[]{:S(2)}) collective-permute-start(bf16[2,4,128,128]{3,2,1,0:T(8,128)(2,1)S(1)} %shard_map.92), channel_id=1, source_target_pairs={{0,4},{4,0},{8,12},{12,8},{16,20},{20,16},{24,28},{28,24},{1,5},{5... | collective-permute-start | bytes 786440 | tf_op jit(solution)/shard_map/ppermute | solution.py:26
  93.8 3.4 %collective-permute-done.21 = bf16[2,4,128,128]{3,2,1,0:T(8,128)(2,1)S(1)} collective-permute-done((bf16[2,4,128,128]{3,2,1,0:T(8,128)(2,1)S(1)}, bf16[2,4,128,128]{3,2,1,0:T(8,128)(2,1)S(1)}, u32[]{:S(2)}, u32[]{:S(2)}) %collective-permute-start.21) | collective-permute-done | bytes 262176 | tf_op jit(solution)/shard_map/ppermute | solution.py:26
  97.4 2.7 %collective-permute-done.23 = bf16[2,4,128,128]{3,2,1,0:T(8,128)(2,1)S(1)} collective-permute-done((bf16[2,4,128,128]{3,2,1,0:T(8,128)(2,1)S(1)}, bf16[2,4,128,128]{3,2,1,0:T(8,128)(2,1)S(1)}, u32[]{:S(2)}, u32[]{:S(2)}) %collective-permute-start.23) | collective-permute-done | bytes 262176 | tf_op jit(solution)/shard_map/ppermute | solution.py:26
  100.4 2.0 %shard_map.82.so_far_ref = bf16[128,4096]{1,0:T(8,128)(2,1)} custom-call(s32[1]{0:T(128)} %bitcast.place_ref, bf16[128,4096]{1,0:T(8,128)(2,1)} %shard_map.78.so_far_ref, bf16[1,4,128,256]{3,2,1,0:T(8,128)(2,1)S(1)} %get-tuple-element.92.near_ref, bf16[1,4,128,256]{3,2,1,0:T(8,128)(2,1)S(1)} %collective-permute-done.13.far_ref), custom_call_target="tpu_custom_call", output_to_operand_aliasing={{}: (1, {})} | custom-call | bytes 1000000 | tf_op jit(solution)/shard_map/pallas_call | solution.py:318
  102.4 2.0 %shard_map.84.so_far_ref = bf16[128,4096]{1,0:T(8,128)(2,1)} custom-call(s32[1]{0:T(128)} %bitcast.place_ref, bf16[128,4096]{1,0:T(8,128)(2,1)} %shard_map.82.so_far_ref, bf16[1,4,128,256]{3,2,1,0:T(8,128)(2,1)S(1)} %get-tuple-element.90.near_ref, bf16[1,4,128,256]{3,2,1,0:T(8,128)(2,1)S(1)} %collective-permute-done.15.far_ref), custom_call_target="tpu_custom_call", output_to_operand_aliasing={{}: (1, {})} | custom-call | bytes 1000000 | tf_op jit(solution)/shard_map/pallas_call | solution.py:318
  104.4 6.4 %collective-permute-done.19.far_ref = bf16[1,4,128,256]{3,2,1,0:T(8,128)(2,1)S(1)} collective-permute-done((bf16[1,4,128,256]{3,2,1,0:T(8,128)(2,1)S(1)}, bf16[1,4,128,256]{3,2,1,0:T(8,128)(2,1)S(1)}, u32[]{:S(2)}, u32[]{:S(2)}) %collective-permute-start.19) | collective-permute-done | bytes 262176 | tf_op jit(solution)/shard_map/ppermute | solution.py:26
  110.8 2.0 %shard_map.87.so_far_ref = bf16[128,4096]{1,0:T(8,128)(2,1)} custom-call(s32[1]{0:T(128)} %bitcast.place_ref, bf16[128,4096]{1,0:T(8,128)(2,1)} %shard_map.84.so_far_ref, bf16[1,4,128,256]{3,2,1,0:T(8,128)(2,1)S(1)} %get-tuple-element.88.near_ref, bf16[1,4,128,256]{3,2,1,0:T(8,128)(2,1)S(1)} %collective-permute-done.19.far_ref), custom_call_target="tpu_custom_call", output_to_operand_aliasing={{}: (1, {})} | custom-call | bytes 1000000 | tf_op jit(solution)/shard_map/pallas_call | solution.py:318
  113.6 1.9 %shard_map.90.so_far_ref = bf16[128,4096]{1,0:T(8,128)(2,1)} custom-call(s32[1]{0:T(128)} %bitcast.place_ref, bf16[128,4096]{1,0:T(8,128)(2,1)} %shard_map.87.so_far_ref, bf16[1,4,128,128]{3,2,1,0:T(8,128)(2,1)S(1)} %get-tuple-element.99.near_ref, bf16[1,4,128,128]{3,2,1,0:T(8,128)(2,1)S(1)} %collective-permute-done.22.far_ref), custom_call_target="tpu_custom_call", output_to_operand_aliasing={{}: (1, {})} | custom-call | bytes 1000000 | tf_op jit(solution)/shard_map/pallas_call | solution.py:318
  115.5 1.9 %shard_map.93 = bf16[128,4096]{1,0:T(8,128)(2,1)} custom-call(s32[1]{0:T(128)} %bitcast.place_ref, bf16[128,4096]{1,0:T(8,128)(2,1)} %shard_map.90.so_far_ref, bf16[1,4,128,128]{3,2,1,0:T(8,128)(2,1)S(1)} %get-tuple-element.97.near_ref, bf16[1,4,128,128]{3,2,1,0:T(8,128)(2,1)S(1)} %collective-permute-done.24.far_ref), custom_call_target="tpu_custom_call", output_to_operand_aliasing={{}: (1, {})} | custom-call | bytes 1000000 | tf_op jit(solution)/shard_map/pallas_call | solution.py:318
  (70 shorter events, 15.1 us)
Async XLA Ops:
  0.0 8.7 %collective-permute-start.2 = (s32[1,128]{1,0:T(1,128)}, s32[1,128]{1,0:T(1,128)S(1)}, u32[]{:S(2)}, u32[]{:S(2)}) collective-permute-start(s32[1,128]{1,0:T(1,128)} %ids_ref.1), channel_id=1, source_target_pairs={{0,24},{4,28},{8,16},{12,20},{16,8},{20,12},{24,0},{28,4},{1,25},{... | collective-permute-start | bytes 1544 | tf_op jit(solution)/shard_map/ppermute | solution.py:26
  5.0 3.7 %collective-permute-start.1 = (s32[1,128]{1,0:T(1,128)}, s32[1,128]{1,0:T(1,128)S(1)}, u32[]{:S(2)}, u32[]{:S(2)}) collective-permute-start(s32[1,128]{1,0:T(1,128)} %ids_ref.1), channel_id=1, source_target_pairs={{0,8},{4,12},{8,0},{12,4},{16,24},{20,28},{24,16},{28,20},{1,9},{5... | collective-permute-start | bytes 1544 | tf_op jit(solution)/shard_map/ppermute | solution.py:26
  5.1 4.6 %collective-permute-start = (s32[1,128]{1,0:T(1,128)}, s32[1,128]{1,0:T(1,128)S(1)}, u32[]{:S(2)}, u32[]{:S(2)}) collective-permute-start(s32[1,128]{1,0:T(1,128)} %ids_ref.1), channel_id=1, source_target_pairs={{0,16},{4,20},{8,24},{12,28},{16,0},{20,4},{24,8},{28,12},{1,17},{... | collective-permute-start | bytes 1544 | tf_op jit(solution)/shard_map/ppermute | solution.py:26
  5.6 2.2 %copy-start.5 = (bf16[32,128]{1,0:T(8,128)(2,1)S(1)}, bf16[32,128]{1,0:T(8,128)(2,1)}, u32[]{:S(2)}) copy-start(bf16[32,128]{1,0:T(8,128)(2,1)} %param.12) | copy-start | bytes 24580
  5.6 4.0 %copy-start.3 = (s32[1,128]{1,0:T(1,128)S(1)}, s32[1,128]{1,0:T(1,128)}, u32[]{:S(2)}) copy-start(s32[1,128]{1,0:T(1,128)} %ids_ref.1) | copy-start | bytes 1540
  9.6 3.7 %collective-permute-start.3 = (s32[4,128]{1,0:T(4,128)S(1)}, s32[4,128]{1,0:T(4,128)S(1)}, u32[]{:S(2)}, u32[]{:S(2)}) collective-permute-start(s32[4,128]{1,0:T(4,128)S(1)} %pad_add_fusion.2), channel_id=1, source_target_pairs={{0,4},{4,0},{8,12},{12,8},{16,20},{20,16},{24,28},{28,24},{1,5},{5... | collective-permute-start | bytes 6152 | tf_op jit(solution)/shard_map/ppermute | solution.py:26
  11.2 18.7 %collective-permute-start.6 = (bf16[512,512]{1,0:T(8,128)(2,1)}, bf16[512,512]{1,0:T(8,128)(2,1)S(1)}, u32[]{:S(2)}, u32[]{:S(2)}) collective-permute-start(bf16[512,512]{1,0:T(8,128)(2,1)} %get-tuple-element.51), channel_id=1, source_target_pairs={{0,8},{4,12},{8,0},{12,4},{16,24},{20,28},{24,16},{28,20},{1,9},{5... | collective-permute-start | bytes 1572872 | tf_op jit(solution)/shard_map/ppermute | solution.py:26
  13.2 29.7 %collective-permute-start.9 = (bf16[512,512]{1,0:T(8,128)(2,1)}, bf16[512,512]{1,0:T(8,128)(2,1)S(1)}, u32[]{:S(2)}, u32[]{:S(2)}) collective-permute-start(bf16[512,512]{1,0:T(8,128)(2,1)} %get-tuple-element.57), channel_id=1, source_target_pairs={{0,8},{4,12},{8,0},{12,4},{16,24},{20,28},{24,16},{28,20},{1,9},{5... | collective-permute-start | bytes 1572872 | tf_op jit(solution)/shard_map/ppermute | solution.py:26
  13.3 16.5 %collective-permute-start.5 = (s32[8,128]{1,0:T(8,128)S(1)}, s32[8,128]{1,0:T(8,128)S(1)}, u32[]{:S(2)}, u32[]{:S(2)}) collective-permute-start(s32[8,128]{1,0:T(8,128)S(1)} %pad_add_fusion.1), channel_id=1, source_target_pairs={{0,1},{1,2},{2,3},{3,0},{4,5},{5,6},{6,7},{7,4},{8,9},{9,10},{10,1... | collective-permute-start | bytes 12296 | tf_op jit(solution)/shard_map/ppermute | solution.py:21
  13.4 16.4 %collective-permute-start.4 = (s32[8,128]{1,0:T(8,128)S(1)}, s32[8,128]{1,0:T(8,128)S(1)}, u32[]{:S(2)}, u32[]{:S(2)}) collective-permute-start(s32[8,128]{1,0:T(8,128)S(1)} %pad_add_fusion.1), channel_id=1, source_target_pairs={{0,2},{1,3},{2,0},{3,1},{4,6},{5,7},{6,4},{7,5},{8,10},{9,11},{10,... | collective-permute-start | bytes 12296 | tf_op jit(solution)/shard_map/ppermute | solution.py:21
  14.9 15.6 %copy-start.4 = (f32[3,3,512]{2,1,0:T(4,128)S(1)}, f32[3,3,512]{2,1,0:T(4,128)}, u32[]{:S(2)}) copy-start(f32[3,3,512]{2,1,0:T(4,128)} %short_ref.3) | copy-start | bytes 55300
  29.9 14.1 %collective-permute-start.8 = (bf16[512,512]{1,0:T(8,128)(2,1)S(1)}, bf16[512,512]{1,0:T(8,128)(2,1)S(1)}, u32[]{:S(2)}, u32[]{:S(2)}) collective-permute-start(bf16[512,512]{1,0:T(8,128)(2,1)S(1)} %collective-permute-done.6), channel_id=1, source_target_pairs={{0,2},{1,3},{2,0},{3,1},{4,6},{5,7},{6,4},{7,5},{8,10},{9,11},{10,... | collective-permute-start | bytes 1572872 | tf_op jit(solution)/shard_map/ppermute | solution.py:26
  30.5 1.4 %copy-start.2 = (bf16[3,512,512]{2,1,0:T(8,128)(2,1)S(1)}, bf16[3,512,512]{2,1,0:T(8,128)(2,1)}, u32[]{:S(2)}) copy-start(bf16[3,512,512]{2,1,0:T(8,128)(2,1)} %shard_map.75.table_ref) | copy-start | bytes 4718596
  34.1 10.2 %copy-start.1 = (bf16[512,4096]{1,0:T(8,128)(2,1)S(1)}, bf16[512,4096]{1,0:T(8,128)(2,1)}, u32[]{:S(2)}) copy-start(bf16[512,4096]{1,0:T(8,128)(2,1)} %rows_ref.1) | copy-start | bytes 12582916
  34.1 9.0 %collective-permute-start.7 = (bf16[2,128,512]{2,1,0:T(8,128)(2,1)S(1)}, bf16[2,128,512]{2,1,0:T(8,128)(2,1)S(1)}, u32[]{:S(2)}, u32[]{:S(2)}) collective-permute-start(bf16[2,128,512]{2,1,0:T(8,128)(2,1)S(1)} %shard_map.76), channel_id=1, source_target_pairs={{0,8},{4,12},{8,0},{12,4},{16,24},{20,28},{24,16},{28,20},{1,9},{5... | collective-permute-start | bytes 786440 | tf_op jit(solution)/shard_map/ppermute | solution.py:26
  44.1 2.9 %copy-start = (bf16[512,4096]{1,0:T(8,128)(2,1)S(1)}, bf16[512,4096]{1,0:T(8,128)(2,1)}, u32[]{:S(2)}) copy-start(bf16[512,4096]{1,0:T(8,128)(2,1)} %refs_3_.19) | copy-start | bytes 12582916
  44.2 2.8 %collective-permute-start.10 = (bf16[2,512,512]{2,1,0:T(8,128)(2,1)S(1)}, bf16[2,512,512]{2,1,0:T(8,128)(2,1)S(1)}, u32[]{:S(2)}, u32[]{:S(2)}) collective-permute-start(bf16[2,512,512]{2,1,0:T(8,128)(2,1)S(1)} %pad_maximum_fusion.refs_4_), channel_id=1, source_target_pairs={{0,1},{1,0},{2,3},{3,2},{4,5},{5,4},{6,7},{7,6},{8,9},{9,8},{10,11... | collective-permute-start | bytes 3145736 | tf_op jit(solution)/shard_map/ppermute | solution.py:26
  47.7 4.0 %collective-permute-start.16 = (bf16[512,512]{1,0:T(8,128)(2,1)S(1)}, bf16[512,512]{1,0:T(8,128)(2,1)S(1)}, u32[]{:S(2)}, u32[]{:S(2)}) collective-permute-start(bf16[512,512]{1,0:T(8,128)(2,1)S(1)} %collective-permute-done.9), channel_id=1, source_target_pairs={{0,1},{1,0},{2,3},{3,2},{4,5},{5,4},{6,7},{7,6},{8,9},{9,8},{10,11... | collective-permute-start | bytes 1572872 | tf_op jit(solution)/shard_map/ppermute | solution.py:26
  48.3 14.8 %collective-permute-start.12 = (bf16[2,4,128,256]{3,2,1,0:T(8,128)(2,1)S(1)}, bf16[2,4,128,256]{3,2,1,0:T(8,128)(2,1)S(1)}, u32[]{:S(2)}, u32[]{:S(2)}) collective-permute-start(bf16[2,4,128,256]{3,2,1,0:T(8,128)(2,1)S(1)} %shard_map.79), channel_id=1, source_target_pairs={{0,4},{4,0},{8,12},{12,8},{16,20},{20,16},{24,28},{28,24},{1,5},{5... | collective-permute-start | bytes 1572872 | tf_op jit(solution)/shard_map/ppermute | solution.py:26
  49.7 8.3 %collective-permute-start.11 = (bf16[2,128,512]{2,1,0:T(8,128)(2,1)S(1)}, bf16[2,128,512]{2,1,0:T(8,128)(2,1)S(1)}, u32[]{:S(2)}, u32[]{:S(2)}) collective-permute-start(bf16[2,128,512]{2,1,0:T(8,128)(2,1)S(1)} %get-tuple-element.64), channel_id=1, source_target_pairs={{0,8},{4,12},{8,0},{12,4},{16,24},{20,28},{24,16},{28,20},{1,9},{5... | collective-permute-start | bytes 786440 | tf_op jit(solution)/shard_map/ppermute | solution.py:26
  51.8 14.9 %collective-permute-start.17 = (bf16[2,512,256]{2,1,0:T(8,128)(2,1)S(1)}, bf16[2,512,256]{2,1,0:T(8,128)(2,1)S(1)}, u32[]{:S(2)}, u32[]{:S(2)}) collective-permute-start(bf16[2,512,256]{2,1,0:T(8,128)(2,1)S(1)} %get-tuple-element.72.refs_4_), channel_id=1, source_target_pairs={{0,2},{1,3},{2,0},{3,1},{4,6},{5,7},{6,4},{7,5},{8,10},{9,11},{10,... | collective-permute-start | bytes 1572872 | tf_op jit(solution)/shard_map/ppermute | solution.py:26
  53.5 20.7 %collective-permute-start.14 = (bf16[2,4,128,256]{3,2,1,0:T(8,128)(2,1)S(1)}, bf16[2,4,128,256]{3,2,1,0:T(8,128)(2,1)S(1)}, u32[]{:S(2)}, u32[]{:S(2)}) collective-permute-start(bf16[2,4,128,256]{3,2,1,0:T(8,128)(2,1)S(1)} %shard_map.80), channel_id=1, source_target_pairs={{0,4},{4,0},{8,12},{12,8},{16,20},{20,16},{24,28},{28,24},{1,5},{5... | collective-permute-start | bytes 1572872 | tf_op jit(solution)/shard_map/ppermute | solution.py:26
  58.8 28.9 %collective-permute-start.20 = (bf16[2,512,256]{2,1,0:T(8,128)(2,1)S(1)}, bf16[2,512,256]{2,1,0:T(8,128)(2,1)S(1)}, u32[]{:S(2)}, u32[]{:S(2)}) collective-permute-start(bf16[2,512,256]{2,1,0:T(8,128)(2,1)S(1)} %get-tuple-element.77.refs_4_), channel_id=1, source_target_pairs={{0,2},{1,3},{2,0},{3,1},{4,6},{5,7},{6,4},{7,5},{8,10},{9,11},{10,... | collective-permute-start | bytes 1572872 | tf_op jit(solution)/shard_map/ppermute | solution.py:26
  67.5 26.1 %collective-permute-start.18 = (bf16[2,4,128,256]{3,2,1,0:T(8,128)(2,1)S(1)}, bf16[2,4,128,256]{3,2,1,0:T(8,128)(2,1)S(1)}, u32[]{:S(2)}, u32[]{:S(2)}) collective-permute-start(bf16[2,4,128,256]{3,2,1,0:T(8,128)(2,1)S(1)} %shard_map.86), channel_id=1, source_target_pairs={{0,4},{4,0},{8,12},{12,8},{16,20},{20,16},{24,28},{28,24},{1,5},{5... | collective-permute-start | bytes 1572872 | tf_op jit(solution)/shard_map/ppermute | solution.py:26
  68.1 19.6 %collective-permute-start.13 = (bf16[1,4,128,256]{3,2,1,0:T(8,128)(2,1)S(1)}, bf16[1,4,128,256]{3,2,1,0:T(8,128)(2,1)S(1)}, u32[]{:S(2)}, u32[]{:S(2)}) collective-permute-start(bf16[1,4,128,256]{3,2,1,0:T(8,128)(2,1)S(1)} %get-tuple-element.91), channel_id=1, source_target_pairs={{0,16},{4,20},{8,24},{12,28},{16,0},{20,4},{24,8},{28,12},{1,17},{... | collective-permute-start | bytes 786440 | tf_op jit(solution)/shard_map/ppermute | solution.py:26
  74.4 28.0 %collective-permute-start.15 = (bf16[1,4,128,256]{3,2,1,0:T(8,128)(2,1)S(1)}, bf16[1,4,128,256]{3,2,1,0:T(8,128)(2,1)S(1)}, u32[]{:S(2)}, u32[]{:S(2)}) collective-permute-start(bf16[1,4,128,256]{3,2,1,0:T(8,128)(2,1)S(1)} %get-tuple-element.89), channel_id=1, source_target_pairs={{0,16},{4,20},{8,24},{12,28},{16,0},{20,4},{24,8},{28,12},{1,17},{... | collective-permute-start | bytes 786440 | tf_op jit(solution)/shard_map/ppermute | solution.py:26
  88.4 8.8 %collective-permute-start.21 = (bf16[2,4,128,128]{3,2,1,0:T(8,128)(2,1)S(1)}, bf16[2,4,128,128]{3,2,1,0:T(8,128)(2,1)S(1)}, u32[]{:S(2)}, u32[]{:S(2)}) collective-permute-start(bf16[2,4,128,128]{3,2,1,0:T(8,128)(2,1)S(1)} %shard_map.89), channel_id=1, source_target_pairs={{0,4},{4,0},{8,12},{12,8},{16,20},{20,16},{24,28},{28,24},{1,5},{5... | collective-permute-start | bytes 786440 | tf_op jit(solution)/shard_map/ppermute | solution.py:26
  92.0 8.0 %collective-permute-start.23 = (bf16[2,4,128,128]{3,2,1,0:T(8,128)(2,1)S(1)}, bf16[2,4,128,128]{3,2,1,0:T(8,128)(2,1)S(1)}, u32[]{:S(2)}, u32[]{:S(2)}) collective-permute-start(bf16[2,4,128,128]{3,2,1,0:T(8,128)(2,1)S(1)} %shard_map.92), channel_id=1, source_target_pairs={{0,4},{4,0},{8,12},{12,8},{16,20},{20,16},{24,28},{28,24},{1,5},{5... | collective-permute-start | bytes 786440 | tf_op jit(solution)/shard_map/ppermute | solution.py:26
  93.7 17.1 %collective-permute-start.19 = (bf16[1,4,128,256]{3,2,1,0:T(8,128)(2,1)S(1)}, bf16[1,4,128,256]{3,2,1,0:T(8,128)(2,1)S(1)}, u32[]{:S(2)}, u32[]{:S(2)}) collective-permute-start(bf16[1,4,128,256]{3,2,1,0:T(8,128)(2,1)S(1)} %get-tuple-element.87), channel_id=1, source_target_pairs={{0,16},{4,20},{8,24},{12,28},{16,0},{20,4},{24,8},{28,12},{1,17},{... | collective-permute-start | bytes 786440 | tf_op jit(solution)/shard_map/ppermute | solution.py:26
  97.3 16.3 %collective-permute-start.22 = (bf16[1,4,128,128]{3,2,1,0:T(8,128)(2,1)S(1)}, bf16[1,4,128,128]{3,2,1,0:T(8,128)(2,1)S(1)}, u32[]{:S(2)}, u32[]{:S(2)}) collective-permute-start(bf16[1,4,128,128]{3,2,1,0:T(8,128)(2,1)S(1)} %get-tuple-element.98), channel_id=1, source_target_pairs={{0,16},{4,20},{8,24},{12,28},{16,0},{20,4},{24,8},{28,12},{1,17},{... | collective-permute-start | bytes 393224 | tf_op jit(solution)/shard_map/ppermute | solution.py:26
  100.1 15.4 %collective-permute-start.24 = (bf16[1,4,128,128]{3,2,1,0:T(8,128)(2,1)S(1)}, bf16[1,4,128,128]{3,2,1,0:T(8,128)(2,1)S(1)}, u32[]{:S(2)}, u32[]{:S(2)}) collective-permute-start(bf16[1,4,128,128]{3,2,1,0:T(8,128)(2,1)S(1)} %get-tuple-element.96), channel_id=1, source_target_pairs={{0,16},{4,20},{8,24},{12,28},{16,0},{20,4},{24,8},{28,12},{1,17},{... | collective-permute-start | bytes 393224 | tf_op jit(solution)/shard_map/ppermute | solution.py:26

commit v9 on v8

--- a/solution.py
+++ b/solution.py
@@ -12,7 +12,7 @@
 SHORT = 3
 LANES = 128
 LEAD = 16
-SPLITS = ((0, 8, (0, 2, 1, 3), ((0, 4), (4, 4))), (8, 8, (0, 1, 2, 3), ((0, 4), (4, 2), (6, 2))))
+SPLITS = ((0, 8, (0, 2, 1, 3), ((0, 4), (4, 4))), (8, 8, (0, 1, 2, 3), ((0, 4), (4, 4))))
 SIXTEENTHS = 16
 
 
@@ -110,7 +110,7 @@
             pltpu.SemaphoreType.DMA((8,)),
             pltpu.SemaphoreType.DMA((count, 4)),
         ],
-        compiler_params=params(59),
+        compiler_params=params(40),
         cost_estimate=cost(3_000_000_000, 0),
     )(embedding, in_proj, norm_gain.reshape(1, width))
 
@@ -350,56 +350,48 @@
     ids = with_lead(ids)
     table = project(embedding_then, norm_gain, in_proj)
     table, early = tie((table, early))
-    early_across = swap(early, "ctx", 2)
+    early_pair = jnp.stack([early, swap(early, "ctx", 2)])
 
     part = ids.shape[0] // 4
-    sent = mix(ids[3 * part :], table, short_taps, toeplitz, tok_len)
-    ids, sent = tie((ids, sent))
-    other = [swap(sent, "fsdp", beside_bit)]
-    gated = mix(ids[: 3 * part], table, short_taps, toeplitz, tok_len)
-    gated, other[0], early, early_across, late = tie((gated, other[0], early, early_across, late))
-    mine = [gated[2 * part :], gated[:part]]
-    sent = gated[part : 2 * part]
-    pair = jnp.stack([early, early_across])
-    beside = [(pair, swap(pair, "ctx", 1))]
+    quarters = [ids[n * part : (n + 1) * part] for n in range(4)]
+    sent = mix(jnp.concatenate([quarters[3], quarters[1]], axis=0), table, short_taps, toeplitz, tok_len)
+    kept, sent = tie((jnp.concatenate([quarters[2], quarters[0]], axis=0), sent))
+    other = swap(sent, "fsdp", beside_bit)
+    mine = mix(kept, table, short_taps, toeplitz, tok_len)
+    middle = early.shape[1] // 2
+    mine, early_pair = tie((mine, early_pair))
+    pairs = [(columns, swap(columns, "ctx", 1)) for columns in (early_pair[:, :, :middle], early_pair[:, :, middle:])]
+    late_pair = jnp.stack([late, swap(late, "ctx", 1)])
+    halves = [late_pair[:, :, :middle], late_pair[:, :, middle:]]
 
     out = residual(token_ids, embedding)
-    away, arrived, behind = [], [], []
-
-    def send(shared, number, step, begin=0):
-        part = panel(at, mine[0], other[0], out_proj, shared, SPLITS[number], step, begin)
-        part, mine[0] = tie((part, mine[0]))
-        away.append(part)
-        arrived.append(swap(part, "fsdp", bits[-1]))
-
-    def sum_up(shared, number, step, begin=0):
-        got, total = arrived[len(behind)], panel(at, mine[1], other[1], out_proj, shared, SPLITS[number], step, begin)
+    (head, body), tail = SPLITS[0][3], SPLITS[1][3]
+    total = panel(at, mine, other, out_proj, pairs[0], SPLITS[0], head)
+    mine, out, halves, total = tie((mine, out, halves, total))
+    mine, other = (mine[:part], mine[part:]), (other[:part], other[part:])
+    total = total.reshape(2, part, *total.shape[1:])
+    for bit in reversed(bits[:-2]):
+        half = total.shape[1] // 2
+        total = add(total[:, :half], swap(total[:, half:], "fsdp", bit))
+    head_sum = (total[1], swap(total[0], "fsdp", bits[-1]), SPLITS[0], head)
+
+    behind = []
+    pairs = pairs[1:] + [(columns, swap(columns, "ctx", 2)) for columns in halves]
+    steps = [(SPLITS[0], body)] + [(SPLITS[1], step) for step in tail]
+    for pair, (split, step) in zip(pairs, steps):
+        begin = step[0]
+        away = panel(at, mine[0], other[0], out_proj, pair, split, step, begin)
+        away, mine = tie((away, mine))
+        got = swap(away, "fsdp", bits[-1])
         if behind:
             got, _ = tie((got, behind[-1][-1]))
+        total = panel(at, mine[1], other[1], out_proj, pair, split, step, begin)
         for bit in reversed(bits[:-2]):
             half = total.shape[0] // 2
             far = add(total[half:], got[half:])
             total, got = add(total[:half], got[:half]), swap(far, "fsdp", bit)
-        behind.append((total, got, SPLITS[number], step, far))
-
-    first, second = SPLITS[0][3]
-    send(beside[0], 0, first)
-    sent, late, out, _ = tie((sent, late, out, away[0]))
-    other.append(swap(sent, "fsdp", beside_bit))
-    pair = jnp.stack([late, swap(late, "ctx", 1)])
-    middle = pair.shape[2] // 2
-    send(beside[0], 0, second)
-    other[1], out, _ = tie((other[1], out, away[1]))
-    sum_up(beside[0], 0, first)
-    sum_up(beside[0], 0, second)
-    third, *rest = SPLITS[1][3]
-    for columns, steps, begin in ((pair[:, :, :middle], [third], 0), (pair[:, :, middle:], rest, third[1])):
-        shared = (columns, swap(columns, "ctx", 2))
-        shared, _ = tie((shared, behind[0][-1] if begin == 0 else behind[0][1]))
-        for step in steps:
-            send(shared, 1, step, begin)
-        for step in steps:
-            sum_up(shared, 1, step, begin)
+        behind.append((total, got, split, step, far))
+    out = place_pieces(at, out, *head_sum)
     for last in behind:
         out = place_pieces(at, out, *last[:-1])
     return out[None]

time: 118 us -> 116 us (0.983)
  Pallas kernels: 46.4 us -> 37.5 us
  waiting for transfers between devices: 41.9 us -> 47.5 us
    ppermute x23 -> x21, waiting for transfers between devices: 41.9 us -> 47.5 us  [swap(): return lax.ppermute(x, axis, [(i, i ^ mask) for i in range(peers)])]
    pallas_call x1, Pallas kernels: 14.8 us -> 9.73 us  [project(): pl.pallas_call(table_kernel, grid=(1,), in_specs=[hbm, hbm, pl.BlockSpec(...]
    pallas_call x5 -> x4, Pallas kernels: 9.8 us -> 7.91 us  [place_pieces(): pl.pallas_call(functools.partial(place_kernel, split, step), grid_spec=pl...]
    pallas_call x10 -> x7, Pallas kernels: 7.27 us -> 5.5 us  [panel(): pl.pallas_call(panel_kernel, grid_spec=pltpu.PrefetchScalarGridSpec(num_s...]
    ppermute x23 -> x21, starting transfers between devices: 24.8 us -> 25.3 us  [swap(): return lax.ppermute(x, axis, [(i, i ^ mask) for i in range(peers)])]
  transfers between devices with their start and end apart: 25 -> 23, of which waited for: 13 -> 11; matrix products, arithmetic and copies ran while one was open for 1% -> 1% of each run, Pallas kernels for 37% -> 31%
where the time goes in v9:
time: 116 us
  waiting for transfers between devices  47.5 us (41%)
  Pallas kernels  37.5 us (32%)
  starting transfers between devices  26.9 us (23%)
  local copies, waits for them, and re-layouts  2.6 us (2%)
    ppermute x21, waiting for transfers between devices, swap(): return lax.ppermute(x, axis, [(i, i ^ mask) for i in range(peers)])  47.5 us
    ppermute x21, starting transfers between devices, swap(): return lax.ppermute(x, axis, [(i, i ^ mask) for i in range(peers)])  25.3 us
    pallas_call x1, Pallas kernels, project(): pl.pallas_call(table_kernel, grid=(1,), in_specs=[hbm, hbm, pl.BlockSpec(...  9.73 us
    pallas_call x2, Pallas kernels, mix(): pl.pallas_call(mixer_kernel, grid=(windows // 2,), in_specs=[pl.BlockSpec...  8.84 us
    pallas_call x4, Pallas kernels, place_pieces(): pl.pallas_call(functools.partial(place_kernel, split, step), grid_spec=pl...  7.91 us
    pallas_call x7, Pallas kernels, panel(): pl.pallas_call(panel_kernel, grid_spec=pltpu.PrefetchScalarGridSpec(num_s...  5.5 us
    pallas_call x1, Pallas kernels, residual(): pl.pallas_call(residual_kernel, grid=(4,), in_specs=[whole(token_ids), pl...  2.67 us
  transfers between devices with their start and end apart: 23, of which 11 were waited for; matrix products, arithmetic and copies ran while one was open for 1% of the time, Pallas kernels for 31%

profile of v9, /device:TPU:0, one launch (start us, length us, event | category | flops | bytes accessed | tf_op | source)
XLA Modules:
  0.0 115.7 jit_solution(14286448192026958266)
XLA Ops:
  0.0 5.0 %collective-permute-start.2 = (s32[1,128]{1,0:T(1,128)}, s32[1,128]{1,0:T(1,128)S(1)}, u32[]{:S(2)}, u32[]{:S(2)}) collective-permute-start(s32[1,128]{1,0:T(1,128)} %ids_ref.1), channel_id=1, source_target_pairs={{0,24},{4,28},{8,16},{12,20},{16,8},{20,12},{24,0},{28,4},{1,25},{... | collective-permute-start | bytes 1544 | tf_op jit(solution)/shard_map/ppermute | solution.py:26
  5.6 2.2 %shard_map.73 = (bf16[512,512]{1,0:T(8,128)(2,1)}, bf16[512,512]{1,0:T(8,128)(2,1)}) custom-call(s32[1]{0:T(128)} %bitcast.place_ref, bf16[512,4096]{1,0:T(8,128)(2,1)} %refs_3_.13, bf16[512,4096]{1,0:T(8,128)(2,1)} %refs_3_.13), custom_call_target="tpu_custom_call" | custom-call | bytes 2000000 | tf_op jit(solution)/shard_map/pallas_call | solution.py:200
  9.6 1.6 %collective-permute-start.3 = (s32[4,128]{1,0:T(4,128)S(1)}, s32[4,128]{1,0:T(4,128)S(1)}, u32[]{:S(2)}, u32[]{:S(2)}) collective-permute-start(s32[4,128]{1,0:T(4,128)S(1)} %pad_add_fusion.3), channel_id=1, source_target_pairs={{0,4},{4,0},{8,12},{12,8},{16,20},{20,16},{24,28},{28,24},{1,5},{5... | collective-permute-start | bytes 6152 | tf_op jit(solution)/shard_map/ppermute | solution.py:26
  11.2 2.0 %collective-permute-start.6 = (bf16[512,512]{1,0:T(8,128)(2,1)}, bf16[512,512]{1,0:T(8,128)(2,1)S(1)}, u32[]{:S(2)}, u32[]{:S(2)}) collective-permute-start(bf16[512,512]{1,0:T(8,128)(2,1)} %get-tuple-element.41), channel_id=1, source_target_pairs={{0,8},{4,12},{8,0},{12,4},{16,24},{20,28},{24,16},{28,20},{1,9},{5... | collective-permute-start | bytes 1572872 | tf_op jit(solution)/shard_map/ppermute | solution.py:26
  13.4 1.6 %collective-permute-start.4 = (s32[8,128]{1,0:T(8,128)S(1)}, s32[8,128]{1,0:T(8,128)S(1)}, u32[]{:S(2)}, u32[]{:S(2)}) collective-permute-start(s32[8,128]{1,0:T(8,128)S(1)} %pad_add_fusion.2), channel_id=1, source_target_pairs={{0,2},{1,3},{2,0},{3,1},{4,6},{5,7},{6,4},{7,5},{8,10},{9,11},{10,... | collective-permute-start | bytes 12296 | tf_op jit(solution)/shard_map/ppermute | solution.py:21
  14.9 2.2 %copy-done.1 = bf16[512,4096]{1,0:T(8,128)(2,1)S(1)} copy-done((bf16[512,4096]{1,0:T(8,128)(2,1)S(1)}, bf16[512,4096]{1,0:T(8,128)(2,1)}, u32[]{:S(2)}) %copy-start.1) | copy-done | bytes 4194328
  17.1 9.7 %shard_map.75.table_ref = bf16[3,512,512]{2,1,0:T(8,128)(2,1)S(1)} custom-call(bf16[512,4096]{1,0:T(8,128)(2,1)S(1)} %copy-done.1, bf16[3,4096,512]{2,1,0:T(8,128)(2,1)} %weight_hbm.1, f32[1,4096]{1,0:T(1,128)S(1)} %bitcast.40), custom_call_target="tpu_custom_call" | custom-call | flops 3000000000 | tf_op jit(solution)/shard_map/pallas_call | solution.py:101
  27.9 4.4 %shard_map.76 = bf16[4,128,512]{2,1,0:T(8,128)(2,1)S(1)} custom-call(s32[4,1,272]{2,1,0:T(1,128)S(1)} %copy.12.ids_ref, bf16[3,512,512]{2,1,0:T(8,128)(2,1)S(1)} %shard_map.75.table_ref, f32[3,3,512]{2,1,0:T(4,128)S(1)} %copy-done.4, bf16[4,1024,256]{2,1,0:T(8,128)(2,1)S(1)} %shard_map.74.toeplitz), custom_call_target="tpu_custom_call" | custom-call | flops 1500000000 | tf_op jit(solution)/shard_map/pallas_call | solution.py:167
  32.3 2.1 %collective-permute-start.10 = (bf16[4,128,512]{2,1,0:T(8,128)(2,1)S(1)}, bf16[4,128,512]{2,1,0:T(8,128)(2,1)S(1)}, u32[]{:S(2)}, u32[]{:S(2)}) collective-permute-start(bf16[4,128,512]{2,1,0:T(8,128)(2,1)S(1)} %shard_map.76), channel_id=1, source_target_pairs={{0,8},{4,12},{8,0},{12,4},{16,24},{20,28},{24,16},{28,20},{1,9},{5... | collective-permute-start | bytes 1572872 | tf_op jit(solution)/shard_map/ppermute | solution.py:26
  34.9 4.4 %shard_map.77 = bf16[4,128,512]{2,1,0:T(8,128)(2,1)S(1)} custom-call(s32[4,1,272]{2,1,0:T(1,128)S(1)} %reshape.52.ids_ref, bf16[3,512,512]{2,1,0:T(8,128)(2,1)S(1)} %shard_map.75.table_ref, f32[3,3,512]{2,1,0:T(4,128)S(1)} %copy-done.4, bf16[4,1024,256]{2,1,0:T(8,128)(2,1)S(1)} %shard_map.74.toeplitz), custom_call_target="tpu_custom_call" | custom-call | flops 1500000000 | tf_op jit(solution)/shard_map/pallas_call | solution.py:167
  39.3 1.9 %collective-permute-done.7 = bf16[512,512]{1,0:T(8,128)(2,1)S(1)} collective-permute-done((bf16[512,512]{1,0:T(8,128)(2,1)S(1)}, bf16[512,512]{1,0:T(8,128)(2,1)S(1)}, u32[]{:S(2)}, u32[]{:S(2)}) %collective-permute-start.7) | collective-permute-done | bytes 524320 | tf_op jit(solution)/shard_map/ppermute | solution.py:26
  41.4 2.7 %shard_map.78.so_far_ref = bf16[128,4096]{1,0:T(8,128)(2,1)} custom-call(s32[1,128]{1,0:T(1,128)S(1)} %copy-done.3, bf16[512,4096]{1,0:T(8,128)(2,1)S(1)} %copy-done.1), custom_call_target="tpu_custom_call" | custom-call | flops 400000000 | tf_op jit(solution)/shard_map/pallas_call | solution.py:290
  44.7 2.4 %collective-permute-done.10 = bf16[4,128,512]{2,1,0:T(8,128)(2,1)S(1)} collective-permute-done((bf16[4,128,512]{2,1,0:T(8,128)(2,1)S(1)}, bf16[4,128,512]{2,1,0:T(8,128)(2,1)S(1)}, u32[]{:S(2)}, u32[]{:S(2)}) %collective-permute-start.10) | collective-permute-done | bytes 524320 | tf_op jit(solution)/shard_map/ppermute | solution.py:26
  47.1 1.2 %shard_map.79 = bf16[4,4,128,256]{3,2,1,0:T(8,128)(2,1)S(1)} custom-call(s32[1]{0:T(128)} %bitcast.place_ref, bf16[512,512]{1,0:T(8,128)(2,1)S(1)} %bitcast.39, bf16[512,512]{1,0:T(8,128)(2,1)S(1)} %bitcast.38, bf16[512,4096]{1,0:T(8,128)(2,1)S(1)} %copy-done, bf16[512,4096]{1,0:T(8,128)(2,1)S(1)} %copy-done, bf16[512,4096]{1,0:T(8,128)(2,1)S(1)} %copy-done, ...), custom_call_target="tpu_custom_call" | custom-call | flops 400000000 | tf_op jit(solution)/shard_map/pallas_call | solution.py:264
  48.4 1.5 %collective-permute-start.12 = (bf16[2,1,4,128,256]{4,3,2,1,0:T(8,128)(2,1)S(1)}, bf16[2,1,4,128,256]{4,3,2,1,0:T(8,128)(2,1)S(1)}, u32[]{:S(2)}, u32[]{:S(2)}) collective-permute-start(bf16[2,1,4,128,256]{4,3,2,1,0:T(8,128)(2,1)S(1)} %slice.123), channel_id=1, source_target_pairs={{0,16},{4,20},{8,24},{12,28},{16,0},{20,4},{24,8},{28,12},{1,17},{... | collective-permute-start | bytes 1572872 | tf_op jit(solution)/shard_map/ppermute | solution.py:26
  49.9 1.1 collective-permute-start.17
  51.8 1.1 collective-permute-start.15
  54.5 10.2 %collective-permute-done.17.refs_5_ = bf16[2,512,256]{2,1,0:T(8,128)(2,1)S(1)} collective-permute-done((bf16[2,512,256]{2,1,0:T(8,128)(2,1)S(1)}, bf16[2,512,256]{2,1,0:T(8,128)(2,1)S(1)}, u32[]{:S(2)}, u32[]{:S(2)}) %collective-permute-start.17) | collective-permute-done | bytes 524320 | tf_op jit(solution)/shard_map/ppermute | solution.py:26
  65.4 1.1 collective-permute-start.18
  66.5 8.0 %collective-permute-done.12 = bf16[2,1,4,128,256]{4,3,2,1,0:T(8,128)(2,1)S(1)} collective-permute-done((bf16[2,1,4,128,256]{4,3,2,1,0:T(8,128)(2,1)S(1)}, bf16[2,1,4,128,256]{4,3,2,1,0:T(8,128)(2,1)S(1)}, u32[]{:S(2)}, u32[]{:S(2)}) %collective-permute-start.12) | collective-permute-done | bytes 524320 | tf_op jit(solution)/shard_map/ppermute | solution.py:26
  74.7 1.1 collective-permute-start.13
  76.6 1.1 collective-permute-start.21
  79.9 2.5 %collective-permute-start.19 = (bf16[1,4,128,256]{3,2,1,0:T(8,128)(2,1)S(1)}, bf16[1,4,128,256]{3,2,1,0:T(8,128)(2,1)S(1)}, u32[]{:S(2)}, u32[]{:S(2)}) collective-permute-start(bf16[1,4,128,256]{3,2,1,0:T(8,128)(2,1)S(1)} %get-tuple-element.67), channel_id=1, source_target_pairs={{0,16},{4,20},{8,24},{12,28},{16,0},{20,4},{24,8},{28,12},{1,17},{... | collective-permute-start | bytes 786440 | tf_op jit(solution)/shard_map/ppermute | solution.py:26
  82.4 11.6 %collective-permute-done.21 = bf16[2,4,128,256]{3,2,1,0:T(8,128)(2,1)S(1)} collective-permute-done((bf16[2,4,128,256]{3,2,1,0:T(8,128)(2,1)S(1)}, bf16[2,4,128,256]{3,2,1,0:T(8,128)(2,1)S(1)}, u32[]{:S(2)}, u32[]{:S(2)}) %collective-permute-start.21) | collective-permute-done | bytes 524320 | tf_op jit(solution)/shard_map/ppermute | solution.py:26
  94.1 1.6 %collective-permute-start.22 = (bf16[1,4,128,256]{3,2,1,0:T(8,128)(2,1)S(1)}, bf16[1,4,128,256]{3,2,1,0:T(8,128)(2,1)S(1)}, u32[]{:S(2)}, u32[]{:S(2)}) collective-permute-start(bf16[1,4,128,256]{3,2,1,0:T(8,128)(2,1)S(1)} %get-tuple-element.65), channel_id=1, source_target_pairs={{0,16},{4,20},{8,24},{12,28},{16,0},{20,4},{24,8},{28,12},{1,17},{... | collective-permute-start | bytes 786440 | tf_op jit(solution)/shard_map/ppermute | solution.py:26
  95.7 2.0 %shard_map.80.so_far_ref = bf16[128,4096]{1,0:T(8,128)(2,1)} custom-call(s32[1]{0:T(128)} %bitcast.place_ref, bf16[128,4096]{1,0:T(8,128)(2,1)} %shard_map.78.so_far_ref, bf16[1,4,128,256]{3,2,1,0:T(8,128)(2,1)S(1)} %get-tuple-element.80.near_ref, bf16[1,4,128,256]{3,2,1,0:T(8,128)(2,1)S(1)} %collective-permute-done.13.far_ref), custom_call_target="tpu_custom_call", output_to_operand_aliasing={{}: (1, {})} | custom-call | bytes 1000000 | tf_op jit(solution)/shard_map/pallas_call | solution.py:318
  97.7 5.7 %collective-permute-done.16.far_ref = bf16[1,4,128,256]{3,2,1,0:T(8,128)(2,1)S(1)} collective-permute-done((bf16[1,4,128,256]{3,2,1,0:T(8,128)(2,1)S(1)}, bf16[1,4,128,256]{3,2,1,0:T(8,128)(2,1)S(1)}, u32[]{:S(2)}, u32[]{:S(2)}) %collective-permute-start.16) | collective-permute-done | bytes 262176 | tf_op jit(solution)/shard_map/ppermute | solution.py:26
  103.3 2.0 %shard_map.83.so_far_ref = bf16[128,4096]{1,0:T(8,128)(2,1)} custom-call(s32[1]{0:T(128)} %bitcast.place_ref, bf16[128,4096]{1,0:T(8,128)(2,1)} %shard_map.80.so_far_ref, bf16[1,4,128,256]{3,2,1,0:T(8,128)(2,1)S(1)} %get-tuple-element.70.near_ref, bf16[1,4,128,256]{3,2,1,0:T(8,128)(2,1)S(1)} %collective-permute-done.16.far_ref), custom_call_target="tpu_custom_call", output_to_operand_aliasing={{}: (1, {})} | custom-call | bytes 1000000 | tf_op jit(solution)/shard_map/pallas_call | solution.py:318
  105.3 3.6 %collective-permute-done.19.far_ref = bf16[1,4,128,256]{3,2,1,0:T(8,128)(2,1)S(1)} collective-permute-done((bf16[1,4,128,256]{3,2,1,0:T(8,128)(2,1)S(1)}, bf16[1,4,128,256]{3,2,1,0:T(8,128)(2,1)S(1)}, u32[]{:S(2)}, u32[]{:S(2)}) %collective-permute-start.19) | collective-permute-done | bytes 262176 | tf_op jit(solution)/shard_map/ppermute | solution.py:26
  109.0 2.0 %shard_map.86.so_far_ref = bf16[128,4096]{1,0:T(8,128)(2,1)} custom-call(s32[1]{0:T(128)} %bitcast.place_ref, bf16[128,4096]{1,0:T(8,128)(2,1)} %shard_map.83.so_far_ref, bf16[1,4,128,256]{3,2,1,0:T(8,128)(2,1)S(1)} %get-tuple-element.68.near_ref, bf16[1,4,128,256]{3,2,1,0:T(8,128)(2,1)S(1)} %collective-permute-done.19.far_ref), custom_call_target="tpu_custom_call", output_to_operand_aliasing={{}: (1, {})} | custom-call | bytes 1000000 | tf_op jit(solution)/shard_map/pallas_call | solution.py:318
  110.9 2.8 %collective-permute-done.22.far_ref = bf16[1,4,128,256]{3,2,1,0:T(8,128)(2,1)S(1)} collective-permute-done((bf16[1,4,128,256]{3,2,1,0:T(8,128)(2,1)S(1)}, bf16[1,4,128,256]{3,2,1,0:T(8,128)(2,1)S(1)}, u32[]{:S(2)}, u32[]{:S(2)}) %collective-permute-start.22) | collective-permute-done | bytes 262176 | tf_op jit(solution)/shard_map/ppermute | solution.py:26
  113.7 2.0 %shard_map.89 = bf16[128,4096]{1,0:T(8,128)(2,1)} custom-call(s32[1]{0:T(128)} %bitcast.place_ref, bf16[128,4096]{1,0:T(8,128)(2,1)} %shard_map.86.so_far_ref, bf16[1,4,128,256]{3,2,1,0:T(8,128)(2,1)S(1)} %get-tuple-element.66.near_ref, bf16[1,4,128,256]{3,2,1,0:T(8,128)(2,1)S(1)} %collective-permute-done.22.far_ref), custom_call_target="tpu_custom_call", output_to_operand_aliasing={{}: (1, {})} | custom-call | bytes 1000000 | tf_op jit(solution)/shard_map/pallas_call | solution.py:318
  (67 shorter events, 11.1 us)
Async XLA Ops:
  0.0 8.7 %collective-permute-start.2 = (s32[1,128]{1,0:T(1,128)}, s32[1,128]{1,0:T(1,128)S(1)}, u32[]{:S(2)}, u32[]{:S(2)}) collective-permute-start(s32[1,128]{1,0:T(1,128)} %ids_ref.1), channel_id=1, source_target_pairs={{0,24},{4,28},{8,16},{12,20},{16,8},{20,12},{24,0},{28,4},{1,25},{... | collective-permute-start | bytes 1544 | tf_op jit(solution)/shard_map/ppermute | solution.py:26
  5.0 3.7 %collective-permute-start.1 = (s32[1,128]{1,0:T(1,128)}, s32[1,128]{1,0:T(1,128)S(1)}, u32[]{:S(2)}, u32[]{:S(2)}) collective-permute-start(s32[1,128]{1,0:T(1,128)} %ids_ref.1), channel_id=1, source_target_pairs={{0,8},{4,12},{8,0},{12,4},{16,24},{20,28},{24,16},{28,20},{1,9},{5... | collective-permute-start | bytes 1544 | tf_op jit(solution)/shard_map/ppermute | solution.py:26
  5.1 4.6 %collective-permute-start = (s32[1,128]{1,0:T(1,128)}, s32[1,128]{1,0:T(1,128)S(1)}, u32[]{:S(2)}, u32[]{:S(2)}) collective-permute-start(s32[1,128]{1,0:T(1,128)} %ids_ref.1), channel_id=1, source_target_pairs={{0,16},{4,20},{8,24},{12,28},{16,0},{20,4},{24,8},{28,12},{1,17},{... | collective-permute-start | bytes 1544 | tf_op jit(solution)/shard_map/ppermute | solution.py:26
  5.6 2.3 %copy-start.5 = (bf16[32,128]{1,0:T(8,128)(2,1)S(1)}, bf16[32,128]{1,0:T(8,128)(2,1)}, u32[]{:S(2)}) copy-start(bf16[32,128]{1,0:T(8,128)(2,1)} %param.12) | copy-start | bytes 24580
  5.6 4.0 %copy-start.3 = (s32[1,128]{1,0:T(1,128)S(1)}, s32[1,128]{1,0:T(1,128)}, u32[]{:S(2)}) copy-start(s32[1,128]{1,0:T(1,128)} %ids_ref.1) | copy-start | bytes 1540
  5.6 9.3 %copy-start.2 = (f32[4096]{0:T(1024)S(1)}, f32[4096]{0:T(1024)}, u32[]{:S(2)}) copy-start(f32[4096]{0:T(1024)} %param.9) | copy-start | bytes 49156
  9.6 3.7 %collective-permute-start.3 = (s32[4,128]{1,0:T(4,128)S(1)}, s32[4,128]{1,0:T(4,128)S(1)}, u32[]{:S(2)}, u32[]{:S(2)}) collective-permute-start(s32[4,128]{1,0:T(4,128)S(1)} %pad_add_fusion.3), channel_id=1, source_target_pairs={{0,4},{4,0},{8,12},{12,8},{16,20},{20,16},{24,28},{28,24},{1,5},{5... | collective-permute-start | bytes 6152 | tf_op jit(solution)/shard_map/ppermute | solution.py:26
  11.2 15.8 %collective-permute-start.6 = (bf16[512,512]{1,0:T(8,128)(2,1)}, bf16[512,512]{1,0:T(8,128)(2,1)S(1)}, u32[]{:S(2)}, u32[]{:S(2)}) collective-permute-start(bf16[512,512]{1,0:T(8,128)(2,1)} %get-tuple-element.41), channel_id=1, source_target_pairs={{0,8},{4,12},{8,0},{12,4},{16,24},{20,28},{24,16},{28,20},{1,9},{5... | collective-permute-start | bytes 1572872 | tf_op jit(solution)/shard_map/ppermute | solution.py:26
  13.2 21.4 %collective-permute-start.8 = (bf16[512,512]{1,0:T(8,128)(2,1)}, bf16[512,512]{1,0:T(8,128)(2,1)S(1)}, u32[]{:S(2)}, u32[]{:S(2)}) collective-permute-start(bf16[512,512]{1,0:T(8,128)(2,1)} %get-tuple-element.47), channel_id=1, source_target_pairs={{0,8},{4,12},{8,0},{12,4},{16,24},{20,28},{24,16},{28,20},{1,9},{5... | collective-permute-start | bytes 1572872 | tf_op jit(solution)/shard_map/ppermute | solution.py:26
  13.3 13.6 %collective-permute-start.5 = (s32[8,128]{1,0:T(8,128)S(1)}, s32[8,128]{1,0:T(8,128)S(1)}, u32[]{:S(2)}, u32[]{:S(2)}) collective-permute-start(s32[8,128]{1,0:T(8,128)S(1)} %pad_add_fusion.2), channel_id=1, source_target_pairs={{0,1},{1,2},{2,3},{3,0},{4,5},{5,6},{6,7},{7,4},{8,9},{9,10},{10,1... | collective-permute-start | bytes 12296 | tf_op jit(solution)/shard_map/ppermute | solution.py:21
  13.4 13.5 %collective-permute-start.4 = (s32[8,128]{1,0:T(8,128)S(1)}, s32[8,128]{1,0:T(8,128)S(1)}, u32[]{:S(2)}, u32[]{:S(2)}) collective-permute-start(s32[8,128]{1,0:T(8,128)S(1)} %pad_add_fusion.2), channel_id=1, source_target_pairs={{0,2},{1,3},{2,0},{3,1},{4,6},{5,7},{6,4},{7,5},{8,10},{9,11},{10,... | collective-permute-start | bytes 12296 | tf_op jit(solution)/shard_map/ppermute | solution.py:21
  14.9 2.2 %copy-start.1 = (bf16[512,4096]{1,0:T(8,128)(2,1)S(1)}, bf16[512,4096]{1,0:T(8,128)(2,1)}, u32[]{:S(2)}) copy-start(bf16[512,4096]{1,0:T(8,128)(2,1)} %rows_ref.1) | copy-start | bytes 12582916
  17.1 10.7 %copy-start.4 = (f32[3,3,512]{2,1,0:T(4,128)S(1)}, f32[3,3,512]{2,1,0:T(4,128)}, u32[]{:S(2)}) copy-start(f32[3,3,512]{2,1,0:T(4,128)} %short_ref.3) | copy-start | bytes 55300
  27.0 14.1 %collective-permute-start.7 = (bf16[512,512]{1,0:T(8,128)(2,1)S(1)}, bf16[512,512]{1,0:T(8,128)(2,1)S(1)}, u32[]{:S(2)}, u32[]{:S(2)}) collective-permute-start(bf16[512,512]{1,0:T(8,128)(2,1)S(1)} %collective-permute-done.6), channel_id=1, source_target_pairs={{0,2},{1,3},{2,0},{3,1},{4,6},{5,7},{6,4},{7,5},{8,10},{9,11},{10,... | collective-permute-start | bytes 1572872 | tf_op jit(solution)/shard_map/ppermute | solution.py:26
  32.3 14.8 %collective-permute-start.10 = (bf16[4,128,512]{2,1,0:T(8,128)(2,1)S(1)}, bf16[4,128,512]{2,1,0:T(8,128)(2,1)S(1)}, u32[]{:S(2)}, u32[]{:S(2)}) collective-permute-start(bf16[4,128,512]{2,1,0:T(8,128)(2,1)S(1)} %shard_map.76), channel_id=1, source_target_pairs={{0,8},{4,12},{8,0},{12,4},{16,24},{20,28},{24,16},{28,20},{1,9},{5... | collective-permute-start | bytes 1572872 | tf_op jit(solution)/shard_map/ppermute | solution.py:26
  34.6 10.0 %collective-permute-start.9 = (bf16[512,512]{1,0:T(8,128)(2,1)S(1)}, bf16[512,512]{1,0:T(8,128)(2,1)S(1)}, u32[]{:S(2)}, u32[]{:S(2)}) collective-permute-start(bf16[512,512]{1,0:T(8,128)(2,1)S(1)} %collective-permute-done.8), channel_id=1, source_target_pairs={{0,1},{1,0},{2,3},{3,2},{4,5},{5,4},{6,7},{7,6},{8,9},{9,8},{10,11... | collective-permute-start | bytes 1572872 | tf_op jit(solution)/shard_map/ppermute | solution.py:26
  41.3 5.8 %copy-start = (bf16[512,4096]{1,0:T(8,128)(2,1)S(1)}, bf16[512,4096]{1,0:T(8,128)(2,1)}, u32[]{:S(2)}) copy-start(bf16[512,4096]{1,0:T(8,128)(2,1)} %refs_3_.13) | copy-start | bytes 12582916
  41.4 5.8 %collective-permute-start.11 = (bf16[2,512,256]{2,1,0:T(8,128)(2,1)S(1)}, bf16[2,512,256]{2,1,0:T(8,128)(2,1)S(1)}, u32[]{:S(2)}, u32[]{:S(2)}) collective-permute-start(bf16[2,512,256]{2,1,0:T(8,128)(2,1)S(1)} %get-tuple-element.72.refs_4_), channel_id=1, source_target_pairs={{0,1},{1,0},{2,3},{3,2},{4,5},{5,4},{6,7},{7,6},{8,9},{9,8},{10,11... | collective-permute-start | bytes 1572872 | tf_op jit(solution)/shard_map/ppermute | solution.py:26
  44.1 7.0 %collective-permute-start.14 = (bf16[2,512,256]{2,1,0:T(8,128)(2,1)S(1)}, bf16[2,512,256]{2,1,0:T(8,128)(2,1)S(1)}, u32[]{:S(2)}, u32[]{:S(2)}) collective-permute-start(bf16[2,512,256]{2,1,0:T(8,128)(2,1)S(1)} %get-tuple-element.71.refs_4_), channel_id=1, source_target_pairs={{0,1},{1,0},{2,3},{3,2},{4,5},{5,4},{6,7},{7,6},{8,9},{9,8},{10,11... | collective-permute-start | bytes 1572872 | tf_op jit(solution)/shard_map/ppermute | solution.py:26
  48.4 26.1 %collective-permute-start.12 = (bf16[2,1,4,128,256]{4,3,2,1,0:T(8,128)(2,1)S(1)}, bf16[2,1,4,128,256]{4,3,2,1,0:T(8,128)(2,1)S(1)}, u32[]{:S(2)}, u32[]{:S(2)}) collective-permute-start(bf16[2,1,4,128,256]{4,3,2,1,0:T(8,128)(2,1)S(1)} %slice.123), channel_id=1, source_target_pairs={{0,16},{4,20},{8,24},{12,28},{16,0},{20,4},{24,8},{28,12},{1,17},{... | collective-permute-start | bytes 1572872 | tf_op jit(solution)/shard_map/ppermute | solution.py:26
  49.9 14.8 %collective-permute-start.17 = (bf16[2,512,256]{2,1,0:T(8,128)(2,1)S(1)}, bf16[2,512,256]{2,1,0:T(8,128)(2,1)S(1)}, u32[]{:S(2)}, u32[]{:S(2)}) collective-permute-start(bf16[2,512,256]{2,1,0:T(8,128)(2,1)S(1)} %get-tuple-element.56.refs_4_), channel_id=1, source_target_pairs={{0,2},{1,3},{2,0},{3,1},{4,6},{5,7},{6,4},{7,5},{8,10},{9,11},{10,... | collective-permute-start | bytes 1572872 | tf_op jit(solution)/shard_map/ppermute | solution.py:26
  51.8 25.8 %collective-permute-start.15 = (bf16[2,4,128,256]{3,2,1,0:T(8,128)(2,1)S(1)}, bf16[2,4,128,256]{3,2,1,0:T(8,128)(2,1)S(1)}, u32[]{:S(2)}, u32[]{:S(2)}) collective-permute-start(bf16[2,4,128,256]{3,2,1,0:T(8,128)(2,1)S(1)} %shard_map.81), channel_id=1, source_target_pairs={{0,4},{4,0},{8,12},{12,8},{16,20},{20,16},{24,28},{28,24},{1,5},{5... | collective-permute-start | bytes 1572872 | tf_op jit(solution)/shard_map/ppermute | solution.py:26
  52.9 22.9 %collective-permute-start.20 = (bf16[2,512,256]{2,1,0:T(8,128)(2,1)S(1)}, bf16[2,512,256]{2,1,0:T(8,128)(2,1)S(1)}, u32[]{:S(2)}, u32[]{:S(2)}) collective-permute-start(bf16[2,512,256]{2,1,0:T(8,128)(2,1)S(1)} %get-tuple-element.61.refs_4_), channel_id=1, source_target_pairs={{0,2},{1,3},{2,0},{3,1},{4,6},{5,7},{6,4},{7,5},{8,10},{9,11},{10,... | collective-permute-start | bytes 1572872 | tf_op jit(solution)/shard_map/ppermute | solution.py:26
  65.4 14.3 %collective-permute-start.18 = (bf16[2,4,128,256]{3,2,1,0:T(8,128)(2,1)S(1)}, bf16[2,4,128,256]{3,2,1,0:T(8,128)(2,1)S(1)}, u32[]{:S(2)}, u32[]{:S(2)}) collective-permute-start(bf16[2,4,128,256]{3,2,1,0:T(8,128)(2,1)S(1)} %shard_map.84), channel_id=1, source_target_pairs={{0,4},{4,0},{8,12},{12,8},{16,20},{20,16},{24,28},{28,24},{1,5},{5... | collective-permute-start | bytes 1572872 | tf_op jit(solution)/shard_map/ppermute | solution.py:26
  74.7 21.0 %collective-permute-start.13 = (bf16[1,4,128,256]{3,2,1,0:T(8,128)(2,1)S(1)}, bf16[1,4,128,256]{3,2,1,0:T(8,128)(2,1)S(1)}, u32[]{:S(2)}, u32[]{:S(2)}) collective-permute-start(bf16[1,4,128,256]{3,2,1,0:T(8,128)(2,1)S(1)} %get-tuple-element.79), channel_id=1, source_target_pairs={{0,4},{4,0},{8,12},{12,8},{16,20},{20,16},{24,28},{28,24},{1,5},{5... | collective-permute-start | bytes 786440 | tf_op jit(solution)/shard_map/ppermute | solution.py:26
  76.6 17.5 %collective-permute-start.21 = (bf16[2,4,128,256]{3,2,1,0:T(8,128)(2,1)S(1)}, bf16[2,4,128,256]{3,2,1,0:T(8,128)(2,1)S(1)}, u32[]{:S(2)}, u32[]{:S(2)}) collective-permute-start(bf16[2,4,128,256]{3,2,1,0:T(8,128)(2,1)S(1)} %shard_map.87), channel_id=1, source_target_pairs={{0,4},{4,0},{8,12},{12,8},{16,20},{20,16},{24,28},{28,24},{1,5},{5... | collective-permute-start | bytes 1572872 | tf_op jit(solution)/shard_map/ppermute | solution.py:26
  77.7 25.6 %collective-permute-start.16 = (bf16[1,4,128,256]{3,2,1,0:T(8,128)(2,1)S(1)}, bf16[1,4,128,256]{3,2,1,0:T(8,128)(2,1)S(1)}, u32[]{:S(2)}, u32[]{:S(2)}) collective-permute-start(bf16[1,4,128,256]{3,2,1,0:T(8,128)(2,1)S(1)} %get-tuple-element.69), channel_id=1, source_target_pairs={{0,16},{4,20},{8,24},{12,28},{16,0},{20,4},{24,8},{28,12},{1,17},{... | collective-permute-start | bytes 786440 | tf_op jit(solution)/shard_map/ppermute | solution.py:26
  79.9 29.1 %collective-permute-start.19 = (bf16[1,4,128,256]{3,2,1,0:T(8,128)(2,1)S(1)}, bf16[1,4,128,256]{3,2,1,0:T(8,128)(2,1)S(1)}, u32[]{:S(2)}, u32[]{:S(2)}) collective-permute-start(bf16[1,4,128,256]{3,2,1,0:T(8,128)(2,1)S(1)} %get-tuple-element.67), channel_id=1, source_target_pairs={{0,16},{4,20},{8,24},{12,28},{16,0},{20,4},{24,8},{28,12},{1,17},{... | collective-permute-start | bytes 786440 | tf_op jit(solution)/shard_map/ppermute | solution.py:26
  94.1 19.6 %collective-permute-start.22 = (bf16[1,4,128,256]{3,2,1,0:T(8,128)(2,1)S(1)}, bf16[1,4,128,256]{3,2,1,0:T(8,128)(2,1)S(1)}, u32[]{:S(2)}, u32[]{:S(2)}) collective-permute-start(bf16[1,4,128,256]{3,2,1,0:T(8,128)(2,1)S(1)} %get-tuple-element.65), channel_id=1, source_target_pairs={{0,16},{4,20},{8,24},{12,28},{16,0},{20,4},{24,8},{28,12},{1,17},{... | collective-permute-start | bytes 786440 | tf_op jit(solution)/shard_map/ppermute | solution.py:26

commit v10 on v9

--- a/solution.py
+++ b/solution.py
@@ -12,7 +12,7 @@
 SHORT = 3
 LANES = 128
 LEAD = 16
-SPLITS = ((0, 8, (0, 2, 1, 3), ((0, 4), (4, 4))), (8, 8, (0, 1, 2, 3), ((0, 4), (4, 4))))
+SPLITS = ((0, 8, (0, 2, 1, 3), ((0, 2), (4, 4), (2, 2))), (8, 8, (0, 1, 2, 3), ((0, 4), (4, 4))))
 SIXTEENTHS = 16
 
 
@@ -360,40 +360,49 @@
     mine = mix(kept, table, short_taps, toeplitz, tok_len)
     middle = early.shape[1] // 2
     mine, early_pair = tie((mine, early_pair))
+    late_pair = jnp.stack([late, swap(late, "ctx", 1)])
     pairs = [(columns, swap(columns, "ctx", 1)) for columns in (early_pair[:, :, :middle], early_pair[:, :, middle:])]
-    late_pair = jnp.stack([late, swap(late, "ctx", 1)])
-    halves = [late_pair[:, :, :middle], late_pair[:, :, middle:]]
-
-    out = residual(token_ids, embedding)
-    (head, body), tail = SPLITS[0][3], SPLITS[1][3]
+
+    own_ids, mine = tie((token_ids, mine))
+    out = residual(own_ids, embedding)
+    late_pair, out = tie((late_pair, out))
+    pairs.append((late_pair[:, :, :middle], swap(late_pair[:, :, :middle], "ctx", 2)))
+    (head, body, foot), tail = SPLITS[0][3], SPLITS[1][3]
     total = panel(at, mine, other, out_proj, pairs[0], SPLITS[0], head)
-    mine, out, halves, total = tie((mine, out, halves, total))
+    mine, out, total = tie((mine, out, total))
     mine, other = (mine[:part], mine[part:]), (other[:part], other[part:])
     total = total.reshape(2, part, *total.shape[1:])
     for bit in reversed(bits[:-2]):
         half = total.shape[1] // 2
-        total = add(total[:, :half], swap(total[:, half:], "fsdp", bit))
+        got = swap(total[:, half:], "fsdp", bit)
+        total = add(total[:, :half], got)
     head_sum = (total[1], swap(total[0], "fsdp", bits[-1]), SPLITS[0], head)
 
-    behind = []
-    pairs = pairs[1:] + [(columns, swap(columns, "ctx", 2)) for columns in halves]
-    steps = [(SPLITS[0], body)] + [(SPLITS[1], step) for step in tail]
-    for pair, (split, step) in zip(pairs, steps):
-        begin = step[0]
+    behind = [(got,)]
+    for number in range(4):
+        if number == 0:
+            pair, split, step, begin = pairs[1], SPLITS[0], body, body[0]
+        elif number < 3:
+            pair, split, step = pairs[number + 1], SPLITS[1], tail[number - 1]
+            begin = step[0]
+        else:
+            pair, split, step, begin = pairs[0], SPLITS[0], foot, 0
+        if number:
+            mine, _ = tie((mine, behind[number - 1][0]))
         away = panel(at, mine[0], other[0], out_proj, pair, split, step, begin)
-        away, mine = tie((away, mine))
+        if number == 0:
+            rest, _ = tie((late_pair[:, :, middle:], away))
+            pairs.append((rest, swap(rest, "ctx", 2)))
         got = swap(away, "fsdp", bits[-1])
-        if behind:
-            got, _ = tie((got, behind[-1][-1]))
         total = panel(at, mine[1], other[1], out_proj, pair, split, step, begin)
         for bit in reversed(bits[:-2]):
             half = total.shape[0] // 2
             far = add(total[half:], got[half:])
             total, got = add(total[:half], got[:half]), swap(far, "fsdp", bit)
-        behind.append((total, got, split, step, far))
+        behind.append((got, total, split, step))
     out = place_pieces(at, out, *head_sum)
-    for last in behind:
-        out = place_pieces(at, out, *last[:-1])
+    for far, near, split, step in behind[1:]:
+        out = place_pieces(at, out, near, far, split, step)
     return out[None]
 
 

time: 116 us -> 120 us (1.034)
  Pallas kernels: 37.5 us -> 41 us
  waiting for transfers between devices: 47.5 us -> 50.4 us
  starting transfers between devices: 26.9 us -> 24.2 us
    ppermute x21 -> x23, waiting for transfers between devices: 47.5 us -> 50.4 us  [swap(): return lax.ppermute(x, axis, [(i, i ^ mask) for i in range(peers)])]
    ppermute x21 -> x23, starting transfers between devices: 25.3 us -> 22.6 us  [swap(): return lax.ppermute(x, axis, [(i, i ^ mask) for i in range(peers)])]
    pallas_call x4 -> x5, Pallas kernels: 7.91 us -> 9.8 us  [place_pieces(): pl.pallas_call(functools.partial(place_kernel, split, step), grid_spec=pl...]
    pallas_call x7 -> x9, Pallas kernels: 5.5 us -> 7.11 us  [panel(): pl.pallas_call(panel_kernel, grid_spec=pltpu.PrefetchScalarGridSpec(num_s...]
  transfers between devices with their start and end apart: 23 -> 25, of which waited for: 11 -> 11; matrix products, arithmetic and copies ran while one was open for 1% -> 1% of each run, Pallas kernels for 31% -> 33%
where the time goes in v10:
time: 120 us; the launch traced here: 119 us
  waiting for transfers between devices  50.4 us (42%)
  Pallas kernels  41 us (34%)
  starting transfers between devices  24.2 us (20%)
  local copies, waits for them, and re-layouts  2.64 us (2%)
    ppermute x23, waiting for transfers between devices, swap(): return lax.ppermute(x, axis, [(i, i ^ mask) for i in range(peers)])  50.4 us
    ppermute x23, starting transfers between devices, swap(): return lax.ppermute(x, axis, [(i, i ^ mask) for i in range(peers)])  22.6 us
    pallas_call x5, Pallas kernels, place_pieces(): pl.pallas_call(functools.partial(place_kernel, split, step), grid_spec=pl...  9.8 us
    pallas_call x1, Pallas kernels, project(): pl.pallas_call(table_kernel, grid=(1,), in_specs=[hbm, hbm, pl.BlockSpec(...  9.73 us
    pallas_call x2, Pallas kernels, mix(): pl.pallas_call(mixer_kernel, grid=(windows // 2,), in_specs=[pl.BlockSpec...  8.84 us
    pallas_call x9, Pallas kernels, panel(): pl.pallas_call(panel_kernel, grid_spec=pltpu.PrefetchScalarGridSpec(num_s...  7.11 us
    pallas_call x1, Pallas kernels, residual(): pl.pallas_call(residual_kernel, grid=(4,), in_specs=[whole(token_ids), pl...  2.66 us
  transfers between devices with their start and end apart: 25, of which 11 were waited for; matrix products, arithmetic and copies ran while one was open for 1% of the time, Pallas kernels for 33%

profile of v10, /device:TPU:0, one launch (start us, length us, event | category | flops | bytes accessed | tf_op | source)
XLA Modules:
  0.0 119.5 jit_solution(8460023697862656944)
XLA Ops:
  0.0 5.0 %collective-permute-start.2 = (s32[1,128]{1,0:T(1,128)}, s32[1,128]{1,0:T(1,128)S(1)}, u32[]{:S(2)}, u32[]{:S(2)}) collective-permute-start(s32[1,128]{1,0:T(1,128)} %ids_ref), channel_id=1, source_target_pairs={{0,24},{4,28},{8,16},{12,20},{16,8},{20,12},{24,0},{28,4},{1,25},{... | collective-permute-start | bytes 1544 | tf_op jit(solution)/shard_map/ppermute | solution.py:26
  5.6 2.2 %shard_map.73 = (bf16[512,512]{1,0:T(8,128)(2,1)}, bf16[512,512]{1,0:T(8,128)(2,1)}) custom-call(s32[1]{0:T(128)} %bitcast.place_ref, bf16[512,4096]{1,0:T(8,128)(2,1)} %refs_3_.17, bf16[512,4096]{1,0:T(8,128)(2,1)} %refs_3_.17), custom_call_target="tpu_custom_call" | custom-call | bytes 2000000 | tf_op jit(solution)/shard_map/pallas_call | solution.py:200
  9.6 1.6 %collective-permute-start.3 = (s32[4,128]{1,0:T(4,128)S(1)}, s32[4,128]{1,0:T(4,128)S(1)}, u32[]{:S(2)}, u32[]{:S(2)}) collective-permute-start(s32[4,128]{1,0:T(4,128)S(1)} %pad_add_fusion.3), channel_id=1, source_target_pairs={{0,4},{4,0},{8,12},{12,8},{16,20},{20,16},{24,28},{28,24},{1,5},{5... | collective-permute-start | bytes 6152 | tf_op jit(solution)/shard_map/ppermute | solution.py:26
  11.2 2.0 %collective-permute-start.6 = (bf16[512,512]{1,0:T(8,128)(2,1)}, bf16[512,512]{1,0:T(8,128)(2,1)S(1)}, u32[]{:S(2)}, u32[]{:S(2)}) collective-permute-start(bf16[512,512]{1,0:T(8,128)(2,1)} %get-tuple-element.40), channel_id=1, source_target_pairs={{0,8},{4,12},{8,0},{12,4},{16,24},{20,28},{24,16},{28,20},{1,9},{5... | collective-permute-start | bytes 1572872 | tf_op jit(solution)/shard_map/ppermute | solution.py:26
  13.4 1.6 %collective-permute-start.4 = (s32[8,128]{1,0:T(8,128)S(1)}, s32[8,128]{1,0:T(8,128)S(1)}, u32[]{:S(2)}, u32[]{:S(2)}) collective-permute-start(s32[8,128]{1,0:T(8,128)S(1)} %pad_add_fusion.2), channel_id=1, source_target_pairs={{0,2},{1,3},{2,0},{3,1},{4,6},{5,7},{6,4},{7,5},{8,10},{9,11},{10,... | collective-permute-start | bytes 12296 | tf_op jit(solution)/shard_map/ppermute | solution.py:21
  14.9 2.2 %copy-done.1 = bf16[512,4096]{1,0:T(8,128)(2,1)S(1)} copy-done((bf16[512,4096]{1,0:T(8,128)(2,1)S(1)}, bf16[512,4096]{1,0:T(8,128)(2,1)}, u32[]{:S(2)}) %copy-start.1) | copy-done | bytes 4194328
  17.1 9.7 %shard_map.75.table_ref = bf16[3,512,512]{2,1,0:T(8,128)(2,1)S(1)} custom-call(bf16[512,4096]{1,0:T(8,128)(2,1)S(1)} %copy-done.1, bf16[3,4096,512]{2,1,0:T(8,128)(2,1)} %weight_hbm.1, f32[1,4096]{1,0:T(1,128)S(1)} %bitcast.46), custom_call_target="tpu_custom_call" | custom-call | flops 3000000000 | tf_op jit(solution)/shard_map/pallas_call | solution.py:101
  27.9 4.4 %shard_map.76 = bf16[4,128,512]{2,1,0:T(8,128)(2,1)S(1)} custom-call(s32[4,1,272]{2,1,0:T(1,128)S(1)} %copy.13.ids_ref, bf16[3,512,512]{2,1,0:T(8,128)(2,1)S(1)} %shard_map.75.table_ref, f32[3,3,512]{2,1,0:T(4,128)S(1)} %copy-done.4, bf16[4,1024,256]{2,1,0:T(8,128)(2,1)S(1)} %shard_map.74.toeplitz), custom_call_target="tpu_custom_call" | custom-call | flops 1500000000 | tf_op jit(solution)/shard_map/pallas_call | solution.py:167
  32.3 2.1 %collective-permute-start.10 = (bf16[4,128,512]{2,1,0:T(8,128)(2,1)S(1)}, bf16[4,128,512]{2,1,0:T(8,128)(2,1)S(1)}, u32[]{:S(2)}, u32[]{:S(2)}) collective-permute-start(bf16[4,128,512]{2,1,0:T(8,128)(2,1)S(1)} %shard_map.76), channel_id=1, source_target_pairs={{0,8},{4,12},{8,0},{12,4},{16,24},{20,28},{24,16},{28,20},{1,9},{5... | collective-permute-start | bytes 1572872 | tf_op jit(solution)/shard_map/ppermute | solution.py:26
  34.9 4.4 %shard_map.77 = bf16[4,128,512]{2,1,0:T(8,128)(2,1)S(1)} custom-call(s32[4,1,272]{2,1,0:T(1,128)S(1)} %reshape.60.ids_ref, bf16[3,512,512]{2,1,0:T(8,128)(2,1)S(1)} %shard_map.75.table_ref, f32[3,3,512]{2,1,0:T(4,128)S(1)} %copy-done.4, bf16[4,1024,256]{2,1,0:T(8,128)(2,1)S(1)} %shard_map.74.toeplitz), custom_call_target="tpu_custom_call" | custom-call | flops 1500000000 | tf_op jit(solution)/shard_map/pallas_call | solution.py:167
  39.3 1.9 %collective-permute-done.7 = bf16[512,512]{1,0:T(8,128)(2,1)S(1)} collective-permute-done((bf16[512,512]{1,0:T(8,128)(2,1)S(1)}, bf16[512,512]{1,0:T(8,128)(2,1)S(1)}, u32[]{:S(2)}, u32[]{:S(2)}) %collective-permute-start.7) | collective-permute-done | bytes 524320 | tf_op jit(solution)/shard_map/ppermute | solution.py:26
  41.5 2.7 %shard_map.78.so_far_ref = bf16[128,4096]{1,0:T(8,128)(2,1)} custom-call(s32[1,128]{1,0:T(1,128)S(1)} %copy-done.3, bf16[512,4096]{1,0:T(8,128)(2,1)S(1)} %copy-done.1), custom_call_target="tpu_custom_call" | custom-call | flops 400000000 | tf_op jit(solution)/shard_map/pallas_call | solution.py:290
  44.8 1.4 %collective-permute-start.17 = (bf16[2,512,256]{2,1,0:T(8,128)(2,1)S(1)}, bf16[2,512,256]{2,1,0:T(8,128)(2,1)S(1)}, u32[]{:S(2)}, u32[]{:S(2)}) collective-permute-start(bf16[2,512,256]{2,1,0:T(8,128)(2,1)S(1)} %get-tuple-element.66.refs_4_), channel_id=1, source_target_pairs={{0,2},{1,3},{2,0},{3,1},{4,6},{5,7},{6,4},{7,5},{8,10},{9,11},{10,... | collective-permute-start | bytes 1572872 | tf_op jit(solution)/shard_map/ppermute | solution.py:26
  46.2 0.9 collective-permute-done.10
  47.2 1.4 %shard_map.79 = bf16[4,4,128,128]{3,2,1,0:T(8,128)(2,1)S(1)} custom-call(s32[1]{0:T(128)} %bitcast.place_ref, bf16[512,512]{1,0:T(8,128)(2,1)S(1)} %bitcast.45, bf16[512,512]{1,0:T(8,128)(2,1)S(1)} %bitcast.44, bf16[512,4096]{1,0:T(8,128)(2,1)S(1)} %copy-done, bf16[512,4096]{1,0:T(8,128)(2,1)S(1)} %copy-done, bf16[512,4096]{1,0:T(8,128)(2,1)S(1)} %copy-done, ...), custom_call_target="tpu_custom_call" | custom-call | flops 400000000 | tf_op jit(solution)/shard_map/pallas_call | solution.py:264
  49.3 1.1 collective-permute-start.15
  50.4 1.5 %collective-permute-start.12 = (bf16[2,1,4,128,128]{4,3,2,1,0:T(8,128)(2,1)S(1)}, bf16[2,1,4,128,128]{4,3,2,1,0:T(8,128)(2,1)S(1)}, u32[]{:S(2)}, u32[]{:S(2)}) collective-permute-start(bf16[2,1,4,128,128]{4,3,2,1,0:T(8,128)(2,1)S(1)} %slice.138), channel_id=1, source_target_pairs={{0,16},{4,20},{8,24},{12,28},{16,0},{20,4},{24,8},{28,12},{1,17},{... | collective-permute-start | bytes 786440 | tf_op jit(solution)/shard_map/ppermute | solution.py:26
  51.9 1.1 collective-permute-start.20
  53.7 11.3 %collective-permute-done.12 = bf16[2,1,4,128,128]{4,3,2,1,0:T(8,128)(2,1)S(1)} collective-permute-done((bf16[2,1,4,128,128]{4,3,2,1,0:T(8,128)(2,1)S(1)}, bf16[2,1,4,128,128]{4,3,2,1,0:T(8,128)(2,1)S(1)}, u32[]{:S(2)}, u32[]{:S(2)}) %collective-permute-start.12) | collective-permute-done | bytes 262176 | tf_op jit(solution)/shard_map/ppermute | solution.py:26
  65.8 1.1 collective-permute-start.18
  67.8 12.6 %collective-permute-done.16.far_ref = bf16[1,4,128,256]{3,2,1,0:T(8,128)(2,1)S(1)} collective-permute-done((bf16[1,4,128,256]{3,2,1,0:T(8,128)(2,1)S(1)}, bf16[1,4,128,256]{3,2,1,0:T(8,128)(2,1)S(1)}, u32[]{:S(2)}, u32[]{:S(2)}) %collective-permute-start.16) | collective-permute-done | bytes 262176 | tf_op jit(solution)/shard_map/ppermute | solution.py:26
  81.2 1.1 collective-permute-start.21
  82.5 1.1 collective-permute-start.13
  84.3 11.2 %collective-permute-done.19.far_ref = bf16[1,4,128,256]{3,2,1,0:T(8,128)(2,1)S(1)} collective-permute-done((bf16[1,4,128,256]{3,2,1,0:T(8,128)(2,1)S(1)}, bf16[1,4,128,256]{3,2,1,0:T(8,128)(2,1)S(1)}, u32[]{:S(2)}, u32[]{:S(2)}) %collective-permute-start.19) | collective-permute-done | bytes 262176 | tf_op jit(solution)/shard_map/ppermute | solution.py:26
  96.2 1.1 collective-permute-start.23
  98.3 6.2 %collective-permute-done.23 = bf16[2,4,128,128]{3,2,1,0:T(8,128)(2,1)S(1)} collective-permute-done((bf16[2,4,128,128]{3,2,1,0:T(8,128)(2,1)S(1)}, bf16[2,4,128,128]{3,2,1,0:T(8,128)(2,1)S(1)}, u32[]{:S(2)}, u32[]{:S(2)}) %collective-permute-start.23) | collective-permute-done | bytes 262176 | tf_op jit(solution)/shard_map/ppermute | solution.py:26
  104.7 1.9 %shard_map.80.so_far_ref = bf16[128,4096]{1,0:T(8,128)(2,1)} custom-call(s32[1]{0:T(128)} %bitcast.place_ref, bf16[128,4096]{1,0:T(8,128)(2,1)} %shard_map.78.so_far_ref, bf16[1,4,128,128]{3,2,1,0:T(8,128)(2,1)S(1)} %get-tuple-element.80.near_ref, bf16[1,4,128,128]{3,2,1,0:T(8,128)(2,1)S(1)} %collective-permute-done.13.far_ref), custom_call_target="tpu_custom_call", output_to_operand_aliasing={{}: (1, {})} | custom-call | bytes 1000000 | tf_op jit(solution)/shard_map/pallas_call | solution.py:318
  106.6 2.0 %shard_map.83.so_far_ref = bf16[128,4096]{1,0:T(8,128)(2,1)} custom-call(s32[1]{0:T(128)} %bitcast.place_ref, bf16[128,4096]{1,0:T(8,128)(2,1)} %shard_map.80.so_far_ref, bf16[1,4,128,256]{3,2,1,0:T(8,128)(2,1)S(1)} %get-tuple-element.70.near_ref, bf16[1,4,128,256]{3,2,1,0:T(8,128)(2,1)S(1)} %collective-permute-done.16.far_ref), custom_call_target="tpu_custom_call", output_to_operand_aliasing={{}: (1, {})} | custom-call | bytes 1000000 | tf_op jit(solution)/shard_map/pallas_call | solution.py:318
  108.6 2.0 %shard_map.86.so_far_ref = bf16[128,4096]{1,0:T(8,128)(2,1)} custom-call(s32[1]{0:T(128)} %bitcast.place_ref, bf16[128,4096]{1,0:T(8,128)(2,1)} %shard_map.83.so_far_ref, bf16[1,4,128,256]{3,2,1,0:T(8,128)(2,1)S(1)} %get-tuple-element.68.near_ref, bf16[1,4,128,256]{3,2,1,0:T(8,128)(2,1)S(1)} %collective-permute-done.19.far_ref), custom_call_target="tpu_custom_call", output_to_operand_aliasing={{}: (1, {})} | custom-call | bytes 1000000 | tf_op jit(solution)/shard_map/pallas_call | solution.py:318
  110.6 4.2 %collective-permute-done.22.far_ref = bf16[1,4,128,256]{3,2,1,0:T(8,128)(2,1)S(1)} collective-permute-done((bf16[1,4,128,256]{3,2,1,0:T(8,128)(2,1)S(1)}, bf16[1,4,128,256]{3,2,1,0:T(8,128)(2,1)S(1)}, u32[]{:S(2)}, u32[]{:S(2)}) %collective-permute-start.22) | collective-permute-done | bytes 262176 | tf_op jit(solution)/shard_map/ppermute | solution.py:26
  114.8 2.0 %shard_map.89.so_far_ref = bf16[128,4096]{1,0:T(8,128)(2,1)} custom-call(s32[1]{0:T(128)} %bitcast.place_ref, bf16[128,4096]{1,0:T(8,128)(2,1)} %shard_map.86.so_far_ref, bf16[1,4,128,256]{3,2,1,0:T(8,128)(2,1)S(1)} %get-tuple-element.64.near_ref, bf16[1,4,128,256]{3,2,1,0:T(8,128)(2,1)S(1)} %collective-permute-done.22.far_ref), custom_call_target="tpu_custom_call", output_to_operand_aliasing={{}: (1, {})} | custom-call | bytes 1000000 | tf_op jit(solution)/shard_map/pallas_call | solution.py:318
  117.5 1.9 %shard_map.92 = bf16[128,4096]{1,0:T(8,128)(2,1)} custom-call(s32[1]{0:T(128)} %bitcast.place_ref, bf16[128,4096]{1,0:T(8,128)(2,1)} %shard_map.89.so_far_ref, bf16[1,4,128,128]{3,2,1,0:T(8,128)(2,1)S(1)} %get-tuple-element.74.near_ref, bf16[1,4,128,128]{3,2,1,0:T(8,128)(2,1)S(1)} %collective-permute-done.24.far_ref), custom_call_target="tpu_custom_call", output_to_operand_aliasing={{}: (1, {})} | custom-call | bytes 1000000 | tf_op jit(solution)/shard_map/pallas_call | solution.py:318
  (76 shorter events, 12.2 us)
Async XLA Ops:
  0.0 8.6 %collective-permute-start.2 = (s32[1,128]{1,0:T(1,128)}, s32[1,128]{1,0:T(1,128)S(1)}, u32[]{:S(2)}, u32[]{:S(2)}) collective-permute-start(s32[1,128]{1,0:T(1,128)} %ids_ref), channel_id=1, source_target_pairs={{0,24},{4,28},{8,16},{12,20},{16,8},{20,12},{24,0},{28,4},{1,25},{... | collective-permute-start | bytes 1544 | tf_op jit(solution)/shard_map/ppermute | solution.py:26
  5.0 3.7 %collective-permute-start.1 = (s32[1,128]{1,0:T(1,128)}, s32[1,128]{1,0:T(1,128)S(1)}, u32[]{:S(2)}, u32[]{:S(2)}) collective-permute-start(s32[1,128]{1,0:T(1,128)} %ids_ref), channel_id=1, source_target_pairs={{0,8},{4,12},{8,0},{12,4},{16,24},{20,28},{24,16},{28,20},{1,9},{5... | collective-permute-start | bytes 1544 | tf_op jit(solution)/shard_map/ppermute | solution.py:26
  5.1 4.6 %collective-permute-start = (s32[1,128]{1,0:T(1,128)}, s32[1,128]{1,0:T(1,128)S(1)}, u32[]{:S(2)}, u32[]{:S(2)}) collective-permute-start(s32[1,128]{1,0:T(1,128)} %ids_ref), channel_id=1, source_target_pairs={{0,16},{4,20},{8,24},{12,28},{16,0},{20,4},{24,8},{28,12},{1,17},{... | collective-permute-start | bytes 1544 | tf_op jit(solution)/shard_map/ppermute | solution.py:26
  5.6 2.2 %copy-start.5 = (bf16[32,128]{1,0:T(8,128)(2,1)S(1)}, bf16[32,128]{1,0:T(8,128)(2,1)}, u32[]{:S(2)}) copy-start(bf16[32,128]{1,0:T(8,128)(2,1)} %param.12) | copy-start | bytes 24580
  5.6 4.0 %copy-start.3 = (s32[1,128]{1,0:T(1,128)S(1)}, s32[1,128]{1,0:T(1,128)}, u32[]{:S(2)}) copy-start(s32[1,128]{1,0:T(1,128)} %ids_ref) | copy-start | bytes 1540
  5.6 9.3 %copy-start.2 = (f32[4096]{0:T(1024)S(1)}, f32[4096]{0:T(1024)}, u32[]{:S(2)}) copy-start(f32[4096]{0:T(1024)} %param.9) | copy-start | bytes 49156
  9.6 3.7 %collective-permute-start.3 = (s32[4,128]{1,0:T(4,128)S(1)}, s32[4,128]{1,0:T(4,128)S(1)}, u32[]{:S(2)}, u32[]{:S(2)}) collective-permute-start(s32[4,128]{1,0:T(4,128)S(1)} %pad_add_fusion.3), channel_id=1, source_target_pairs={{0,4},{4,0},{8,12},{12,8},{16,20},{20,16},{24,28},{28,24},{1,5},{5... | collective-permute-start | bytes 6152 | tf_op jit(solution)/shard_map/ppermute | solution.py:26
  11.2 15.8 %collective-permute-start.6 = (bf16[512,512]{1,0:T(8,128)(2,1)}, bf16[512,512]{1,0:T(8,128)(2,1)S(1)}, u32[]{:S(2)}, u32[]{:S(2)}) collective-permute-start(bf16[512,512]{1,0:T(8,128)(2,1)} %get-tuple-element.40), channel_id=1, source_target_pairs={{0,8},{4,12},{8,0},{12,4},{16,24},{20,28},{24,16},{28,20},{1,9},{5... | collective-permute-start | bytes 1572872 | tf_op jit(solution)/shard_map/ppermute | solution.py:26
  13.2 21.4 %collective-permute-start.8 = (bf16[512,512]{1,0:T(8,128)(2,1)}, bf16[512,512]{1,0:T(8,128)(2,1)S(1)}, u32[]{:S(2)}, u32[]{:S(2)}) collective-permute-start(bf16[512,512]{1,0:T(8,128)(2,1)} %get-tuple-element.47), channel_id=1, source_target_pairs={{0,8},{4,12},{8,0},{12,4},{16,24},{20,28},{24,16},{28,20},{1,9},{5... | collective-permute-start | bytes 1572872 | tf_op jit(solution)/shard_map/ppermute | solution.py:26
  13.3 13.6 %collective-permute-start.5 = (s32[8,128]{1,0:T(8,128)S(1)}, s32[8,128]{1,0:T(8,128)S(1)}, u32[]{:S(2)}, u32[]{:S(2)}) collective-permute-start(s32[8,128]{1,0:T(8,128)S(1)} %pad_add_fusion.2), channel_id=1, source_target_pairs={{0,1},{1,2},{2,3},{3,0},{4,5},{5,6},{6,7},{7,4},{8,9},{9,10},{10,1... | collective-permute-start | bytes 12296 | tf_op jit(solution)/shard_map/ppermute | solution.py:21
  13.4 13.5 %collective-permute-start.4 = (s32[8,128]{1,0:T(8,128)S(1)}, s32[8,128]{1,0:T(8,128)S(1)}, u32[]{:S(2)}, u32[]{:S(2)}) collective-permute-start(s32[8,128]{1,0:T(8,128)S(1)} %pad_add_fusion.2), channel_id=1, source_target_pairs={{0,2},{1,3},{2,0},{3,1},{4,6},{5,7},{6,4},{7,5},{8,10},{9,11},{10,... | collective-permute-start | bytes 12296 | tf_op jit(solution)/shard_map/ppermute | solution.py:21
  14.9 2.2 %copy-start.1 = (bf16[512,4096]{1,0:T(8,128)(2,1)S(1)}, bf16[512,4096]{1,0:T(8,128)(2,1)}, u32[]{:S(2)}) copy-start(bf16[512,4096]{1,0:T(8,128)(2,1)} %rows_ref.1) | copy-start | bytes 12582916
  17.1 10.7 %copy-start.4 = (f32[3,3,512]{2,1,0:T(4,128)S(1)}, f32[3,3,512]{2,1,0:T(4,128)}, u32[]{:S(2)}) copy-start(f32[3,3,512]{2,1,0:T(4,128)} %short_ref.3) | copy-start | bytes 55300
  27.0 14.1 %collective-permute-start.7 = (bf16[512,512]{1,0:T(8,128)(2,1)S(1)}, bf16[512,512]{1,0:T(8,128)(2,1)S(1)}, u32[]{:S(2)}, u32[]{:S(2)}) collective-permute-start(bf16[512,512]{1,0:T(8,128)(2,1)S(1)} %collective-permute-done.6), channel_id=1, source_target_pairs={{0,2},{1,3},{2,0},{3,1},{4,6},{5,7},{6,4},{7,5},{8,10},{9,11},{10,... | collective-permute-start | bytes 1572872 | tf_op jit(solution)/shard_map/ppermute | solution.py:26
  32.3 14.8 %collective-permute-start.10 = (bf16[4,128,512]{2,1,0:T(8,128)(2,1)S(1)}, bf16[4,128,512]{2,1,0:T(8,128)(2,1)S(1)}, u32[]{:S(2)}, u32[]{:S(2)}) collective-permute-start(bf16[4,128,512]{2,1,0:T(8,128)(2,1)S(1)} %shard_map.76), channel_id=1, source_target_pairs={{0,8},{4,12},{8,0},{12,4},{16,24},{20,28},{24,16},{28,20},{1,9},{5... | collective-permute-start | bytes 1572872 | tf_op jit(solution)/shard_map/ppermute | solution.py:26
  34.6 6.8 %collective-permute-start.9 = (bf16[512,512]{1,0:T(8,128)(2,1)S(1)}, bf16[512,512]{1,0:T(8,128)(2,1)S(1)}, u32[]{:S(2)}, u32[]{:S(2)}) collective-permute-start(bf16[512,512]{1,0:T(8,128)(2,1)S(1)} %collective-permute-done.8), channel_id=1, source_target_pairs={{0,1},{1,0},{2,3},{3,2},{4,5},{5,4},{6,7},{7,6},{8,9},{9,8},{10,11... | collective-permute-start | bytes 1572872 | tf_op jit(solution)/shard_map/ppermute | solution.py:26
  41.3 5.8 %collective-permute-start.11 = (bf16[2,512,256]{2,1,0:T(8,128)(2,1)S(1)}, bf16[2,512,256]{2,1,0:T(8,128)(2,1)S(1)}, u32[]{:S(2)}, u32[]{:S(2)}) collective-permute-start(bf16[2,512,256]{2,1,0:T(8,128)(2,1)S(1)} %get-tuple-element.72.refs_4_), channel_id=1, source_target_pairs={{0,1},{1,0},{2,3},{3,2},{4,5},{5,4},{6,7},{7,6},{8,9},{9,8},{10,11... | collective-permute-start | bytes 1572872 | tf_op jit(solution)/shard_map/ppermute | solution.py:26
  41.5 5.6 %copy-start = (bf16[512,4096]{1,0:T(8,128)(2,1)S(1)}, bf16[512,4096]{1,0:T(8,128)(2,1)}, u32[]{:S(2)}) copy-start(bf16[512,4096]{1,0:T(8,128)(2,1)} %refs_3_.17) | copy-start | bytes 12582916
  44.2 4.4 %collective-permute-start.14 = (bf16[2,512,256]{2,1,0:T(8,128)(2,1)S(1)}, bf16[2,512,256]{2,1,0:T(8,128)(2,1)S(1)}, u32[]{:S(2)}, u32[]{:S(2)}) collective-permute-start(bf16[2,512,256]{2,1,0:T(8,128)(2,1)S(1)} %get-tuple-element.71.refs_4_), channel_id=1, source_target_pairs={{0,1},{1,0},{2,3},{3,2},{4,5},{5,4},{6,7},{7,6},{8,9},{9,8},{10,11... | collective-permute-start | bytes 1572872 | tf_op jit(solution)/shard_map/ppermute | solution.py:26
  44.8 20.3 %collective-permute-start.17 = (bf16[2,512,256]{2,1,0:T(8,128)(2,1)S(1)}, bf16[2,512,256]{2,1,0:T(8,128)(2,1)S(1)}, u32[]{:S(2)}, u32[]{:S(2)}) collective-permute-start(bf16[2,512,256]{2,1,0:T(8,128)(2,1)S(1)} %get-tuple-element.66.refs_4_), channel_id=1, source_target_pairs={{0,2},{1,3},{2,0},{3,1},{4,6},{5,7},{6,4},{7,5},{8,10},{9,11},{10,... | collective-permute-start | bytes 1572872 | tf_op jit(solution)/shard_map/ppermute | solution.py:26
  49.3 17.5 %collective-permute-start.15 = (bf16[2,4,128,256]{3,2,1,0:T(8,128)(2,1)S(1)}, bf16[2,4,128,256]{3,2,1,0:T(8,128)(2,1)S(1)}, u32[]{:S(2)}, u32[]{:S(2)}) collective-permute-start(bf16[2,4,128,256]{3,2,1,0:T(8,128)(2,1)S(1)} %shard_map.82), channel_id=1, source_target_pairs={{0,4},{4,0},{8,12},{12,8},{16,20},{20,16},{24,28},{28,24},{1,5},{5... | collective-permute-start | bytes 1572872 | tf_op jit(solution)/shard_map/ppermute | solution.py:26
  50.4 14.6 %collective-permute-start.12 = (bf16[2,1,4,128,128]{4,3,2,1,0:T(8,128)(2,1)S(1)}, bf16[2,1,4,128,128]{4,3,2,1,0:T(8,128)(2,1)S(1)}, u32[]{:S(2)}, u32[]{:S(2)}) collective-permute-start(bf16[2,1,4,128,128]{4,3,2,1,0:T(8,128)(2,1)S(1)} %slice.138), channel_id=1, source_target_pairs={{0,16},{4,20},{8,24},{12,28},{16,0},{20,4},{24,8},{28,12},{1,17},{... | collective-permute-start | bytes 786440 | tf_op jit(solution)/shard_map/ppermute | solution.py:26
  51.9 28.5 %collective-permute-start.20 = (bf16[2,512,256]{2,1,0:T(8,128)(2,1)S(1)}, bf16[2,512,256]{2,1,0:T(8,128)(2,1)S(1)}, u32[]{:S(2)}, u32[]{:S(2)}) collective-permute-start(bf16[2,512,256]{2,1,0:T(8,128)(2,1)S(1)} %get-tuple-element.59.refs_4_), channel_id=1, source_target_pairs={{0,2},{1,3},{2,0},{3,1},{4,6},{5,7},{6,4},{7,5},{8,10},{9,11},{10,... | collective-permute-start | bytes 1572872 | tf_op jit(solution)/shard_map/ppermute | solution.py:26
  65.8 16.5 %collective-permute-start.18 = (bf16[2,4,128,256]{3,2,1,0:T(8,128)(2,1)S(1)}, bf16[2,4,128,256]{3,2,1,0:T(8,128)(2,1)S(1)}, u32[]{:S(2)}, u32[]{:S(2)}) collective-permute-start(bf16[2,4,128,256]{3,2,1,0:T(8,128)(2,1)S(1)} %shard_map.85), channel_id=1, source_target_pairs={{0,4},{4,0},{8,12},{12,8},{16,20},{20,16},{24,28},{28,24},{1,5},{5... | collective-permute-start | bytes 1572872 | tf_op jit(solution)/shard_map/ppermute | solution.py:26
  67.0 13.5 %collective-permute-start.16 = (bf16[1,4,128,256]{3,2,1,0:T(8,128)(2,1)S(1)}, bf16[1,4,128,256]{3,2,1,0:T(8,128)(2,1)S(1)}, u32[]{:S(2)}, u32[]{:S(2)}) collective-permute-start(bf16[1,4,128,256]{3,2,1,0:T(8,128)(2,1)S(1)} %get-tuple-element.69), channel_id=1, source_target_pairs={{0,16},{4,20},{8,24},{12,28},{16,0},{20,4},{24,8},{28,12},{1,17},{... | collective-permute-start | bytes 786440 | tf_op jit(solution)/shard_map/ppermute | solution.py:26
  81.2 16.9 %collective-permute-start.21 = (bf16[2,4,128,256]{3,2,1,0:T(8,128)(2,1)S(1)}, bf16[2,4,128,256]{3,2,1,0:T(8,128)(2,1)S(1)}, u32[]{:S(2)}, u32[]{:S(2)}) collective-permute-start(bf16[2,4,128,256]{3,2,1,0:T(8,128)(2,1)S(1)} %shard_map.88), channel_id=1, source_target_pairs={{0,4},{4,0},{8,12},{12,8},{16,20},{20,16},{24,28},{28,24},{1,5},{5... | collective-permute-start | bytes 1572872 | tf_op jit(solution)/shard_map/ppermute | solution.py:26
  82.4 13.1 %collective-permute-start.19 = (bf16[1,4,128,256]{3,2,1,0:T(8,128)(2,1)S(1)}, bf16[1,4,128,256]{3,2,1,0:T(8,128)(2,1)S(1)}, u32[]{:S(2)}, u32[]{:S(2)}) collective-permute-start(bf16[1,4,128,256]{3,2,1,0:T(8,128)(2,1)S(1)} %get-tuple-element.67), channel_id=1, source_target_pairs={{0,16},{4,20},{8,24},{12,28},{16,0},{20,4},{24,8},{28,12},{1,17},{... | collective-permute-start | bytes 786440 | tf_op jit(solution)/shard_map/ppermute | solution.py:26
  82.5 22.2 %collective-permute-start.13 = (bf16[1,4,128,128]{3,2,1,0:T(8,128)(2,1)S(1)}, bf16[1,4,128,128]{3,2,1,0:T(8,128)(2,1)S(1)}, u32[]{:S(2)}, u32[]{:S(2)}) collective-permute-start(bf16[1,4,128,128]{3,2,1,0:T(8,128)(2,1)S(1)} %get-tuple-element.79), channel_id=1, source_target_pairs={{0,4},{4,0},{8,12},{12,8},{16,20},{20,16},{24,28},{28,24},{1,5},{5... | collective-permute-start | bytes 393224 | tf_op jit(solution)/shard_map/ppermute | solution.py:26
  96.2 8.3 %collective-permute-start.23 = (bf16[2,4,128,128]{3,2,1,0:T(8,128)(2,1)S(1)}, bf16[2,4,128,128]{3,2,1,0:T(8,128)(2,1)S(1)}, u32[]{:S(2)}, u32[]{:S(2)}) collective-permute-start(bf16[2,4,128,128]{3,2,1,0:T(8,128)(2,1)S(1)} %shard_map.91), channel_id=1, source_target_pairs={{0,4},{4,0},{8,12},{12,8},{16,20},{20,16},{24,28},{28,24},{1,5},{5... | collective-permute-start | bytes 786440 | tf_op jit(solution)/shard_map/ppermute | solution.py:26
  98.2 16.6 %collective-permute-start.22 = (bf16[1,4,128,256]{3,2,1,0:T(8,128)(2,1)S(1)}, bf16[1,4,128,256]{3,2,1,0:T(8,128)(2,1)S(1)}, u32[]{:S(2)}, u32[]{:S(2)}) collective-permute-start(bf16[1,4,128,256]{3,2,1,0:T(8,128)(2,1)S(1)} %get-tuple-element.63), channel_id=1, source_target_pairs={{0,16},{4,20},{8,24},{12,28},{16,0},{20,4},{24,8},{28,12},{1,17},{... | collective-permute-start | bytes 786440 | tf_op jit(solution)/shard_map/ppermute | solution.py:26
  104.6 12.9 %collective-permute-start.24 = (bf16[1,4,128,128]{3,2,1,0:T(8,128)(2,1)S(1)}, bf16[1,4,128,128]{3,2,1,0:T(8,128)(2,1)S(1)}, u32[]{:S(2)}, u32[]{:S(2)}) collective-permute-start(bf16[1,4,128,128]{3,2,1,0:T(8,128)(2,1)S(1)} %get-tuple-element.73), channel_id=1, source_target_pairs={{0,16},{4,20},{8,24},{12,28},{16,0},{20,4},{24,8},{28,12},{1,17},{... | collective-permute-start | bytes 393224 | tf_op jit(solution)/shard_map/ppermute | solution.py:26

commit v11 on v9

--- a/solution.py
+++ b/solution.py
@@ -12,7 +12,7 @@
 SHORT = 3
 LANES = 128
 LEAD = 16
-SPLITS = ((0, 8, (0, 2, 1, 3), ((0, 4), (4, 4))), (8, 8, (0, 1, 2, 3), ((0, 4), (4, 4))))
+SPLITS = ((0, 8, (0, 2, 1, 3), ((0, 2), (4, 4), (2, 2))), (8, 8, (0, 1, 2, 3), ((0, 4), (4, 4))))
 SIXTEENTHS = 16
 
 
@@ -354,46 +354,67 @@
 
     part = ids.shape[0] // 4
     quarters = [ids[n * part : (n + 1) * part] for n in range(4)]
-    sent = mix(jnp.concatenate([quarters[3], quarters[1]], axis=0), table, short_taps, toeplitz, tok_len)
-    kept, sent = tie((jnp.concatenate([quarters[2], quarters[0]], axis=0), sent))
-    other = swap(sent, "fsdp", beside_bit)
-    mine = mix(kept, table, short_taps, toeplitz, tok_len)
+    sent = mix(quarters[3], table, short_taps, toeplitz, tok_len)
+    kept, sent = tie((jnp.concatenate([quarters[1], quarters[2], quarters[0]], axis=0), sent))
+    other = [swap(sent, "fsdp", beside_bit)]
+    gated = mix(kept, table, short_taps, toeplitz, tok_len)
+    gated, early_pair = tie((gated, early_pair))
+    other.append(swap(gated[:part], "fsdp", beside_bit))
+    mine = [gated[part : 2 * part], gated[2 * part :]]
     middle = early.shape[1] // 2
-    mine, early_pair = tie((mine, early_pair))
     pairs = [(columns, swap(columns, "ctx", 1)) for columns in (early_pair[:, :, :middle], early_pair[:, :, middle:])]
     late_pair = jnp.stack([late, swap(late, "ctx", 1)])
-    halves = [late_pair[:, :, :middle], late_pair[:, :, middle:]]
-
-    out = residual(token_ids, embedding)
-    (head, body), tail = SPLITS[0][3], SPLITS[1][3]
-    total = panel(at, mine, other, out_proj, pairs[0], SPLITS[0], head)
-    mine, out, halves, total = tie((mine, out, halves, total))
-    mine, other = (mine[:part], mine[part:]), (other[:part], other[part:])
-    total = total.reshape(2, part, *total.shape[1:])
-    for bit in reversed(bits[:-2]):
-        half = total.shape[1] // 2
-        total = add(total[:, :half], swap(total[:, half:], "fsdp", bit))
-    head_sum = (total[1], swap(total[0], "fsdp", bits[-1]), SPLITS[0], head)
-
-    behind = []
-    pairs = pairs[1:] + [(columns, swap(columns, "ctx", 2)) for columns in halves]
-    steps = [(SPLITS[0], body)] + [(SPLITS[1], step) for step in tail]
-    for pair, (split, step) in zip(pairs, steps):
-        begin = step[0]
+    own_ids, gated = tie((token_ids, gated))
+    out = residual(own_ids, embedding)
+    late_pair, out = tie((late_pair, out))
+    pairs += [(columns, swap(columns, "ctx", 2)) for columns in (late_pair[:, :, :middle],)]
+    (head, body, foot), tail = SPLITS[0][3], SPLITS[1][3]
+
+    def send(pair, split, step, begin):
         away = panel(at, mine[0], other[0], out_proj, pair, split, step, begin)
-        away, mine = tie((away, mine))
-        got = swap(away, "fsdp", bits[-1])
-        if behind:
-            got, _ = tie((got, behind[-1][-1]))
+        return away, swap(away, "fsdp", bits[-1])
+
+    def sum_up(pair, split, step, begin, got):
         total = panel(at, mine[1], other[1], out_proj, pair, split, step, begin)
         for bit in reversed(bits[:-2]):
             half = total.shape[0] // 2
             far = add(total[half:], got[half:])
             total, got = add(total[:half], got[:half]), swap(far, "fsdp", bit)
-        behind.append((total, got, split, step, far))
+        return far, (total, got, split, step)
+
+    chunk = (pairs[1], SPLITS[0], body, body[0])
+    away, got = send(*chunk)
+    other[1], late_rest, _ = tie((other[1], late_pair[:, :, middle:], away))
+    pairs.append((late_rest, swap(late_rest, "ctx", 2)))
+
+    all_mine, all_other = (jnp.concatenate(parts, axis=0) for parts in (mine, other))
+    total = panel(at, all_mine, all_other, out_proj, pairs[0], SPLITS[0], head)
+    other[1], total = tie((other[1], total))
+    total = total.reshape(2, part, *total.shape[1:])
+    head_got = swap(total[:, part // 2 :], "fsdp", bits[-3])
+
+    far, first_sum = sum_up(*chunk, got)
+    mine[0], _ = tie((mine[0], far))
+    head_got, _ = tie((head_got, far))
+    total = add(total[:, : part // 2], head_got)
+    for bit in reversed(bits[:-3]):
+        half = total.shape[1] // 2
+        total = add(total[:, :half], swap(total[:, half:], "fsdp", bit))
+    head_sum = (total[1], swap(total[0], "fsdp", bits[-1]), SPLITS[0], head)
+    sums = [first_sum]
+    for pair, split, step, begin in (
+        (pairs[2], SPLITS[1], tail[0], tail[0][0]),
+        (pairs[3], SPLITS[1], tail[1], tail[1][0]),
+        (pairs[0], SPLITS[0], foot, 0),
+    ):
+        away, got = send(pair, split, step, begin)
+        mine[0], away = tie((mine[0], away))
+        got, _ = tie((got, far))
+        far, one = sum_up(pair, split, step, begin, got)
+        sums.append(one)
     out = place_pieces(at, out, *head_sum)
-    for last in behind:
-        out = place_pieces(at, out, *last[:-1])
+    for one in sums:
+        out = place_pieces(at, out, *one)
     return out[None]
 
 

time: 116 us -> 118 us (1.017)
  Pallas kernels: 37.5 us -> 40.9 us
  waiting for transfers between devices: 47.5 us -> 45.2 us
    ppermute x21 -> x24, waiting for transfers between devices: 47.5 us -> 45.2 us  [swap(): return lax.ppermute(x, axis, [(i, i ^ mask) for i in range(peers)])]
    pallas_call x4 -> x5, Pallas kernels: 7.91 us -> 9.8 us  [place_pieces(): pl.pallas_call(functools.partial(place_kernel, split, step), grid_spec=pl...]
    pallas_call x7 -> x9, Pallas kernels: 5.5 us -> 7.11 us  [panel(): pl.pallas_call(panel_kernel, grid_spec=pltpu.PrefetchScalarGridSpec(num_s...]
    ppermute x21 -> x24, starting transfers between devices: 25.3 us -> 25.7 us  [swap(): return lax.ppermute(x, axis, [(i, i ^ mask) for i in range(peers)])]
  transfers between devices with their start and end apart: 23 -> 26, of which waited for: 11 -> 12; matrix products, arithmetic and copies ran while one was open for 1% -> 1% of each run, Pallas kernels for 31% -> 33%
where the time goes in v11:
time: 118 us; the launch traced here: 117 us
  waiting for transfers between devices  45.2 us (38%)
  Pallas kernels  40.9 us (35%)
  starting transfers between devices  27.3 us (23%)
  local copies, waits for them, and re-layouts  2.68 us (2%)
    ppermute x24, waiting for transfers between devices, swap(): return lax.ppermute(x, axis, [(i, i ^ mask) for i in range(peers)])  45.2 us
    ppermute x24, starting transfers between devices, swap(): return lax.ppermute(x, axis, [(i, i ^ mask) for i in range(peers)])  25.7 us
    pallas_call x5, Pallas kernels, place_pieces(): pl.pallas_call(functools.partial(place_kernel, split, step), grid_spec=pl...  9.8 us
    pallas_call x1, Pallas kernels, project(): pl.pallas_call(table_kernel, grid=(1,), in_specs=[hbm, hbm, pl.BlockSpec(...  9.73 us
    pallas_call x2, Pallas kernels, mix(): pl.pallas_call(mixer_kernel, grid=(windows // 2,), in_specs=[pl.BlockSpec...  8.77 us
    pallas_call x9, Pallas kernels, panel(): pl.pallas_call(panel_kernel, grid_spec=pltpu.PrefetchScalarGridSpec(num_s...  7.11 us
    pallas_call x1, Pallas kernels, residual(): pl.pallas_call(residual_kernel, grid=(4,), in_specs=[whole(token_ids), pl...  2.66 us
  transfers between devices with their start and end apart: 26, of which 12 were waited for; matrix products, arithmetic and copies ran while one was open for 1% of the time, Pallas kernels for 33%

profile of v11, /device:TPU:0, one launch (start us, length us, event | category | flops | bytes accessed | tf_op | source)
XLA Modules:
  0.0 117.4 jit_solution(1911218474645761331)
XLA Ops:
  0.0 5.0 %collective-permute-start.4 = (s32[1,128]{1,0:T(1,128)}, s32[1,128]{1,0:T(1,128)S(1)}, u32[]{:S(2)}, u32[]{:S(2)}) collective-permute-start(s32[1,128]{1,0:T(1,128)} %ids_ref), channel_id=1, source_target_pairs={{0,24},{4,28},{8,16},{12,20},{16,8},{20,12},{24,0},{28,4},{1,25},{... | collective-permute-start | bytes 1544 | tf_op jit(solution)/shard_map/ppermute | solution.py:26
  5.6 2.2 %shard_map.73 = (bf16[512,512]{1,0:T(8,128)(2,1)}, bf16[512,512]{1,0:T(8,128)(2,1)}) custom-call(s32[1]{0:T(128)} %bitcast.place_ref, bf16[512,4096]{1,0:T(8,128)(2,1)} %refs_3_.17, bf16[512,4096]{1,0:T(8,128)(2,1)} %refs_3_.17), custom_call_target="tpu_custom_call" | custom-call | bytes 2000000 | tf_op jit(solution)/shard_map/pallas_call | solution.py:200
  8.7 0.9 collective-permute-done.2
  9.6 1.6 %collective-permute-start.5 = (s32[4,128]{1,0:T(4,128)S(1)}, s32[4,128]{1,0:T(4,128)S(1)}, u32[]{:S(2)}, u32[]{:S(2)}) collective-permute-start(s32[4,128]{1,0:T(4,128)S(1)} %pad_add_fusion.4), channel_id=1, source_target_pairs={{0,4},{4,0},{8,12},{12,8},{16,20},{20,16},{24,28},{28,24},{1,5},{5... | collective-permute-start | bytes 6152 | tf_op jit(solution)/shard_map/ppermute | solution.py:26
  11.2 2.0 %collective-permute-start = (bf16[512,512]{1,0:T(8,128)(2,1)}, bf16[512,512]{1,0:T(8,128)(2,1)S(1)}, u32[]{:S(2)}, u32[]{:S(2)}) collective-permute-start(bf16[512,512]{1,0:T(8,128)(2,1)} %get-tuple-element.36), channel_id=1, source_target_pairs={{0,8},{4,12},{8,0},{12,4},{16,24},{20,28},{24,16},{28,20},{1,9},{5... | collective-permute-start | bytes 1572872 | tf_op jit(solution)/shard_map/ppermute | solution.py:26
  13.4 1.6 %collective-permute-start.6 = (s32[8,128]{1,0:T(8,128)S(1)}, s32[8,128]{1,0:T(8,128)S(1)}, u32[]{:S(2)}, u32[]{:S(2)}) collective-permute-start(s32[8,128]{1,0:T(8,128)S(1)} %pad_add_fusion.2), channel_id=1, source_target_pairs={{0,2},{1,3},{2,0},{3,1},{4,6},{5,7},{6,4},{7,5},{8,10},{9,11},{10,... | collective-permute-start | bytes 12296 | tf_op jit(solution)/shard_map/ppermute | solution.py:21
  14.9 2.2 %copy-done.1 = bf16[512,4096]{1,0:T(8,128)(2,1)S(1)} copy-done((bf16[512,4096]{1,0:T(8,128)(2,1)S(1)}, bf16[512,4096]{1,0:T(8,128)(2,1)}, u32[]{:S(2)}) %copy-start.1) | copy-done | bytes 4194328
  17.1 9.7 %shard_map.75.table_ref = bf16[3,512,512]{2,1,0:T(8,128)(2,1)S(1)} custom-call(bf16[512,4096]{1,0:T(8,128)(2,1)S(1)} %copy-done.1, bf16[3,4096,512]{2,1,0:T(8,128)(2,1)} %weight_hbm.1, f32[1,4096]{1,0:T(1,128)S(1)} %bitcast.43), custom_call_target="tpu_custom_call" | custom-call | flops 3000000000 | tf_op jit(solution)/shard_map/pallas_call | solution.py:101
  27.0 7.7 %collective-permute-done.8 = bf16[512,512]{1,0:T(8,128)(2,1)S(1)} collective-permute-done((bf16[512,512]{1,0:T(8,128)(2,1)}, bf16[512,512]{1,0:T(8,128)(2,1)S(1)}, u32[]{:S(2)}, u32[]{:S(2)}) %collective-permute-start.8) | collective-permute-done | bytes 524320 | tf_op jit(solution)/shard_map/ppermute | solution.py:26
  34.6 1.5 %collective-permute-start.9 = (bf16[512,512]{1,0:T(8,128)(2,1)S(1)}, bf16[512,512]{1,0:T(8,128)(2,1)S(1)}, u32[]{:S(2)}, u32[]{:S(2)}) collective-permute-start(bf16[512,512]{1,0:T(8,128)(2,1)S(1)} %collective-permute-done.8), channel_id=1, source_target_pairs={{0,2},{1,3},{2,0},{3,1},{4,6},{5,7},{6,4},{7,5},{8,10},{9,11},{10,... | collective-permute-start | bytes 1572872 | tf_op jit(solution)/shard_map/ppermute | solution.py:26
  36.3 2.2 %shard_map.76 = bf16[2,128,512]{2,1,0:T(8,128)(2,1)S(1)} custom-call(s32[2,1,272]{2,1,0:T(1,128)S(1)} %copy.13.ids_ref, bf16[3,512,512]{2,1,0:T(8,128)(2,1)S(1)} %shard_map.75.table_ref, f32[3,3,512]{2,1,0:T(4,128)S(1)} %copy-done.4, bf16[4,1024,256]{2,1,0:T(8,128)(2,1)S(1)} %shard_map.74.toeplitz), custom_call_target="tpu_custom_call" | custom-call | flops 1500000000 | tf_op jit(solution)/shard_map/pallas_call | solution.py:167
  38.5 1.8 %collective-permute-start.11 = (bf16[2,128,512]{2,1,0:T(8,128)(2,1)S(1)}, bf16[2,128,512]{2,1,0:T(8,128)(2,1)S(1)}, u32[]{:S(2)}, u32[]{:S(2)}) collective-permute-start(bf16[2,128,512]{2,1,0:T(8,128)(2,1)S(1)} %shard_map.76), channel_id=1, source_target_pairs={{0,8},{4,12},{8,0},{12,4},{16,24},{20,28},{24,16},{28,20},{1,9},{5... | collective-permute-start | bytes 786440 | tf_op jit(solution)/shard_map/ppermute | solution.py:26
  40.3 6.6 %shard_map.77 = bf16[6,128,512]{2,1,0:T(8,128)(2,1)S(1)} custom-call(s32[6,1,272]{2,1,0:T(1,128)S(1)} %reshape.54.ids_ref, bf16[3,512,512]{2,1,0:T(8,128)(2,1)S(1)} %shard_map.75.table_ref, f32[3,3,512]{2,1,0:T(4,128)S(1)} %copy-done.4, bf16[4,1024,256]{2,1,0:T(8,128)(2,1)S(1)} %shard_map.74.toeplitz), custom_call_target="tpu_custom_call" | custom-call | flops 1500000000 | tf_op jit(solution)/shard_map/pallas_call | solution.py:167
  47.8 2.7 %shard_map.78.so_far_ref = bf16[128,4096]{1,0:T(8,128)(2,1)} custom-call(s32[1,128]{1,0:T(1,128)S(1)} %copy-done.3, bf16[512,4096]{1,0:T(8,128)(2,1)S(1)} %copy-done.1), custom_call_target="tpu_custom_call" | custom-call | flops 400000000 | tf_op jit(solution)/shard_map/pallas_call | solution.py:290
  51.0 1.2 %collective-permute-start.18 = (bf16[2,512,256]{2,1,0:T(8,128)(2,1)S(1)}, bf16[2,512,256]{2,1,0:T(8,128)(2,1)S(1)}, u32[]{:S(2)}, u32[]{:S(2)}) collective-permute-start(bf16[2,512,256]{2,1,0:T(8,128)(2,1)S(1)} %get-tuple-element.67.refs_4_), channel_id=1, source_target_pairs={{0,2},{1,3},{2,0},{3,1},{4,6},{5,7},{6,4},{7,5},{8,10},{9,11},{10,... | collective-permute-start | bytes 1572872 | tf_op jit(solution)/shard_map/ppermute | solution.py:26
  53.5 5.4 %collective-permute-done.10 = bf16[2,128,512]{2,1,0:T(8,128)(2,1)S(1)} collective-permute-done((bf16[2,128,512]{2,1,0:T(8,128)(2,1)S(1)}, bf16[2,128,512]{2,1,0:T(8,128)(2,1)S(1)}, u32[]{:S(2)}, u32[]{:S(2)}) %collective-permute-start.10) | collective-permute-done | bytes 262176 | tf_op jit(solution)/shard_map/ppermute | solution.py:26
  59.5 1.4 %shard_map.80 = bf16[4,4,128,128]{3,2,1,0:T(8,128)(2,1)S(1)} custom-call(s32[1]{0:T(128)} %bitcast.place_ref, bf16[512,512]{1,0:T(8,128)(2,1)S(1)} %bitcast.41, bf16[512,512]{1,0:T(8,128)(2,1)S(1)} %bitcast.42, bf16[512,4096]{1,0:T(8,128)(2,1)S(1)} %copy-done, bf16[512,4096]{1,0:T(8,128)(2,1)S(1)} %copy-done, bf16[512,4096]{1,0:T(8,128)(2,1)S(1)} %copy-done, ...), custom_call_target="tpu_custom_call" | custom-call | flops 400000000 | tf_op jit(solution)/shard_map/pallas_call | solution.py:264
  60.9 2.9 %collective-permute-start.14 = (bf16[2,1,4,128,128]{4,3,2,1,0:T(8,128)(2,1)S(1)}, bf16[2,1,4,128,128]{4,3,2,1,0:T(8,128)(2,1)S(1)}, u32[]{:S(2)}, u32[]{:S(2)}) collective-permute-start(bf16[2,1,4,128,128]{4,3,2,1,0:T(8,128)(2,1)S(1)} %slice.129), channel_id=1, source_target_pairs={{0,16},{4,20},{8,24},{12,28},{16,0},{20,4},{24,8},{28,12},{1,17},{... | collective-permute-start | bytes 786440 | tf_op jit(solution)/shard_map/ppermute | solution.py:26
  64.4 0.8 shard_map.90
  66.9 3.2 %collective-permute-start.17 = (bf16[1,4,128,256]{3,2,1,0:T(8,128)(2,1)S(1)}, bf16[1,4,128,256]{3,2,1,0:T(8,128)(2,1)S(1)}, u32[]{:S(2)}, u32[]{:S(2)}) collective-permute-start(bf16[1,4,128,256]{3,2,1,0:T(8,128)(2,1)S(1)} %get-tuple-element.70), channel_id=1, source_target_pairs={{0,16},{4,20},{8,24},{12,28},{16,0},{20,4},{24,8},{28,12},{1,17},{... | collective-permute-start | bytes 786440 | tf_op jit(solution)/shard_map/ppermute | solution.py:26
  71.4 5.2 %collective-permute-done.21.refs_5_ = bf16[2,512,256]{2,1,0:T(8,128)(2,1)S(1)} collective-permute-done((bf16[2,512,256]{2,1,0:T(8,128)(2,1)S(1)}, bf16[2,512,256]{2,1,0:T(8,128)(2,1)S(1)}, u32[]{:S(2)}, u32[]{:S(2)}) %collective-permute-start.21) | collective-permute-done | bytes 524320 | tf_op jit(solution)/shard_map/ppermute | solution.py:26
  77.9 4.0 %collective-permute-done.14 = bf16[2,1,4,128,128]{4,3,2,1,0:T(8,128)(2,1)S(1)} collective-permute-done((bf16[2,1,4,128,128]{4,3,2,1,0:T(8,128)(2,1)S(1)}, bf16[2,1,4,128,128]{4,3,2,1,0:T(8,128)(2,1)S(1)}, u32[]{:S(2)}, u32[]{:S(2)}) %collective-permute-start.14) | collective-permute-done | bytes 262176 | tf_op jit(solution)/shard_map/ppermute | solution.py:26
  82.6 0.8 shard_map.91
  83.3 1.6 %collective-permute-start.24 = (bf16[2,4,128,128]{3,2,1,0:T(8,128)(2,1)S(1)}, bf16[2,4,128,128]{3,2,1,0:T(8,128)(2,1)S(1)}, u32[]{:S(2)}, u32[]{:S(2)}) collective-permute-start(bf16[2,4,128,128]{3,2,1,0:T(8,128)(2,1)S(1)} %shard_map.91), channel_id=1, source_target_pairs={{0,4},{4,0},{8,12},{12,8},{16,20},{20,16},{24,28},{28,24},{1,5},{5... | collective-permute-start | bytes 786440 | tf_op jit(solution)/shard_map/ppermute | solution.py:26
  86.0 11.0 %collective-permute-done.22 = bf16[2,4,128,256]{3,2,1,0:T(8,128)(2,1)S(1)} collective-permute-done((bf16[2,4,128,256]{3,2,1,0:T(8,128)(2,1)S(1)}, bf16[2,4,128,256]{3,2,1,0:T(8,128)(2,1)S(1)}, u32[]{:S(2)}, u32[]{:S(2)}) %collective-permute-start.22) | collective-permute-done | bytes 524320 | tf_op jit(solution)/shard_map/ppermute | solution.py:26
  97.2 6.1 %collective-permute-done.24 = bf16[2,4,128,128]{3,2,1,0:T(8,128)(2,1)S(1)} collective-permute-done((bf16[2,4,128,128]{3,2,1,0:T(8,128)(2,1)S(1)}, bf16[2,4,128,128]{3,2,1,0:T(8,128)(2,1)S(1)}, u32[]{:S(2)}, u32[]{:S(2)}) %collective-permute-start.24) | collective-permute-done | bytes 262176 | tf_op jit(solution)/shard_map/ppermute | solution.py:26
  103.8 1.9 %shard_map.82.so_far_ref = bf16[128,4096]{1,0:T(8,128)(2,1)} custom-call(s32[1]{0:T(128)} %bitcast.place_ref, bf16[128,4096]{1,0:T(8,128)(2,1)} %shard_map.78.so_far_ref, bf16[1,4,128,128]{3,2,1,0:T(8,128)(2,1)S(1)} %get-tuple-element.79.near_ref, bf16[1,4,128,128]{3,2,1,0:T(8,128)(2,1)S(1)} %collective-permute-done.16.far_ref), custom_call_target="tpu_custom_call", output_to_operand_aliasing={{}: (1, {})} | custom-call | bytes 1000000 | tf_op jit(solution)/shard_map/pallas_call | solution.py:318
  105.7 2.0 %shard_map.83.so_far_ref = bf16[128,4096]{1,0:T(8,128)(2,1)} custom-call(s32[1]{0:T(128)} %bitcast.place_ref, bf16[128,4096]{1,0:T(8,128)(2,1)} %shard_map.82.so_far_ref, bf16[1,4,128,256]{3,2,1,0:T(8,128)(2,1)S(1)} %get-tuple-element.69.near_ref, bf16[1,4,128,256]{3,2,1,0:T(8,128)(2,1)S(1)} %collective-permute-done.17.far_ref), custom_call_target="tpu_custom_call", output_to_operand_aliasing={{}: (1, {})} | custom-call | bytes 1000000 | tf_op jit(solution)/shard_map/pallas_call | solution.py:318
  107.7 2.0 %shard_map.86.so_far_ref = bf16[128,4096]{1,0:T(8,128)(2,1)} custom-call(s32[1]{0:T(128)} %bitcast.place_ref, bf16[128,4096]{1,0:T(8,128)(2,1)} %shard_map.83.so_far_ref, bf16[1,4,128,256]{3,2,1,0:T(8,128)(2,1)S(1)} %get-tuple-element.66.near_ref, bf16[1,4,128,256]{3,2,1,0:T(8,128)(2,1)S(1)} %collective-permute-done.20.far_ref), custom_call_target="tpu_custom_call", output_to_operand_aliasing={{}: (1, {})} | custom-call | bytes 1000000 | tf_op jit(solution)/shard_map/pallas_call | solution.py:318
  109.7 3.8 %collective-permute-done.23.far_ref = bf16[1,4,128,256]{3,2,1,0:T(8,128)(2,1)S(1)} collective-permute-done((bf16[1,4,128,256]{3,2,1,0:T(8,128)(2,1)S(1)}, bf16[1,4,128,256]{3,2,1,0:T(8,128)(2,1)S(1)}, u32[]{:S(2)}, u32[]{:S(2)}) %collective-permute-start.23) | collective-permute-done | bytes 262176 | tf_op jit(solution)/shard_map/ppermute | solution.py:26
  113.5 2.0 %shard_map.89.so_far_ref = bf16[128,4096]{1,0:T(8,128)(2,1)} custom-call(s32[1]{0:T(128)} %bitcast.place_ref, bf16[128,4096]{1,0:T(8,128)(2,1)} %shard_map.86.so_far_ref, bf16[1,4,128,256]{3,2,1,0:T(8,128)(2,1)S(1)} %get-tuple-element.64.near_ref, bf16[1,4,128,256]{3,2,1,0:T(8,128)(2,1)S(1)} %collective-permute-done.23.far_ref), custom_call_target="tpu_custom_call", output_to_operand_aliasing={{}: (1, {})} | custom-call | bytes 1000000 | tf_op jit(solution)/shard_map/pallas_call | solution.py:318
  115.5 1.9 %shard_map.92 = bf16[128,4096]{1,0:T(8,128)(2,1)} custom-call(s32[1]{0:T(128)} %bitcast.place_ref, bf16[128,4096]{1,0:T(8,128)(2,1)} %shard_map.89.so_far_ref, bf16[1,4,128,128]{3,2,1,0:T(8,128)(2,1)S(1)} %get-tuple-element.77.near_ref, bf16[1,4,128,128]{3,2,1,0:T(8,128)(2,1)S(1)} %collective-permute-done.25.far_ref), custom_call_target="tpu_custom_call", output_to_operand_aliasing={{}: (1, {})} | custom-call | bytes 1000000 | tf_op jit(solution)/shard_map/pallas_call | solution.py:318
  (79 shorter events, 12.5 us)
Async XLA Ops:
  0.0 8.6 %collective-permute-start.4 = (s32[1,128]{1,0:T(1,128)}, s32[1,128]{1,0:T(1,128)S(1)}, u32[]{:S(2)}, u32[]{:S(2)}) collective-permute-start(s32[1,128]{1,0:T(1,128)} %ids_ref), channel_id=1, source_target_pairs={{0,24},{4,28},{8,16},{12,20},{16,8},{20,12},{24,0},{28,4},{1,25},{... | collective-permute-start | bytes 1544 | tf_op jit(solution)/shard_map/ppermute | solution.py:26
  5.0 3.7 %collective-permute-start.3 = (s32[1,128]{1,0:T(1,128)}, s32[1,128]{1,0:T(1,128)S(1)}, u32[]{:S(2)}, u32[]{:S(2)}) collective-permute-start(s32[1,128]{1,0:T(1,128)} %ids_ref), channel_id=1, source_target_pairs={{0,8},{4,12},{8,0},{12,4},{16,24},{20,28},{24,16},{28,20},{1,9},{5... | collective-permute-start | bytes 1544 | tf_op jit(solution)/shard_map/ppermute | solution.py:26
  5.1 4.6 %collective-permute-start.2 = (s32[1,128]{1,0:T(1,128)}, s32[1,128]{1,0:T(1,128)S(1)}, u32[]{:S(2)}, u32[]{:S(2)}) collective-permute-start(s32[1,128]{1,0:T(1,128)} %ids_ref), channel_id=1, source_target_pairs={{0,16},{4,20},{8,24},{12,28},{16,0},{20,4},{24,8},{28,12},{1,17},{... | collective-permute-start | bytes 1544 | tf_op jit(solution)/shard_map/ppermute | solution.py:26
  5.6 2.2 %copy-start.5 = (bf16[32,128]{1,0:T(8,128)(2,1)S(1)}, bf16[32,128]{1,0:T(8,128)(2,1)}, u32[]{:S(2)}) copy-start(bf16[32,128]{1,0:T(8,128)(2,1)} %param.12) | copy-start | bytes 24580
  5.6 4.0 %copy-start.3 = (s32[1,128]{1,0:T(1,128)S(1)}, s32[1,128]{1,0:T(1,128)}, u32[]{:S(2)}) copy-start(s32[1,128]{1,0:T(1,128)} %ids_ref) | copy-start | bytes 1540
  5.6 9.3 %copy-start.2 = (f32[4096]{0:T(1024)S(1)}, f32[4096]{0:T(1024)}, u32[]{:S(2)}) copy-start(f32[4096]{0:T(1024)} %param.9) | copy-start | bytes 49156
  9.6 3.7 %collective-permute-start.5 = (s32[4,128]{1,0:T(4,128)S(1)}, s32[4,128]{1,0:T(4,128)S(1)}, u32[]{:S(2)}, u32[]{:S(2)}) collective-permute-start(s32[4,128]{1,0:T(4,128)S(1)} %pad_add_fusion.4), channel_id=1, source_target_pairs={{0,4},{4,0},{8,12},{12,8},{16,20},{20,16},{24,28},{28,24},{1,5},{5... | collective-permute-start | bytes 6152 | tf_op jit(solution)/shard_map/ppermute | solution.py:26
  11.2 29.1 %collective-permute-start = (bf16[512,512]{1,0:T(8,128)(2,1)}, bf16[512,512]{1,0:T(8,128)(2,1)S(1)}, u32[]{:S(2)}, u32[]{:S(2)}) collective-permute-start(bf16[512,512]{1,0:T(8,128)(2,1)} %get-tuple-element.36), channel_id=1, source_target_pairs={{0,8},{4,12},{8,0},{12,4},{16,24},{20,28},{24,16},{28,20},{1,9},{5... | collective-permute-start | bytes 1572872 | tf_op jit(solution)/shard_map/ppermute | solution.py:26
  13.2 21.4 %collective-permute-start.8 = (bf16[512,512]{1,0:T(8,128)(2,1)}, bf16[512,512]{1,0:T(8,128)(2,1)S(1)}, u32[]{:S(2)}, u32[]{:S(2)}) collective-permute-start(bf16[512,512]{1,0:T(8,128)(2,1)} %get-tuple-element.41), channel_id=1, source_target_pairs={{0,8},{4,12},{8,0},{12,4},{16,24},{20,28},{24,16},{28,20},{1,9},{5... | collective-permute-start | bytes 1572872 | tf_op jit(solution)/shard_map/ppermute | solution.py:26
  13.3 13.6 %collective-permute-start.7 = (s32[8,128]{1,0:T(8,128)S(1)}, s32[8,128]{1,0:T(8,128)S(1)}, u32[]{:S(2)}, u32[]{:S(2)}) collective-permute-start(s32[8,128]{1,0:T(8,128)S(1)} %pad_add_fusion.2), channel_id=1, source_target_pairs={{0,1},{1,2},{2,3},{3,0},{4,5},{5,6},{6,7},{7,4},{8,9},{9,10},{10,1... | collective-permute-start | bytes 12296 | tf_op jit(solution)/shard_map/ppermute | solution.py:21
  13.4 13.5 %collective-permute-start.6 = (s32[8,128]{1,0:T(8,128)S(1)}, s32[8,128]{1,0:T(8,128)S(1)}, u32[]{:S(2)}, u32[]{:S(2)}) collective-permute-start(s32[8,128]{1,0:T(8,128)S(1)} %pad_add_fusion.2), channel_id=1, source_target_pairs={{0,2},{1,3},{2,0},{3,1},{4,6},{5,7},{6,4},{7,5},{8,10},{9,11},{10,... | collective-permute-start | bytes 12296 | tf_op jit(solution)/shard_map/ppermute | solution.py:21
  14.9 2.2 %copy-start.1 = (bf16[512,4096]{1,0:T(8,128)(2,1)S(1)}, bf16[512,4096]{1,0:T(8,128)(2,1)}, u32[]{:S(2)}) copy-start(bf16[512,4096]{1,0:T(8,128)(2,1)} %rows_ref.1) | copy-start | bytes 12582916
  17.1 19.2 %copy-start.4 = (f32[3,3,512]{2,1,0:T(4,128)S(1)}, f32[3,3,512]{2,1,0:T(4,128)}, u32[]{:S(2)}) copy-start(f32[3,3,512]{2,1,0:T(4,128)} %short_ref.3) | copy-start | bytes 55300
  34.6 12.3 %collective-permute-start.9 = (bf16[512,512]{1,0:T(8,128)(2,1)S(1)}, bf16[512,512]{1,0:T(8,128)(2,1)S(1)}, u32[]{:S(2)}, u32[]{:S(2)}) collective-permute-start(bf16[512,512]{1,0:T(8,128)(2,1)S(1)} %collective-permute-done.8), channel_id=1, source_target_pairs={{0,2},{1,3},{2,0},{3,1},{4,6},{5,7},{6,4},{7,5},{8,10},{9,11},{10,... | collective-permute-start | bytes 1572872 | tf_op jit(solution)/shard_map/ppermute | solution.py:26
  38.5 13.7 %collective-permute-start.11 = (bf16[2,128,512]{2,1,0:T(8,128)(2,1)S(1)}, bf16[2,128,512]{2,1,0:T(8,128)(2,1)S(1)}, u32[]{:S(2)}, u32[]{:S(2)}) collective-permute-start(bf16[2,128,512]{2,1,0:T(8,128)(2,1)S(1)} %shard_map.76), channel_id=1, source_target_pairs={{0,8},{4,12},{8,0},{12,4},{16,24},{20,28},{24,16},{28,20},{1,9},{5... | collective-permute-start | bytes 786440 | tf_op jit(solution)/shard_map/ppermute | solution.py:26
  40.3 7.4 %collective-permute-start.1 = (bf16[512,512]{1,0:T(8,128)(2,1)S(1)}, bf16[512,512]{1,0:T(8,128)(2,1)S(1)}, u32[]{:S(2)}, u32[]{:S(2)}) collective-permute-start(bf16[512,512]{1,0:T(8,128)(2,1)S(1)} %collective-permute-done), channel_id=1, source_target_pairs={{0,1},{1,0},{2,3},{3,2},{4,5},{5,4},{6,7},{7,6},{8,9},{9,8},{10,11... | collective-permute-start | bytes 1572872 | tf_op jit(solution)/shard_map/ppermute | solution.py:26
  47.1 5.0 %collective-permute-start.12 = (bf16[2,512,256]{2,1,0:T(8,128)(2,1)S(1)}, bf16[2,512,256]{2,1,0:T(8,128)(2,1)S(1)}, u32[]{:S(2)}, u32[]{:S(2)}) collective-permute-start(bf16[2,512,256]{2,1,0:T(8,128)(2,1)S(1)} %get-tuple-element.72.refs_4_), channel_id=1, source_target_pairs={{0,1},{1,0},{2,3},{3,2},{4,5},{5,4},{6,7},{7,6},{8,9},{9,8},{10,11... | collective-permute-start | bytes 1572872 | tf_op jit(solution)/shard_map/ppermute | solution.py:26
  47.8 4.4 %copy-start = (bf16[512,4096]{1,0:T(8,128)(2,1)S(1)}, bf16[512,4096]{1,0:T(8,128)(2,1)}, u32[]{:S(2)}) copy-start(bf16[512,4096]{1,0:T(8,128)(2,1)} %refs_3_.17) | copy-start | bytes 12582916
  50.6 8.3 %collective-permute-start.10 = (bf16[2,128,512]{2,1,0:T(8,128)(2,1)S(1)}, bf16[2,128,512]{2,1,0:T(8,128)(2,1)S(1)}, u32[]{:S(2)}, u32[]{:S(2)}) collective-permute-start(bf16[2,128,512]{2,1,0:T(8,128)(2,1)S(1)} %get-tuple-element.75), channel_id=1, source_target_pairs={{0,8},{4,12},{8,0},{12,4},{16,24},{20,28},{24,16},{28,20},{1,9},{5... | collective-permute-start | bytes 786440 | tf_op jit(solution)/shard_map/ppermute | solution.py:26
  50.9 8.6 %collective-permute-start.13 = (bf16[2,512,256]{2,1,0:T(8,128)(2,1)S(1)}, bf16[2,512,256]{2,1,0:T(8,128)(2,1)S(1)}, u32[]{:S(2)}, u32[]{:S(2)}) collective-permute-start(bf16[2,512,256]{2,1,0:T(8,128)(2,1)S(1)} %get-tuple-element.71.refs_4_), channel_id=1, source_target_pairs={{0,1},{1,0},{2,3},{3,2},{4,5},{5,4},{6,7},{7,6},{8,9},{9,8},{10,11... | collective-permute-start | bytes 1572872 | tf_op jit(solution)/shard_map/ppermute | solution.py:26
  51.0 14.8 %collective-permute-start.18 = (bf16[2,512,256]{2,1,0:T(8,128)(2,1)S(1)}, bf16[2,512,256]{2,1,0:T(8,128)(2,1)S(1)}, u32[]{:S(2)}, u32[]{:S(2)}) collective-permute-start(bf16[2,512,256]{2,1,0:T(8,128)(2,1)S(1)} %get-tuple-element.67.refs_4_), channel_id=1, source_target_pairs={{0,2},{1,3},{2,0},{3,1},{4,6},{5,7},{6,4},{7,5},{8,10},{9,11},{10,... | collective-permute-start | bytes 1572872 | tf_op jit(solution)/shard_map/ppermute | solution.py:26
  52.9 13.9 %collective-permute-start.15 = (bf16[2,4,128,256]{3,2,1,0:T(8,128)(2,1)S(1)}, bf16[2,4,128,256]{3,2,1,0:T(8,128)(2,1)S(1)}, u32[]{:S(2)}, u32[]{:S(2)}) collective-permute-start(bf16[2,4,128,256]{3,2,1,0:T(8,128)(2,1)S(1)} %shard_map.79), channel_id=1, source_target_pairs={{0,4},{4,0},{8,12},{12,8},{16,20},{20,16},{24,28},{28,24},{1,5},{5... | collective-permute-start | bytes 1572872 | tf_op jit(solution)/shard_map/ppermute | solution.py:26
  58.9 17.7 %collective-permute-start.21 = (bf16[2,512,256]{2,1,0:T(8,128)(2,1)S(1)}, bf16[2,512,256]{2,1,0:T(8,128)(2,1)S(1)}, u32[]{:S(2)}, u32[]{:S(2)}) collective-permute-start(bf16[2,512,256]{2,1,0:T(8,128)(2,1)S(1)} %get-tuple-element.58.refs_4_), channel_id=1, source_target_pairs={{0,2},{1,3},{2,0},{3,1},{4,6},{5,7},{6,4},{7,5},{8,10},{9,11},{10,... | collective-permute-start | bytes 1572872 | tf_op jit(solution)/shard_map/ppermute | solution.py:26
  60.9 21.0 %collective-permute-start.14 = (bf16[2,1,4,128,128]{4,3,2,1,0:T(8,128)(2,1)S(1)}, bf16[2,1,4,128,128]{4,3,2,1,0:T(8,128)(2,1)S(1)}, u32[]{:S(2)}, u32[]{:S(2)}) collective-permute-start(bf16[2,1,4,128,128]{4,3,2,1,0:T(8,128)(2,1)S(1)} %slice.129), channel_id=1, source_target_pairs={{0,16},{4,20},{8,24},{12,28},{16,0},{20,4},{24,8},{28,12},{1,17},{... | collective-permute-start | bytes 786440 | tf_op jit(solution)/shard_map/ppermute | solution.py:26
  66.9 38.8 %collective-permute-start.17 = (bf16[1,4,128,256]{3,2,1,0:T(8,128)(2,1)S(1)}, bf16[1,4,128,256]{3,2,1,0:T(8,128)(2,1)S(1)}, u32[]{:S(2)}, u32[]{:S(2)}) collective-permute-start(bf16[1,4,128,256]{3,2,1,0:T(8,128)(2,1)S(1)} %get-tuple-element.70), channel_id=1, source_target_pairs={{0,16},{4,20},{8,24},{12,28},{16,0},{20,4},{24,8},{28,12},{1,17},{... | collective-permute-start | bytes 786440 | tf_op jit(solution)/shard_map/ppermute | solution.py:26
  70.9 14.9 %collective-permute-start.19 = (bf16[2,4,128,256]{3,2,1,0:T(8,128)(2,1)S(1)}, bf16[2,4,128,256]{3,2,1,0:T(8,128)(2,1)S(1)}, u32[]{:S(2)}, u32[]{:S(2)}) collective-permute-start(bf16[2,4,128,256]{3,2,1,0:T(8,128)(2,1)S(1)} %shard_map.85), channel_id=1, source_target_pairs={{0,4},{4,0},{8,12},{12,8},{16,20},{20,16},{24,28},{28,24},{1,5},{5... | collective-permute-start | bytes 1572872 | tf_op jit(solution)/shard_map/ppermute | solution.py:26
  77.3 19.7 %collective-permute-start.22 = (bf16[2,4,128,256]{3,2,1,0:T(8,128)(2,1)S(1)}, bf16[2,4,128,256]{3,2,1,0:T(8,128)(2,1)S(1)}, u32[]{:S(2)}, u32[]{:S(2)}) collective-permute-start(bf16[2,4,128,256]{3,2,1,0:T(8,128)(2,1)S(1)} %shard_map.88), channel_id=1, source_target_pairs={{0,4},{4,0},{8,12},{12,8},{16,20},{20,16},{24,28},{28,24},{1,5},{5... | collective-permute-start | bytes 1572872 | tf_op jit(solution)/shard_map/ppermute | solution.py:26
  82.0 21.8 %collective-permute-start.16 = (bf16[1,4,128,128]{3,2,1,0:T(8,128)(2,1)S(1)}, bf16[1,4,128,128]{3,2,1,0:T(8,128)(2,1)S(1)}, u32[]{:S(2)}, u32[]{:S(2)}) collective-permute-start(bf16[1,4,128,128]{3,2,1,0:T(8,128)(2,1)S(1)} %get-tuple-element.78), channel_id=1, source_target_pairs={{0,4},{4,0},{8,12},{12,8},{16,20},{20,16},{24,28},{28,24},{1,5},{5... | collective-permute-start | bytes 393224 | tf_op jit(solution)/shard_map/ppermute | solution.py:26
  83.3 20.0 %collective-permute-start.24 = (bf16[2,4,128,128]{3,2,1,0:T(8,128)(2,1)S(1)}, bf16[2,4,128,128]{3,2,1,0:T(8,128)(2,1)S(1)}, u32[]{:S(2)}, u32[]{:S(2)}) collective-permute-start(bf16[2,4,128,128]{3,2,1,0:T(8,128)(2,1)S(1)} %shard_map.91), channel_id=1, source_target_pairs={{0,4},{4,0},{8,12},{12,8},{16,20},{20,16},{24,28},{28,24},{1,5},{5... | collective-permute-start | bytes 786440 | tf_op jit(solution)/shard_map/ppermute | solution.py:26
  85.9 21.8 %collective-permute-start.20 = (bf16[1,4,128,256]{3,2,1,0:T(8,128)(2,1)S(1)}, bf16[1,4,128,256]{3,2,1,0:T(8,128)(2,1)S(1)}, u32[]{:S(2)}, u32[]{:S(2)}) collective-permute-start(bf16[1,4,128,256]{3,2,1,0:T(8,128)(2,1)S(1)} %get-tuple-element.65), channel_id=1, source_target_pairs={{0,16},{4,20},{8,24},{12,28},{16,0},{20,4},{24,8},{28,12},{1,17},{... | collective-permute-start | bytes 786440 | tf_op jit(solution)/shard_map/ppermute | solution.py:26
  97.2 16.3 %collective-permute-start.23 = (bf16[1,4,128,256]{3,2,1,0:T(8,128)(2,1)S(1)}, bf16[1,4,128,256]{3,2,1,0:T(8,128)(2,1)S(1)}, u32[]{:S(2)}, u32[]{:S(2)}) collective-permute-start(bf16[1,4,128,256]{3,2,1,0:T(8,128)(2,1)S(1)} %get-tuple-element.63), channel_id=1, source_target_pairs={{0,16},{4,20},{8,24},{12,28},{16,0},{20,4},{24,8},{28,12},{1,17},{... | collective-permute-start | bytes 786440 | tf_op jit(solution)/shard_map/ppermute | solution.py:26
  103.4 12.1 %collective-permute-start.25 = (bf16[1,4,128,128]{3,2,1,0:T(8,128)(2,1)S(1)}, bf16[1,4,128,128]{3,2,1,0:T(8,128)(2,1)S(1)}, u32[]{:S(2)}, u32[]{:S(2)}) collective-permute-start(bf16[1,4,128,128]{3,2,1,0:T(8,128)(2,1)S(1)} %get-tuple-element.76), channel_id=1, source_target_pairs={{0,16},{4,20},{8,24},{12,28},{16,0},{20,4},{24,8},{28,12},{1,17},{... | collective-permute-start | bytes 393224 | tf_op jit(solution)/shard_map/ppermute | solution.py:26

commit v12 on v11

--- a/solution.py
+++ b/solution.py
@@ -345,8 +345,9 @@
     ids, toeplitz = tie((ids, toeplitz))
     for group in [bits[i : i + 2] for i in range(2, len(bits), 2)]:
         ids = level_ids(ids, group)
-    early, late = swap(early, "fsdp", beside_bit), swap(late, "fsdp", beside_bit)
-    ids, embedding_then = tie((ids, embedding))
+    early = swap(early, "fsdp", beside_bit)
+    ids, embedding_then, late = tie((ids, embedding, late))
+    late = swap(late, "fsdp", beside_bit)
     ids = with_lead(ids)
     table = project(embedding_then, norm_gain, in_proj)
     table, early = tie((table, early))

time: 118 us -> 112 us (0.949)
  waiting for transfers between devices: 45.2 us -> 34.2 us
  starting transfers between devices: 27.3 us -> 32.4 us
    ppermute x24, waiting for transfers between devices: 45.2 us -> 34.2 us  [swap(): return lax.ppermute(x, axis, [(i, i ^ mask) for i in range(peers)])]
    ppermute x24, starting transfers between devices: 25.7 us -> 30.8 us  [swap(): return lax.ppermute(x, axis, [(i, i ^ mask) for i in range(peers)])]
  transfers between devices with their start and end apart: 26 -> 26, of which waited for: 12 -> 13; matrix products, arithmetic and copies ran while one was open for 1% -> 1% of each run, Pallas kernels for 33% -> 35%
where the time goes in v12:
time: 112 us; the launch traced here: 111 us
  Pallas kernels  40.7 us (36%)
  waiting for transfers between devices  34.2 us (31%)
  starting transfers between devices  32.4 us (29%)
  local copies, waits for them, and re-layouts  2.68 us (2%)
    ppermute x24, waiting for transfers between devices, swap(): return lax.ppermute(x, axis, [(i, i ^ mask) for i in range(peers)])  34.2 us
    ppermute x24, starting transfers between devices, swap(): return lax.ppermute(x, axis, [(i, i ^ mask) for i in range(peers)])  30.8 us
    pallas_call x5, Pallas kernels, place_pieces(): pl.pallas_call(functools.partial(place_kernel, split, step), grid_spec=pl...  9.81 us
    pallas_call x1, Pallas kernels, project(): pl.pallas_call(table_kernel, grid=(1,), in_specs=[hbm, hbm, pl.BlockSpec(...  9.69 us
    pallas_call x2, Pallas kernels, mix(): pl.pallas_call(mixer_kernel, grid=(windows // 2,), in_specs=[pl.BlockSpec...  8.5 us
    pallas_call x9, Pallas kernels, panel(): pl.pallas_call(panel_kernel, grid_spec=pltpu.PrefetchScalarGridSpec(num_s...  7.19 us
    pallas_call x1, Pallas kernels, residual(): pl.pallas_call(residual_kernel, grid=(4,), in_specs=[whole(token_ids), pl...  2.64 us
  transfers between devices with their start and end apart: 26, of which 13 were waited for; matrix products, arithmetic and copies ran while one was open for 1% of the time, Pallas kernels for 35%

profile of v12, /device:TPU:0, one launch (start us, length us, event | category | flops | bytes accessed | tf_op | source)
XLA Modules:
  0.0 111.4 jit_solution(1464776422961431131)
XLA Ops:
  0.0 5.0 %collective-permute-start.2 = (s32[1,128]{1,0:T(1,128)}, s32[1,128]{1,0:T(1,128)S(1)}, u32[]{:S(2)}, u32[]{:S(2)}) collective-permute-start(s32[1,128]{1,0:T(1,128)} %ids_ref), channel_id=1, source_target_pairs={{0,24},{4,28},{8,16},{12,20},{16,8},{20,12},{24,0},{28,4},{1,25},{... | collective-permute-start | bytes 1544 | tf_op jit(solution)/shard_map/ppermute | solution.py:26
  5.6 2.2 %shard_map.73 = (bf16[512,512]{1,0:T(8,128)(2,1)}, bf16[512,512]{1,0:T(8,128)(2,1)}) custom-call(s32[1]{0:T(128)} %bitcast.place_ref, bf16[512,4096]{1,0:T(8,128)(2,1)} %refs_3_.17, bf16[512,4096]{1,0:T(8,128)(2,1)} %refs_3_.17), custom_call_target="tpu_custom_call" | custom-call | bytes 2000000 | tf_op jit(solution)/shard_map/pallas_call | solution.py:200
  9.6 1.6 %collective-permute-start.3 = (s32[4,128]{1,0:T(4,128)S(1)}, s32[4,128]{1,0:T(4,128)S(1)}, u32[]{:S(2)}, u32[]{:S(2)}) collective-permute-start(s32[4,128]{1,0:T(4,128)S(1)} %pad_add_fusion.4), channel_id=1, source_target_pairs={{0,4},{4,0},{8,12},{12,8},{16,20},{20,16},{24,28},{28,24},{1,5},{5... | collective-permute-start | bytes 6152 | tf_op jit(solution)/shard_map/ppermute | solution.py:26
  11.2 2.0 %collective-permute-start.8 = (bf16[512,512]{1,0:T(8,128)(2,1)}, bf16[512,512]{1,0:T(8,128)(2,1)S(1)}, u32[]{:S(2)}, u32[]{:S(2)}) collective-permute-start(bf16[512,512]{1,0:T(8,128)(2,1)} %get-tuple-element.43), channel_id=1, source_target_pairs={{0,8},{4,12},{8,0},{12,4},{16,24},{20,28},{24,16},{28,20},{1,9},{5... | collective-permute-start | bytes 1572872 | tf_op jit(solution)/shard_map/ppermute | solution.py:26
  13.3 1.6 %collective-permute-start.6 = (s32[8,128]{1,0:T(8,128)S(1)}, s32[8,128]{1,0:T(8,128)S(1)}, u32[]{:S(2)}, u32[]{:S(2)}) collective-permute-start(s32[8,128]{1,0:T(8,128)S(1)} %pad_add_fusion.2), channel_id=1, source_target_pairs={{0,2},{1,3},{2,0},{3,1},{4,6},{5,7},{6,4},{7,5},{8,10},{9,11},{10,... | collective-permute-start | bytes 12296 | tf_op jit(solution)/shard_map/ppermute | solution.py:21
  14.9 2.0 %collective-permute-start.4 = (bf16[512,512]{1,0:T(8,128)(2,1)}, bf16[512,512]{1,0:T(8,128)(2,1)S(1)}, u32[]{:S(2)}, u32[]{:S(2)}) collective-permute-start(bf16[512,512]{1,0:T(8,128)(2,1)} %get-tuple-element.40), channel_id=1, source_target_pairs={{0,8},{4,12},{8,0},{12,4},{16,24},{20,28},{24,16},{28,20},{1,9},{5... | collective-permute-start | bytes 1572872 | tf_op jit(solution)/shard_map/ppermute | solution.py:26
  16.9 2.2 %copy-done.1 = bf16[512,4096]{1,0:T(8,128)(2,1)S(1)} copy-done((bf16[512,4096]{1,0:T(8,128)(2,1)S(1)}, bf16[512,4096]{1,0:T(8,128)(2,1)}, u32[]{:S(2)}) %copy-start.1) | copy-done | bytes 4194328
  19.1 9.7 %shard_map.75.table_ref = bf16[3,512,512]{2,1,0:T(8,128)(2,1)S(1)} custom-call(bf16[512,4096]{1,0:T(8,128)(2,1)S(1)} %copy-done.1, bf16[3,4096,512]{2,1,0:T(8,128)(2,1)} %weight_hbm.1, f32[1,4096]{1,0:T(1,128)S(1)} %bitcast.43), custom_call_target="tpu_custom_call" | custom-call | flops 3000000000 | tf_op jit(solution)/shard_map/pallas_call | solution.py:101
  29.7 2.1 %shard_map.76 = bf16[2,128,512]{2,1,0:T(8,128)(2,1)S(1)} custom-call(s32[2,1,272]{2,1,0:T(1,128)S(1)} %copy.13.ids_ref, bf16[3,512,512]{2,1,0:T(8,128)(2,1)S(1)} %shard_map.75.table_ref, f32[3,3,512]{2,1,0:T(4,128)S(1)} %copy-done.4, bf16[4,1024,256]{2,1,0:T(8,128)(2,1)S(1)} %shard_map.74.toeplitz), custom_call_target="tpu_custom_call" | custom-call | flops 1500000000 | tf_op jit(solution)/shard_map/pallas_call | solution.py:167
  32.2 6.4 %shard_map.77 = bf16[6,128,512]{2,1,0:T(8,128)(2,1)S(1)} custom-call(s32[6,1,272]{2,1,0:T(1,128)S(1)} %reshape.54.ids_ref, bf16[3,512,512]{2,1,0:T(8,128)(2,1)S(1)} %shard_map.75.table_ref, f32[3,3,512]{2,1,0:T(4,128)S(1)} %copy-done.4, bf16[4,1024,256]{2,1,0:T(8,128)(2,1)S(1)} %shard_map.74.toeplitz), custom_call_target="tpu_custom_call" | custom-call | flops 1500000000 | tf_op jit(solution)/shard_map/pallas_call | solution.py:167
  39.1 3.7 %collective-permute-done.9 = bf16[512,512]{1,0:T(8,128)(2,1)S(1)} collective-permute-done((bf16[512,512]{1,0:T(8,128)(2,1)S(1)}, bf16[512,512]{1,0:T(8,128)(2,1)S(1)}, u32[]{:S(2)}, u32[]{:S(2)}) %collective-permute-start.9) | collective-permute-done | bytes 524320 | tf_op jit(solution)/shard_map/ppermute | solution.py:26
  43.8 2.6 %shard_map.78.so_far_ref = bf16[128,4096]{1,0:T(8,128)(2,1)} custom-call(s32[1,128]{1,0:T(1,128)S(1)} %copy-done.3, bf16[512,4096]{1,0:T(8,128)(2,1)S(1)} %copy-done.1), custom_call_target="tpu_custom_call" | custom-call | flops 400000000 | tf_op jit(solution)/shard_map/pallas_call | solution.py:290
  46.6 1.5 %collective-permute-start.18 = (bf16[2,512,256]{2,1,0:T(8,128)(2,1)S(1)}, bf16[2,512,256]{2,1,0:T(8,128)(2,1)S(1)}, u32[]{:S(2)}, u32[]{:S(2)}) collective-permute-start(bf16[2,512,256]{2,1,0:T(8,128)(2,1)S(1)} %get-tuple-element.69.refs_4_), channel_id=1, source_target_pairs={{0,2},{1,3},{2,0},{3,1},{4,6},{5,7},{6,4},{7,5},{8,10},{9,11},{10,... | collective-permute-start | bytes 1572872 | tf_op jit(solution)/shard_map/ppermute | solution.py:26
  48.9 1.6 %collective-permute-start.15 = (bf16[2,4,128,256]{3,2,1,0:T(8,128)(2,1)S(1)}, bf16[2,4,128,256]{3,2,1,0:T(8,128)(2,1)S(1)}, u32[]{:S(2)}, u32[]{:S(2)}) collective-permute-start(bf16[2,4,128,256]{3,2,1,0:T(8,128)(2,1)S(1)} %shard_map.79), channel_id=1, source_target_pairs={{0,4},{4,0},{8,12},{12,8},{16,20},{20,16},{24,28},{28,24},{1,5},{5... | collective-permute-start | bytes 1572872 | tf_op jit(solution)/shard_map/ppermute | solution.py:26
  54.9 1.5 %collective-permute-start.14 = (bf16[2,1,4,128,128]{4,3,2,1,0:T(8,128)(2,1)S(1)}, bf16[2,1,4,128,128]{4,3,2,1,0:T(8,128)(2,1)S(1)}, u32[]{:S(2)}, u32[]{:S(2)}) collective-permute-start(bf16[2,1,4,128,128]{4,3,2,1,0:T(8,128)(2,1)S(1)} %slice.129), channel_id=1, source_target_pairs={{0,16},{4,20},{8,24},{12,28},{16,0},{20,4},{24,8},{28,12},{1,17},{... | collective-permute-start | bytes 786440 | tf_op jit(solution)/shard_map/ppermute | solution.py:26
  57.9 3.6 %collective-permute-done.18.refs_5_ = bf16[2,512,256]{2,1,0:T(8,128)(2,1)S(1)} collective-permute-done((bf16[2,512,256]{2,1,0:T(8,128)(2,1)S(1)}, bf16[2,512,256]{2,1,0:T(8,128)(2,1)S(1)}, u32[]{:S(2)}, u32[]{:S(2)}) %collective-permute-start.18) | collective-permute-done | bytes 524320 | tf_op jit(solution)/shard_map/ppermute | solution.py:26
  63.0 1.5 %collective-permute-start.17 = (bf16[1,4,128,256]{3,2,1,0:T(8,128)(2,1)S(1)}, bf16[1,4,128,256]{3,2,1,0:T(8,128)(2,1)S(1)}, u32[]{:S(2)}, u32[]{:S(2)}) collective-permute-start(bf16[1,4,128,256]{3,2,1,0:T(8,128)(2,1)S(1)} %get-tuple-element.72), channel_id=1, source_target_pairs={{0,16},{4,20},{8,24},{12,28},{16,0},{20,4},{24,8},{28,12},{1,17},{... | collective-permute-start | bytes 786440 | tf_op jit(solution)/shard_map/ppermute | solution.py:26
  66.6 5.4 %collective-permute-done.21.refs_5_ = bf16[2,512,256]{2,1,0:T(8,128)(2,1)S(1)} collective-permute-done((bf16[2,512,256]{2,1,0:T(8,128)(2,1)S(1)}, bf16[2,512,256]{2,1,0:T(8,128)(2,1)S(1)}, u32[]{:S(2)}, u32[]{:S(2)}) %collective-permute-start.21) | collective-permute-done | bytes 524320 | tf_op jit(solution)/shard_map/ppermute | solution.py:26
  72.7 1.6 %collective-permute-start.22 = (bf16[2,4,128,256]{3,2,1,0:T(8,128)(2,1)S(1)}, bf16[2,4,128,256]{3,2,1,0:T(8,128)(2,1)S(1)}, u32[]{:S(2)}, u32[]{:S(2)}) collective-permute-start(bf16[2,4,128,256]{3,2,1,0:T(8,128)(2,1)S(1)} %shard_map.88), channel_id=1, source_target_pairs={{0,4},{4,0},{8,12},{12,8},{16,20},{20,16},{24,28},{28,24},{1,5},{5... | collective-permute-start | bytes 1572872 | tf_op jit(solution)/shard_map/ppermute | solution.py:26
  74.6 1.7 %collective-permute-start.16 = (bf16[1,4,128,128]{3,2,1,0:T(8,128)(2,1)S(1)}, bf16[1,4,128,128]{3,2,1,0:T(8,128)(2,1)S(1)}, u32[]{:S(2)}, u32[]{:S(2)}) collective-permute-start(bf16[1,4,128,128]{3,2,1,0:T(8,128)(2,1)S(1)} %get-tuple-element.80), channel_id=1, source_target_pairs={{0,4},{4,0},{8,12},{12,8},{16,20},{20,16},{24,28},{28,24},{1,5},{5... | collective-permute-start | bytes 393224 | tf_op jit(solution)/shard_map/ppermute | solution.py:26
  78.3 1.8 %collective-permute-done.19 = bf16[2,4,128,256]{3,2,1,0:T(8,128)(2,1)S(1)} collective-permute-done((bf16[2,4,128,256]{3,2,1,0:T(8,128)(2,1)S(1)}, bf16[2,4,128,256]{3,2,1,0:T(8,128)(2,1)S(1)}, u32[]{:S(2)}, u32[]{:S(2)}) %collective-permute-start.19) | collective-permute-done | bytes 524320 | tf_op jit(solution)/shard_map/ppermute | solution.py:26
  80.2 1.6 %collective-permute-start.20 = (bf16[1,4,128,256]{3,2,1,0:T(8,128)(2,1)S(1)}, bf16[1,4,128,256]{3,2,1,0:T(8,128)(2,1)S(1)}, u32[]{:S(2)}, u32[]{:S(2)}) collective-permute-start(bf16[1,4,128,256]{3,2,1,0:T(8,128)(2,1)S(1)} %get-tuple-element.67), channel_id=1, source_target_pairs={{0,16},{4,20},{8,24},{12,28},{16,0},{20,4},{24,8},{28,12},{1,17},{... | collective-permute-start | bytes 786440 | tf_op jit(solution)/shard_map/ppermute | solution.py:26
  81.8 9.5 %collective-permute-done.22 = bf16[2,4,128,256]{3,2,1,0:T(8,128)(2,1)S(1)} collective-permute-done((bf16[2,4,128,256]{3,2,1,0:T(8,128)(2,1)S(1)}, bf16[2,4,128,256]{3,2,1,0:T(8,128)(2,1)S(1)}, u32[]{:S(2)}, u32[]{:S(2)}) %collective-permute-start.22) | collective-permute-done | bytes 524320 | tf_op jit(solution)/shard_map/ppermute | solution.py:26
  91.5 1.6 %collective-permute-start.23 = (bf16[1,4,128,256]{3,2,1,0:T(8,128)(2,1)S(1)}, bf16[1,4,128,256]{3,2,1,0:T(8,128)(2,1)S(1)}, u32[]{:S(2)}, u32[]{:S(2)}) collective-permute-start(bf16[1,4,128,256]{3,2,1,0:T(8,128)(2,1)S(1)} %get-tuple-element.65), channel_id=1, source_target_pairs={{0,16},{4,20},{8,24},{12,28},{16,0},{20,4},{24,8},{28,12},{1,17},{... | collective-permute-start | bytes 786440 | tf_op jit(solution)/shard_map/ppermute | solution.py:26
  93.0 4.6 %collective-permute-done.24 = bf16[2,4,128,128]{3,2,1,0:T(8,128)(2,1)S(1)} collective-permute-done((bf16[2,4,128,128]{3,2,1,0:T(8,128)(2,1)S(1)}, bf16[2,4,128,128]{3,2,1,0:T(8,128)(2,1)S(1)}, u32[]{:S(2)}, u32[]{:S(2)}) %collective-permute-start.24) | collective-permute-done | bytes 262176 | tf_op jit(solution)/shard_map/ppermute | solution.py:26
  97.7 1.6 %collective-permute-start.25 = (bf16[1,4,128,128]{3,2,1,0:T(8,128)(2,1)S(1)}, bf16[1,4,128,128]{3,2,1,0:T(8,128)(2,1)S(1)}, u32[]{:S(2)}, u32[]{:S(2)}) collective-permute-start(bf16[1,4,128,128]{3,2,1,0:T(8,128)(2,1)S(1)} %get-tuple-element.78), channel_id=1, source_target_pairs={{0,16},{4,20},{8,24},{12,28},{16,0},{20,4},{24,8},{28,12},{1,17},{... | collective-permute-start | bytes 393224 | tf_op jit(solution)/shard_map/ppermute | solution.py:26
  99.2 1.9 %shard_map.82.so_far_ref = bf16[128,4096]{1,0:T(8,128)(2,1)} custom-call(s32[1]{0:T(128)} %bitcast.place_ref, bf16[128,4096]{1,0:T(8,128)(2,1)} %shard_map.78.so_far_ref, bf16[1,4,128,128]{3,2,1,0:T(8,128)(2,1)S(1)} %get-tuple-element.81.near_ref, bf16[1,4,128,128]{3,2,1,0:T(8,128)(2,1)S(1)} %collective-permute-done.16.far_ref), custom_call_target="tpu_custom_call", output_to_operand_aliasing={{}: (1, {})} | custom-call | bytes 1000000 | tf_op jit(solution)/shard_map/pallas_call | solution.py:318
  101.2 2.0 %shard_map.83.so_far_ref = bf16[128,4096]{1,0:T(8,128)(2,1)} custom-call(s32[1]{0:T(128)} %bitcast.place_ref, bf16[128,4096]{1,0:T(8,128)(2,1)} %shard_map.82.so_far_ref, bf16[1,4,128,256]{3,2,1,0:T(8,128)(2,1)S(1)} %get-tuple-element.71.near_ref, bf16[1,4,128,256]{3,2,1,0:T(8,128)(2,1)S(1)} %collective-permute-done.17.far_ref), custom_call_target="tpu_custom_call", output_to_operand_aliasing={{}: (1, {})} | custom-call | bytes 1000000 | tf_op jit(solution)/shard_map/pallas_call | solution.py:318
  103.2 2.0 %shard_map.86.so_far_ref = bf16[128,4096]{1,0:T(8,128)(2,1)} custom-call(s32[1]{0:T(128)} %bitcast.place_ref, bf16[128,4096]{1,0:T(8,128)(2,1)} %shard_map.83.so_far_ref, bf16[1,4,128,256]{3,2,1,0:T(8,128)(2,1)S(1)} %get-tuple-element.68.near_ref, bf16[1,4,128,256]{3,2,1,0:T(8,128)(2,1)S(1)} %collective-permute-done.20.far_ref), custom_call_target="tpu_custom_call", output_to_operand_aliasing={{}: (1, {})} | custom-call | bytes 1000000 | tf_op jit(solution)/shard_map/pallas_call | solution.py:318
  105.1 2.1 %collective-permute-done.23.far_ref = bf16[1,4,128,256]{3,2,1,0:T(8,128)(2,1)S(1)} collective-permute-done((bf16[1,4,128,256]{3,2,1,0:T(8,128)(2,1)S(1)}, bf16[1,4,128,256]{3,2,1,0:T(8,128)(2,1)S(1)}, u32[]{:S(2)}, u32[]{:S(2)}) %collective-permute-start.23) | collective-permute-done | bytes 262176 | tf_op jit(solution)/shard_map/ppermute | solution.py:26
  107.3 2.0 %shard_map.89.so_far_ref = bf16[128,4096]{1,0:T(8,128)(2,1)} custom-call(s32[1]{0:T(128)} %bitcast.place_ref, bf16[128,4096]{1,0:T(8,128)(2,1)} %shard_map.86.so_far_ref, bf16[1,4,128,256]{3,2,1,0:T(8,128)(2,1)S(1)} %get-tuple-element.66.near_ref, bf16[1,4,128,256]{3,2,1,0:T(8,128)(2,1)S(1)} %collective-permute-done.23.far_ref), custom_call_target="tpu_custom_call", output_to_operand_aliasing={{}: (1, {})} | custom-call | bytes 1000000 | tf_op jit(solution)/shard_map/pallas_call | solution.py:318
  109.4 1.9 %shard_map.92 = bf16[128,4096]{1,0:T(8,128)(2,1)} custom-call(s32[1]{0:T(128)} %bitcast.place_ref, bf16[128,4096]{1,0:T(8,128)(2,1)} %shard_map.89.so_far_ref, bf16[1,4,128,128]{3,2,1,0:T(8,128)(2,1)S(1)} %get-tuple-element.79.near_ref, bf16[1,4,128,128]{3,2,1,0:T(8,128)(2,1)S(1)} %collective-permute-done.25.far_ref), custom_call_target="tpu_custom_call", output_to_operand_aliasing={{}: (1, {})} | custom-call | bytes 1000000 | tf_op jit(solution)/shard_map/pallas_call | solution.py:318
  (79 shorter events, 18.9 us)
Async XLA Ops:
  0.0 8.6 %collective-permute-start.2 = (s32[1,128]{1,0:T(1,128)}, s32[1,128]{1,0:T(1,128)S(1)}, u32[]{:S(2)}, u32[]{:S(2)}) collective-permute-start(s32[1,128]{1,0:T(1,128)} %ids_ref), channel_id=1, source_target_pairs={{0,24},{4,28},{8,16},{12,20},{16,8},{20,12},{24,0},{28,4},{1,25},{... | collective-permute-start | bytes 1544 | tf_op jit(solution)/shard_map/ppermute | solution.py:26
  5.0 3.7 %collective-permute-start.1 = (s32[1,128]{1,0:T(1,128)}, s32[1,128]{1,0:T(1,128)S(1)}, u32[]{:S(2)}, u32[]{:S(2)}) collective-permute-start(s32[1,128]{1,0:T(1,128)} %ids_ref), channel_id=1, source_target_pairs={{0,8},{4,12},{8,0},{12,4},{16,24},{20,28},{24,16},{28,20},{1,9},{5... | collective-permute-start | bytes 1544 | tf_op jit(solution)/shard_map/ppermute | solution.py:26
  5.1 4.6 %collective-permute-start = (s32[1,128]{1,0:T(1,128)}, s32[1,128]{1,0:T(1,128)S(1)}, u32[]{:S(2)}, u32[]{:S(2)}) collective-permute-start(s32[1,128]{1,0:T(1,128)} %ids_ref), channel_id=1, source_target_pairs={{0,16},{4,20},{8,24},{12,28},{16,0},{20,4},{24,8},{28,12},{1,17},{... | collective-permute-start | bytes 1544 | tf_op jit(solution)/shard_map/ppermute | solution.py:26
  5.6 2.2 %copy-start.5 = (bf16[32,128]{1,0:T(8,128)(2,1)S(1)}, bf16[32,128]{1,0:T(8,128)(2,1)}, u32[]{:S(2)}) copy-start(bf16[32,128]{1,0:T(8,128)(2,1)} %param.12) | copy-start | bytes 24580
  5.6 4.0 %copy-start.3 = (s32[1,128]{1,0:T(1,128)S(1)}, s32[1,128]{1,0:T(1,128)}, u32[]{:S(2)}) copy-start(s32[1,128]{1,0:T(1,128)} %ids_ref) | copy-start | bytes 1540
  5.6 11.3 %copy-start.2 = (f32[4096]{0:T(1024)S(1)}, f32[4096]{0:T(1024)}, u32[]{:S(2)}) copy-start(f32[4096]{0:T(1024)} %param.9) | copy-start | bytes 49156
  9.6 3.7 %collective-permute-start.3 = (s32[4,128]{1,0:T(4,128)S(1)}, s32[4,128]{1,0:T(4,128)S(1)}, u32[]{:S(2)}, u32[]{:S(2)}) collective-permute-start(s32[4,128]{1,0:T(4,128)S(1)} %pad_add_fusion.4), channel_id=1, source_target_pairs={{0,4},{4,0},{8,12},{12,8},{16,20},{20,16},{24,28},{28,24},{1,5},{5... | collective-permute-start | bytes 6152 | tf_op jit(solution)/shard_map/ppermute | solution.py:26
  11.2 17.7 %collective-permute-start.8 = (bf16[512,512]{1,0:T(8,128)(2,1)}, bf16[512,512]{1,0:T(8,128)(2,1)S(1)}, u32[]{:S(2)}, u32[]{:S(2)}) collective-permute-start(bf16[512,512]{1,0:T(8,128)(2,1)} %get-tuple-element.43), channel_id=1, source_target_pairs={{0,8},{4,12},{8,0},{12,4},{16,24},{20,28},{24,16},{28,20},{1,9},{5... | collective-permute-start | bytes 1572872 | tf_op jit(solution)/shard_map/ppermute | solution.py:26
  13.3 15.6 %collective-permute-start.7 = (s32[8,128]{1,0:T(8,128)S(1)}, s32[8,128]{1,0:T(8,128)S(1)}, u32[]{:S(2)}, u32[]{:S(2)}) collective-permute-start(s32[8,128]{1,0:T(8,128)S(1)} %pad_add_fusion.2), channel_id=1, source_target_pairs={{0,1},{1,2},{2,3},{3,0},{4,5},{5,6},{6,7},{7,4},{8,9},{9,10},{10,1... | collective-permute-start | bytes 12296 | tf_op jit(solution)/shard_map/ppermute | solution.py:21
  13.3 15.4 %collective-permute-start.6 = (s32[8,128]{1,0:T(8,128)S(1)}, s32[8,128]{1,0:T(8,128)S(1)}, u32[]{:S(2)}, u32[]{:S(2)}) collective-permute-start(s32[8,128]{1,0:T(8,128)S(1)} %pad_add_fusion.2), channel_id=1, source_target_pairs={{0,2},{1,3},{2,0},{3,1},{4,6},{5,7},{6,4},{7,5},{8,10},{9,11},{10,... | collective-permute-start | bytes 12296 | tf_op jit(solution)/shard_map/ppermute | solution.py:21
  14.9 23.7 %collective-permute-start.4 = (bf16[512,512]{1,0:T(8,128)(2,1)}, bf16[512,512]{1,0:T(8,128)(2,1)S(1)}, u32[]{:S(2)}, u32[]{:S(2)}) collective-permute-start(bf16[512,512]{1,0:T(8,128)(2,1)} %get-tuple-element.40), channel_id=1, source_target_pairs={{0,8},{4,12},{8,0},{12,4},{16,24},{20,28},{24,16},{28,20},{1,9},{5... | collective-permute-start | bytes 1572872 | tf_op jit(solution)/shard_map/ppermute | solution.py:26
  16.9 2.2 %copy-start.1 = (bf16[512,4096]{1,0:T(8,128)(2,1)S(1)}, bf16[512,4096]{1,0:T(8,128)(2,1)}, u32[]{:S(2)}) copy-start(bf16[512,4096]{1,0:T(8,128)(2,1)} %rows_ref.1) | copy-start | bytes 12582916
  19.1 10.6 %copy-start.4 = (f32[3,3,512]{2,1,0:T(4,128)S(1)}, f32[3,3,512]{2,1,0:T(4,128)}, u32[]{:S(2)}) copy-start(f32[3,3,512]{2,1,0:T(4,128)} %short_ref.3) | copy-start | bytes 55300
  28.9 13.9 %collective-permute-start.9 = (bf16[512,512]{1,0:T(8,128)(2,1)S(1)}, bf16[512,512]{1,0:T(8,128)(2,1)S(1)}, u32[]{:S(2)}, u32[]{:S(2)}) collective-permute-start(bf16[512,512]{1,0:T(8,128)(2,1)S(1)} %collective-permute-done.8), channel_id=1, source_target_pairs={{0,2},{1,3},{2,0},{3,1},{4,6},{5,7},{6,4},{7,5},{8,10},{9,11},{10,... | collective-permute-start | bytes 1572872 | tf_op jit(solution)/shard_map/ppermute | solution.py:26
  31.8 16.4 %collective-permute-start.11 = (bf16[2,128,512]{2,1,0:T(8,128)(2,1)S(1)}, bf16[2,128,512]{2,1,0:T(8,128)(2,1)S(1)}, u32[]{:S(2)}, u32[]{:S(2)}) collective-permute-start(bf16[2,128,512]{2,1,0:T(8,128)(2,1)S(1)} %shard_map.76), channel_id=1, source_target_pairs={{0,8},{4,12},{8,0},{12,4},{16,24},{20,28},{24,16},{28,20},{1,9},{5... | collective-permute-start | bytes 786440 | tf_op jit(solution)/shard_map/ppermute | solution.py:26
  38.6 7.8 %collective-permute-start.5 = (bf16[512,512]{1,0:T(8,128)(2,1)S(1)}, bf16[512,512]{1,0:T(8,128)(2,1)S(1)}, u32[]{:S(2)}, u32[]{:S(2)}) collective-permute-start(bf16[512,512]{1,0:T(8,128)(2,1)S(1)} %collective-permute-done.4), channel_id=1, source_target_pairs={{0,1},{1,0},{2,3},{3,2},{4,5},{5,4},{6,7},{7,6},{8,9},{9,8},{10,11... | collective-permute-start | bytes 1572872 | tf_op jit(solution)/shard_map/ppermute | solution.py:26
  43.0 5.2 %collective-permute-start.12 = (bf16[2,512,256]{2,1,0:T(8,128)(2,1)S(1)}, bf16[2,512,256]{2,1,0:T(8,128)(2,1)S(1)}, u32[]{:S(2)}, u32[]{:S(2)}) collective-permute-start(bf16[2,512,256]{2,1,0:T(8,128)(2,1)S(1)} %get-tuple-element.74.refs_4_), channel_id=1, source_target_pairs={{0,1},{1,0},{2,3},{3,2},{4,5},{5,4},{6,7},{7,6},{8,9},{9,8},{10,11... | collective-permute-start | bytes 1572872 | tf_op jit(solution)/shard_map/ppermute | solution.py:26
  43.1 8.8 %collective-permute-start.10 = (bf16[2,128,512]{2,1,0:T(8,128)(2,1)S(1)}, bf16[2,128,512]{2,1,0:T(8,128)(2,1)S(1)}, u32[]{:S(2)}, u32[]{:S(2)}) collective-permute-start(bf16[2,128,512]{2,1,0:T(8,128)(2,1)S(1)} %get-tuple-element.77), channel_id=1, source_target_pairs={{0,8},{4,12},{8,0},{12,4},{16,24},{20,28},{24,16},{28,20},{1,9},{5... | collective-permute-start | bytes 786440 | tf_op jit(solution)/shard_map/ppermute | solution.py:26
  43.5 4.7 %copy-start = (bf16[512,4096]{1,0:T(8,128)(2,1)S(1)}, bf16[512,4096]{1,0:T(8,128)(2,1)}, u32[]{:S(2)}) copy-start(bf16[512,4096]{1,0:T(8,128)(2,1)} %refs_3_.17) | copy-start | bytes 12582916
  43.5 10.0 %collective-permute-start.13 = (bf16[2,512,256]{2,1,0:T(8,128)(2,1)S(1)}, bf16[2,512,256]{2,1,0:T(8,128)(2,1)S(1)}, u32[]{:S(2)}, u32[]{:S(2)}) collective-permute-start(bf16[2,512,256]{2,1,0:T(8,128)(2,1)S(1)} %get-tuple-element.73.refs_4_), channel_id=1, source_target_pairs={{0,1},{1,0},{2,3},{3,2},{4,5},{5,4},{6,7},{7,6},{8,9},{9,8},{10,11... | collective-permute-start | bytes 1572872 | tf_op jit(solution)/shard_map/ppermute | solution.py:26
  46.6 14.8 %collective-permute-start.18 = (bf16[2,512,256]{2,1,0:T(8,128)(2,1)S(1)}, bf16[2,512,256]{2,1,0:T(8,128)(2,1)S(1)}, u32[]{:S(2)}, u32[]{:S(2)}) collective-permute-start(bf16[2,512,256]{2,1,0:T(8,128)(2,1)S(1)} %get-tuple-element.69.refs_4_), channel_id=1, source_target_pairs={{0,2},{1,3},{2,0},{3,1},{4,6},{5,7},{6,4},{7,5},{8,10},{9,11},{10,... | collective-permute-start | bytes 1572872 | tf_op jit(solution)/shard_map/ppermute | solution.py:26
  48.9 13.9 %collective-permute-start.15 = (bf16[2,4,128,256]{3,2,1,0:T(8,128)(2,1)S(1)}, bf16[2,4,128,256]{3,2,1,0:T(8,128)(2,1)S(1)}, u32[]{:S(2)}, u32[]{:S(2)}) collective-permute-start(bf16[2,4,128,256]{3,2,1,0:T(8,128)(2,1)S(1)} %shard_map.79), channel_id=1, source_target_pairs={{0,4},{4,0},{8,12},{12,8},{16,20},{20,16},{24,28},{28,24},{1,5},{5... | collective-permute-start | bytes 1572872 | tf_op jit(solution)/shard_map/ppermute | solution.py:26
  51.9 20.1 %collective-permute-start.21 = (bf16[2,512,256]{2,1,0:T(8,128)(2,1)S(1)}, bf16[2,512,256]{2,1,0:T(8,128)(2,1)S(1)}, u32[]{:S(2)}, u32[]{:S(2)}) collective-permute-start(bf16[2,512,256]{2,1,0:T(8,128)(2,1)S(1)} %get-tuple-element.60.refs_4_), channel_id=1, source_target_pairs={{0,2},{1,3},{2,0},{3,1},{4,6},{5,7},{6,4},{7,5},{8,10},{9,11},{10,... | collective-permute-start | bytes 1572872 | tf_op jit(solution)/shard_map/ppermute | solution.py:26
  54.9 19.6 %collective-permute-start.14 = (bf16[2,1,4,128,128]{4,3,2,1,0:T(8,128)(2,1)S(1)}, bf16[2,1,4,128,128]{4,3,2,1,0:T(8,128)(2,1)S(1)}, u32[]{:S(2)}, u32[]{:S(2)}) collective-permute-start(bf16[2,1,4,128,128]{4,3,2,1,0:T(8,128)(2,1)S(1)} %slice.129), channel_id=1, source_target_pairs={{0,16},{4,20},{8,24},{12,28},{16,0},{20,4},{24,8},{28,12},{1,17},{... | collective-permute-start | bytes 786440 | tf_op jit(solution)/shard_map/ppermute | solution.py:26
  63.0 38.2 %collective-permute-start.17 = (bf16[1,4,128,256]{3,2,1,0:T(8,128)(2,1)S(1)}, bf16[1,4,128,256]{3,2,1,0:T(8,128)(2,1)S(1)}, u32[]{:S(2)}, u32[]{:S(2)}) collective-permute-start(bf16[1,4,128,256]{3,2,1,0:T(8,128)(2,1)S(1)} %get-tuple-element.72), channel_id=1, source_target_pairs={{0,16},{4,20},{8,24},{12,28},{16,0},{20,4},{24,8},{28,12},{1,17},{... | collective-permute-start | bytes 786440 | tf_op jit(solution)/shard_map/ppermute | solution.py:26
  65.2 14.9 %collective-permute-start.19 = (bf16[2,4,128,256]{3,2,1,0:T(8,128)(2,1)S(1)}, bf16[2,4,128,256]{3,2,1,0:T(8,128)(2,1)S(1)}, u32[]{:S(2)}, u32[]{:S(2)}) collective-permute-start(bf16[2,4,128,256]{3,2,1,0:T(8,128)(2,1)S(1)} %shard_map.85), channel_id=1, source_target_pairs={{0,4},{4,0},{8,12},{12,8},{16,20},{20,16},{24,28},{28,24},{1,5},{5... | collective-permute-start | bytes 1572872 | tf_op jit(solution)/shard_map/ppermute | solution.py:26
  72.7 18.6 %collective-permute-start.22 = (bf16[2,4,128,256]{3,2,1,0:T(8,128)(2,1)S(1)}, bf16[2,4,128,256]{3,2,1,0:T(8,128)(2,1)S(1)}, u32[]{:S(2)}, u32[]{:S(2)}) collective-permute-start(bf16[2,4,128,256]{3,2,1,0:T(8,128)(2,1)S(1)} %shard_map.88), channel_id=1, source_target_pairs={{0,4},{4,0},{8,12},{12,8},{16,20},{20,16},{24,28},{28,24},{1,5},{5... | collective-permute-start | bytes 1572872 | tf_op jit(solution)/shard_map/ppermute | solution.py:26
  74.6 24.6 %collective-permute-start.16 = (bf16[1,4,128,128]{3,2,1,0:T(8,128)(2,1)S(1)}, bf16[1,4,128,128]{3,2,1,0:T(8,128)(2,1)S(1)}, u32[]{:S(2)}, u32[]{:S(2)}) collective-permute-start(bf16[1,4,128,128]{3,2,1,0:T(8,128)(2,1)S(1)} %get-tuple-element.80), channel_id=1, source_target_pairs={{0,4},{4,0},{8,12},{12,8},{16,20},{20,16},{24,28},{28,24},{1,5},{5... | collective-permute-start | bytes 393224 | tf_op jit(solution)/shard_map/ppermute | solution.py:26
  77.1 20.5 %collective-permute-start.24 = (bf16[2,4,128,128]{3,2,1,0:T(8,128)(2,1)S(1)}, bf16[2,4,128,128]{3,2,1,0:T(8,128)(2,1)S(1)}, u32[]{:S(2)}, u32[]{:S(2)}) collective-permute-start(bf16[2,4,128,128]{3,2,1,0:T(8,128)(2,1)S(1)} %shard_map.91), channel_id=1, source_target_pairs={{0,4},{4,0},{8,12},{12,8},{16,20},{20,16},{24,28},{28,24},{1,5},{5... | collective-permute-start | bytes 786440 | tf_op jit(solution)/shard_map/ppermute | solution.py:26
  80.2 22.9 %collective-permute-start.20 = (bf16[1,4,128,256]{3,2,1,0:T(8,128)(2,1)S(1)}, bf16[1,4,128,256]{3,2,1,0:T(8,128)(2,1)S(1)}, u32[]{:S(2)}, u32[]{:S(2)}) collective-permute-start(bf16[1,4,128,256]{3,2,1,0:T(8,128)(2,1)S(1)} %get-tuple-element.67), channel_id=1, source_target_pairs={{0,16},{4,20},{8,24},{12,28},{16,0},{20,4},{24,8},{28,12},{1,17},{... | collective-permute-start | bytes 786440 | tf_op jit(solution)/shard_map/ppermute | solution.py:26
  91.5 15.8 %collective-permute-start.23 = (bf16[1,4,128,256]{3,2,1,0:T(8,128)(2,1)S(1)}, bf16[1,4,128,256]{3,2,1,0:T(8,128)(2,1)S(1)}, u32[]{:S(2)}, u32[]{:S(2)}) collective-permute-start(bf16[1,4,128,256]{3,2,1,0:T(8,128)(2,1)S(1)} %get-tuple-element.65), channel_id=1, source_target_pairs={{0,16},{4,20},{8,24},{12,28},{16,0},{20,4},{24,8},{28,12},{1,17},{... | collective-permute-start | bytes 786440 | tf_op jit(solution)/shard_map/ppermute | solution.py:26
  97.7 11.8 %collective-permute-start.25 = (bf16[1,4,128,128]{3,2,1,0:T(8,128)(2,1)S(1)}, bf16[1,4,128,128]{3,2,1,0:T(8,128)(2,1)S(1)}, u32[]{:S(2)}, u32[]{:S(2)}) collective-permute-start(bf16[1,4,128,128]{3,2,1,0:T(8,128)(2,1)S(1)} %get-tuple-element.78), channel_id=1, source_target_pairs={{0,16},{4,20},{8,24},{12,28},{16,0},{20,4},{24,8},{28,12},{1,17},{... | collective-permute-start | bytes 393224 | tf_op jit(solution)/shard_map/ppermute | solution.py:26

commit v13 on v12

--- a/solution.py
+++ b/solution.py
@@ -346,28 +346,32 @@
     for group in [bits[i : i + 2] for i in range(2, len(bits), 2)]:
         ids = level_ids(ids, group)
     early = swap(early, "fsdp", beside_bit)
-    ids, embedding_then, late = tie((ids, embedding, late))
+    ids, in_proj, late = tie((ids, in_proj, late))
     late = swap(late, "fsdp", beside_bit)
     ids = with_lead(ids)
-    table = project(embedding_then, norm_gain, in_proj)
+    table = project(embedding, norm_gain, in_proj)
     table, early = tie((table, early))
-    early_pair = jnp.stack([early, swap(early, "ctx", 2)])
+    middle = early.shape[1] // 2
+    body_columns, head_columns = early[:, middle:], early[:, :middle]
+    body_pair = jnp.stack([body_columns, swap(body_columns, "ctx", 2)])
 
     part = ids.shape[0] // 4
     quarters = [ids[n * part : (n + 1) * part] for n in range(4)]
     sent = mix(quarters[3], table, short_taps, toeplitz, tok_len)
     kept, sent = tie((jnp.concatenate([quarters[1], quarters[2], quarters[0]], axis=0), sent))
     other = [swap(sent, "fsdp", beside_bit)]
+    head_columns, sent = tie((head_columns, sent))
+    head_pair = jnp.stack([head_columns, swap(head_columns, "ctx", 2)])
     gated = mix(kept, table, short_taps, toeplitz, tok_len)
-    gated, early_pair = tie((gated, early_pair))
+    gated, body_pair = tie((gated, body_pair))
     other.append(swap(gated[:part], "fsdp", beside_bit))
     mine = [gated[part : 2 * part], gated[2 * part :]]
-    middle = early.shape[1] // 2
-    pairs = [(columns, swap(columns, "ctx", 1)) for columns in (early_pair[:, :, :middle], early_pair[:, :, middle:])]
+    pairs = [None, (body_pair, swap(body_pair, "ctx", 1))]
     late_pair = jnp.stack([late, swap(late, "ctx", 1)])
     own_ids, gated = tie((token_ids, gated))
     out = residual(own_ids, embedding)
-    late_pair, out = tie((late_pair, out))
+    late_pair, head_pair, out = tie((late_pair, head_pair, out))
+    pairs[0] = (head_pair, swap(head_pair, "ctx", 1))
     pairs += [(columns, swap(columns, "ctx", 2)) for columns in (late_pair[:, :, :middle],)]
     (head, body, foot), tail = SPLITS[0][3], SPLITS[1][3]
 

time: 112 us -> 110 us (0.982)
  waiting for transfers between devices: 34.2 us -> 30.4 us
  starting transfers between devices: 32.4 us -> 34.2 us
    ppermute x24 -> x25, waiting for transfers between devices: 34.2 us -> 30.3 us  [swap(): return lax.ppermute(x, axis, [(i, i ^ mask) for i in range(peers)])]
    ppermute x24 -> x25, starting transfers between devices: 30.8 us -> 32.6 us  [swap(): return lax.ppermute(x, axis, [(i, i ^ mask) for i in range(peers)])]
  transfers between devices with their start and end apart: 26 -> 27, of which waited for: 13 -> 10; matrix products, arithmetic and copies ran while one was open for 1% -> 1% of each run, Pallas kernels for 35% -> 35%
where the time goes in v13:
time: 110 us; the launch traced here: 109 us
  Pallas kernels  40.7 us (37%)
  starting transfers between devices  34.2 us (31%)
  waiting for transfers between devices  30.4 us (28%)
  local copies, waits for them, and re-layouts  2.66 us (2%)
    ppermute x25, starting transfers between devices, swap(): return lax.ppermute(x, axis, [(i, i ^ mask) for i in range(peers)])  32.6 us
    ppermute x25, waiting for transfers between devices, swap(): return lax.ppermute(x, axis, [(i, i ^ mask) for i in range(peers)])  30.3 us
    pallas_call x5, Pallas kernels, place_pieces(): pl.pallas_call(functools.partial(place_kernel, split, step), grid_spec=pl...  9.81 us
    pallas_call x1, Pallas kernels, project(): pl.pallas_call(table_kernel, grid=(1,), in_specs=[hbm, hbm, pl.BlockSpec(...  9.69 us
    pallas_call x2, Pallas kernels, mix(): pl.pallas_call(mixer_kernel, grid=(windows // 2,), in_specs=[pl.BlockSpec...  8.5 us
    pallas_call x9, Pallas kernels, panel(): pl.pallas_call(panel_kernel, grid_spec=pltpu.PrefetchScalarGridSpec(num_s...  7.19 us
    pallas_call x1, Pallas kernels, residual(): pl.pallas_call(residual_kernel, grid=(4,), in_specs=[whole(token_ids), pl...  2.65 us
    pallas_call x1, Pallas kernels, cut_pieces(): pl.pallas_call(cut_kernel, grid_spec=pltpu.PrefetchScalarGridSpec(num_sca...  2.23 us
  transfers between devices with their start and end apart: 27, of which 10 were waited for; matrix products, arithmetic and copies ran while one was open for 1% of the time, Pallas kernels for 35%

profile of v13, /device:TPU:0, one launch (start us, length us, event | category | flops | bytes accessed | tf_op | source)
XLA Modules:
  0.0 109.4 jit_solution(5337283647157348869)
XLA Ops:
  0.0 5.0 %collective-permute-start.2 = (s32[1,128]{1,0:T(1,128)}, s32[1,128]{1,0:T(1,128)S(1)}, u32[]{:S(2)}, u32[]{:S(2)}) collective-permute-start(s32[1,128]{1,0:T(1,128)} %ids_ref), channel_id=1, source_target_pairs={{0,24},{4,28},{8,16},{12,20},{16,8},{20,12},{24,0},{28,4},{1,25},{... | collective-permute-start | bytes 1544 | tf_op jit(solution)/shard_map/ppermute | solution.py:26
  5.6 2.2 %shard_map.73 = (bf16[512,512]{1,0:T(8,128)(2,1)}, bf16[512,512]{1,0:T(8,128)(2,1)}) custom-call(s32[1]{0:T(128)} %bitcast.place_ref, bf16[512,4096]{1,0:T(8,128)(2,1)} %refs_3_.17, bf16[512,4096]{1,0:T(8,128)(2,1)} %refs_3_.17), custom_call_target="tpu_custom_call" | custom-call | bytes 2000000 | tf_op jit(solution)/shard_map/pallas_call | solution.py:200
  9.6 1.6 %collective-permute-start.3 = (s32[4,128]{1,0:T(4,128)S(1)}, s32[4,128]{1,0:T(4,128)S(1)}, u32[]{:S(2)}, u32[]{:S(2)}) collective-permute-start(s32[4,128]{1,0:T(4,128)S(1)} %pad_add_fusion.4), channel_id=1, source_target_pairs={{0,4},{4,0},{8,12},{12,8},{16,20},{20,16},{24,28},{28,24},{1,5},{5... | collective-permute-start | bytes 6152 | tf_op jit(solution)/shard_map/ppermute | solution.py:26
  11.2 2.0 %collective-permute-start.6 = (bf16[512,512]{1,0:T(8,128)(2,1)}, bf16[512,512]{1,0:T(8,128)(2,1)S(1)}, u32[]{:S(2)}, u32[]{:S(2)}) collective-permute-start(bf16[512,512]{1,0:T(8,128)(2,1)} %get-tuple-element.44), channel_id=1, source_target_pairs={{0,8},{4,12},{8,0},{12,4},{16,24},{20,28},{24,16},{28,20},{1,9},{5... | collective-permute-start | bytes 1572872 | tf_op jit(solution)/shard_map/ppermute | solution.py:26
  13.3 1.6 %collective-permute-start.7 = (s32[8,128]{1,0:T(8,128)S(1)}, s32[8,128]{1,0:T(8,128)S(1)}, u32[]{:S(2)}, u32[]{:S(2)}) collective-permute-start(s32[8,128]{1,0:T(8,128)S(1)} %pad_add_fusion.2), channel_id=1, source_target_pairs={{0,2},{1,3},{2,0},{3,1},{4,6},{5,7},{6,4},{7,5},{8,10},{9,11},{10,... | collective-permute-start | bytes 12296 | tf_op jit(solution)/shard_map/ppermute | solution.py:21
  14.9 2.0 %collective-permute-start.4 = (bf16[512,512]{1,0:T(8,128)(2,1)}, bf16[512,512]{1,0:T(8,128)(2,1)S(1)}, u32[]{:S(2)}, u32[]{:S(2)}) collective-permute-start(bf16[512,512]{1,0:T(8,128)(2,1)} %get-tuple-element.42), channel_id=1, source_target_pairs={{0,8},{4,12},{8,0},{12,4},{16,24},{20,28},{24,16},{28,20},{1,9},{5... | collective-permute-start | bytes 1572872 | tf_op jit(solution)/shard_map/ppermute | solution.py:26
  16.9 2.2 %copy-done.1 = bf16[512,4096]{1,0:T(8,128)(2,1)S(1)} copy-done((bf16[512,4096]{1,0:T(8,128)(2,1)S(1)}, bf16[512,4096]{1,0:T(8,128)(2,1)}, u32[]{:S(2)}) %copy-start.1) | copy-done | bytes 4194328
  19.1 9.7 %shard_map.75.table_ref = bf16[3,512,512]{2,1,0:T(8,128)(2,1)S(1)} custom-call(bf16[512,4096]{1,0:T(8,128)(2,1)S(1)} %copy-done.1, bf16[3,4096,512]{2,1,0:T(8,128)(2,1)} %weight_hbm, f32[1,4096]{1,0:T(1,128)S(1)} %bitcast.46), custom_call_target="tpu_custom_call" | custom-call | flops 3000000000 | tf_op jit(solution)/shard_map/pallas_call | solution.py:101
  29.7 2.1 %shard_map.76 = bf16[2,128,512]{2,1,0:T(8,128)(2,1)S(1)} custom-call(s32[2,1,272]{2,1,0:T(1,128)S(1)} %copy.13.ids_ref, bf16[3,512,512]{2,1,0:T(8,128)(2,1)S(1)} %shard_map.75.table_ref, f32[3,3,512]{2,1,0:T(4,128)S(1)} %copy-done.4, bf16[4,1024,256]{2,1,0:T(8,128)(2,1)S(1)} %shard_map.74.toeplitz), custom_call_target="tpu_custom_call" | custom-call | flops 1500000000 | tf_op jit(solution)/shard_map/pallas_call | solution.py:167
  32.1 1.4 %collective-permute-start.9 = (bf16[512,256]{1,0:T(8,128)(2,1)S(1)}, bf16[512,256]{1,0:T(8,128)(2,1)S(1)}, u32[]{:S(2)}, u32[]{:S(2)}) collective-permute-start(bf16[512,256]{1,0:T(8,128)(2,1)S(1)} %get-tuple-element.50), channel_id=1, source_target_pairs={{0,2},{1,3},{2,0},{3,1},{4,6},{5,7},{6,4},{7,5},{8,10},{9,11},{10,... | collective-permute-start | bytes 786440 | tf_op jit(solution)/shard_map/ppermute | solution.py:26
  33.5 6.4 %shard_map.77 = bf16[6,128,512]{2,1,0:T(8,128)(2,1)S(1)} custom-call(s32[6,1,272]{2,1,0:T(1,128)S(1)} %reshape.54.ids_ref, bf16[3,512,512]{2,1,0:T(8,128)(2,1)S(1)} %shard_map.75.table_ref, f32[3,3,512]{2,1,0:T(4,128)S(1)} %copy-done.4, bf16[4,1024,256]{2,1,0:T(8,128)(2,1)S(1)} %shard_map.74.toeplitz), custom_call_target="tpu_custom_call" | custom-call | flops 1500000000 | tf_op jit(solution)/shard_map/pallas_call | solution.py:167
  40.2 2.0 %collective-permute-start.11 = (bf16[2,128,512]{2,1,0:T(8,128)(2,1)S(1)}, bf16[2,128,512]{2,1,0:T(8,128)(2,1)S(1)}, u32[]{:S(2)}, u32[]{:S(2)}) collective-permute-start(bf16[2,128,512]{2,1,0:T(8,128)(2,1)S(1)} %get-tuple-element.79), channel_id=1, source_target_pairs={{0,8},{4,12},{8,0},{12,4},{16,24},{20,28},{24,16},{28,20},{1,9},{5... | collective-permute-start | bytes 786440 | tf_op jit(solution)/shard_map/ppermute | solution.py:26
  42.4 2.7 %shard_map.78.so_far_ref = bf16[128,4096]{1,0:T(8,128)(2,1)} custom-call(s32[1,128]{1,0:T(1,128)S(1)} %copy-done.3, bf16[512,4096]{1,0:T(8,128)(2,1)S(1)} %copy-done.1), custom_call_target="tpu_custom_call" | custom-call | flops 400000000 | tf_op jit(solution)/shard_map/pallas_call | solution.py:290
  47.1 1.6 %collective-permute-start.16 = (bf16[2,4,128,256]{3,2,1,0:T(8,128)(2,1)S(1)}, bf16[2,4,128,256]{3,2,1,0:T(8,128)(2,1)S(1)}, u32[]{:S(2)}, u32[]{:S(2)}) collective-permute-start(bf16[2,4,128,256]{3,2,1,0:T(8,128)(2,1)S(1)} %shard_map.79), channel_id=1, source_target_pairs={{0,4},{4,0},{8,12},{12,8},{16,20},{20,16},{24,28},{28,24},{1,5},{5... | collective-permute-start | bytes 1572872 | tf_op jit(solution)/shard_map/ppermute | solution.py:26
  51.6 1.5 %collective-permute-start.15 = (bf16[2,1,4,128,128]{4,3,2,1,0:T(8,128)(2,1)S(1)}, bf16[2,1,4,128,128]{4,3,2,1,0:T(8,128)(2,1)S(1)}, u32[]{:S(2)}, u32[]{:S(2)}) collective-permute-start(bf16[2,1,4,128,128]{4,3,2,1,0:T(8,128)(2,1)S(1)} %slice.129), channel_id=1, source_target_pairs={{0,16},{4,20},{8,24},{12,28},{16,0},{20,4},{24,8},{28,12},{1,17},{... | collective-permute-start | bytes 786440 | tf_op jit(solution)/shard_map/ppermute | solution.py:26
  54.6 5.8 %collective-permute-done.19.refs_5_ = bf16[2,512,256]{2,1,0:T(8,128)(2,1)S(1)} collective-permute-done((bf16[2,512,256]{2,1,0:T(8,128)(2,1)S(1)}, bf16[2,512,256]{2,1,0:T(8,128)(2,1)S(1)}, u32[]{:S(2)}, u32[]{:S(2)}) %collective-permute-start.19) | collective-permute-done | bytes 524320 | tf_op jit(solution)/shard_map/ppermute | solution.py:26
  61.4 1.5 %collective-permute-start.18 = (bf16[1,4,128,256]{3,2,1,0:T(8,128)(2,1)S(1)}, bf16[1,4,128,256]{3,2,1,0:T(8,128)(2,1)S(1)}, u32[]{:S(2)}, u32[]{:S(2)}) collective-permute-start(bf16[1,4,128,256]{3,2,1,0:T(8,128)(2,1)S(1)} %get-tuple-element.76), channel_id=1, source_target_pairs={{0,16},{4,20},{8,24},{12,28},{16,0},{20,4},{24,8},{28,12},{1,17},{... | collective-permute-start | bytes 786440 | tf_op jit(solution)/shard_map/ppermute | solution.py:26
  63.6 1.6 %collective-permute-start.20 = (bf16[2,4,128,256]{3,2,1,0:T(8,128)(2,1)S(1)}, bf16[2,4,128,256]{3,2,1,0:T(8,128)(2,1)S(1)}, u32[]{:S(2)}, u32[]{:S(2)}) collective-permute-start(bf16[2,4,128,256]{3,2,1,0:T(8,128)(2,1)S(1)} %shard_map.85), channel_id=1, source_target_pairs={{0,4},{4,0},{8,12},{12,8},{16,20},{20,16},{24,28},{28,24},{1,5},{5... | collective-permute-start | bytes 1572872 | tf_op jit(solution)/shard_map/ppermute | solution.py:26
  65.1 5.9 %collective-permute-done.22.refs_5_ = bf16[2,512,256]{2,1,0:T(8,128)(2,1)S(1)} collective-permute-done((bf16[2,512,256]{2,1,0:T(8,128)(2,1)S(1)}, bf16[2,512,256]{2,1,0:T(8,128)(2,1)S(1)}, u32[]{:S(2)}, u32[]{:S(2)}) %collective-permute-start.22) | collective-permute-done | bytes 524320 | tf_op jit(solution)/shard_map/ppermute | solution.py:26
  71.7 1.6 %collective-permute-start.23 = (bf16[2,4,128,256]{3,2,1,0:T(8,128)(2,1)S(1)}, bf16[2,4,128,256]{3,2,1,0:T(8,128)(2,1)S(1)}, u32[]{:S(2)}, u32[]{:S(2)}) collective-permute-start(bf16[2,4,128,256]{3,2,1,0:T(8,128)(2,1)S(1)} %shard_map.88), channel_id=1, source_target_pairs={{0,4},{4,0},{8,12},{12,8},{16,20},{20,16},{24,28},{28,24},{1,5},{5... | collective-permute-start | bytes 1572872 | tf_op jit(solution)/shard_map/ppermute | solution.py:26
  75.5 1.6 %collective-permute-start.17 = (bf16[1,4,128,128]{3,2,1,0:T(8,128)(2,1)S(1)}, bf16[1,4,128,128]{3,2,1,0:T(8,128)(2,1)S(1)}, u32[]{:S(2)}, u32[]{:S(2)}) collective-permute-start(bf16[1,4,128,128]{3,2,1,0:T(8,128)(2,1)S(1)} %get-tuple-element.85), channel_id=1, source_target_pairs={{0,4},{4,0},{8,12},{12,8},{16,20},{20,16},{24,28},{28,24},{1,5},{5... | collective-permute-start | bytes 393224 | tf_op jit(solution)/shard_map/ppermute | solution.py:26
  78.0 1.7 %collective-permute-start.21 = (bf16[1,4,128,256]{3,2,1,0:T(8,128)(2,1)S(1)}, bf16[1,4,128,256]{3,2,1,0:T(8,128)(2,1)S(1)}, u32[]{:S(2)}, u32[]{:S(2)}) collective-permute-start(bf16[1,4,128,256]{3,2,1,0:T(8,128)(2,1)S(1)} %get-tuple-element.71), channel_id=1, source_target_pairs={{0,16},{4,20},{8,24},{12,28},{16,0},{20,4},{24,8},{28,12},{1,17},{... | collective-permute-start | bytes 786440 | tf_op jit(solution)/shard_map/ppermute | solution.py:26
  79.7 9.4 %collective-permute-done.23 = bf16[2,4,128,256]{3,2,1,0:T(8,128)(2,1)S(1)} collective-permute-done((bf16[2,4,128,256]{3,2,1,0:T(8,128)(2,1)S(1)}, bf16[2,4,128,256]{3,2,1,0:T(8,128)(2,1)S(1)}, u32[]{:S(2)}, u32[]{:S(2)}) %collective-permute-start.23) | collective-permute-done | bytes 524320 | tf_op jit(solution)/shard_map/ppermute | solution.py:26
  89.2 1.7 %collective-permute-start.24 = (bf16[1,4,128,256]{3,2,1,0:T(8,128)(2,1)S(1)}, bf16[1,4,128,256]{3,2,1,0:T(8,128)(2,1)S(1)}, u32[]{:S(2)}, u32[]{:S(2)}) collective-permute-start(bf16[1,4,128,256]{3,2,1,0:T(8,128)(2,1)S(1)} %get-tuple-element.69), channel_id=1, source_target_pairs={{0,16},{4,20},{8,24},{12,28},{16,0},{20,4},{24,8},{28,12},{1,17},{... | collective-permute-start | bytes 786440 | tf_op jit(solution)/shard_map/ppermute | solution.py:26
  90.9 3.2 %collective-permute-done.25 = bf16[2,4,128,128]{3,2,1,0:T(8,128)(2,1)S(1)} collective-permute-done((bf16[2,4,128,128]{3,2,1,0:T(8,128)(2,1)S(1)}, bf16[2,4,128,128]{3,2,1,0:T(8,128)(2,1)S(1)}, u32[]{:S(2)}, u32[]{:S(2)}) %collective-permute-start.25) | collective-permute-done | bytes 262176 | tf_op jit(solution)/shard_map/ppermute | solution.py:26
  94.2 1.6 %collective-permute-start.26 = (bf16[1,4,128,128]{3,2,1,0:T(8,128)(2,1)S(1)}, bf16[1,4,128,128]{3,2,1,0:T(8,128)(2,1)S(1)}, u32[]{:S(2)}, u32[]{:S(2)}) collective-permute-start(bf16[1,4,128,128]{3,2,1,0:T(8,128)(2,1)S(1)} %get-tuple-element.80), channel_id=1, source_target_pairs={{0,16},{4,20},{8,24},{12,28},{16,0},{20,4},{24,8},{28,12},{1,17},{... | collective-permute-start | bytes 393224 | tf_op jit(solution)/shard_map/ppermute | solution.py:26
  95.8 1.9 %shard_map.82.so_far_ref = bf16[128,4096]{1,0:T(8,128)(2,1)} custom-call(s32[1]{0:T(128)} %bitcast.place_ref, bf16[128,4096]{1,0:T(8,128)(2,1)} %shard_map.78.so_far_ref, bf16[1,4,128,128]{3,2,1,0:T(8,128)(2,1)S(1)} %get-tuple-element.86.near_ref, bf16[1,4,128,128]{3,2,1,0:T(8,128)(2,1)S(1)} %collective-permute-done.17.far_ref), custom_call_target="tpu_custom_call", output_to_operand_aliasing={{}: (1, {})} | custom-call | bytes 1000000 | tf_op jit(solution)/shard_map/pallas_call | solution.py:318
  97.7 2.0 %shard_map.83.so_far_ref = bf16[128,4096]{1,0:T(8,128)(2,1)} custom-call(s32[1]{0:T(128)} %bitcast.place_ref, bf16[128,4096]{1,0:T(8,128)(2,1)} %shard_map.82.so_far_ref, bf16[1,4,128,256]{3,2,1,0:T(8,128)(2,1)S(1)} %get-tuple-element.75.near_ref, bf16[1,4,128,256]{3,2,1,0:T(8,128)(2,1)S(1)} %collective-permute-done.18.far_ref), custom_call_target="tpu_custom_call", output_to_operand_aliasing={{}: (1, {})} | custom-call | bytes 1000000 | tf_op jit(solution)/shard_map/pallas_call | solution.py:318
  99.7 2.0 %shard_map.86.so_far_ref = bf16[128,4096]{1,0:T(8,128)(2,1)} custom-call(s32[1]{0:T(128)} %bitcast.place_ref, bf16[128,4096]{1,0:T(8,128)(2,1)} %shard_map.83.so_far_ref, bf16[1,4,128,256]{3,2,1,0:T(8,128)(2,1)S(1)} %get-tuple-element.72.near_ref, bf16[1,4,128,256]{3,2,1,0:T(8,128)(2,1)S(1)} %collective-permute-done.21.far_ref), custom_call_target="tpu_custom_call", output_to_operand_aliasing={{}: (1, {})} | custom-call | bytes 1000000 | tf_op jit(solution)/shard_map/pallas_call | solution.py:318
  101.7 3.4 %collective-permute-done.24.far_ref = bf16[1,4,128,256]{3,2,1,0:T(8,128)(2,1)S(1)} collective-permute-done((bf16[1,4,128,256]{3,2,1,0:T(8,128)(2,1)S(1)}, bf16[1,4,128,256]{3,2,1,0:T(8,128)(2,1)S(1)}, u32[]{:S(2)}, u32[]{:S(2)}) %collective-permute-start.24) | collective-permute-done | bytes 262176 | tf_op jit(solution)/shard_map/ppermute | solution.py:26
  105.1 2.0 %shard_map.89.so_far_ref = bf16[128,4096]{1,0:T(8,128)(2,1)} custom-call(s32[1]{0:T(128)} %bitcast.place_ref, bf16[128,4096]{1,0:T(8,128)(2,1)} %shard_map.86.so_far_ref, bf16[1,4,128,256]{3,2,1,0:T(8,128)(2,1)S(1)} %get-tuple-element.70.near_ref, bf16[1,4,128,256]{3,2,1,0:T(8,128)(2,1)S(1)} %collective-permute-done.24.far_ref), custom_call_target="tpu_custom_call", output_to_operand_aliasing={{}: (1, {})} | custom-call | bytes 1000000 | tf_op jit(solution)/shard_map/pallas_call | solution.py:318
  107.4 1.9 %shard_map.92 = bf16[128,4096]{1,0:T(8,128)(2,1)} custom-call(s32[1]{0:T(128)} %bitcast.place_ref, bf16[128,4096]{1,0:T(8,128)(2,1)} %shard_map.89.so_far_ref, bf16[1,4,128,128]{3,2,1,0:T(8,128)(2,1)S(1)} %get-tuple-element.81.near_ref, bf16[1,4,128,128]{3,2,1,0:T(8,128)(2,1)S(1)} %collective-permute-done.26.far_ref), custom_call_target="tpu_custom_call", output_to_operand_aliasing={{}: (1, {})} | custom-call | bytes 1000000 | tf_op jit(solution)/shard_map/pallas_call | solution.py:318
  (82 shorter events, 16.4 us)
Async XLA Ops:
  0.0 8.6 %collective-permute-start.2 = (s32[1,128]{1,0:T(1,128)}, s32[1,128]{1,0:T(1,128)S(1)}, u32[]{:S(2)}, u32[]{:S(2)}) collective-permute-start(s32[1,128]{1,0:T(1,128)} %ids_ref), channel_id=1, source_target_pairs={{0,24},{4,28},{8,16},{12,20},{16,8},{20,12},{24,0},{28,4},{1,25},{... | collective-permute-start | bytes 1544 | tf_op jit(solution)/shard_map/ppermute | solution.py:26
  5.0 3.7 %collective-permute-start.1 = (s32[1,128]{1,0:T(1,128)}, s32[1,128]{1,0:T(1,128)S(1)}, u32[]{:S(2)}, u32[]{:S(2)}) collective-permute-start(s32[1,128]{1,0:T(1,128)} %ids_ref), channel_id=1, source_target_pairs={{0,8},{4,12},{8,0},{12,4},{16,24},{20,28},{24,16},{28,20},{1,9},{5... | collective-permute-start | bytes 1544 | tf_op jit(solution)/shard_map/ppermute | solution.py:26
  5.1 4.6 %collective-permute-start = (s32[1,128]{1,0:T(1,128)}, s32[1,128]{1,0:T(1,128)S(1)}, u32[]{:S(2)}, u32[]{:S(2)}) collective-permute-start(s32[1,128]{1,0:T(1,128)} %ids_ref), channel_id=1, source_target_pairs={{0,16},{4,20},{8,24},{12,28},{16,0},{20,4},{24,8},{28,12},{1,17},{... | collective-permute-start | bytes 1544 | tf_op jit(solution)/shard_map/ppermute | solution.py:26
  5.6 2.2 %copy-start.5 = (bf16[32,128]{1,0:T(8,128)(2,1)S(1)}, bf16[32,128]{1,0:T(8,128)(2,1)}, u32[]{:S(2)}) copy-start(bf16[32,128]{1,0:T(8,128)(2,1)} %param.12) | copy-start | bytes 24580
  5.6 4.0 %copy-start.3 = (s32[1,128]{1,0:T(1,128)S(1)}, s32[1,128]{1,0:T(1,128)}, u32[]{:S(2)}) copy-start(s32[1,128]{1,0:T(1,128)} %ids_ref) | copy-start | bytes 1540
  5.6 11.3 %copy-start.2 = (f32[4096]{0:T(1024)S(1)}, f32[4096]{0:T(1024)}, u32[]{:S(2)}) copy-start(f32[4096]{0:T(1024)} %param.9) | copy-start | bytes 49156
  9.6 3.7 %collective-permute-start.3 = (s32[4,128]{1,0:T(4,128)S(1)}, s32[4,128]{1,0:T(4,128)S(1)}, u32[]{:S(2)}, u32[]{:S(2)}) collective-permute-start(s32[4,128]{1,0:T(4,128)S(1)} %pad_add_fusion.4), channel_id=1, source_target_pairs={{0,4},{4,0},{8,12},{12,8},{16,20},{20,16},{24,28},{28,24},{1,5},{5... | collective-permute-start | bytes 6152 | tf_op jit(solution)/shard_map/ppermute | solution.py:26
  11.2 17.9 %collective-permute-start.6 = (bf16[512,512]{1,0:T(8,128)(2,1)}, bf16[512,512]{1,0:T(8,128)(2,1)S(1)}, u32[]{:S(2)}, u32[]{:S(2)}) collective-permute-start(bf16[512,512]{1,0:T(8,128)(2,1)} %get-tuple-element.44), channel_id=1, source_target_pairs={{0,8},{4,12},{8,0},{12,4},{16,24},{20,28},{24,16},{28,20},{1,9},{5... | collective-permute-start | bytes 1572872 | tf_op jit(solution)/shard_map/ppermute | solution.py:26
  13.3 15.6 %collective-permute-start.8 = (s32[8,128]{1,0:T(8,128)S(1)}, s32[8,128]{1,0:T(8,128)S(1)}, u32[]{:S(2)}, u32[]{:S(2)}) collective-permute-start(s32[8,128]{1,0:T(8,128)S(1)} %pad_add_fusion.2), channel_id=1, source_target_pairs={{0,1},{1,2},{2,3},{3,0},{4,5},{5,6},{6,7},{7,4},{8,9},{9,10},{10,1... | collective-permute-start | bytes 12296 | tf_op jit(solution)/shard_map/ppermute | solution.py:21
  13.3 15.4 %collective-permute-start.7 = (s32[8,128]{1,0:T(8,128)S(1)}, s32[8,128]{1,0:T(8,128)S(1)}, u32[]{:S(2)}, u32[]{:S(2)}) collective-permute-start(s32[8,128]{1,0:T(8,128)S(1)} %pad_add_fusion.2), channel_id=1, source_target_pairs={{0,2},{1,3},{2,0},{3,1},{4,6},{5,7},{6,4},{7,5},{8,10},{9,11},{10,... | collective-permute-start | bytes 12296 | tf_op jit(solution)/shard_map/ppermute | solution.py:21
  14.9 25.0 %collective-permute-start.4 = (bf16[512,512]{1,0:T(8,128)(2,1)}, bf16[512,512]{1,0:T(8,128)(2,1)S(1)}, u32[]{:S(2)}, u32[]{:S(2)}) collective-permute-start(bf16[512,512]{1,0:T(8,128)(2,1)} %get-tuple-element.42), channel_id=1, source_target_pairs={{0,8},{4,12},{8,0},{12,4},{16,24},{20,28},{24,16},{28,20},{1,9},{5... | collective-permute-start | bytes 1572872 | tf_op jit(solution)/shard_map/ppermute | solution.py:26
  19.1 10.7 %copy-start.4 = (f32[3,3,512]{2,1,0:T(4,128)S(1)}, f32[3,3,512]{2,1,0:T(4,128)}, u32[]{:S(2)}) copy-start(f32[3,3,512]{2,1,0:T(4,128)} %short_ref.3) | copy-start | bytes 55300
  29.1 10.9 %collective-permute-start.10 = (bf16[512,256]{1,0:T(8,128)(2,1)S(1)}, bf16[512,256]{1,0:T(8,128)(2,1)S(1)}, u32[]{:S(2)}, u32[]{:S(2)}) collective-permute-start(bf16[512,256]{1,0:T(8,128)(2,1)S(1)} %get-tuple-element.83), channel_id=1, source_target_pairs={{0,2},{1,3},{2,0},{3,1},{4,6},{5,7},{6,4},{7,5},{8,10},{9,11},{10,... | collective-permute-start | bytes 786440 | tf_op jit(solution)/shard_map/ppermute | solution.py:26
  31.8 14.6 %collective-permute-start.12 = (bf16[2,128,512]{2,1,0:T(8,128)(2,1)S(1)}, bf16[2,128,512]{2,1,0:T(8,128)(2,1)S(1)}, u32[]{:S(2)}, u32[]{:S(2)}) collective-permute-start(bf16[2,128,512]{2,1,0:T(8,128)(2,1)S(1)} %shard_map.76), channel_id=1, source_target_pairs={{0,8},{4,12},{8,0},{12,4},{16,24},{20,28},{24,16},{28,20},{1,9},{5... | collective-permute-start | bytes 786440 | tf_op jit(solution)/shard_map/ppermute | solution.py:26
  32.1 13.0 %collective-permute-start.9 = (bf16[512,256]{1,0:T(8,128)(2,1)S(1)}, bf16[512,256]{1,0:T(8,128)(2,1)S(1)}, u32[]{:S(2)}, u32[]{:S(2)}) collective-permute-start(bf16[512,256]{1,0:T(8,128)(2,1)S(1)} %get-tuple-element.50), channel_id=1, source_target_pairs={{0,2},{1,3},{2,0},{3,1},{4,6},{5,7},{6,4},{7,5},{8,10},{9,11},{10,... | collective-permute-start | bytes 786440 | tf_op jit(solution)/shard_map/ppermute | solution.py:26
  39.9 5.2 %collective-permute-start.5 = (bf16[512,512]{1,0:T(8,128)(2,1)S(1)}, bf16[512,512]{1,0:T(8,128)(2,1)S(1)}, u32[]{:S(2)}, u32[]{:S(2)}) collective-permute-start(bf16[512,512]{1,0:T(8,128)(2,1)S(1)} %collective-permute-done.4), channel_id=1, source_target_pairs={{0,1},{1,0},{2,3},{3,2},{4,5},{5,4},{6,7},{7,6},{8,9},{9,8},{10,11... | collective-permute-start | bytes 1572872 | tf_op jit(solution)/shard_map/ppermute | solution.py:26
  40.2 6.2 %copy-start = (bf16[512,4096]{1,0:T(8,128)(2,1)S(1)}, bf16[512,4096]{1,0:T(8,128)(2,1)}, u32[]{:S(2)}) copy-start(bf16[512,4096]{1,0:T(8,128)(2,1)} %refs_3_.17) | copy-start | bytes 12582916
  40.2 9.0 %collective-permute-start.11 = (bf16[2,128,512]{2,1,0:T(8,128)(2,1)S(1)}, bf16[2,128,512]{2,1,0:T(8,128)(2,1)S(1)}, u32[]{:S(2)}, u32[]{:S(2)}) collective-permute-start(bf16[2,128,512]{2,1,0:T(8,128)(2,1)S(1)} %get-tuple-element.79), channel_id=1, source_target_pairs={{0,8},{4,12},{8,0},{12,4},{16,24},{20,28},{24,16},{28,20},{1,9},{5... | collective-permute-start | bytes 786440 | tf_op jit(solution)/shard_map/ppermute | solution.py:26
  42.2 4.2 %collective-permute-start.13 = (bf16[2,512,256]{2,1,0:T(8,128)(2,1)S(1)}, bf16[2,512,256]{2,1,0:T(8,128)(2,1)S(1)}, u32[]{:S(2)}, u32[]{:S(2)}) collective-permute-start(bf16[2,512,256]{2,1,0:T(8,128)(2,1)S(1)} %pad_maximum_fusion.2.refs_4_), channel_id=1, source_target_pairs={{0,1},{1,0},{2,3},{3,2},{4,5},{5,4},{6,7},{7,6},{8,9},{9,8},{10,11... | collective-permute-start | bytes 1572872 | tf_op jit(solution)/shard_map/ppermute | solution.py:26
  45.2 5.0 %collective-permute-start.14 = (bf16[2,512,256]{2,1,0:T(8,128)(2,1)S(1)}, bf16[2,512,256]{2,1,0:T(8,128)(2,1)S(1)}, u32[]{:S(2)}, u32[]{:S(2)}) collective-permute-start(bf16[2,512,256]{2,1,0:T(8,128)(2,1)S(1)} %pad_maximum_fusion.1.refs_4_), channel_id=1, source_target_pairs={{0,1},{1,0},{2,3},{3,2},{4,5},{5,4},{6,7},{7,6},{8,9},{9,8},{10,11... | collective-permute-start | bytes 1572872 | tf_op jit(solution)/shard_map/ppermute | solution.py:26
  45.7 14.8 %collective-permute-start.19 = (bf16[2,512,256]{2,1,0:T(8,128)(2,1)S(1)}, bf16[2,512,256]{2,1,0:T(8,128)(2,1)S(1)}, u32[]{:S(2)}, u32[]{:S(2)}) collective-permute-start(bf16[2,512,256]{2,1,0:T(8,128)(2,1)S(1)} %get-tuple-element.73.refs_4_), channel_id=1, source_target_pairs={{0,2},{1,3},{2,0},{3,1},{4,6},{5,7},{6,4},{7,5},{8,10},{9,11},{10,... | collective-permute-start | bytes 1572872 | tf_op jit(solution)/shard_map/ppermute | solution.py:26
  47.1 14.1 %collective-permute-start.16 = (bf16[2,4,128,256]{3,2,1,0:T(8,128)(2,1)S(1)}, bf16[2,4,128,256]{3,2,1,0:T(8,128)(2,1)S(1)}, u32[]{:S(2)}, u32[]{:S(2)}) collective-permute-start(bf16[2,4,128,256]{3,2,1,0:T(8,128)(2,1)S(1)} %shard_map.79), channel_id=1, source_target_pairs={{0,4},{4,0},{8,12},{12,8},{16,20},{20,16},{24,28},{28,24},{1,5},{5... | collective-permute-start | bytes 1572872 | tf_op jit(solution)/shard_map/ppermute | solution.py:26
  49.1 21.9 %collective-permute-start.22 = (bf16[2,512,256]{2,1,0:T(8,128)(2,1)S(1)}, bf16[2,512,256]{2,1,0:T(8,128)(2,1)S(1)}, u32[]{:S(2)}, u32[]{:S(2)}) collective-permute-start(bf16[2,512,256]{2,1,0:T(8,128)(2,1)S(1)} %get-tuple-element.64.refs_4_), channel_id=1, source_target_pairs={{0,2},{1,3},{2,0},{3,1},{4,6},{5,7},{6,4},{7,5},{8,10},{9,11},{10,... | collective-permute-start | bytes 1572872 | tf_op jit(solution)/shard_map/ppermute | solution.py:26
  51.6 23.7 %collective-permute-start.15 = (bf16[2,1,4,128,128]{4,3,2,1,0:T(8,128)(2,1)S(1)}, bf16[2,1,4,128,128]{4,3,2,1,0:T(8,128)(2,1)S(1)}, u32[]{:S(2)}, u32[]{:S(2)}) collective-permute-start(bf16[2,1,4,128,128]{4,3,2,1,0:T(8,128)(2,1)S(1)} %slice.129), channel_id=1, source_target_pairs={{0,16},{4,20},{8,24},{12,28},{16,0},{20,4},{24,8},{28,12},{1,17},{... | collective-permute-start | bytes 786440 | tf_op jit(solution)/shard_map/ppermute | solution.py:26
  61.4 36.3 %collective-permute-start.18 = (bf16[1,4,128,256]{3,2,1,0:T(8,128)(2,1)S(1)}, bf16[1,4,128,256]{3,2,1,0:T(8,128)(2,1)S(1)}, u32[]{:S(2)}, u32[]{:S(2)}) collective-permute-start(bf16[1,4,128,256]{3,2,1,0:T(8,128)(2,1)S(1)} %get-tuple-element.76), channel_id=1, source_target_pairs={{0,16},{4,20},{8,24},{12,28},{16,0},{20,4},{24,8},{28,12},{1,17},{... | collective-permute-start | bytes 786440 | tf_op jit(solution)/shard_map/ppermute | solution.py:26
  63.6 14.3 %collective-permute-start.20 = (bf16[2,4,128,256]{3,2,1,0:T(8,128)(2,1)S(1)}, bf16[2,4,128,256]{3,2,1,0:T(8,128)(2,1)S(1)}, u32[]{:S(2)}, u32[]{:S(2)}) collective-permute-start(bf16[2,4,128,256]{3,2,1,0:T(8,128)(2,1)S(1)} %shard_map.85), channel_id=1, source_target_pairs={{0,4},{4,0},{8,12},{12,8},{16,20},{20,16},{24,28},{28,24},{1,5},{5... | collective-permute-start | bytes 1572872 | tf_op jit(solution)/shard_map/ppermute | solution.py:26
  71.7 17.4 %collective-permute-start.23 = (bf16[2,4,128,256]{3,2,1,0:T(8,128)(2,1)S(1)}, bf16[2,4,128,256]{3,2,1,0:T(8,128)(2,1)S(1)}, u32[]{:S(2)}, u32[]{:S(2)}) collective-permute-start(bf16[2,4,128,256]{3,2,1,0:T(8,128)(2,1)S(1)} %shard_map.88), channel_id=1, source_target_pairs={{0,4},{4,0},{8,12},{12,8},{16,20},{20,16},{24,28},{28,24},{1,5},{5... | collective-permute-start | bytes 1572872 | tf_op jit(solution)/shard_map/ppermute | solution.py:26
  74.1 20.0 %collective-permute-start.25 = (bf16[2,4,128,128]{3,2,1,0:T(8,128)(2,1)S(1)}, bf16[2,4,128,128]{3,2,1,0:T(8,128)(2,1)S(1)}, u32[]{:S(2)}, u32[]{:S(2)}) collective-permute-start(bf16[2,4,128,128]{3,2,1,0:T(8,128)(2,1)S(1)} %shard_map.91), channel_id=1, source_target_pairs={{0,4},{4,0},{8,12},{12,8},{16,20},{20,16},{24,28},{28,24},{1,5},{5... | collective-permute-start | bytes 786440 | tf_op jit(solution)/shard_map/ppermute | solution.py:26
  75.5 20.3 %collective-permute-start.17 = (bf16[1,4,128,128]{3,2,1,0:T(8,128)(2,1)S(1)}, bf16[1,4,128,128]{3,2,1,0:T(8,128)(2,1)S(1)}, u32[]{:S(2)}, u32[]{:S(2)}) collective-permute-start(bf16[1,4,128,128]{3,2,1,0:T(8,128)(2,1)S(1)} %get-tuple-element.85), channel_id=1, source_target_pairs={{0,4},{4,0},{8,12},{12,8},{16,20},{20,16},{24,28},{28,24},{1,5},{5... | collective-permute-start | bytes 393224 | tf_op jit(solution)/shard_map/ppermute | solution.py:26
  78.0 21.7 %collective-permute-start.21 = (bf16[1,4,128,256]{3,2,1,0:T(8,128)(2,1)S(1)}, bf16[1,4,128,256]{3,2,1,0:T(8,128)(2,1)S(1)}, u32[]{:S(2)}, u32[]{:S(2)}) collective-permute-start(bf16[1,4,128,256]{3,2,1,0:T(8,128)(2,1)S(1)} %get-tuple-element.71), channel_id=1, source_target_pairs={{0,16},{4,20},{8,24},{12,28},{16,0},{20,4},{24,8},{28,12},{1,17},{... | collective-permute-start | bytes 786440 | tf_op jit(solution)/shard_map/ppermute | solution.py:26
  89.2 15.8 %collective-permute-start.24 = (bf16[1,4,128,256]{3,2,1,0:T(8,128)(2,1)S(1)}, bf16[1,4,128,256]{3,2,1,0:T(8,128)(2,1)S(1)}, u32[]{:S(2)}, u32[]{:S(2)}) collective-permute-start(bf16[1,4,128,256]{3,2,1,0:T(8,128)(2,1)S(1)} %get-tuple-element.69), channel_id=1, source_target_pairs={{0,16},{4,20},{8,24},{12,28},{16,0},{20,4},{24,8},{28,12},{1,17},{... | collective-permute-start | bytes 786440 | tf_op jit(solution)/shard_map/ppermute | solution.py:26
  94.2 13.2 %collective-permute-start.26 = (bf16[1,4,128,128]{3,2,1,0:T(8,128)(2,1)S(1)}, bf16[1,4,128,128]{3,2,1,0:T(8,128)(2,1)S(1)}, u32[]{:S(2)}, u32[]{:S(2)}) collective-permute-start(bf16[1,4,128,128]{3,2,1,0:T(8,128)(2,1)S(1)} %get-tuple-element.80), channel_id=1, source_target_pairs={{0,16},{4,20},{8,24},{12,28},{16,0},{20,4},{24,8},{28,12},{1,17},{... | collective-permute-start | bytes 393224 | tf_op jit(solution)/shard_map/ppermute | solution.py:26
  (1 other events, 2.2 us)

commit v14 on v13

--- a/solution.py
+++ b/solution.py
@@ -231,7 +231,7 @@
         out_specs=whole(shape),
         out_shape=shape,
         compiler_params=params(8),
-        cost_estimate=cost(0, 2_000_000),
+        cost_estimate=cost(4_000_000_000, 0),
     )(base)
 
 

time: 110 us -> 110 us (level)
    unnamed x12 -> x14, local copies, waits for them, and re-layouts: 2.21 us -> 2.21 us
  transfers between devices with their start and end apart: 27 -> 27, of which waited for: 10 -> 10; matrix products, arithmetic and copies ran while one was open for 1% -> 1% of each run, Pallas kernels for 35% -> 36%
where the time goes in v14:
time: 110 us
  Pallas kernels  40.9 us (37%)
  starting transfers between devices  34.4 us (31%)
  waiting for transfers between devices  30.2 us (27%)
  local copies, waits for them, and re-layouts  2.66 us (2%)
    ppermute x25, starting transfers between devices, swap(): return lax.ppermute(x, axis, [(i, i ^ mask) for i in range(peers)])  32.8 us
    ppermute x25, waiting for transfers between devices, swap(): return lax.ppermute(x, axis, [(i, i ^ mask) for i in range(peers)])  30.2 us
    pallas_call x5, Pallas kernels, place_pieces(): pl.pallas_call(functools.partial(place_kernel, split, step), grid_spec=pl...  9.81 us
    pallas_call x1, Pallas kernels, project(): pl.pallas_call(table_kernel, grid=(1,), in_specs=[hbm, hbm, pl.BlockSpec(...  9.69 us
    pallas_call x2, Pallas kernels, mix(): pl.pallas_call(mixer_kernel, grid=(windows // 2,), in_specs=[pl.BlockSpec...  8.77 us
    pallas_call x9, Pallas kernels, panel(): pl.pallas_call(panel_kernel, grid_spec=pltpu.PrefetchScalarGridSpec(num_s...  7.19 us
    pallas_call x1, Pallas kernels, residual(): pl.pallas_call(residual_kernel, grid=(4,), in_specs=[whole(token_ids), pl...  2.65 us
    unnamed x14, local copies, waits for them, and re-layouts  2.21 us
  transfers between devices with their start and end apart: 27, of which 10 were waited for; matrix products, arithmetic and copies ran while one was open for 1% of the time, Pallas kernels for 36%

profile of v14, /device:TPU:0, one launch (start us, length us, event | category | flops | bytes accessed | tf_op | source)
XLA Modules:
  0.0 109.6 jit_solution(5372381466040308351)
XLA Ops:
  0.0 5.0 %collective-permute-start.2 = (s32[1,128]{1,0:T(1,128)}, s32[1,128]{1,0:T(1,128)S(1)}, u32[]{:S(2)}, u32[]{:S(2)}) collective-permute-start(s32[1,128]{1,0:T(1,128)} %ids_ref), channel_id=1, source_target_pairs={{0,24},{4,28},{8,16},{12,20},{16,8},{20,12},{24,0},{28,4},{1,25},{... | collective-permute-start | bytes 1544 | tf_op jit(solution)/shard_map/ppermute | solution.py:26
  5.6 2.2 %shard_map.73 = (bf16[512,512]{1,0:T(8,128)(2,1)}, bf16[512,512]{1,0:T(8,128)(2,1)}) custom-call(s32[1]{0:T(128)} %bitcast.place_ref, bf16[512,4096]{1,0:T(8,128)(2,1)} %refs_3_.17, bf16[512,4096]{1,0:T(8,128)(2,1)} %refs_3_.17), custom_call_target="tpu_custom_call" | custom-call | bytes 2000000 | tf_op jit(solution)/shard_map/pallas_call | solution.py:200
  9.6 1.6 %collective-permute-start.3 = (s32[4,128]{1,0:T(4,128)S(1)}, s32[4,128]{1,0:T(4,128)S(1)}, u32[]{:S(2)}, u32[]{:S(2)}) collective-permute-start(s32[4,128]{1,0:T(4,128)S(1)} %pad_add_fusion.4), channel_id=1, source_target_pairs={{0,4},{4,0},{8,12},{12,8},{16,20},{20,16},{24,28},{28,24},{1,5},{5... | collective-permute-start | bytes 6152 | tf_op jit(solution)/shard_map/ppermute | solution.py:26
  11.2 2.0 %collective-permute-start.6 = (bf16[512,512]{1,0:T(8,128)(2,1)}, bf16[512,512]{1,0:T(8,128)(2,1)S(1)}, u32[]{:S(2)}, u32[]{:S(2)}) collective-permute-start(bf16[512,512]{1,0:T(8,128)(2,1)} %get-tuple-element.44), channel_id=1, source_target_pairs={{0,8},{4,12},{8,0},{12,4},{16,24},{20,28},{24,16},{28,20},{1,9},{5... | collective-permute-start | bytes 1572872 | tf_op jit(solution)/shard_map/ppermute | solution.py:26
  13.3 1.6 %collective-permute-start.7 = (s32[8,128]{1,0:T(8,128)S(1)}, s32[8,128]{1,0:T(8,128)S(1)}, u32[]{:S(2)}, u32[]{:S(2)}) collective-permute-start(s32[8,128]{1,0:T(8,128)S(1)} %pad_add_fusion.2), channel_id=1, source_target_pairs={{0,2},{1,3},{2,0},{3,1},{4,6},{5,7},{6,4},{7,5},{8,10},{9,11},{10,... | collective-permute-start | bytes 12296 | tf_op jit(solution)/shard_map/ppermute | solution.py:21
  14.9 2.0 %collective-permute-start.4 = (bf16[512,512]{1,0:T(8,128)(2,1)S(1)}, bf16[512,512]{1,0:T(8,128)(2,1)S(1)}, u32[]{:S(2)}, u32[]{:S(2)}) collective-permute-start(bf16[512,512]{1,0:T(8,128)(2,1)S(1)} %copy-done.6), channel_id=1, source_target_pairs={{0,8},{4,12},{8,0},{12,4},{16,24},{20,28},{24,16},{28,20},{1,9},{5... | collective-permute-start | bytes 1572872 | tf_op jit(solution)/shard_map/ppermute | solution.py:26
  16.9 2.2 %copy-done.1 = bf16[512,4096]{1,0:T(8,128)(2,1)S(1)} copy-done((bf16[512,4096]{1,0:T(8,128)(2,1)S(1)}, bf16[512,4096]{1,0:T(8,128)(2,1)}, u32[]{:S(2)}) %copy-start.1) | copy-done | bytes 4194328
  19.1 9.7 %shard_map.75.table_ref = bf16[3,512,512]{2,1,0:T(8,128)(2,1)S(1)} custom-call(bf16[512,4096]{1,0:T(8,128)(2,1)S(1)} %copy-done.1, bf16[3,4096,512]{2,1,0:T(8,128)(2,1)} %weight_hbm, f32[1,4096]{1,0:T(1,128)S(1)} %bitcast.46), custom_call_target="tpu_custom_call" | custom-call | flops 3000000000 | tf_op jit(solution)/shard_map/pallas_call | solution.py:101
  29.8 2.2 %shard_map.76 = bf16[2,128,512]{2,1,0:T(8,128)(2,1)S(1)} custom-call(s32[2,1,272]{2,1,0:T(1,128)S(1)} %copy.13.ids_ref, bf16[3,512,512]{2,1,0:T(8,128)(2,1)S(1)} %shard_map.75.table_ref, f32[3,3,512]{2,1,0:T(4,128)S(1)} %copy-done.4, bf16[4,1024,256]{2,1,0:T(8,128)(2,1)S(1)} %shard_map.74.toeplitz), custom_call_target="tpu_custom_call" | custom-call | flops 1500000000 | tf_op jit(solution)/shard_map/pallas_call | solution.py:167
  32.2 1.4 %collective-permute-start.9 = (bf16[512,256]{1,0:T(8,128)(2,1)S(1)}, bf16[512,256]{1,0:T(8,128)(2,1)S(1)}, u32[]{:S(2)}, u32[]{:S(2)}) collective-permute-start(bf16[512,256]{1,0:T(8,128)(2,1)S(1)} %get-tuple-element.50), channel_id=1, source_target_pairs={{0,2},{1,3},{2,0},{3,1},{4,6},{5,7},{6,4},{7,5},{8,10},{9,11},{10,... | collective-permute-start | bytes 786440 | tf_op jit(solution)/shard_map/ppermute | solution.py:26
  33.6 6.6 %shard_map.77 = bf16[6,128,512]{2,1,0:T(8,128)(2,1)S(1)} custom-call(s32[6,1,272]{2,1,0:T(1,128)S(1)} %reshape.54.ids_ref, bf16[3,512,512]{2,1,0:T(8,128)(2,1)S(1)} %shard_map.75.table_ref, f32[3,3,512]{2,1,0:T(4,128)S(1)} %copy-done.4, bf16[4,1024,256]{2,1,0:T(8,128)(2,1)S(1)} %shard_map.74.toeplitz), custom_call_target="tpu_custom_call" | custom-call | flops 1500000000 | tf_op jit(solution)/shard_map/pallas_call | solution.py:167
  40.4 2.0 %collective-permute-start.11 = (bf16[2,128,512]{2,1,0:T(8,128)(2,1)S(1)}, bf16[2,128,512]{2,1,0:T(8,128)(2,1)S(1)}, u32[]{:S(2)}, u32[]{:S(2)}) collective-permute-start(bf16[2,128,512]{2,1,0:T(8,128)(2,1)S(1)} %get-tuple-element.79), channel_id=1, source_target_pairs={{0,8},{4,12},{8,0},{12,4},{16,24},{20,28},{24,16},{28,20},{1,9},{5... | collective-permute-start | bytes 786440 | tf_op jit(solution)/shard_map/ppermute | solution.py:26
  42.6 2.7 %shard_map.78.so_far_ref = bf16[128,4096]{1,0:T(8,128)(2,1)} custom-call(s32[1,128]{1,0:T(1,128)S(1)} %copy-done.3, bf16[512,4096]{1,0:T(8,128)(2,1)S(1)} %copy-done.1), custom_call_target="tpu_custom_call" | custom-call | flops 400000000 | tf_op jit(solution)/shard_map/pallas_call | solution.py:290
  47.4 1.6 %collective-permute-start.16 = (bf16[2,4,128,256]{3,2,1,0:T(8,128)(2,1)S(1)}, bf16[2,4,128,256]{3,2,1,0:T(8,128)(2,1)S(1)}, u32[]{:S(2)}, u32[]{:S(2)}) collective-permute-start(bf16[2,4,128,256]{3,2,1,0:T(8,128)(2,1)S(1)} %shard_map.79), channel_id=1, source_target_pairs={{0,4},{4,0},{8,12},{12,8},{16,20},{20,16},{24,28},{28,24},{1,5},{5... | collective-permute-start | bytes 1572872 | tf_op jit(solution)/shard_map/ppermute | solution.py:26
  51.9 1.5 %collective-permute-start.15 = (bf16[2,1,4,128,128]{4,3,2,1,0:T(8,128)(2,1)S(1)}, bf16[2,1,4,128,128]{4,3,2,1,0:T(8,128)(2,1)S(1)}, u32[]{:S(2)}, u32[]{:S(2)}) collective-permute-start(bf16[2,1,4,128,128]{4,3,2,1,0:T(8,128)(2,1)S(1)} %slice.129), channel_id=1, source_target_pairs={{0,16},{4,20},{8,24},{12,28},{16,0},{20,4},{24,8},{28,12},{1,17},{... | collective-permute-start | bytes 786440 | tf_op jit(solution)/shard_map/ppermute | solution.py:26
  54.9 5.9 %collective-permute-done.19.refs_5_ = bf16[2,512,256]{2,1,0:T(8,128)(2,1)S(1)} collective-permute-done((bf16[2,512,256]{2,1,0:T(8,128)(2,1)S(1)}, bf16[2,512,256]{2,1,0:T(8,128)(2,1)S(1)}, u32[]{:S(2)}, u32[]{:S(2)}) %collective-permute-start.19) | collective-permute-done | bytes 524320 | tf_op jit(solution)/shard_map/ppermute | solution.py:26
  61.6 1.5 %collective-permute-start.18 = (bf16[1,4,128,256]{3,2,1,0:T(8,128)(2,1)S(1)}, bf16[1,4,128,256]{3,2,1,0:T(8,128)(2,1)S(1)}, u32[]{:S(2)}, u32[]{:S(2)}) collective-permute-start(bf16[1,4,128,256]{3,2,1,0:T(8,128)(2,1)S(1)} %get-tuple-element.76), channel_id=1, source_target_pairs={{0,16},{4,20},{8,24},{12,28},{16,0},{20,4},{24,8},{28,12},{1,17},{... | collective-permute-start | bytes 786440 | tf_op jit(solution)/shard_map/ppermute | solution.py:26
  63.8 1.6 %collective-permute-start.20 = (bf16[2,4,128,256]{3,2,1,0:T(8,128)(2,1)S(1)}, bf16[2,4,128,256]{3,2,1,0:T(8,128)(2,1)S(1)}, u32[]{:S(2)}, u32[]{:S(2)}) collective-permute-start(bf16[2,4,128,256]{3,2,1,0:T(8,128)(2,1)S(1)} %shard_map.85), channel_id=1, source_target_pairs={{0,4},{4,0},{8,12},{12,8},{16,20},{20,16},{24,28},{28,24},{1,5},{5... | collective-permute-start | bytes 1572872 | tf_op jit(solution)/shard_map/ppermute | solution.py:26
  65.4 5.9 %collective-permute-done.22.refs_5_ = bf16[2,512,256]{2,1,0:T(8,128)(2,1)S(1)} collective-permute-done((bf16[2,512,256]{2,1,0:T(8,128)(2,1)S(1)}, bf16[2,512,256]{2,1,0:T(8,128)(2,1)S(1)}, u32[]{:S(2)}, u32[]{:S(2)}) %collective-permute-start.22) | collective-permute-done | bytes 524320 | tf_op jit(solution)/shard_map/ppermute | solution.py:26
  72.0 1.6 %collective-permute-start.23 = (bf16[2,4,128,256]{3,2,1,0:T(8,128)(2,1)S(1)}, bf16[2,4,128,256]{3,2,1,0:T(8,128)(2,1)S(1)}, u32[]{:S(2)}, u32[]{:S(2)}) collective-permute-start(bf16[2,4,128,256]{3,2,1,0:T(8,128)(2,1)S(1)} %shard_map.88), channel_id=1, source_target_pairs={{0,4},{4,0},{8,12},{12,8},{16,20},{20,16},{24,28},{28,24},{1,5},{5... | collective-permute-start | bytes 1572872 | tf_op jit(solution)/shard_map/ppermute | solution.py:26
  75.8 1.6 %collective-permute-start.17 = (bf16[1,4,128,128]{3,2,1,0:T(8,128)(2,1)S(1)}, bf16[1,4,128,128]{3,2,1,0:T(8,128)(2,1)S(1)}, u32[]{:S(2)}, u32[]{:S(2)}) collective-permute-start(bf16[1,4,128,128]{3,2,1,0:T(8,128)(2,1)S(1)} %get-tuple-element.85), channel_id=1, source_target_pairs={{0,4},{4,0},{8,12},{12,8},{16,20},{20,16},{24,28},{28,24},{1,5},{5... | collective-permute-start | bytes 393224 | tf_op jit(solution)/shard_map/ppermute | solution.py:26
  78.2 1.7 %collective-permute-start.21 = (bf16[1,4,128,256]{3,2,1,0:T(8,128)(2,1)S(1)}, bf16[1,4,128,256]{3,2,1,0:T(8,128)(2,1)S(1)}, u32[]{:S(2)}, u32[]{:S(2)}) collective-permute-start(bf16[1,4,128,256]{3,2,1,0:T(8,128)(2,1)S(1)} %get-tuple-element.71), channel_id=1, source_target_pairs={{0,16},{4,20},{8,24},{12,28},{16,0},{20,4},{24,8},{28,12},{1,17},{... | collective-permute-start | bytes 786440 | tf_op jit(solution)/shard_map/ppermute | solution.py:26
  79.9 9.4 %collective-permute-done.23 = bf16[2,4,128,256]{3,2,1,0:T(8,128)(2,1)S(1)} collective-permute-done((bf16[2,4,128,256]{3,2,1,0:T(8,128)(2,1)S(1)}, bf16[2,4,128,256]{3,2,1,0:T(8,128)(2,1)S(1)}, u32[]{:S(2)}, u32[]{:S(2)}) %collective-permute-start.23) | collective-permute-done | bytes 524320 | tf_op jit(solution)/shard_map/ppermute | solution.py:26
  89.4 1.7 %collective-permute-start.24 = (bf16[1,4,128,256]{3,2,1,0:T(8,128)(2,1)S(1)}, bf16[1,4,128,256]{3,2,1,0:T(8,128)(2,1)S(1)}, u32[]{:S(2)}, u32[]{:S(2)}) collective-permute-start(bf16[1,4,128,256]{3,2,1,0:T(8,128)(2,1)S(1)} %get-tuple-element.69), channel_id=1, source_target_pairs={{0,16},{4,20},{8,24},{12,28},{16,0},{20,4},{24,8},{28,12},{1,17},{... | collective-permute-start | bytes 786440 | tf_op jit(solution)/shard_map/ppermute | solution.py:26
  91.2 3.2 %collective-permute-done.25 = bf16[2,4,128,128]{3,2,1,0:T(8,128)(2,1)S(1)} collective-permute-done((bf16[2,4,128,128]{3,2,1,0:T(8,128)(2,1)S(1)}, bf16[2,4,128,128]{3,2,1,0:T(8,128)(2,1)S(1)}, u32[]{:S(2)}, u32[]{:S(2)}) %collective-permute-start.25) | collective-permute-done | bytes 262176 | tf_op jit(solution)/shard_map/ppermute | solution.py:26
  94.4 1.6 %collective-permute-start.26 = (bf16[1,4,128,128]{3,2,1,0:T(8,128)(2,1)S(1)}, bf16[1,4,128,128]{3,2,1,0:T(8,128)(2,1)S(1)}, u32[]{:S(2)}, u32[]{:S(2)}) collective-permute-start(bf16[1,4,128,128]{3,2,1,0:T(8,128)(2,1)S(1)} %get-tuple-element.80), channel_id=1, source_target_pairs={{0,16},{4,20},{8,24},{12,28},{16,0},{20,4},{24,8},{28,12},{1,17},{... | collective-permute-start | bytes 393224 | tf_op jit(solution)/shard_map/ppermute | solution.py:26
  96.0 1.9 %shard_map.82.so_far_ref = bf16[128,4096]{1,0:T(8,128)(2,1)} custom-call(s32[1]{0:T(128)} %bitcast.place_ref, bf16[128,4096]{1,0:T(8,128)(2,1)} %shard_map.78.so_far_ref, bf16[1,4,128,128]{3,2,1,0:T(8,128)(2,1)S(1)} %get-tuple-element.86.near_ref, bf16[1,4,128,128]{3,2,1,0:T(8,128)(2,1)S(1)} %collective-permute-done.17.far_ref), custom_call_target="tpu_custom_call", output_to_operand_aliasing={{}: (1, {})} | custom-call | bytes 1000000 | tf_op jit(solution)/shard_map/pallas_call | solution.py:318
  97.9 2.0 %shard_map.83.so_far_ref = bf16[128,4096]{1,0:T(8,128)(2,1)} custom-call(s32[1]{0:T(128)} %bitcast.place_ref, bf16[128,4096]{1,0:T(8,128)(2,1)} %shard_map.82.so_far_ref, bf16[1,4,128,256]{3,2,1,0:T(8,128)(2,1)S(1)} %get-tuple-element.75.near_ref, bf16[1,4,128,256]{3,2,1,0:T(8,128)(2,1)S(1)} %collective-permute-done.18.far_ref), custom_call_target="tpu_custom_call", output_to_operand_aliasing={{}: (1, {})} | custom-call | bytes 1000000 | tf_op jit(solution)/shard_map/pallas_call | solution.py:318
  99.9 2.0 %shard_map.86.so_far_ref = bf16[128,4096]{1,0:T(8,128)(2,1)} custom-call(s32[1]{0:T(128)} %bitcast.place_ref, bf16[128,4096]{1,0:T(8,128)(2,1)} %shard_map.83.so_far_ref, bf16[1,4,128,256]{3,2,1,0:T(8,128)(2,1)S(1)} %get-tuple-element.72.near_ref, bf16[1,4,128,256]{3,2,1,0:T(8,128)(2,1)S(1)} %collective-permute-done.21.far_ref), custom_call_target="tpu_custom_call", output_to_operand_aliasing={{}: (1, {})} | custom-call | bytes 1000000 | tf_op jit(solution)/shard_map/pallas_call | solution.py:318
  101.9 3.4 %collective-permute-done.24.far_ref = bf16[1,4,128,256]{3,2,1,0:T(8,128)(2,1)S(1)} collective-permute-done((bf16[1,4,128,256]{3,2,1,0:T(8,128)(2,1)S(1)}, bf16[1,4,128,256]{3,2,1,0:T(8,128)(2,1)S(1)}, u32[]{:S(2)}, u32[]{:S(2)}) %collective-permute-start.24) | collective-permute-done | bytes 262176 | tf_op jit(solution)/shard_map/ppermute | solution.py:26
  105.3 2.0 %shard_map.89.so_far_ref = bf16[128,4096]{1,0:T(8,128)(2,1)} custom-call(s32[1]{0:T(128)} %bitcast.place_ref, bf16[128,4096]{1,0:T(8,128)(2,1)} %shard_map.86.so_far_ref, bf16[1,4,128,256]{3,2,1,0:T(8,128)(2,1)S(1)} %get-tuple-element.70.near_ref, bf16[1,4,128,256]{3,2,1,0:T(8,128)(2,1)S(1)} %collective-permute-done.24.far_ref), custom_call_target="tpu_custom_call", output_to_operand_aliasing={{}: (1, {})} | custom-call | bytes 1000000 | tf_op jit(solution)/shard_map/pallas_call | solution.py:318
  107.7 1.9 %shard_map.92 = bf16[128,4096]{1,0:T(8,128)(2,1)} custom-call(s32[1]{0:T(128)} %bitcast.place_ref, bf16[128,4096]{1,0:T(8,128)(2,1)} %shard_map.89.so_far_ref, bf16[1,4,128,128]{3,2,1,0:T(8,128)(2,1)S(1)} %get-tuple-element.81.near_ref, bf16[1,4,128,128]{3,2,1,0:T(8,128)(2,1)S(1)} %collective-permute-done.26.far_ref), custom_call_target="tpu_custom_call", output_to_operand_aliasing={{}: (1, {})} | custom-call | bytes 1000000 | tf_op jit(solution)/shard_map/pallas_call | solution.py:318
  (84 shorter events, 16.4 us)
Async XLA Ops:
  0.0 8.6 %collective-permute-start.2 = (s32[1,128]{1,0:T(1,128)}, s32[1,128]{1,0:T(1,128)S(1)}, u32[]{:S(2)}, u32[]{:S(2)}) collective-permute-start(s32[1,128]{1,0:T(1,128)} %ids_ref), channel_id=1, source_target_pairs={{0,24},{4,28},{8,16},{12,20},{16,8},{20,12},{24,0},{28,4},{1,25},{... | collective-permute-start | bytes 1544 | tf_op jit(solution)/shard_map/ppermute | solution.py:26
  5.0 3.7 %collective-permute-start.1 = (s32[1,128]{1,0:T(1,128)}, s32[1,128]{1,0:T(1,128)S(1)}, u32[]{:S(2)}, u32[]{:S(2)}) collective-permute-start(s32[1,128]{1,0:T(1,128)} %ids_ref), channel_id=1, source_target_pairs={{0,8},{4,12},{8,0},{12,4},{16,24},{20,28},{24,16},{28,20},{1,9},{5... | collective-permute-start | bytes 1544 | tf_op jit(solution)/shard_map/ppermute | solution.py:26
  5.1 4.6 %collective-permute-start = (s32[1,128]{1,0:T(1,128)}, s32[1,128]{1,0:T(1,128)S(1)}, u32[]{:S(2)}, u32[]{:S(2)}) collective-permute-start(s32[1,128]{1,0:T(1,128)} %ids_ref), channel_id=1, source_target_pairs={{0,16},{4,20},{8,24},{12,28},{16,0},{20,4},{24,8},{28,12},{1,17},{... | collective-permute-start | bytes 1544 | tf_op jit(solution)/shard_map/ppermute | solution.py:26
  5.6 2.2 %copy-start.5 = (bf16[32,128]{1,0:T(8,128)(2,1)S(1)}, bf16[32,128]{1,0:T(8,128)(2,1)}, u32[]{:S(2)}) copy-start(bf16[32,128]{1,0:T(8,128)(2,1)} %param.12) | copy-start | bytes 24580
  8.0 6.9 %copy-start.6 = (bf16[512,512]{1,0:T(8,128)(2,1)S(1)}, bf16[512,512]{1,0:T(8,128)(2,1)}, u32[]{:S(2)}) copy-start(bf16[512,512]{1,0:T(8,128)(2,1)} %get-tuple-element.42) | copy-start | bytes 1572868
  8.0 8.9 %copy-start.2 = (f32[4096]{0:T(1024)S(1)}, f32[4096]{0:T(1024)}, u32[]{:S(2)}) copy-start(f32[4096]{0:T(1024)} %param.9) | copy-start | bytes 49156
  9.6 3.7 %collective-permute-start.3 = (s32[4,128]{1,0:T(4,128)S(1)}, s32[4,128]{1,0:T(4,128)S(1)}, u32[]{:S(2)}, u32[]{:S(2)}) collective-permute-start(s32[4,128]{1,0:T(4,128)S(1)} %pad_add_fusion.4), channel_id=1, source_target_pairs={{0,4},{4,0},{8,12},{12,8},{16,20},{20,16},{24,28},{28,24},{1,5},{5... | collective-permute-start | bytes 6152 | tf_op jit(solution)/shard_map/ppermute | solution.py:26
  11.2 17.9 %collective-permute-start.6 = (bf16[512,512]{1,0:T(8,128)(2,1)}, bf16[512,512]{1,0:T(8,128)(2,1)S(1)}, u32[]{:S(2)}, u32[]{:S(2)}) collective-permute-start(bf16[512,512]{1,0:T(8,128)(2,1)} %get-tuple-element.44), channel_id=1, source_target_pairs={{0,8},{4,12},{8,0},{12,4},{16,24},{20,28},{24,16},{28,20},{1,9},{5... | collective-permute-start | bytes 1572872 | tf_op jit(solution)/shard_map/ppermute | solution.py:26
  13.3 15.6 %collective-permute-start.8 = (s32[8,128]{1,0:T(8,128)S(1)}, s32[8,128]{1,0:T(8,128)S(1)}, u32[]{:S(2)}, u32[]{:S(2)}) collective-permute-start(s32[8,128]{1,0:T(8,128)S(1)} %pad_add_fusion.2), channel_id=1, source_target_pairs={{0,1},{1,2},{2,3},{3,0},{4,5},{5,6},{6,7},{7,4},{8,9},{9,10},{10,1... | collective-permute-start | bytes 12296 | tf_op jit(solution)/shard_map/ppermute | solution.py:21
  13.3 15.4 %collective-permute-start.7 = (s32[8,128]{1,0:T(8,128)S(1)}, s32[8,128]{1,0:T(8,128)S(1)}, u32[]{:S(2)}, u32[]{:S(2)}) collective-permute-start(s32[8,128]{1,0:T(8,128)S(1)} %pad_add_fusion.2), channel_id=1, source_target_pairs={{0,2},{1,3},{2,0},{3,1},{4,6},{5,7},{6,4},{7,5},{8,10},{9,11},{10,... | collective-permute-start | bytes 12296 | tf_op jit(solution)/shard_map/ppermute | solution.py:21
  14.9 25.3 %collective-permute-start.4 = (bf16[512,512]{1,0:T(8,128)(2,1)S(1)}, bf16[512,512]{1,0:T(8,128)(2,1)S(1)}, u32[]{:S(2)}, u32[]{:S(2)}) collective-permute-start(bf16[512,512]{1,0:T(8,128)(2,1)S(1)} %copy-done.6), channel_id=1, source_target_pairs={{0,8},{4,12},{8,0},{12,4},{16,24},{20,28},{24,16},{28,20},{1,9},{5... | collective-permute-start | bytes 1572872 | tf_op jit(solution)/shard_map/ppermute | solution.py:26
  19.1 10.7 %copy-start.4 = (f32[3,3,512]{2,1,0:T(4,128)S(1)}, f32[3,3,512]{2,1,0:T(4,128)}, u32[]{:S(2)}) copy-start(f32[3,3,512]{2,1,0:T(4,128)} %short_ref.3) | copy-start | bytes 55300
  29.1 11.1 %collective-permute-start.10 = (bf16[512,256]{1,0:T(8,128)(2,1)S(1)}, bf16[512,256]{1,0:T(8,128)(2,1)S(1)}, u32[]{:S(2)}, u32[]{:S(2)}) collective-permute-start(bf16[512,256]{1,0:T(8,128)(2,1)S(1)} %get-tuple-element.83), channel_id=1, source_target_pairs={{0,2},{1,3},{2,0},{3,1},{4,6},{5,7},{6,4},{7,5},{8,10},{9,11},{10,... | collective-permute-start | bytes 786440 | tf_op jit(solution)/shard_map/ppermute | solution.py:26
  31.9 14.8 %collective-permute-start.12 = (bf16[2,128,512]{2,1,0:T(8,128)(2,1)S(1)}, bf16[2,128,512]{2,1,0:T(8,128)(2,1)S(1)}, u32[]{:S(2)}, u32[]{:S(2)}) collective-permute-start(bf16[2,128,512]{2,1,0:T(8,128)(2,1)S(1)} %shard_map.76), channel_id=1, source_target_pairs={{0,8},{4,12},{8,0},{12,4},{16,24},{20,28},{24,16},{28,20},{1,9},{5... | collective-permute-start | bytes 786440 | tf_op jit(solution)/shard_map/ppermute | solution.py:26
  32.2 13.1 %collective-permute-start.9 = (bf16[512,256]{1,0:T(8,128)(2,1)S(1)}, bf16[512,256]{1,0:T(8,128)(2,1)S(1)}, u32[]{:S(2)}, u32[]{:S(2)}) collective-permute-start(bf16[512,256]{1,0:T(8,128)(2,1)S(1)} %get-tuple-element.50), channel_id=1, source_target_pairs={{0,2},{1,3},{2,0},{3,1},{4,6},{5,7},{6,4},{7,5},{8,10},{9,11},{10,... | collective-permute-start | bytes 786440 | tf_op jit(solution)/shard_map/ppermute | solution.py:26
  40.2 5.2 %collective-permute-start.5 = (bf16[512,512]{1,0:T(8,128)(2,1)S(1)}, bf16[512,512]{1,0:T(8,128)(2,1)S(1)}, u32[]{:S(2)}, u32[]{:S(2)}) collective-permute-start(bf16[512,512]{1,0:T(8,128)(2,1)S(1)} %collective-permute-done.4), channel_id=1, source_target_pairs={{0,1},{1,0},{2,3},{3,2},{4,5},{5,4},{6,7},{7,6},{8,9},{9,8},{10,11... | collective-permute-start | bytes 1572872 | tf_op jit(solution)/shard_map/ppermute | solution.py:26
  40.4 6.3 %copy-start = (bf16[512,4096]{1,0:T(8,128)(2,1)S(1)}, bf16[512,4096]{1,0:T(8,128)(2,1)}, u32[]{:S(2)}) copy-start(bf16[512,4096]{1,0:T(8,128)(2,1)} %refs_3_.17) | copy-start | bytes 12582916
  40.4 9.0 %collective-permute-start.11 = (bf16[2,128,512]{2,1,0:T(8,128)(2,1)S(1)}, bf16[2,128,512]{2,1,0:T(8,128)(2,1)S(1)}, u32[]{:S(2)}, u32[]{:S(2)}) collective-permute-start(bf16[2,128,512]{2,1,0:T(8,128)(2,1)S(1)} %get-tuple-element.79), channel_id=1, source_target_pairs={{0,8},{4,12},{8,0},{12,4},{16,24},{20,28},{24,16},{28,20},{1,9},{5... | collective-permute-start | bytes 786440 | tf_op jit(solution)/shard_map/ppermute | solution.py:26
  42.4 4.2 %collective-permute-start.13 = (bf16[2,512,256]{2,1,0:T(8,128)(2,1)S(1)}, bf16[2,512,256]{2,1,0:T(8,128)(2,1)S(1)}, u32[]{:S(2)}, u32[]{:S(2)}) collective-permute-start(bf16[2,512,256]{2,1,0:T(8,128)(2,1)S(1)} %pad_maximum_fusion.2.refs_4_), channel_id=1, source_target_pairs={{0,1},{1,0},{2,3},{3,2},{4,5},{5,4},{6,7},{7,6},{8,9},{9,8},{10,11... | collective-permute-start | bytes 1572872 | tf_op jit(solution)/shard_map/ppermute | solution.py:26
  45.5 5.0 %collective-permute-start.14 = (bf16[2,512,256]{2,1,0:T(8,128)(2,1)S(1)}, bf16[2,512,256]{2,1,0:T(8,128)(2,1)S(1)}, u32[]{:S(2)}, u32[]{:S(2)}) collective-permute-start(bf16[2,512,256]{2,1,0:T(8,128)(2,1)S(1)} %pad_maximum_fusion.1.refs_4_), channel_id=1, source_target_pairs={{0,1},{1,0},{2,3},{3,2},{4,5},{5,4},{6,7},{7,6},{8,9},{9,8},{10,11... | collective-permute-start | bytes 1572872 | tf_op jit(solution)/shard_map/ppermute | solution.py:26
  45.9 14.8 %collective-permute-start.19 = (bf16[2,512,256]{2,1,0:T(8,128)(2,1)S(1)}, bf16[2,512,256]{2,1,0:T(8,128)(2,1)S(1)}, u32[]{:S(2)}, u32[]{:S(2)}) collective-permute-start(bf16[2,512,256]{2,1,0:T(8,128)(2,1)S(1)} %get-tuple-element.73.refs_4_), channel_id=1, source_target_pairs={{0,2},{1,3},{2,0},{3,1},{4,6},{5,7},{6,4},{7,5},{8,10},{9,11},{10,... | collective-permute-start | bytes 1572872 | tf_op jit(solution)/shard_map/ppermute | solution.py:26
  47.4 14.1 %collective-permute-start.16 = (bf16[2,4,128,256]{3,2,1,0:T(8,128)(2,1)S(1)}, bf16[2,4,128,256]{3,2,1,0:T(8,128)(2,1)S(1)}, u32[]{:S(2)}, u32[]{:S(2)}) collective-permute-start(bf16[2,4,128,256]{3,2,1,0:T(8,128)(2,1)S(1)} %shard_map.79), channel_id=1, source_target_pairs={{0,4},{4,0},{8,12},{12,8},{16,20},{20,16},{24,28},{28,24},{1,5},{5... | collective-permute-start | bytes 1572872 | tf_op jit(solution)/shard_map/ppermute | solution.py:26
  49.4 21.9 %collective-permute-start.22 = (bf16[2,512,256]{2,1,0:T(8,128)(2,1)S(1)}, bf16[2,512,256]{2,1,0:T(8,128)(2,1)S(1)}, u32[]{:S(2)}, u32[]{:S(2)}) collective-permute-start(bf16[2,512,256]{2,1,0:T(8,128)(2,1)S(1)} %get-tuple-element.64.refs_4_), channel_id=1, source_target_pairs={{0,2},{1,3},{2,0},{3,1},{4,6},{5,7},{6,4},{7,5},{8,10},{9,11},{10,... | collective-permute-start | bytes 1572872 | tf_op jit(solution)/shard_map/ppermute | solution.py:26
  51.9 23.7 %collective-permute-start.15 = (bf16[2,1,4,128,128]{4,3,2,1,0:T(8,128)(2,1)S(1)}, bf16[2,1,4,128,128]{4,3,2,1,0:T(8,128)(2,1)S(1)}, u32[]{:S(2)}, u32[]{:S(2)}) collective-permute-start(bf16[2,1,4,128,128]{4,3,2,1,0:T(8,128)(2,1)S(1)} %slice.129), channel_id=1, source_target_pairs={{0,16},{4,20},{8,24},{12,28},{16,0},{20,4},{24,8},{28,12},{1,17},{... | collective-permute-start | bytes 786440 | tf_op jit(solution)/shard_map/ppermute | solution.py:26
  61.6 36.3 %collective-permute-start.18 = (bf16[1,4,128,256]{3,2,1,0:T(8,128)(2,1)S(1)}, bf16[1,4,128,256]{3,2,1,0:T(8,128)(2,1)S(1)}, u32[]{:S(2)}, u32[]{:S(2)}) collective-permute-start(bf16[1,4,128,256]{3,2,1,0:T(8,128)(2,1)S(1)} %get-tuple-element.76), channel_id=1, source_target_pairs={{0,16},{4,20},{8,24},{12,28},{16,0},{20,4},{24,8},{28,12},{1,17},{... | collective-permute-start | bytes 786440 | tf_op jit(solution)/shard_map/ppermute | solution.py:26
  63.8 14.2 %collective-permute-start.20 = (bf16[2,4,128,256]{3,2,1,0:T(8,128)(2,1)S(1)}, bf16[2,4,128,256]{3,2,1,0:T(8,128)(2,1)S(1)}, u32[]{:S(2)}, u32[]{:S(2)}) collective-permute-start(bf16[2,4,128,256]{3,2,1,0:T(8,128)(2,1)S(1)} %shard_map.85), channel_id=1, source_target_pairs={{0,4},{4,0},{8,12},{12,8},{16,20},{20,16},{24,28},{28,24},{1,5},{5... | collective-permute-start | bytes 1572872 | tf_op jit(solution)/shard_map/ppermute | solution.py:26
  72.0 17.3 %collective-permute-start.23 = (bf16[2,4,128,256]{3,2,1,0:T(8,128)(2,1)S(1)}, bf16[2,4,128,256]{3,2,1,0:T(8,128)(2,1)S(1)}, u32[]{:S(2)}, u32[]{:S(2)}) collective-permute-start(bf16[2,4,128,256]{3,2,1,0:T(8,128)(2,1)S(1)} %shard_map.88), channel_id=1, source_target_pairs={{0,4},{4,0},{8,12},{12,8},{16,20},{20,16},{24,28},{28,24},{1,5},{5... | collective-permute-start | bytes 1572872 | tf_op jit(solution)/shard_map/ppermute | solution.py:26
  74.3 20.0 %collective-permute-start.25 = (bf16[2,4,128,128]{3,2,1,0:T(8,128)(2,1)S(1)}, bf16[2,4,128,128]{3,2,1,0:T(8,128)(2,1)S(1)}, u32[]{:S(2)}, u32[]{:S(2)}) collective-permute-start(bf16[2,4,128,128]{3,2,1,0:T(8,128)(2,1)S(1)} %shard_map.91), channel_id=1, source_target_pairs={{0,4},{4,0},{8,12},{12,8},{16,20},{20,16},{24,28},{28,24},{1,5},{5... | collective-permute-start | bytes 786440 | tf_op jit(solution)/shard_map/ppermute | solution.py:26
  75.8 20.2 %collective-permute-start.17 = (bf16[1,4,128,128]{3,2,1,0:T(8,128)(2,1)S(1)}, bf16[1,4,128,128]{3,2,1,0:T(8,128)(2,1)S(1)}, u32[]{:S(2)}, u32[]{:S(2)}) collective-permute-start(bf16[1,4,128,128]{3,2,1,0:T(8,128)(2,1)S(1)} %get-tuple-element.85), channel_id=1, source_target_pairs={{0,4},{4,0},{8,12},{12,8},{16,20},{20,16},{24,28},{28,24},{1,5},{5... | collective-permute-start | bytes 393224 | tf_op jit(solution)/shard_map/ppermute | solution.py:26
  78.2 21.7 %collective-permute-start.21 = (bf16[1,4,128,256]{3,2,1,0:T(8,128)(2,1)S(1)}, bf16[1,4,128,256]{3,2,1,0:T(8,128)(2,1)S(1)}, u32[]{:S(2)}, u32[]{:S(2)}) collective-permute-start(bf16[1,4,128,256]{3,2,1,0:T(8,128)(2,1)S(1)} %get-tuple-element.71), channel_id=1, source_target_pairs={{0,16},{4,20},{8,24},{12,28},{16,0},{20,4},{24,8},{28,12},{1,17},{... | collective-permute-start | bytes 786440 | tf_op jit(solution)/shard_map/ppermute | solution.py:26
  89.4 15.8 %collective-permute-start.24 = (bf16[1,4,128,256]{3,2,1,0:T(8,128)(2,1)S(1)}, bf16[1,4,128,256]{3,2,1,0:T(8,128)(2,1)S(1)}, u32[]{:S(2)}, u32[]{:S(2)}) collective-permute-start(bf16[1,4,128,256]{3,2,1,0:T(8,128)(2,1)S(1)} %get-tuple-element.69), channel_id=1, source_target_pairs={{0,16},{4,20},{8,24},{12,28},{16,0},{20,4},{24,8},{28,12},{1,17},{... | collective-permute-start | bytes 786440 | tf_op jit(solution)/shard_map/ppermute | solution.py:26
  94.4 13.3 %collective-permute-start.26 = (bf16[1,4,128,128]{3,2,1,0:T(8,128)(2,1)S(1)}, bf16[1,4,128,128]{3,2,1,0:T(8,128)(2,1)S(1)}, u32[]{:S(2)}, u32[]{:S(2)}) collective-permute-start(bf16[1,4,128,128]{3,2,1,0:T(8,128)(2,1)S(1)} %get-tuple-element.80), channel_id=1, source_target_pairs={{0,16},{4,20},{8,24},{12,28},{16,0},{20,4},{24,8},{28,12},{1,17},{... | collective-permute-start | bytes 393224 | tf_op jit(solution)/shard_map/ppermute | solution.py:26
  (2 other events, 3.8 us)

commit v15 on v13

--- a/solution.py
+++ b/solution.py
@@ -389,12 +389,12 @@
 
     chunk = (pairs[1], SPLITS[0], body, body[0])
     away, got = send(*chunk)
-    other[1], late_rest, _ = tie((other[1], late_pair[:, :, middle:], away))
-    pairs.append((late_rest, swap(late_rest, "ctx", 2)))
+    other[1], _ = tie((other[1], away))
 
     all_mine, all_other = (jnp.concatenate(parts, axis=0) for parts in (mine, other))
     total = panel(at, all_mine, all_other, out_proj, pairs[0], SPLITS[0], head)
-    other[1], total = tie((other[1], total))
+    other[1], late_rest, total = tie((other[1], late_pair[:, :, middle:], total))
+    pairs.append((late_rest, swap(late_rest, "ctx", 2)))
     total = total.reshape(2, part, *total.shape[1:])
     head_got = swap(total[:, part // 2 :], "fsdp", bits[-3])
 

time: 110 us -> 110 us (level)
  transfers between devices with their start and end apart: 27 -> 27, of which waited for: 10 -> 9; matrix products, arithmetic and copies ran while one was open for 1% -> 1% of each run, Pallas kernels for 35% -> 35%
where the time goes in v15:
time: 110 us; the launch traced here: 109 us
  Pallas kernels  40.7 us (37%)
  starting transfers between devices  33.9 us (31%)
  waiting for transfers between devices  30.6 us (28%)
  local copies, waits for them, and re-layouts  2.66 us (2%)
    ppermute x25, starting transfers between devices, swap(): return lax.ppermute(x, axis, [(i, i ^ mask) for i in range(peers)])  32.4 us
    ppermute x25, waiting for transfers between devices, swap(): return lax.ppermute(x, axis, [(i, i ^ mask) for i in range(peers)])  30.6 us
    pallas_call x5, Pallas kernels, place_pieces(): pl.pallas_call(functools.partial(place_kernel, split, step), grid_spec=pl...  9.81 us
    pallas_call x1, Pallas kernels, project(): pl.pallas_call(table_kernel, grid=(1,), in_specs=[hbm, hbm, pl.BlockSpec(...  9.69 us
    pallas_call x2, Pallas kernels, mix(): pl.pallas_call(mixer_kernel, grid=(windows // 2,), in_specs=[pl.BlockSpec...  8.48 us
    pallas_call x9, Pallas kernels, panel(): pl.pallas_call(panel_kernel, grid_spec=pltpu.PrefetchScalarGridSpec(num_s...  7.19 us
    pallas_call x1, Pallas kernels, residual(): pl.pallas_call(residual_kernel, grid=(4,), in_specs=[whole(token_ids), pl...  2.65 us
    pallas_call x1, Pallas kernels, cut_pieces(): pl.pallas_call(cut_kernel, grid_spec=pltpu.PrefetchScalarGridSpec(num_sca...  2.23 us
  transfers between devices with their start and end apart: 27, of which 9 were waited for; matrix products, arithmetic and copies ran while one was open for 1% of the time, Pallas kernels for 35%

profile of v15, /device:TPU:0, one launch (start us, length us, event | category | flops | bytes accessed | tf_op | source)
XLA Modules:
  0.0 109.3 jit_solution(6472898076487747156)
XLA Ops:
  0.0 5.0 %collective-permute-start.2 = (s32[1,128]{1,0:T(1,128)}, s32[1,128]{1,0:T(1,128)S(1)}, u32[]{:S(2)}, u32[]{:S(2)}) collective-permute-start(s32[1,128]{1,0:T(1,128)} %ids_ref), channel_id=1, source_target_pairs={{0,24},{4,28},{8,16},{12,20},{16,8},{20,12},{24,0},{28,4},{1,25},{... | collective-permute-start | bytes 1544 | tf_op jit(solution)/shard_map/ppermute | solution.py:26
  5.6 2.2 %shard_map.73 = (bf16[512,512]{1,0:T(8,128)(2,1)}, bf16[512,512]{1,0:T(8,128)(2,1)}) custom-call(s32[1]{0:T(128)} %bitcast.place_ref, bf16[512,4096]{1,0:T(8,128)(2,1)} %refs_3_.17, bf16[512,4096]{1,0:T(8,128)(2,1)} %refs_3_.17), custom_call_target="tpu_custom_call" | custom-call | bytes 2000000 | tf_op jit(solution)/shard_map/pallas_call | solution.py:200
  9.6 1.6 %collective-permute-start.3 = (s32[4,128]{1,0:T(4,128)S(1)}, s32[4,128]{1,0:T(4,128)S(1)}, u32[]{:S(2)}, u32[]{:S(2)}) collective-permute-start(s32[4,128]{1,0:T(4,128)S(1)} %pad_add_fusion.4), channel_id=1, source_target_pairs={{0,4},{4,0},{8,12},{12,8},{16,20},{20,16},{24,28},{28,24},{1,5},{5... | collective-permute-start | bytes 6152 | tf_op jit(solution)/shard_map/ppermute | solution.py:26
  11.2 2.0 %collective-permute-start.6 = (bf16[512,512]{1,0:T(8,128)(2,1)}, bf16[512,512]{1,0:T(8,128)(2,1)S(1)}, u32[]{:S(2)}, u32[]{:S(2)}) collective-permute-start(bf16[512,512]{1,0:T(8,128)(2,1)} %get-tuple-element.44), channel_id=1, source_target_pairs={{0,8},{4,12},{8,0},{12,4},{16,24},{20,28},{24,16},{28,20},{1,9},{5... | collective-permute-start | bytes 1572872 | tf_op jit(solution)/shard_map/ppermute | solution.py:26
  13.3 1.6 %collective-permute-start.7 = (s32[8,128]{1,0:T(8,128)S(1)}, s32[8,128]{1,0:T(8,128)S(1)}, u32[]{:S(2)}, u32[]{:S(2)}) collective-permute-start(s32[8,128]{1,0:T(8,128)S(1)} %pad_add_fusion.2), channel_id=1, source_target_pairs={{0,2},{1,3},{2,0},{3,1},{4,6},{5,7},{6,4},{7,5},{8,10},{9,11},{10,... | collective-permute-start | bytes 12296 | tf_op jit(solution)/shard_map/ppermute | solution.py:21
  14.9 2.0 %collective-permute-start.4 = (bf16[512,512]{1,0:T(8,128)(2,1)}, bf16[512,512]{1,0:T(8,128)(2,1)S(1)}, u32[]{:S(2)}, u32[]{:S(2)}) collective-permute-start(bf16[512,512]{1,0:T(8,128)(2,1)} %get-tuple-element.42), channel_id=1, source_target_pairs={{0,8},{4,12},{8,0},{12,4},{16,24},{20,28},{24,16},{28,20},{1,9},{5... | collective-permute-start | bytes 1572872 | tf_op jit(solution)/shard_map/ppermute | solution.py:26
  16.9 2.2 %copy-done.1 = bf16[512,4096]{1,0:T(8,128)(2,1)S(1)} copy-done((bf16[512,4096]{1,0:T(8,128)(2,1)S(1)}, bf16[512,4096]{1,0:T(8,128)(2,1)}, u32[]{:S(2)}) %copy-start.1) | copy-done | bytes 4194328
  19.1 9.7 %shard_map.75.table_ref = bf16[3,512,512]{2,1,0:T(8,128)(2,1)S(1)} custom-call(bf16[512,4096]{1,0:T(8,128)(2,1)S(1)} %copy-done.1, bf16[3,4096,512]{2,1,0:T(8,128)(2,1)} %weight_hbm, f32[1,4096]{1,0:T(1,128)S(1)} %bitcast.46), custom_call_target="tpu_custom_call" | custom-call | flops 3000000000 | tf_op jit(solution)/shard_map/pallas_call | solution.py:101
  29.7 2.1 %shard_map.76 = bf16[2,128,512]{2,1,0:T(8,128)(2,1)S(1)} custom-call(s32[2,1,272]{2,1,0:T(1,128)S(1)} %copy.13.ids_ref, bf16[3,512,512]{2,1,0:T(8,128)(2,1)S(1)} %shard_map.75.table_ref, f32[3,3,512]{2,1,0:T(4,128)S(1)} %copy-done.4, bf16[4,1024,256]{2,1,0:T(8,128)(2,1)S(1)} %shard_map.74.toeplitz), custom_call_target="tpu_custom_call" | custom-call | flops 1500000000 | tf_op jit(solution)/shard_map/pallas_call | solution.py:167
  32.1 1.4 %collective-permute-start.9 = (bf16[512,256]{1,0:T(8,128)(2,1)S(1)}, bf16[512,256]{1,0:T(8,128)(2,1)S(1)}, u32[]{:S(2)}, u32[]{:S(2)}) collective-permute-start(bf16[512,256]{1,0:T(8,128)(2,1)S(1)} %get-tuple-element.50), channel_id=1, source_target_pairs={{0,2},{1,3},{2,0},{3,1},{4,6},{5,7},{6,4},{7,5},{8,10},{9,11},{10,... | collective-permute-start | bytes 786440 | tf_op jit(solution)/shard_map/ppermute | solution.py:26
  33.5 6.4 %shard_map.77 = bf16[6,128,512]{2,1,0:T(8,128)(2,1)S(1)} custom-call(s32[6,1,272]{2,1,0:T(1,128)S(1)} %reshape.54.ids_ref, bf16[3,512,512]{2,1,0:T(8,128)(2,1)S(1)} %shard_map.75.table_ref, f32[3,3,512]{2,1,0:T(4,128)S(1)} %copy-done.4, bf16[4,1024,256]{2,1,0:T(8,128)(2,1)S(1)} %shard_map.74.toeplitz), custom_call_target="tpu_custom_call" | custom-call | flops 1500000000 | tf_op jit(solution)/shard_map/pallas_call | solution.py:167
  40.2 2.0 %collective-permute-start.11 = (bf16[2,128,512]{2,1,0:T(8,128)(2,1)S(1)}, bf16[2,128,512]{2,1,0:T(8,128)(2,1)S(1)}, u32[]{:S(2)}, u32[]{:S(2)}) collective-permute-start(bf16[2,128,512]{2,1,0:T(8,128)(2,1)S(1)} %get-tuple-element.79), channel_id=1, source_target_pairs={{0,8},{4,12},{8,0},{12,4},{16,24},{20,28},{24,16},{28,20},{1,9},{5... | collective-permute-start | bytes 786440 | tf_op jit(solution)/shard_map/ppermute | solution.py:26
  42.4 2.7 %shard_map.78.so_far_ref = bf16[128,4096]{1,0:T(8,128)(2,1)} custom-call(s32[1,128]{1,0:T(1,128)S(1)} %copy-done.3, bf16[512,4096]{1,0:T(8,128)(2,1)S(1)} %copy-done.1), custom_call_target="tpu_custom_call" | custom-call | flops 400000000 | tf_op jit(solution)/shard_map/pallas_call | solution.py:290
  47.1 1.6 %collective-permute-start.16 = (bf16[2,4,128,256]{3,2,1,0:T(8,128)(2,1)S(1)}, bf16[2,4,128,256]{3,2,1,0:T(8,128)(2,1)S(1)}, u32[]{:S(2)}, u32[]{:S(2)}) collective-permute-start(bf16[2,4,128,256]{3,2,1,0:T(8,128)(2,1)S(1)} %shard_map.79), channel_id=1, source_target_pairs={{0,4},{4,0},{8,12},{12,8},{16,20},{20,16},{24,28},{28,24},{1,5},{5... | collective-permute-start | bytes 1572872 | tf_op jit(solution)/shard_map/ppermute | solution.py:26
  50.6 1.5 %collective-permute-start.15 = (bf16[2,1,4,128,128]{4,3,2,1,0:T(8,128)(2,1)S(1)}, bf16[2,1,4,128,128]{4,3,2,1,0:T(8,128)(2,1)S(1)}, u32[]{:S(2)}, u32[]{:S(2)}) collective-permute-start(bf16[2,1,4,128,128]{4,3,2,1,0:T(8,128)(2,1)S(1)} %slice.129), channel_id=1, source_target_pairs={{0,16},{4,20},{8,24},{12,28},{16,0},{20,4},{24,8},{28,12},{1,17},{... | collective-permute-start | bytes 786440 | tf_op jit(solution)/shard_map/ppermute | solution.py:26
  54.6 5.9 %collective-permute-done.19.refs_5_ = bf16[2,512,256]{2,1,0:T(8,128)(2,1)S(1)} collective-permute-done((bf16[2,512,256]{2,1,0:T(8,128)(2,1)S(1)}, bf16[2,512,256]{2,1,0:T(8,128)(2,1)S(1)}, u32[]{:S(2)}, u32[]{:S(2)}) %collective-permute-start.19) | collective-permute-done | bytes 524320 | tf_op jit(solution)/shard_map/ppermute | solution.py:26
  61.3 1.5 %collective-permute-start.18 = (bf16[1,4,128,256]{3,2,1,0:T(8,128)(2,1)S(1)}, bf16[1,4,128,256]{3,2,1,0:T(8,128)(2,1)S(1)}, u32[]{:S(2)}, u32[]{:S(2)}) collective-permute-start(bf16[1,4,128,256]{3,2,1,0:T(8,128)(2,1)S(1)} %get-tuple-element.76), channel_id=1, source_target_pairs={{0,16},{4,20},{8,24},{12,28},{16,0},{20,4},{24,8},{28,12},{1,17},{... | collective-permute-start | bytes 786440 | tf_op jit(solution)/shard_map/ppermute | solution.py:26
  63.5 1.6 %collective-permute-start.20 = (bf16[2,4,128,256]{3,2,1,0:T(8,128)(2,1)S(1)}, bf16[2,4,128,256]{3,2,1,0:T(8,128)(2,1)S(1)}, u32[]{:S(2)}, u32[]{:S(2)}) collective-permute-start(bf16[2,4,128,256]{3,2,1,0:T(8,128)(2,1)S(1)} %shard_map.85), channel_id=1, source_target_pairs={{0,4},{4,0},{8,12},{12,8},{16,20},{20,16},{24,28},{28,24},{1,5},{5... | collective-permute-start | bytes 1572872 | tf_op jit(solution)/shard_map/ppermute | solution.py:26
  65.1 6.9 %collective-permute-done.15 = bf16[2,1,4,128,128]{4,3,2,1,0:T(8,128)(2,1)S(1)} collective-permute-done((bf16[2,1,4,128,128]{4,3,2,1,0:T(8,128)(2,1)S(1)}, bf16[2,1,4,128,128]{4,3,2,1,0:T(8,128)(2,1)S(1)}, u32[]{:S(2)}, u32[]{:S(2)}) %collective-permute-start.15) | collective-permute-done | bytes 262176 | tf_op jit(solution)/shard_map/ppermute | solution.py:26
  72.8 1.6 %collective-permute-start.23 = (bf16[2,4,128,256]{3,2,1,0:T(8,128)(2,1)S(1)}, bf16[2,4,128,256]{3,2,1,0:T(8,128)(2,1)S(1)}, u32[]{:S(2)}, u32[]{:S(2)}) collective-permute-start(bf16[2,4,128,256]{3,2,1,0:T(8,128)(2,1)S(1)} %shard_map.88), channel_id=1, source_target_pairs={{0,4},{4,0},{8,12},{12,8},{16,20},{20,16},{24,28},{28,24},{1,5},{5... | collective-permute-start | bytes 1572872 | tf_op jit(solution)/shard_map/ppermute | solution.py:26
  75.8 1.6 %collective-permute-start.25 = (bf16[2,4,128,128]{3,2,1,0:T(8,128)(2,1)S(1)}, bf16[2,4,128,128]{3,2,1,0:T(8,128)(2,1)S(1)}, u32[]{:S(2)}, u32[]{:S(2)}) collective-permute-start(bf16[2,4,128,128]{3,2,1,0:T(8,128)(2,1)S(1)} %shard_map.91), channel_id=1, source_target_pairs={{0,4},{4,0},{8,12},{12,8},{16,20},{20,16},{24,28},{28,24},{1,5},{5... | collective-permute-start | bytes 786440 | tf_op jit(solution)/shard_map/ppermute | solution.py:26
  78.2 1.4 %collective-permute-start.21 = (bf16[1,4,128,256]{3,2,1,0:T(8,128)(2,1)S(1)}, bf16[1,4,128,256]{3,2,1,0:T(8,128)(2,1)S(1)}, u32[]{:S(2)}, u32[]{:S(2)}) collective-permute-start(bf16[1,4,128,256]{3,2,1,0:T(8,128)(2,1)S(1)} %get-tuple-element.71), channel_id=1, source_target_pairs={{0,16},{4,20},{8,24},{12,28},{16,0},{20,4},{24,8},{28,12},{1,17},{... | collective-permute-start | bytes 786440 | tf_op jit(solution)/shard_map/ppermute | solution.py:26
  79.6 9.4 %collective-permute-done.23 = bf16[2,4,128,256]{3,2,1,0:T(8,128)(2,1)S(1)} collective-permute-done((bf16[2,4,128,256]{3,2,1,0:T(8,128)(2,1)S(1)}, bf16[2,4,128,256]{3,2,1,0:T(8,128)(2,1)S(1)}, u32[]{:S(2)}, u32[]{:S(2)}) %collective-permute-start.23) | collective-permute-done | bytes 524320 | tf_op jit(solution)/shard_map/ppermute | solution.py:26
  89.2 1.7 %collective-permute-start.24 = (bf16[1,4,128,256]{3,2,1,0:T(8,128)(2,1)S(1)}, bf16[1,4,128,256]{3,2,1,0:T(8,128)(2,1)S(1)}, u32[]{:S(2)}, u32[]{:S(2)}) collective-permute-start(bf16[1,4,128,256]{3,2,1,0:T(8,128)(2,1)S(1)} %get-tuple-element.69), channel_id=1, source_target_pairs={{0,16},{4,20},{8,24},{12,28},{16,0},{20,4},{24,8},{28,12},{1,17},{... | collective-permute-start | bytes 786440 | tf_op jit(solution)/shard_map/ppermute | solution.py:26
  90.9 4.6 %collective-permute-done.25 = bf16[2,4,128,128]{3,2,1,0:T(8,128)(2,1)S(1)} collective-permute-done((bf16[2,4,128,128]{3,2,1,0:T(8,128)(2,1)S(1)}, bf16[2,4,128,128]{3,2,1,0:T(8,128)(2,1)S(1)}, u32[]{:S(2)}, u32[]{:S(2)}) %collective-permute-start.25) | collective-permute-done | bytes 262176 | tf_op jit(solution)/shard_map/ppermute | solution.py:26
  95.6 1.6 %collective-permute-start.26 = (bf16[1,4,128,128]{3,2,1,0:T(8,128)(2,1)S(1)}, bf16[1,4,128,128]{3,2,1,0:T(8,128)(2,1)S(1)}, u32[]{:S(2)}, u32[]{:S(2)}) collective-permute-start(bf16[1,4,128,128]{3,2,1,0:T(8,128)(2,1)S(1)} %get-tuple-element.80), channel_id=1, source_target_pairs={{0,16},{4,20},{8,24},{12,28},{16,0},{20,4},{24,8},{28,12},{1,17},{... | collective-permute-start | bytes 393224 | tf_op jit(solution)/shard_map/ppermute | solution.py:26
  97.1 1.9 %shard_map.82.so_far_ref = bf16[128,4096]{1,0:T(8,128)(2,1)} custom-call(s32[1]{0:T(128)} %bitcast.place_ref, bf16[128,4096]{1,0:T(8,128)(2,1)} %shard_map.78.so_far_ref, bf16[1,4,128,128]{3,2,1,0:T(8,128)(2,1)S(1)} %get-tuple-element.86.near_ref, bf16[1,4,128,128]{3,2,1,0:T(8,128)(2,1)S(1)} %collective-permute-done.17.far_ref), custom_call_target="tpu_custom_call", output_to_operand_aliasing={{}: (1, {})} | custom-call | bytes 1000000 | tf_op jit(solution)/shard_map/pallas_call | solution.py:318
  99.1 2.0 %shard_map.83.so_far_ref = bf16[128,4096]{1,0:T(8,128)(2,1)} custom-call(s32[1]{0:T(128)} %bitcast.place_ref, bf16[128,4096]{1,0:T(8,128)(2,1)} %shard_map.82.so_far_ref, bf16[1,4,128,256]{3,2,1,0:T(8,128)(2,1)S(1)} %get-tuple-element.75.near_ref, bf16[1,4,128,256]{3,2,1,0:T(8,128)(2,1)S(1)} %collective-permute-done.18.far_ref), custom_call_target="tpu_custom_call", output_to_operand_aliasing={{}: (1, {})} | custom-call | bytes 1000000 | tf_op jit(solution)/shard_map/pallas_call | solution.py:318
  101.1 2.0 %shard_map.86.so_far_ref = bf16[128,4096]{1,0:T(8,128)(2,1)} custom-call(s32[1]{0:T(128)} %bitcast.place_ref, bf16[128,4096]{1,0:T(8,128)(2,1)} %shard_map.83.so_far_ref, bf16[1,4,128,256]{3,2,1,0:T(8,128)(2,1)S(1)} %get-tuple-element.72.near_ref, bf16[1,4,128,256]{3,2,1,0:T(8,128)(2,1)S(1)} %collective-permute-done.21.far_ref), custom_call_target="tpu_custom_call", output_to_operand_aliasing={{}: (1, {})} | custom-call | bytes 1000000 | tf_op jit(solution)/shard_map/pallas_call | solution.py:318
  103.1 2.1 %collective-permute-done.24.far_ref = bf16[1,4,128,256]{3,2,1,0:T(8,128)(2,1)S(1)} collective-permute-done((bf16[1,4,128,256]{3,2,1,0:T(8,128)(2,1)S(1)}, bf16[1,4,128,256]{3,2,1,0:T(8,128)(2,1)S(1)}, u32[]{:S(2)}, u32[]{:S(2)}) %collective-permute-start.24) | collective-permute-done | bytes 262176 | tf_op jit(solution)/shard_map/ppermute | solution.py:26
  105.2 2.0 %shard_map.89.so_far_ref = bf16[128,4096]{1,0:T(8,128)(2,1)} custom-call(s32[1]{0:T(128)} %bitcast.place_ref, bf16[128,4096]{1,0:T(8,128)(2,1)} %shard_map.86.so_far_ref, bf16[1,4,128,256]{3,2,1,0:T(8,128)(2,1)S(1)} %get-tuple-element.70.near_ref, bf16[1,4,128,256]{3,2,1,0:T(8,128)(2,1)S(1)} %collective-permute-done.24.far_ref), custom_call_target="tpu_custom_call", output_to_operand_aliasing={{}: (1, {})} | custom-call | bytes 1000000 | tf_op jit(solution)/shard_map/pallas_call | solution.py:318
  107.3 1.9 %shard_map.92 = bf16[128,4096]{1,0:T(8,128)(2,1)} custom-call(s32[1]{0:T(128)} %bitcast.place_ref, bf16[128,4096]{1,0:T(8,128)(2,1)} %shard_map.89.so_far_ref, bf16[1,4,128,128]{3,2,1,0:T(8,128)(2,1)S(1)} %get-tuple-element.81.near_ref, bf16[1,4,128,128]{3,2,1,0:T(8,128)(2,1)S(1)} %collective-permute-done.26.far_ref), custom_call_target="tpu_custom_call", output_to_operand_aliasing={{}: (1, {})} | custom-call | bytes 1000000 | tf_op jit(solution)/shard_map/pallas_call | solution.py:318
  (82 shorter events, 15.4 us)
Async XLA Ops:
  0.0 8.6 %collective-permute-start.2 = (s32[1,128]{1,0:T(1,128)}, s32[1,128]{1,0:T(1,128)S(1)}, u32[]{:S(2)}, u32[]{:S(2)}) collective-permute-start(s32[1,128]{1,0:T(1,128)} %ids_ref), channel_id=1, source_target_pairs={{0,24},{4,28},{8,16},{12,20},{16,8},{20,12},{24,0},{28,4},{1,25},{... | collective-permute-start | bytes 1544 | tf_op jit(solution)/shard_map/ppermute | solution.py:26
  5.0 3.7 %collective-permute-start.1 = (s32[1,128]{1,0:T(1,128)}, s32[1,128]{1,0:T(1,128)S(1)}, u32[]{:S(2)}, u32[]{:S(2)}) collective-permute-start(s32[1,128]{1,0:T(1,128)} %ids_ref), channel_id=1, source_target_pairs={{0,8},{4,12},{8,0},{12,4},{16,24},{20,28},{24,16},{28,20},{1,9},{5... | collective-permute-start | bytes 1544 | tf_op jit(solution)/shard_map/ppermute | solution.py:26
  5.1 4.6 %collective-permute-start = (s32[1,128]{1,0:T(1,128)}, s32[1,128]{1,0:T(1,128)S(1)}, u32[]{:S(2)}, u32[]{:S(2)}) collective-permute-start(s32[1,128]{1,0:T(1,128)} %ids_ref), channel_id=1, source_target_pairs={{0,16},{4,20},{8,24},{12,28},{16,0},{20,4},{24,8},{28,12},{1,17},{... | collective-permute-start | bytes 1544 | tf_op jit(solution)/shard_map/ppermute | solution.py:26
  5.6 2.2 %copy-start.5 = (bf16[32,128]{1,0:T(8,128)(2,1)S(1)}, bf16[32,128]{1,0:T(8,128)(2,1)}, u32[]{:S(2)}) copy-start(bf16[32,128]{1,0:T(8,128)(2,1)} %param.12) | copy-start | bytes 24580
  5.6 4.0 %copy-start.3 = (s32[1,128]{1,0:T(1,128)S(1)}, s32[1,128]{1,0:T(1,128)}, u32[]{:S(2)}) copy-start(s32[1,128]{1,0:T(1,128)} %ids_ref) | copy-start | bytes 1540
  5.6 11.3 %copy-start.2 = (f32[4096]{0:T(1024)S(1)}, f32[4096]{0:T(1024)}, u32[]{:S(2)}) copy-start(f32[4096]{0:T(1024)} %param.9) | copy-start | bytes 49156
  9.6 3.7 %collective-permute-start.3 = (s32[4,128]{1,0:T(4,128)S(1)}, s32[4,128]{1,0:T(4,128)S(1)}, u32[]{:S(2)}, u32[]{:S(2)}) collective-permute-start(s32[4,128]{1,0:T(4,128)S(1)} %pad_add_fusion.4), channel_id=1, source_target_pairs={{0,4},{4,0},{8,12},{12,8},{16,20},{20,16},{24,28},{28,24},{1,5},{5... | collective-permute-start | bytes 6152 | tf_op jit(solution)/shard_map/ppermute | solution.py:26
  11.2 17.9 %collective-permute-start.6 = (bf16[512,512]{1,0:T(8,128)(2,1)}, bf16[512,512]{1,0:T(8,128)(2,1)S(1)}, u32[]{:S(2)}, u32[]{:S(2)}) collective-permute-start(bf16[512,512]{1,0:T(8,128)(2,1)} %get-tuple-element.44), channel_id=1, source_target_pairs={{0,8},{4,12},{8,0},{12,4},{16,24},{20,28},{24,16},{28,20},{1,9},{5... | collective-permute-start | bytes 1572872 | tf_op jit(solution)/shard_map/ppermute | solution.py:26
  13.3 15.6 %collective-permute-start.8 = (s32[8,128]{1,0:T(8,128)S(1)}, s32[8,128]{1,0:T(8,128)S(1)}, u32[]{:S(2)}, u32[]{:S(2)}) collective-permute-start(s32[8,128]{1,0:T(8,128)S(1)} %pad_add_fusion.2), channel_id=1, source_target_pairs={{0,1},{1,2},{2,3},{3,0},{4,5},{5,6},{6,7},{7,4},{8,9},{9,10},{10,1... | collective-permute-start | bytes 12296 | tf_op jit(solution)/shard_map/ppermute | solution.py:21
  13.3 15.4 %collective-permute-start.7 = (s32[8,128]{1,0:T(8,128)S(1)}, s32[8,128]{1,0:T(8,128)S(1)}, u32[]{:S(2)}, u32[]{:S(2)}) collective-permute-start(s32[8,128]{1,0:T(8,128)S(1)} %pad_add_fusion.2), channel_id=1, source_target_pairs={{0,2},{1,3},{2,0},{3,1},{4,6},{5,7},{6,4},{7,5},{8,10},{9,11},{10,... | collective-permute-start | bytes 12296 | tf_op jit(solution)/shard_map/ppermute | solution.py:21
  14.9 25.0 %collective-permute-start.4 = (bf16[512,512]{1,0:T(8,128)(2,1)}, bf16[512,512]{1,0:T(8,128)(2,1)S(1)}, u32[]{:S(2)}, u32[]{:S(2)}) collective-permute-start(bf16[512,512]{1,0:T(8,128)(2,1)} %get-tuple-element.42), channel_id=1, source_target_pairs={{0,8},{4,12},{8,0},{12,4},{16,24},{20,28},{24,16},{28,20},{1,9},{5... | collective-permute-start | bytes 1572872 | tf_op jit(solution)/shard_map/ppermute | solution.py:26
  19.1 10.7 %copy-start.4 = (f32[3,3,512]{2,1,0:T(4,128)S(1)}, f32[3,3,512]{2,1,0:T(4,128)}, u32[]{:S(2)}) copy-start(f32[3,3,512]{2,1,0:T(4,128)} %short_ref.3) | copy-start | bytes 55300
  29.1 10.8 %collective-permute-start.10 = (bf16[512,256]{1,0:T(8,128)(2,1)S(1)}, bf16[512,256]{1,0:T(8,128)(2,1)S(1)}, u32[]{:S(2)}, u32[]{:S(2)}) collective-permute-start(bf16[512,256]{1,0:T(8,128)(2,1)S(1)} %get-tuple-element.83), channel_id=1, source_target_pairs={{0,2},{1,3},{2,0},{3,1},{4,6},{5,7},{6,4},{7,5},{8,10},{9,11},{10,... | collective-permute-start | bytes 786440 | tf_op jit(solution)/shard_map/ppermute | solution.py:26
  31.9 14.5 %collective-permute-start.12 = (bf16[2,128,512]{2,1,0:T(8,128)(2,1)S(1)}, bf16[2,128,512]{2,1,0:T(8,128)(2,1)S(1)}, u32[]{:S(2)}, u32[]{:S(2)}) collective-permute-start(bf16[2,128,512]{2,1,0:T(8,128)(2,1)S(1)} %shard_map.76), channel_id=1, source_target_pairs={{0,8},{4,12},{8,0},{12,4},{16,24},{20,28},{24,16},{28,20},{1,9},{5... | collective-permute-start | bytes 786440 | tf_op jit(solution)/shard_map/ppermute | solution.py:26
  32.1 12.9 %collective-permute-start.9 = (bf16[512,256]{1,0:T(8,128)(2,1)S(1)}, bf16[512,256]{1,0:T(8,128)(2,1)S(1)}, u32[]{:S(2)}, u32[]{:S(2)}) collective-permute-start(bf16[512,256]{1,0:T(8,128)(2,1)S(1)} %get-tuple-element.50), channel_id=1, source_target_pairs={{0,2},{1,3},{2,0},{3,1},{4,6},{5,7},{6,4},{7,5},{8,10},{9,11},{10,... | collective-permute-start | bytes 786440 | tf_op jit(solution)/shard_map/ppermute | solution.py:26
  39.9 5.2 %collective-permute-start.5 = (bf16[512,512]{1,0:T(8,128)(2,1)S(1)}, bf16[512,512]{1,0:T(8,128)(2,1)S(1)}, u32[]{:S(2)}, u32[]{:S(2)}) collective-permute-start(bf16[512,512]{1,0:T(8,128)(2,1)S(1)} %collective-permute-done.4), channel_id=1, source_target_pairs={{0,1},{1,0},{2,3},{3,2},{4,5},{5,4},{6,7},{7,6},{8,9},{9,8},{10,11... | collective-permute-start | bytes 1572872 | tf_op jit(solution)/shard_map/ppermute | solution.py:26
  40.1 6.2 %copy-start = (bf16[512,4096]{1,0:T(8,128)(2,1)S(1)}, bf16[512,4096]{1,0:T(8,128)(2,1)}, u32[]{:S(2)}) copy-start(bf16[512,4096]{1,0:T(8,128)(2,1)} %refs_3_.17) | copy-start | bytes 12582916
  40.2 9.0 %collective-permute-start.11 = (bf16[2,128,512]{2,1,0:T(8,128)(2,1)S(1)}, bf16[2,128,512]{2,1,0:T(8,128)(2,1)S(1)}, u32[]{:S(2)}, u32[]{:S(2)}) collective-permute-start(bf16[2,128,512]{2,1,0:T(8,128)(2,1)S(1)} %get-tuple-element.79), channel_id=1, source_target_pairs={{0,8},{4,12},{8,0},{12,4},{16,24},{20,28},{24,16},{28,20},{1,9},{5... | collective-permute-start | bytes 786440 | tf_op jit(solution)/shard_map/ppermute | solution.py:26
  42.2 4.2 %collective-permute-start.13 = (bf16[2,512,256]{2,1,0:T(8,128)(2,1)S(1)}, bf16[2,512,256]{2,1,0:T(8,128)(2,1)S(1)}, u32[]{:S(2)}, u32[]{:S(2)}) collective-permute-start(bf16[2,512,256]{2,1,0:T(8,128)(2,1)S(1)} %pad_maximum_fusion.2.refs_4_), channel_id=1, source_target_pairs={{0,1},{1,0},{2,3},{3,2},{4,5},{5,4},{6,7},{7,6},{8,9},{9,8},{10,11... | collective-permute-start | bytes 1572872 | tf_op jit(solution)/shard_map/ppermute | solution.py:26
  45.2 4.0 %collective-permute-start.14 = (bf16[2,512,256]{2,1,0:T(8,128)(2,1)S(1)}, bf16[2,512,256]{2,1,0:T(8,128)(2,1)S(1)}, u32[]{:S(2)}, u32[]{:S(2)}) collective-permute-start(bf16[2,512,256]{2,1,0:T(8,128)(2,1)S(1)} %pad_maximum_fusion.1.refs_4_), channel_id=1, source_target_pairs={{0,1},{1,0},{2,3},{3,2},{4,5},{5,4},{6,7},{7,6},{8,9},{9,8},{10,11... | collective-permute-start | bytes 1572872 | tf_op jit(solution)/shard_map/ppermute | solution.py:26
  45.7 14.8 %collective-permute-start.19 = (bf16[2,512,256]{2,1,0:T(8,128)(2,1)S(1)}, bf16[2,512,256]{2,1,0:T(8,128)(2,1)S(1)}, u32[]{:S(2)}, u32[]{:S(2)}) collective-permute-start(bf16[2,512,256]{2,1,0:T(8,128)(2,1)S(1)} %get-tuple-element.73.refs_4_), channel_id=1, source_target_pairs={{0,2},{1,3},{2,0},{3,1},{4,6},{5,7},{6,4},{7,5},{8,10},{9,11},{10,... | collective-permute-start | bytes 1572872 | tf_op jit(solution)/shard_map/ppermute | solution.py:26
  47.1 14.1 %collective-permute-start.16 = (bf16[2,4,128,256]{3,2,1,0:T(8,128)(2,1)S(1)}, bf16[2,4,128,256]{3,2,1,0:T(8,128)(2,1)S(1)}, u32[]{:S(2)}, u32[]{:S(2)}) collective-permute-start(bf16[2,4,128,256]{3,2,1,0:T(8,128)(2,1)S(1)} %shard_map.79), channel_id=1, source_target_pairs={{0,4},{4,0},{8,12},{12,8},{16,20},{20,16},{24,28},{28,24},{1,5},{5... | collective-permute-start | bytes 1572872 | tf_op jit(solution)/shard_map/ppermute | solution.py:26
  50.6 21.4 %collective-permute-start.15 = (bf16[2,1,4,128,128]{4,3,2,1,0:T(8,128)(2,1)S(1)}, bf16[2,1,4,128,128]{4,3,2,1,0:T(8,128)(2,1)S(1)}, u32[]{:S(2)}, u32[]{:S(2)}) collective-permute-start(bf16[2,1,4,128,128]{4,3,2,1,0:T(8,128)(2,1)S(1)} %slice.129), channel_id=1, source_target_pairs={{0,16},{4,20},{8,24},{12,28},{16,0},{20,4},{24,8},{28,12},{1,17},{... | collective-permute-start | bytes 786440 | tf_op jit(solution)/shard_map/ppermute | solution.py:26
  52.1 20.0 %collective-permute-start.22 = (bf16[2,512,256]{2,1,0:T(8,128)(2,1)S(1)}, bf16[2,512,256]{2,1,0:T(8,128)(2,1)S(1)}, u32[]{:S(2)}, u32[]{:S(2)}) collective-permute-start(bf16[2,512,256]{2,1,0:T(8,128)(2,1)S(1)} %get-tuple-element.64.refs_4_), channel_id=1, source_target_pairs={{0,2},{1,3},{2,0},{3,1},{4,6},{5,7},{6,4},{7,5},{8,10},{9,11},{10,... | collective-permute-start | bytes 1572872 | tf_op jit(solution)/shard_map/ppermute | solution.py:26
  61.3 37.7 %collective-permute-start.18 = (bf16[1,4,128,256]{3,2,1,0:T(8,128)(2,1)S(1)}, bf16[1,4,128,256]{3,2,1,0:T(8,128)(2,1)S(1)}, u32[]{:S(2)}, u32[]{:S(2)}) collective-permute-start(bf16[1,4,128,256]{3,2,1,0:T(8,128)(2,1)S(1)} %get-tuple-element.76), channel_id=1, source_target_pairs={{0,16},{4,20},{8,24},{12,28},{16,0},{20,4},{24,8},{28,12},{1,17},{... | collective-permute-start | bytes 786440 | tf_op jit(solution)/shard_map/ppermute | solution.py:26
  63.5 14.5 %collective-permute-start.20 = (bf16[2,4,128,256]{3,2,1,0:T(8,128)(2,1)S(1)}, bf16[2,4,128,256]{3,2,1,0:T(8,128)(2,1)S(1)}, u32[]{:S(2)}, u32[]{:S(2)}) collective-permute-start(bf16[2,4,128,256]{3,2,1,0:T(8,128)(2,1)S(1)} %shard_map.85), channel_id=1, source_target_pairs={{0,4},{4,0},{8,12},{12,8},{16,20},{20,16},{24,28},{28,24},{1,5},{5... | collective-permute-start | bytes 1572872 | tf_op jit(solution)/shard_map/ppermute | solution.py:26
  72.8 16.3 %collective-permute-start.23 = (bf16[2,4,128,256]{3,2,1,0:T(8,128)(2,1)S(1)}, bf16[2,4,128,256]{3,2,1,0:T(8,128)(2,1)S(1)}, u32[]{:S(2)}, u32[]{:S(2)}) collective-permute-start(bf16[2,4,128,256]{3,2,1,0:T(8,128)(2,1)S(1)} %shard_map.88), channel_id=1, source_target_pairs={{0,4},{4,0},{8,12},{12,8},{16,20},{20,16},{24,28},{28,24},{1,5},{5... | collective-permute-start | bytes 1572872 | tf_op jit(solution)/shard_map/ppermute | solution.py:26
  74.4 22.7 %collective-permute-start.17 = (bf16[1,4,128,128]{3,2,1,0:T(8,128)(2,1)S(1)}, bf16[1,4,128,128]{3,2,1,0:T(8,128)(2,1)S(1)}, u32[]{:S(2)}, u32[]{:S(2)}) collective-permute-start(bf16[1,4,128,128]{3,2,1,0:T(8,128)(2,1)S(1)} %get-tuple-element.85), channel_id=1, source_target_pairs={{0,4},{4,0},{8,12},{12,8},{16,20},{20,16},{24,28},{28,24},{1,5},{5... | collective-permute-start | bytes 393224 | tf_op jit(solution)/shard_map/ppermute | solution.py:26
  75.8 19.7 %collective-permute-start.25 = (bf16[2,4,128,128]{3,2,1,0:T(8,128)(2,1)S(1)}, bf16[2,4,128,128]{3,2,1,0:T(8,128)(2,1)S(1)}, u32[]{:S(2)}, u32[]{:S(2)}) collective-permute-start(bf16[2,4,128,128]{3,2,1,0:T(8,128)(2,1)S(1)} %shard_map.91), channel_id=1, source_target_pairs={{0,4},{4,0},{8,12},{12,8},{16,20},{20,16},{24,28},{28,24},{1,5},{5... | collective-permute-start | bytes 786440 | tf_op jit(solution)/shard_map/ppermute | solution.py:26
  78.2 22.8 %collective-permute-start.21 = (bf16[1,4,128,256]{3,2,1,0:T(8,128)(2,1)S(1)}, bf16[1,4,128,256]{3,2,1,0:T(8,128)(2,1)S(1)}, u32[]{:S(2)}, u32[]{:S(2)}) collective-permute-start(bf16[1,4,128,256]{3,2,1,0:T(8,128)(2,1)S(1)} %get-tuple-element.71), channel_id=1, source_target_pairs={{0,16},{4,20},{8,24},{12,28},{16,0},{20,4},{24,8},{28,12},{1,17},{... | collective-permute-start | bytes 786440 | tf_op jit(solution)/shard_map/ppermute | solution.py:26
  89.2 15.9 %collective-permute-start.24 = (bf16[1,4,128,256]{3,2,1,0:T(8,128)(2,1)S(1)}, bf16[1,4,128,256]{3,2,1,0:T(8,128)(2,1)S(1)}, u32[]{:S(2)}, u32[]{:S(2)}) collective-permute-start(bf16[1,4,128,256]{3,2,1,0:T(8,128)(2,1)S(1)} %get-tuple-element.69), channel_id=1, source_target_pairs={{0,16},{4,20},{8,24},{12,28},{16,0},{20,4},{24,8},{28,12},{1,17},{... | collective-permute-start | bytes 786440 | tf_op jit(solution)/shard_map/ppermute | solution.py:26
  95.6 11.8 %collective-permute-start.26 = (bf16[1,4,128,128]{3,2,1,0:T(8,128)(2,1)S(1)}, bf16[1,4,128,128]{3,2,1,0:T(8,128)(2,1)S(1)}, u32[]{:S(2)}, u32[]{:S(2)}) collective-permute-start(bf16[1,4,128,128]{3,2,1,0:T(8,128)(2,1)S(1)} %get-tuple-element.80), channel_id=1, source_target_pairs={{0,16},{4,20},{8,24},{12,28},{16,0},{20,4},{24,8},{28,12},{1,17},{... | collective-permute-start | bytes 393224 | tf_op jit(solution)/shard_map/ppermute | solution.py:26
  (1 other events, 2.2 us)

commit v16 on v13

--- a/solution.py
+++ b/solution.py
@@ -126,15 +126,11 @@
     names = lax.broadcasted_iota(jnp.int32, (vocab, rows), 0)
     lane_group = lax.broadcasted_iota(jnp.int32, (tok_len, 2 * LANES), 1) % LANES // GROUP
 
-    def look_up(one_hot, table):
-        found = lax.dot_general(one_hot, table, (((0,), (0,)), ((), ())), preferred_element_type=jnp.float32)
-        return found.astype(jnp.bfloat16).astype(jnp.float32)
-
     for v in range(2):
-        one_hot = (names == ids_ref[v]).astype(jnp.float32).astype(jnp.bfloat16)
-        held[v, 0] = look_up(one_hot, table_ref[1])
-        held[v, 1] = look_up(one_hot, table_ref[2])
-        held_query[v] = look_up(one_hot[:, rows - lead - tok_len :], table_ref[0])
+        one_hot = (names == ids_ref[v]).astype(jnp.float32).T.astype(jnp.bfloat16)
+        held[v, 0] = jnp.dot(one_hot, table_ref[1], preferred_element_type=jnp.float32)
+        held[v, 1] = jnp.dot(one_hot, table_ref[2], preferred_element_type=jnp.float32)
+        held_query[v] = jnp.dot(one_hot[rows - lead - tok_len :], table_ref[0], preferred_element_type=jnp.float32)
 
     def featured(source, i, count, cols):
         total = short_ref[0, i : i + 1, cols] * source[pl.ds(lead, count), cols]

time: 110 us -> 109 us (level)
  no operation moved by 1% of the time
where the time goes in v16:
time: 109 us
  Pallas kernels  40.4 us (37%)
  starting transfers between devices  34.2 us (31%)
  waiting for transfers between devices  30.4 us (28%)
  local copies, waits for them, and re-layouts  2.66 us (2%)
  other arithmetic  1.09 us (1%)
    ppermute x25, starting transfers between devices, swap(): return lax.ppermute(x, axis, [(i, i ^ mask) for i in range(peers)])  32.6 us
    ppermute x25, waiting for transfers between devices, swap(): return lax.ppermute(x, axis, [(i, i ^ mask) for i in range(peers)])  30.3 us
    pallas_call x5, Pallas kernels, place_pieces(): pl.pallas_call(functools.partial(place_kernel, split, step), grid_spec=pl...  9.81 us
    pallas_call x1, Pallas kernels, project(): pl.pallas_call(table_kernel, grid=(1,), in_specs=[hbm, hbm, pl.BlockSpec(...  9.69 us
    pallas_call x2, Pallas kernels, mix(): pl.pallas_call(mixer_kernel, grid=(windows // 2,), in_specs=[pl.BlockSpec...  8.23 us
    pallas_call x9, Pallas kernels, panel(): pl.pallas_call(panel_kernel, grid_spec=pltpu.PrefetchScalarGridSpec(num_s...  7.18 us
    pallas_call x1, Pallas kernels, residual(): pl.pallas_call(residual_kernel, grid=(4,), in_specs=[whole(token_ids), pl...  2.65 us
    pallas_call x1, Pallas kernels, cut_pieces(): pl.pallas_call(cut_kernel, grid_spec=pltpu.PrefetchScalarGridSpec(num_sca...  2.23 us
  transfers between devices with their start and end apart: 27, of which 10 were waited for; matrix products, arithmetic and copies ran while one was open for 1% of the time, Pallas kernels for 35%

profile of v16, /device:TPU:0, one launch (start us, length us, event | category | flops | bytes accessed | tf_op | source)
XLA Modules:
  0.0 109.1 jit_solution(6645162928279019023)
XLA Ops:
  0.0 5.0 %collective-permute-start.2 = (s32[1,128]{1,0:T(1,128)}, s32[1,128]{1,0:T(1,128)S(1)}, u32[]{:S(2)}, u32[]{:S(2)}) collective-permute-start(s32[1,128]{1,0:T(1,128)} %ids_ref), channel_id=1, source_target_pairs={{0,24},{4,28},{8,16},{12,20},{16,8},{20,12},{24,0},{28,4},{1,25},{... | collective-permute-start | bytes 1544 | tf_op jit(solution)/shard_map/ppermute | solution.py:26
  5.6 2.2 %shard_map.73 = (bf16[512,512]{1,0:T(8,128)(2,1)}, bf16[512,512]{1,0:T(8,128)(2,1)}) custom-call(s32[1]{0:T(128)} %bitcast.place_ref, bf16[512,4096]{1,0:T(8,128)(2,1)} %refs_3_.17, bf16[512,4096]{1,0:T(8,128)(2,1)} %refs_3_.17), custom_call_target="tpu_custom_call" | custom-call | bytes 2000000 | tf_op jit(solution)/shard_map/pallas_call | solution.py:196
  9.6 1.6 %collective-permute-start.3 = (s32[4,128]{1,0:T(4,128)S(1)}, s32[4,128]{1,0:T(4,128)S(1)}, u32[]{:S(2)}, u32[]{:S(2)}) collective-permute-start(s32[4,128]{1,0:T(4,128)S(1)} %pad_add_fusion.4), channel_id=1, source_target_pairs={{0,4},{4,0},{8,12},{12,8},{16,20},{20,16},{24,28},{28,24},{1,5},{5... | collective-permute-start | bytes 6152 | tf_op jit(solution)/shard_map/ppermute | solution.py:26
  11.2 2.0 %collective-permute-start.6 = (bf16[512,512]{1,0:T(8,128)(2,1)}, bf16[512,512]{1,0:T(8,128)(2,1)S(1)}, u32[]{:S(2)}, u32[]{:S(2)}) collective-permute-start(bf16[512,512]{1,0:T(8,128)(2,1)} %get-tuple-element.44), channel_id=1, source_target_pairs={{0,8},{4,12},{8,0},{12,4},{16,24},{20,28},{24,16},{28,20},{1,9},{5... | collective-permute-start | bytes 1572872 | tf_op jit(solution)/shard_map/ppermute | solution.py:26
  13.3 1.6 %collective-permute-start.7 = (s32[8,128]{1,0:T(8,128)S(1)}, s32[8,128]{1,0:T(8,128)S(1)}, u32[]{:S(2)}, u32[]{:S(2)}) collective-permute-start(s32[8,128]{1,0:T(8,128)S(1)} %pad_add_fusion.2), channel_id=1, source_target_pairs={{0,2},{1,3},{2,0},{3,1},{4,6},{5,7},{6,4},{7,5},{8,10},{9,11},{10,... | collective-permute-start | bytes 12296 | tf_op jit(solution)/shard_map/ppermute | solution.py:21
  14.9 2.0 %collective-permute-start.4 = (bf16[512,512]{1,0:T(8,128)(2,1)}, bf16[512,512]{1,0:T(8,128)(2,1)S(1)}, u32[]{:S(2)}, u32[]{:S(2)}) collective-permute-start(bf16[512,512]{1,0:T(8,128)(2,1)} %get-tuple-element.42), channel_id=1, source_target_pairs={{0,8},{4,12},{8,0},{12,4},{16,24},{20,28},{24,16},{28,20},{1,9},{5... | collective-permute-start | bytes 1572872 | tf_op jit(solution)/shard_map/ppermute | solution.py:26
  16.9 2.2 %copy-done.1 = bf16[512,4096]{1,0:T(8,128)(2,1)S(1)} copy-done((bf16[512,4096]{1,0:T(8,128)(2,1)S(1)}, bf16[512,4096]{1,0:T(8,128)(2,1)}, u32[]{:S(2)}) %copy-start.1) | copy-done | bytes 4194328
  19.1 9.7 %shard_map.75.table_ref = bf16[3,512,512]{2,1,0:T(8,128)(2,1)S(1)} custom-call(bf16[512,4096]{1,0:T(8,128)(2,1)S(1)} %copy-done.1, bf16[3,4096,512]{2,1,0:T(8,128)(2,1)} %weight_hbm, f32[1,4096]{1,0:T(1,128)S(1)} %bitcast.46), custom_call_target="tpu_custom_call" | custom-call | flops 3000000000 | tf_op jit(solution)/shard_map/pallas_call | solution.py:101
  29.7 2.0 %shard_map.76 = bf16[2,128,512]{2,1,0:T(8,128)(2,1)S(1)} custom-call(s32[2,1,272]{2,1,0:T(1,128)S(1)} %copy.13.ids_ref, bf16[3,512,512]{2,1,0:T(8,128)(2,1)S(1)} %shard_map.75.table_ref, f32[3,3,512]{2,1,0:T(4,128)S(1)} %copy-done.4, bf16[4,1024,256]{2,1,0:T(8,128)(2,1)S(1)} %shard_map.74.toeplitz), custom_call_target="tpu_custom_call" | custom-call | flops 1500000000 | tf_op jit(solution)/shard_map/pallas_call | solution.py:163
  32.1 1.4 %collective-permute-start.9 = (bf16[512,256]{1,0:T(8,128)(2,1)S(1)}, bf16[512,256]{1,0:T(8,128)(2,1)S(1)}, u32[]{:S(2)}, u32[]{:S(2)}) collective-permute-start(bf16[512,256]{1,0:T(8,128)(2,1)S(1)} %get-tuple-element.50), channel_id=1, source_target_pairs={{0,2},{1,3},{2,0},{3,1},{4,6},{5,7},{6,4},{7,5},{8,10},{9,11},{10,... | collective-permute-start | bytes 786440 | tf_op jit(solution)/shard_map/ppermute | solution.py:26
  33.4 6.2 %shard_map.77 = bf16[6,128,512]{2,1,0:T(8,128)(2,1)S(1)} custom-call(s32[6,1,272]{2,1,0:T(1,128)S(1)} %reshape.54.ids_ref, bf16[3,512,512]{2,1,0:T(8,128)(2,1)S(1)} %shard_map.75.table_ref, f32[3,3,512]{2,1,0:T(4,128)S(1)} %copy-done.4, bf16[4,1024,256]{2,1,0:T(8,128)(2,1)S(1)} %shard_map.74.toeplitz), custom_call_target="tpu_custom_call" | custom-call | flops 1500000000 | tf_op jit(solution)/shard_map/pallas_call | solution.py:163
  39.9 2.0 %collective-permute-start.11 = (bf16[2,128,512]{2,1,0:T(8,128)(2,1)S(1)}, bf16[2,128,512]{2,1,0:T(8,128)(2,1)S(1)}, u32[]{:S(2)}, u32[]{:S(2)}) collective-permute-start(bf16[2,128,512]{2,1,0:T(8,128)(2,1)S(1)} %get-tuple-element.79), channel_id=1, source_target_pairs={{0,8},{4,12},{8,0},{12,4},{16,24},{20,28},{24,16},{28,20},{1,9},{5... | collective-permute-start | bytes 786440 | tf_op jit(solution)/shard_map/ppermute | solution.py:26
  42.1 2.6 %shard_map.78.so_far_ref = bf16[128,4096]{1,0:T(8,128)(2,1)} custom-call(s32[1,128]{1,0:T(1,128)S(1)} %copy-done.3, bf16[512,4096]{1,0:T(8,128)(2,1)S(1)} %copy-done.1), custom_call_target="tpu_custom_call" | custom-call | flops 400000000 | tf_op jit(solution)/shard_map/pallas_call | solution.py:286
  46.8 1.6 %collective-permute-start.16 = (bf16[2,4,128,256]{3,2,1,0:T(8,128)(2,1)S(1)}, bf16[2,4,128,256]{3,2,1,0:T(8,128)(2,1)S(1)}, u32[]{:S(2)}, u32[]{:S(2)}) collective-permute-start(bf16[2,4,128,256]{3,2,1,0:T(8,128)(2,1)S(1)} %shard_map.79), channel_id=1, source_target_pairs={{0,4},{4,0},{8,12},{12,8},{16,20},{20,16},{24,28},{28,24},{1,5},{5... | collective-permute-start | bytes 1572872 | tf_op jit(solution)/shard_map/ppermute | solution.py:26
  51.4 1.5 %collective-permute-start.15 = (bf16[2,1,4,128,128]{4,3,2,1,0:T(8,128)(2,1)S(1)}, bf16[2,1,4,128,128]{4,3,2,1,0:T(8,128)(2,1)S(1)}, u32[]{:S(2)}, u32[]{:S(2)}) collective-permute-start(bf16[2,1,4,128,128]{4,3,2,1,0:T(8,128)(2,1)S(1)} %slice.129), channel_id=1, source_target_pairs={{0,16},{4,20},{8,24},{12,28},{16,0},{20,4},{24,8},{28,12},{1,17},{... | collective-permute-start | bytes 786440 | tf_op jit(solution)/shard_map/ppermute | solution.py:26
  54.4 5.8 %collective-permute-done.19.refs_5_ = bf16[2,512,256]{2,1,0:T(8,128)(2,1)S(1)} collective-permute-done((bf16[2,512,256]{2,1,0:T(8,128)(2,1)S(1)}, bf16[2,512,256]{2,1,0:T(8,128)(2,1)S(1)}, u32[]{:S(2)}, u32[]{:S(2)}) %collective-permute-start.19) | collective-permute-done | bytes 524320 | tf_op jit(solution)/shard_map/ppermute | solution.py:26
  61.1 1.5 %collective-permute-start.18 = (bf16[1,4,128,256]{3,2,1,0:T(8,128)(2,1)S(1)}, bf16[1,4,128,256]{3,2,1,0:T(8,128)(2,1)S(1)}, u32[]{:S(2)}, u32[]{:S(2)}) collective-permute-start(bf16[1,4,128,256]{3,2,1,0:T(8,128)(2,1)S(1)} %get-tuple-element.76), channel_id=1, source_target_pairs={{0,16},{4,20},{8,24},{12,28},{16,0},{20,4},{24,8},{28,12},{1,17},{... | collective-permute-start | bytes 786440 | tf_op jit(solution)/shard_map/ppermute | solution.py:26
  63.3 1.6 %collective-permute-start.20 = (bf16[2,4,128,256]{3,2,1,0:T(8,128)(2,1)S(1)}, bf16[2,4,128,256]{3,2,1,0:T(8,128)(2,1)S(1)}, u32[]{:S(2)}, u32[]{:S(2)}) collective-permute-start(bf16[2,4,128,256]{3,2,1,0:T(8,128)(2,1)S(1)} %shard_map.85), channel_id=1, source_target_pairs={{0,4},{4,0},{8,12},{12,8},{16,20},{20,16},{24,28},{28,24},{1,5},{5... | collective-permute-start | bytes 1572872 | tf_op jit(solution)/shard_map/ppermute | solution.py:26
  64.9 5.8 %collective-permute-done.22.refs_5_ = bf16[2,512,256]{2,1,0:T(8,128)(2,1)S(1)} collective-permute-done((bf16[2,512,256]{2,1,0:T(8,128)(2,1)S(1)}, bf16[2,512,256]{2,1,0:T(8,128)(2,1)S(1)}, u32[]{:S(2)}, u32[]{:S(2)}) %collective-permute-start.22) | collective-permute-done | bytes 524320 | tf_op jit(solution)/shard_map/ppermute | solution.py:26
  71.4 1.6 %collective-permute-start.23 = (bf16[2,4,128,256]{3,2,1,0:T(8,128)(2,1)S(1)}, bf16[2,4,128,256]{3,2,1,0:T(8,128)(2,1)S(1)}, u32[]{:S(2)}, u32[]{:S(2)}) collective-permute-start(bf16[2,4,128,256]{3,2,1,0:T(8,128)(2,1)S(1)} %shard_map.88), channel_id=1, source_target_pairs={{0,4},{4,0},{8,12},{12,8},{16,20},{20,16},{24,28},{28,24},{1,5},{5... | collective-permute-start | bytes 1572872 | tf_op jit(solution)/shard_map/ppermute | solution.py:26
  75.2 1.6 %collective-permute-start.17 = (bf16[1,4,128,128]{3,2,1,0:T(8,128)(2,1)S(1)}, bf16[1,4,128,128]{3,2,1,0:T(8,128)(2,1)S(1)}, u32[]{:S(2)}, u32[]{:S(2)}) collective-permute-start(bf16[1,4,128,128]{3,2,1,0:T(8,128)(2,1)S(1)} %get-tuple-element.85), channel_id=1, source_target_pairs={{0,4},{4,0},{8,12},{12,8},{16,20},{20,16},{24,28},{28,24},{1,5},{5... | collective-permute-start | bytes 393224 | tf_op jit(solution)/shard_map/ppermute | solution.py:26
  77.7 1.7 %collective-permute-start.21 = (bf16[1,4,128,256]{3,2,1,0:T(8,128)(2,1)S(1)}, bf16[1,4,128,256]{3,2,1,0:T(8,128)(2,1)S(1)}, u32[]{:S(2)}, u32[]{:S(2)}) collective-permute-start(bf16[1,4,128,256]{3,2,1,0:T(8,128)(2,1)S(1)} %get-tuple-element.71), channel_id=1, source_target_pairs={{0,16},{4,20},{8,24},{12,28},{16,0},{20,4},{24,8},{28,12},{1,17},{... | collective-permute-start | bytes 786440 | tf_op jit(solution)/shard_map/ppermute | solution.py:26
  79.4 9.4 %collective-permute-done.23 = bf16[2,4,128,256]{3,2,1,0:T(8,128)(2,1)S(1)} collective-permute-done((bf16[2,4,128,256]{3,2,1,0:T(8,128)(2,1)S(1)}, bf16[2,4,128,256]{3,2,1,0:T(8,128)(2,1)S(1)}, u32[]{:S(2)}, u32[]{:S(2)}) %collective-permute-start.23) | collective-permute-done | bytes 524320 | tf_op jit(solution)/shard_map/ppermute | solution.py:26
  88.9 1.7 %collective-permute-start.24 = (bf16[1,4,128,256]{3,2,1,0:T(8,128)(2,1)S(1)}, bf16[1,4,128,256]{3,2,1,0:T(8,128)(2,1)S(1)}, u32[]{:S(2)}, u32[]{:S(2)}) collective-permute-start(bf16[1,4,128,256]{3,2,1,0:T(8,128)(2,1)S(1)} %get-tuple-element.69), channel_id=1, source_target_pairs={{0,16},{4,20},{8,24},{12,28},{16,0},{20,4},{24,8},{28,12},{1,17},{... | collective-permute-start | bytes 786440 | tf_op jit(solution)/shard_map/ppermute | solution.py:26
  90.6 3.2 %collective-permute-done.25 = bf16[2,4,128,128]{3,2,1,0:T(8,128)(2,1)S(1)} collective-permute-done((bf16[2,4,128,128]{3,2,1,0:T(8,128)(2,1)S(1)}, bf16[2,4,128,128]{3,2,1,0:T(8,128)(2,1)S(1)}, u32[]{:S(2)}, u32[]{:S(2)}) %collective-permute-start.25) | collective-permute-done | bytes 262176 | tf_op jit(solution)/shard_map/ppermute | solution.py:26
  93.9 1.6 %collective-permute-start.26 = (bf16[1,4,128,128]{3,2,1,0:T(8,128)(2,1)S(1)}, bf16[1,4,128,128]{3,2,1,0:T(8,128)(2,1)S(1)}, u32[]{:S(2)}, u32[]{:S(2)}) collective-permute-start(bf16[1,4,128,128]{3,2,1,0:T(8,128)(2,1)S(1)} %get-tuple-element.80), channel_id=1, source_target_pairs={{0,16},{4,20},{8,24},{12,28},{16,0},{20,4},{24,8},{28,12},{1,17},{... | collective-permute-start | bytes 393224 | tf_op jit(solution)/shard_map/ppermute | solution.py:26
  95.5 1.9 %shard_map.82.so_far_ref = bf16[128,4096]{1,0:T(8,128)(2,1)} custom-call(s32[1]{0:T(128)} %bitcast.place_ref, bf16[128,4096]{1,0:T(8,128)(2,1)} %shard_map.78.so_far_ref, bf16[1,4,128,128]{3,2,1,0:T(8,128)(2,1)S(1)} %get-tuple-element.86.near_ref, bf16[1,4,128,128]{3,2,1,0:T(8,128)(2,1)S(1)} %collective-permute-done.17.far_ref), custom_call_target="tpu_custom_call", output_to_operand_aliasing={{}: (1, {})} | custom-call | bytes 1000000 | tf_op jit(solution)/shard_map/pallas_call | solution.py:314
  97.4 2.0 %shard_map.83.so_far_ref = bf16[128,4096]{1,0:T(8,128)(2,1)} custom-call(s32[1]{0:T(128)} %bitcast.place_ref, bf16[128,4096]{1,0:T(8,128)(2,1)} %shard_map.82.so_far_ref, bf16[1,4,128,256]{3,2,1,0:T(8,128)(2,1)S(1)} %get-tuple-element.75.near_ref, bf16[1,4,128,256]{3,2,1,0:T(8,128)(2,1)S(1)} %collective-permute-done.18.far_ref), custom_call_target="tpu_custom_call", output_to_operand_aliasing={{}: (1, {})} | custom-call | bytes 1000000 | tf_op jit(solution)/shard_map/pallas_call | solution.py:314
  99.4 2.0 %shard_map.86.so_far_ref = bf16[128,4096]{1,0:T(8,128)(2,1)} custom-call(s32[1]{0:T(128)} %bitcast.place_ref, bf16[128,4096]{1,0:T(8,128)(2,1)} %shard_map.83.so_far_ref, bf16[1,4,128,256]{3,2,1,0:T(8,128)(2,1)S(1)} %get-tuple-element.72.near_ref, bf16[1,4,128,256]{3,2,1,0:T(8,128)(2,1)S(1)} %collective-permute-done.21.far_ref), custom_call_target="tpu_custom_call", output_to_operand_aliasing={{}: (1, {})} | custom-call | bytes 1000000 | tf_op jit(solution)/shard_map/pallas_call | solution.py:314
  101.4 3.4 %collective-permute-done.24.far_ref = bf16[1,4,128,256]{3,2,1,0:T(8,128)(2,1)S(1)} collective-permute-done((bf16[1,4,128,256]{3,2,1,0:T(8,128)(2,1)S(1)}, bf16[1,4,128,256]{3,2,1,0:T(8,128)(2,1)S(1)}, u32[]{:S(2)}, u32[]{:S(2)}) %collective-permute-start.24) | collective-permute-done | bytes 262176 | tf_op jit(solution)/shard_map/ppermute | solution.py:26
  104.8 2.0 %shard_map.89.so_far_ref = bf16[128,4096]{1,0:T(8,128)(2,1)} custom-call(s32[1]{0:T(128)} %bitcast.place_ref, bf16[128,4096]{1,0:T(8,128)(2,1)} %shard_map.86.so_far_ref, bf16[1,4,128,256]{3,2,1,0:T(8,128)(2,1)S(1)} %get-tuple-element.70.near_ref, bf16[1,4,128,256]{3,2,1,0:T(8,128)(2,1)S(1)} %collective-permute-done.24.far_ref), custom_call_target="tpu_custom_call", output_to_operand_aliasing={{}: (1, {})} | custom-call | bytes 1000000 | tf_op jit(solution)/shard_map/pallas_call | solution.py:314
  107.1 1.9 %shard_map.92 = bf16[128,4096]{1,0:T(8,128)(2,1)} custom-call(s32[1]{0:T(128)} %bitcast.place_ref, bf16[128,4096]{1,0:T(8,128)(2,1)} %shard_map.89.so_far_ref, bf16[1,4,128,128]{3,2,1,0:T(8,128)(2,1)S(1)} %get-tuple-element.81.near_ref, bf16[1,4,128,128]{3,2,1,0:T(8,128)(2,1)S(1)} %collective-permute-done.26.far_ref), custom_call_target="tpu_custom_call", output_to_operand_aliasing={{}: (1, {})} | custom-call | bytes 1000000 | tf_op jit(solution)/shard_map/pallas_call | solution.py:314
  (82 shorter events, 16.4 us)
Async XLA Ops:
  0.0 8.6 %collective-permute-start.2 = (s32[1,128]{1,0:T(1,128)}, s32[1,128]{1,0:T(1,128)S(1)}, u32[]{:S(2)}, u32[]{:S(2)}) collective-permute-start(s32[1,128]{1,0:T(1,128)} %ids_ref), channel_id=1, source_target_pairs={{0,24},{4,28},{8,16},{12,20},{16,8},{20,12},{24,0},{28,4},{1,25},{... | collective-permute-start | bytes 1544 | tf_op jit(solution)/shard_map/ppermute | solution.py:26
  5.0 3.7 %collective-permute-start.1 = (s32[1,128]{1,0:T(1,128)}, s32[1,128]{1,0:T(1,128)S(1)}, u32[]{:S(2)}, u32[]{:S(2)}) collective-permute-start(s32[1,128]{1,0:T(1,128)} %ids_ref), channel_id=1, source_target_pairs={{0,8},{4,12},{8,0},{12,4},{16,24},{20,28},{24,16},{28,20},{1,9},{5... | collective-permute-start | bytes 1544 | tf_op jit(solution)/shard_map/ppermute | solution.py:26
  5.1 4.6 %collective-permute-start = (s32[1,128]{1,0:T(1,128)}, s32[1,128]{1,0:T(1,128)S(1)}, u32[]{:S(2)}, u32[]{:S(2)}) collective-permute-start(s32[1,128]{1,0:T(1,128)} %ids_ref), channel_id=1, source_target_pairs={{0,16},{4,20},{8,24},{12,28},{16,0},{20,4},{24,8},{28,12},{1,17},{... | collective-permute-start | bytes 1544 | tf_op jit(solution)/shard_map/ppermute | solution.py:26
  5.6 2.2 %copy-start.5 = (bf16[32,128]{1,0:T(8,128)(2,1)S(1)}, bf16[32,128]{1,0:T(8,128)(2,1)}, u32[]{:S(2)}) copy-start(bf16[32,128]{1,0:T(8,128)(2,1)} %param.12) | copy-start | bytes 24580
  5.6 4.0 %copy-start.3 = (s32[1,128]{1,0:T(1,128)S(1)}, s32[1,128]{1,0:T(1,128)}, u32[]{:S(2)}) copy-start(s32[1,128]{1,0:T(1,128)} %ids_ref) | copy-start | bytes 1540
  5.6 11.3 %copy-start.2 = (f32[4096]{0:T(1024)S(1)}, f32[4096]{0:T(1024)}, u32[]{:S(2)}) copy-start(f32[4096]{0:T(1024)} %param.9) | copy-start | bytes 49156
  9.6 3.7 %collective-permute-start.3 = (s32[4,128]{1,0:T(4,128)S(1)}, s32[4,128]{1,0:T(4,128)S(1)}, u32[]{:S(2)}, u32[]{:S(2)}) collective-permute-start(s32[4,128]{1,0:T(4,128)S(1)} %pad_add_fusion.4), channel_id=1, source_target_pairs={{0,4},{4,0},{8,12},{12,8},{16,20},{20,16},{24,28},{28,24},{1,5},{5... | collective-permute-start | bytes 6152 | tf_op jit(solution)/shard_map/ppermute | solution.py:26
  11.2 17.9 %collective-permute-start.6 = (bf16[512,512]{1,0:T(8,128)(2,1)}, bf16[512,512]{1,0:T(8,128)(2,1)S(1)}, u32[]{:S(2)}, u32[]{:S(2)}) collective-permute-start(bf16[512,512]{1,0:T(8,128)(2,1)} %get-tuple-element.44), channel_id=1, source_target_pairs={{0,8},{4,12},{8,0},{12,4},{16,24},{20,28},{24,16},{28,20},{1,9},{5... | collective-permute-start | bytes 1572872 | tf_op jit(solution)/shard_map/ppermute | solution.py:26
  13.3 15.6 %collective-permute-start.8 = (s32[8,128]{1,0:T(8,128)S(1)}, s32[8,128]{1,0:T(8,128)S(1)}, u32[]{:S(2)}, u32[]{:S(2)}) collective-permute-start(s32[8,128]{1,0:T(8,128)S(1)} %pad_add_fusion.2), channel_id=1, source_target_pairs={{0,1},{1,2},{2,3},{3,0},{4,5},{5,6},{6,7},{7,4},{8,9},{9,10},{10,1... | collective-permute-start | bytes 12296 | tf_op jit(solution)/shard_map/ppermute | solution.py:21
  13.3 15.4 %collective-permute-start.7 = (s32[8,128]{1,0:T(8,128)S(1)}, s32[8,128]{1,0:T(8,128)S(1)}, u32[]{:S(2)}, u32[]{:S(2)}) collective-permute-start(s32[8,128]{1,0:T(8,128)S(1)} %pad_add_fusion.2), channel_id=1, source_target_pairs={{0,2},{1,3},{2,0},{3,1},{4,6},{5,7},{6,4},{7,5},{8,10},{9,11},{10,... | collective-permute-start | bytes 12296 | tf_op jit(solution)/shard_map/ppermute | solution.py:21
  14.9 24.8 %collective-permute-start.4 = (bf16[512,512]{1,0:T(8,128)(2,1)}, bf16[512,512]{1,0:T(8,128)(2,1)S(1)}, u32[]{:S(2)}, u32[]{:S(2)}) collective-permute-start(bf16[512,512]{1,0:T(8,128)(2,1)} %get-tuple-element.42), channel_id=1, source_target_pairs={{0,8},{4,12},{8,0},{12,4},{16,24},{20,28},{24,16},{28,20},{1,9},{5... | collective-permute-start | bytes 1572872 | tf_op jit(solution)/shard_map/ppermute | solution.py:26
  19.1 10.7 %copy-start.4 = (f32[3,3,512]{2,1,0:T(4,128)S(1)}, f32[3,3,512]{2,1,0:T(4,128)}, u32[]{:S(2)}) copy-start(f32[3,3,512]{2,1,0:T(4,128)} %short_ref.3) | copy-start | bytes 55300
  29.1 10.6 %collective-permute-start.10 = (bf16[512,256]{1,0:T(8,128)(2,1)S(1)}, bf16[512,256]{1,0:T(8,128)(2,1)S(1)}, u32[]{:S(2)}, u32[]{:S(2)}) collective-permute-start(bf16[512,256]{1,0:T(8,128)(2,1)S(1)} %get-tuple-element.83), channel_id=1, source_target_pairs={{0,2},{1,3},{2,0},{3,1},{4,6},{5,7},{6,4},{7,5},{8,10},{9,11},{10,... | collective-permute-start | bytes 786440 | tf_op jit(solution)/shard_map/ppermute | solution.py:26
  31.8 14.3 %collective-permute-start.12 = (bf16[2,128,512]{2,1,0:T(8,128)(2,1)S(1)}, bf16[2,128,512]{2,1,0:T(8,128)(2,1)S(1)}, u32[]{:S(2)}, u32[]{:S(2)}) collective-permute-start(bf16[2,128,512]{2,1,0:T(8,128)(2,1)S(1)} %shard_map.76), channel_id=1, source_target_pairs={{0,8},{4,12},{8,0},{12,4},{16,24},{20,28},{24,16},{28,20},{1,9},{5... | collective-permute-start | bytes 786440 | tf_op jit(solution)/shard_map/ppermute | solution.py:26
  32.1 12.7 %collective-permute-start.9 = (bf16[512,256]{1,0:T(8,128)(2,1)S(1)}, bf16[512,256]{1,0:T(8,128)(2,1)S(1)}, u32[]{:S(2)}, u32[]{:S(2)}) collective-permute-start(bf16[512,256]{1,0:T(8,128)(2,1)S(1)} %get-tuple-element.50), channel_id=1, source_target_pairs={{0,2},{1,3},{2,0},{3,1},{4,6},{5,7},{6,4},{7,5},{8,10},{9,11},{10,... | collective-permute-start | bytes 786440 | tf_op jit(solution)/shard_map/ppermute | solution.py:26
  39.7 5.2 %collective-permute-start.5 = (bf16[512,512]{1,0:T(8,128)(2,1)S(1)}, bf16[512,512]{1,0:T(8,128)(2,1)S(1)}, u32[]{:S(2)}, u32[]{:S(2)}) collective-permute-start(bf16[512,512]{1,0:T(8,128)(2,1)S(1)} %collective-permute-done.4), channel_id=1, source_target_pairs={{0,1},{1,0},{2,3},{3,2},{4,5},{5,4},{6,7},{7,6},{8,9},{9,8},{10,11... | collective-permute-start | bytes 1572872 | tf_op jit(solution)/shard_map/ppermute | solution.py:26
  39.9 6.2 %copy-start = (bf16[512,4096]{1,0:T(8,128)(2,1)S(1)}, bf16[512,4096]{1,0:T(8,128)(2,1)}, u32[]{:S(2)}) copy-start(bf16[512,4096]{1,0:T(8,128)(2,1)} %refs_3_.17) | copy-start | bytes 12582916
  39.9 9.0 %collective-permute-start.11 = (bf16[2,128,512]{2,1,0:T(8,128)(2,1)S(1)}, bf16[2,128,512]{2,1,0:T(8,128)(2,1)S(1)}, u32[]{:S(2)}, u32[]{:S(2)}) collective-permute-start(bf16[2,128,512]{2,1,0:T(8,128)(2,1)S(1)} %get-tuple-element.79), channel_id=1, source_target_pairs={{0,8},{4,12},{8,0},{12,4},{16,24},{20,28},{24,16},{28,20},{1,9},{5... | collective-permute-start | bytes 786440 | tf_op jit(solution)/shard_map/ppermute | solution.py:26
  41.9 4.2 %collective-permute-start.13 = (bf16[2,512,256]{2,1,0:T(8,128)(2,1)S(1)}, bf16[2,512,256]{2,1,0:T(8,128)(2,1)S(1)}, u32[]{:S(2)}, u32[]{:S(2)}) collective-permute-start(bf16[2,512,256]{2,1,0:T(8,128)(2,1)S(1)} %pad_maximum_fusion.2.refs_4_), channel_id=1, source_target_pairs={{0,1},{1,0},{2,3},{3,2},{4,5},{5,4},{6,7},{7,6},{8,9},{9,8},{10,11... | collective-permute-start | bytes 1572872 | tf_op jit(solution)/shard_map/ppermute | solution.py:26
  44.9 5.0 %collective-permute-start.14 = (bf16[2,512,256]{2,1,0:T(8,128)(2,1)S(1)}, bf16[2,512,256]{2,1,0:T(8,128)(2,1)S(1)}, u32[]{:S(2)}, u32[]{:S(2)}) collective-permute-start(bf16[2,512,256]{2,1,0:T(8,128)(2,1)S(1)} %pad_maximum_fusion.1.refs_4_), channel_id=1, source_target_pairs={{0,1},{1,0},{2,3},{3,2},{4,5},{5,4},{6,7},{7,6},{8,9},{9,8},{10,11... | collective-permute-start | bytes 1572872 | tf_op jit(solution)/shard_map/ppermute | solution.py:26
  45.4 14.8 %collective-permute-start.19 = (bf16[2,512,256]{2,1,0:T(8,128)(2,1)S(1)}, bf16[2,512,256]{2,1,0:T(8,128)(2,1)S(1)}, u32[]{:S(2)}, u32[]{:S(2)}) collective-permute-start(bf16[2,512,256]{2,1,0:T(8,128)(2,1)S(1)} %get-tuple-element.73.refs_4_), channel_id=1, source_target_pairs={{0,2},{1,3},{2,0},{3,1},{4,6},{5,7},{6,4},{7,5},{8,10},{9,11},{10,... | collective-permute-start | bytes 1572872 | tf_op jit(solution)/shard_map/ppermute | solution.py:26
  46.8 14.1 %collective-permute-start.16 = (bf16[2,4,128,256]{3,2,1,0:T(8,128)(2,1)S(1)}, bf16[2,4,128,256]{3,2,1,0:T(8,128)(2,1)S(1)}, u32[]{:S(2)}, u32[]{:S(2)}) collective-permute-start(bf16[2,4,128,256]{3,2,1,0:T(8,128)(2,1)S(1)} %shard_map.79), channel_id=1, source_target_pairs={{0,4},{4,0},{8,12},{12,8},{16,20},{20,16},{24,28},{28,24},{1,5},{5... | collective-permute-start | bytes 1572872 | tf_op jit(solution)/shard_map/ppermute | solution.py:26
  48.9 21.8 %collective-permute-start.22 = (bf16[2,512,256]{2,1,0:T(8,128)(2,1)S(1)}, bf16[2,512,256]{2,1,0:T(8,128)(2,1)S(1)}, u32[]{:S(2)}, u32[]{:S(2)}) collective-permute-start(bf16[2,512,256]{2,1,0:T(8,128)(2,1)S(1)} %get-tuple-element.64.refs_4_), channel_id=1, source_target_pairs={{0,2},{1,3},{2,0},{3,1},{4,6},{5,7},{6,4},{7,5},{8,10},{9,11},{10,... | collective-permute-start | bytes 1572872 | tf_op jit(solution)/shard_map/ppermute | solution.py:26
  51.4 23.7 %collective-permute-start.15 = (bf16[2,1,4,128,128]{4,3,2,1,0:T(8,128)(2,1)S(1)}, bf16[2,1,4,128,128]{4,3,2,1,0:T(8,128)(2,1)S(1)}, u32[]{:S(2)}, u32[]{:S(2)}) collective-permute-start(bf16[2,1,4,128,128]{4,3,2,1,0:T(8,128)(2,1)S(1)} %slice.129), channel_id=1, source_target_pairs={{0,16},{4,20},{8,24},{12,28},{16,0},{20,4},{24,8},{28,12},{1,17},{... | collective-permute-start | bytes 786440 | tf_op jit(solution)/shard_map/ppermute | solution.py:26
  61.1 36.3 %collective-permute-start.18 = (bf16[1,4,128,256]{3,2,1,0:T(8,128)(2,1)S(1)}, bf16[1,4,128,256]{3,2,1,0:T(8,128)(2,1)S(1)}, u32[]{:S(2)}, u32[]{:S(2)}) collective-permute-start(bf16[1,4,128,256]{3,2,1,0:T(8,128)(2,1)S(1)} %get-tuple-element.76), channel_id=1, source_target_pairs={{0,16},{4,20},{8,24},{12,28},{16,0},{20,4},{24,8},{28,12},{1,17},{... | collective-permute-start | bytes 786440 | tf_op jit(solution)/shard_map/ppermute | solution.py:26
  63.3 14.3 %collective-permute-start.20 = (bf16[2,4,128,256]{3,2,1,0:T(8,128)(2,1)S(1)}, bf16[2,4,128,256]{3,2,1,0:T(8,128)(2,1)S(1)}, u32[]{:S(2)}, u32[]{:S(2)}) collective-permute-start(bf16[2,4,128,256]{3,2,1,0:T(8,128)(2,1)S(1)} %shard_map.85), channel_id=1, source_target_pairs={{0,4},{4,0},{8,12},{12,8},{16,20},{20,16},{24,28},{28,24},{1,5},{5... | collective-permute-start | bytes 1572872 | tf_op jit(solution)/shard_map/ppermute | solution.py:26
  71.4 17.4 %collective-permute-start.23 = (bf16[2,4,128,256]{3,2,1,0:T(8,128)(2,1)S(1)}, bf16[2,4,128,256]{3,2,1,0:T(8,128)(2,1)S(1)}, u32[]{:S(2)}, u32[]{:S(2)}) collective-permute-start(bf16[2,4,128,256]{3,2,1,0:T(8,128)(2,1)S(1)} %shard_map.88), channel_id=1, source_target_pairs={{0,4},{4,0},{8,12},{12,8},{16,20},{20,16},{24,28},{28,24},{1,5},{5... | collective-permute-start | bytes 1572872 | tf_op jit(solution)/shard_map/ppermute | solution.py:26
  73.8 20.0 %collective-permute-start.25 = (bf16[2,4,128,128]{3,2,1,0:T(8,128)(2,1)S(1)}, bf16[2,4,128,128]{3,2,1,0:T(8,128)(2,1)S(1)}, u32[]{:S(2)}, u32[]{:S(2)}) collective-permute-start(bf16[2,4,128,128]{3,2,1,0:T(8,128)(2,1)S(1)} %shard_map.91), channel_id=1, source_target_pairs={{0,4},{4,0},{8,12},{12,8},{16,20},{20,16},{24,28},{28,24},{1,5},{5... | collective-permute-start | bytes 786440 | tf_op jit(solution)/shard_map/ppermute | solution.py:26
  75.2 20.2 %collective-permute-start.17 = (bf16[1,4,128,128]{3,2,1,0:T(8,128)(2,1)S(1)}, bf16[1,4,128,128]{3,2,1,0:T(8,128)(2,1)S(1)}, u32[]{:S(2)}, u32[]{:S(2)}) collective-permute-start(bf16[1,4,128,128]{3,2,1,0:T(8,128)(2,1)S(1)} %get-tuple-element.85), channel_id=1, source_target_pairs={{0,4},{4,0},{8,12},{12,8},{16,20},{20,16},{24,28},{28,24},{1,5},{5... | collective-permute-start | bytes 393224 | tf_op jit(solution)/shard_map/ppermute | solution.py:26
  77.7 21.7 %collective-permute-start.21 = (bf16[1,4,128,256]{3,2,1,0:T(8,128)(2,1)S(1)}, bf16[1,4,128,256]{3,2,1,0:T(8,128)(2,1)S(1)}, u32[]{:S(2)}, u32[]{:S(2)}) collective-permute-start(bf16[1,4,128,256]{3,2,1,0:T(8,128)(2,1)S(1)} %get-tuple-element.71), channel_id=1, source_target_pairs={{0,16},{4,20},{8,24},{12,28},{16,0},{20,4},{24,8},{28,12},{1,17},{... | collective-permute-start | bytes 786440 | tf_op jit(solution)/shard_map/ppermute | solution.py:26
  88.9 15.8 %collective-permute-start.24 = (bf16[1,4,128,256]{3,2,1,0:T(8,128)(2,1)S(1)}, bf16[1,4,128,256]{3,2,1,0:T(8,128)(2,1)S(1)}, u32[]{:S(2)}, u32[]{:S(2)}) collective-permute-start(bf16[1,4,128,256]{3,2,1,0:T(8,128)(2,1)S(1)} %get-tuple-element.69), channel_id=1, source_target_pairs={{0,16},{4,20},{8,24},{12,28},{16,0},{20,4},{24,8},{28,12},{1,17},{... | collective-permute-start | bytes 786440 | tf_op jit(solution)/shard_map/ppermute | solution.py:26
  93.9 13.2 %collective-permute-start.26 = (bf16[1,4,128,128]{3,2,1,0:T(8,128)(2,1)S(1)}, bf16[1,4,128,128]{3,2,1,0:T(8,128)(2,1)S(1)}, u32[]{:S(2)}, u32[]{:S(2)}) collective-permute-start(bf16[1,4,128,128]{3,2,1,0:T(8,128)(2,1)S(1)} %get-tuple-element.80), channel_id=1, source_target_pairs={{0,16},{4,20},{8,24},{12,28},{16,0},{20,4},{24,8},{28,12},{1,17},{... | collective-permute-start | bytes 393224 | tf_op jit(solution)/shard_map/ppermute | solution.py:26
  (1 other events, 2.2 us)

commit v17 on v16

--- a/solution.py
+++ b/solution.py
@@ -146,12 +146,10 @@
             value = featured(held.at[v, 1], 2, reach, cols)
             products.append((key * value).astype(jnp.bfloat16))
         both = jnp.concatenate(products, axis=1)
-        filtered = None
-        for k in range(per_tile):
-            one = jnp.dot(
-                toeplitz[tile, pl.ds(k * tok_len, tok_len), :], both, preferred_element_type=jnp.float32
-            )
-            filtered = one if k == 0 else jnp.where(lane_group == k, one, filtered)
+        stacked = jnp.dot(toeplitz[tile], both, preferred_element_type=jnp.float32)
+        filtered = stacked[:tok_len]
+        for k in range(1, per_tile):
+            filtered = jnp.where(lane_group == k, stacked[k * tok_len : (k + 1) * tok_len], filtered)
         for v in range(2):
             query = featured(held_query.at[v], 0, tok_len, cols)
             gated_ref[v, :, cols] = (query * filtered[:, v * LANES : (v + 1) * LANES]).astype(jnp.bfloat16)

time: 109 us -> 109 us (level)
  no operation moved by 1% of the time
where the time goes in v17:
time: 109 us; the launch traced here: 108 us
  Pallas kernels  39.4 us (36%)
  starting transfers between devices  34.3 us (31%)
  waiting for transfers between devices  30.3 us (28%)
  local copies, waits for them, and re-layouts  2.66 us (2%)
  other arithmetic  1.09 us (1%)
    ppermute x25, starting transfers between devices, swap(): return lax.ppermute(x, axis, [(i, i ^ mask) for i in range(peers)])  32.7 us
    ppermute x25, waiting for transfers between devices, swap(): return lax.ppermute(x, axis, [(i, i ^ mask) for i in range(peers)])  30.3 us
    pallas_call x5, Pallas kernels, place_pieces(): pl.pallas_call(functools.partial(place_kernel, split, step), grid_spec=pl...  9.81 us
    pallas_call x1, Pallas kernels, project(): pl.pallas_call(table_kernel, grid=(1,), in_specs=[hbm, hbm, pl.BlockSpec(...  9.69 us
    pallas_call x2, Pallas kernels, mix(): pl.pallas_call(mixer_kernel, grid=(windows // 2,), in_specs=[pl.BlockSpec...  7.28 us
    pallas_call x9, Pallas kernels, panel(): pl.pallas_call(panel_kernel, grid_spec=pltpu.PrefetchScalarGridSpec(num_s...  7.19 us
    pallas_call x1, Pallas kernels, residual(): pl.pallas_call(residual_kernel, grid=(4,), in_specs=[whole(token_ids), pl...  2.64 us
    pallas_call x1, Pallas kernels, cut_pieces(): pl.pallas_call(cut_kernel, grid_spec=pltpu.PrefetchScalarGridSpec(num_sca...  2.23 us
  transfers between devices with their start and end apart: 27, of which 10 were waited for; matrix products, arithmetic and copies ran while one was open for 1% of the time, Pallas kernels for 35%

profile of v17, /device:TPU:0, one launch (start us, length us, event | category | flops | bytes accessed | tf_op | source)
XLA Modules:
  0.0 108.1 jit_solution(7097582780191248542)
XLA Ops:
  0.0 5.0 %collective-permute-start.2 = (s32[1,128]{1,0:T(1,128)}, s32[1,128]{1,0:T(1,128)S(1)}, u32[]{:S(2)}, u32[]{:S(2)}) collective-permute-start(s32[1,128]{1,0:T(1,128)} %ids_ref), channel_id=1, source_target_pairs={{0,24},{4,28},{8,16},{12,20},{16,8},{20,12},{24,0},{28,4},{1,25},{... | collective-permute-start | bytes 1544 | tf_op jit(solution)/shard_map/ppermute | solution.py:26
  5.6 2.2 %shard_map.73 = (bf16[512,512]{1,0:T(8,128)(2,1)}, bf16[512,512]{1,0:T(8,128)(2,1)}) custom-call(s32[1]{0:T(128)} %bitcast.place_ref, bf16[512,4096]{1,0:T(8,128)(2,1)} %refs_3_.17, bf16[512,4096]{1,0:T(8,128)(2,1)} %refs_3_.17), custom_call_target="tpu_custom_call" | custom-call | bytes 2000000 | tf_op jit(solution)/shard_map/pallas_call | solution.py:194
  9.6 1.6 %collective-permute-start.3 = (s32[4,128]{1,0:T(4,128)S(1)}, s32[4,128]{1,0:T(4,128)S(1)}, u32[]{:S(2)}, u32[]{:S(2)}) collective-permute-start(s32[4,128]{1,0:T(4,128)S(1)} %pad_add_fusion.4), channel_id=1, source_target_pairs={{0,4},{4,0},{8,12},{12,8},{16,20},{20,16},{24,28},{28,24},{1,5},{5... | collective-permute-start | bytes 6152 | tf_op jit(solution)/shard_map/ppermute | solution.py:26
  11.2 2.0 %collective-permute-start.6 = (bf16[512,512]{1,0:T(8,128)(2,1)}, bf16[512,512]{1,0:T(8,128)(2,1)S(1)}, u32[]{:S(2)}, u32[]{:S(2)}) collective-permute-start(bf16[512,512]{1,0:T(8,128)(2,1)} %get-tuple-element.44), channel_id=1, source_target_pairs={{0,8},{4,12},{8,0},{12,4},{16,24},{20,28},{24,16},{28,20},{1,9},{5... | collective-permute-start | bytes 1572872 | tf_op jit(solution)/shard_map/ppermute | solution.py:26
  13.3 1.6 %collective-permute-start.7 = (s32[8,128]{1,0:T(8,128)S(1)}, s32[8,128]{1,0:T(8,128)S(1)}, u32[]{:S(2)}, u32[]{:S(2)}) collective-permute-start(s32[8,128]{1,0:T(8,128)S(1)} %pad_add_fusion.2), channel_id=1, source_target_pairs={{0,2},{1,3},{2,0},{3,1},{4,6},{5,7},{6,4},{7,5},{8,10},{9,11},{10,... | collective-permute-start | bytes 12296 | tf_op jit(solution)/shard_map/ppermute | solution.py:21
  14.9 2.0 %collective-permute-start.4 = (bf16[512,512]{1,0:T(8,128)(2,1)}, bf16[512,512]{1,0:T(8,128)(2,1)S(1)}, u32[]{:S(2)}, u32[]{:S(2)}) collective-permute-start(bf16[512,512]{1,0:T(8,128)(2,1)} %get-tuple-element.42), channel_id=1, source_target_pairs={{0,8},{4,12},{8,0},{12,4},{16,24},{20,28},{24,16},{28,20},{1,9},{5... | collective-permute-start | bytes 1572872 | tf_op jit(solution)/shard_map/ppermute | solution.py:26
  16.9 2.2 %copy-done.1 = bf16[512,4096]{1,0:T(8,128)(2,1)S(1)} copy-done((bf16[512,4096]{1,0:T(8,128)(2,1)S(1)}, bf16[512,4096]{1,0:T(8,128)(2,1)}, u32[]{:S(2)}) %copy-start.1) | copy-done | bytes 4194328
  19.1 9.7 %shard_map.75.table_ref = bf16[3,512,512]{2,1,0:T(8,128)(2,1)S(1)} custom-call(bf16[512,4096]{1,0:T(8,128)(2,1)S(1)} %copy-done.1, bf16[3,4096,512]{2,1,0:T(8,128)(2,1)} %weight_hbm, f32[1,4096]{1,0:T(1,128)S(1)} %bitcast.46), custom_call_target="tpu_custom_call" | custom-call | flops 3000000000 | tf_op jit(solution)/shard_map/pallas_call | solution.py:101
  29.7 1.8 %shard_map.76 = bf16[2,128,512]{2,1,0:T(8,128)(2,1)S(1)} custom-call(s32[2,1,272]{2,1,0:T(1,128)S(1)} %copy.13.ids_ref, bf16[3,512,512]{2,1,0:T(8,128)(2,1)S(1)} %shard_map.75.table_ref, f32[3,3,512]{2,1,0:T(4,128)S(1)} %copy-done.4, bf16[4,1024,256]{2,1,0:T(8,128)(2,1)S(1)} %shard_map.74.toeplitz), custom_call_target="tpu_custom_call" | custom-call | flops 1500000000 | tf_op jit(solution)/shard_map/pallas_call | solution.py:161
  31.8 1.4 %collective-permute-start.9 = (bf16[512,256]{1,0:T(8,128)(2,1)S(1)}, bf16[512,256]{1,0:T(8,128)(2,1)S(1)}, u32[]{:S(2)}, u32[]{:S(2)}) collective-permute-start(bf16[512,256]{1,0:T(8,128)(2,1)S(1)} %get-tuple-element.50), channel_id=1, source_target_pairs={{0,2},{1,3},{2,0},{3,1},{4,6},{5,7},{6,4},{7,5},{8,10},{9,11},{10,... | collective-permute-start | bytes 786440 | tf_op jit(solution)/shard_map/ppermute | solution.py:26
  33.2 5.5 %shard_map.77 = bf16[6,128,512]{2,1,0:T(8,128)(2,1)S(1)} custom-call(s32[6,1,272]{2,1,0:T(1,128)S(1)} %reshape.54.ids_ref, bf16[3,512,512]{2,1,0:T(8,128)(2,1)S(1)} %shard_map.75.table_ref, f32[3,3,512]{2,1,0:T(4,128)S(1)} %copy-done.4, bf16[4,1024,256]{2,1,0:T(8,128)(2,1)S(1)} %shard_map.74.toeplitz), custom_call_target="tpu_custom_call" | custom-call | flops 1500000000 | tf_op jit(solution)/shard_map/pallas_call | solution.py:161
  38.9 2.0 %collective-permute-start.11 = (bf16[2,128,512]{2,1,0:T(8,128)(2,1)S(1)}, bf16[2,128,512]{2,1,0:T(8,128)(2,1)S(1)}, u32[]{:S(2)}, u32[]{:S(2)}) collective-permute-start(bf16[2,128,512]{2,1,0:T(8,128)(2,1)S(1)} %get-tuple-element.79), channel_id=1, source_target_pairs={{0,8},{4,12},{8,0},{12,4},{16,24},{20,28},{24,16},{28,20},{1,9},{5... | collective-permute-start | bytes 786440 | tf_op jit(solution)/shard_map/ppermute | solution.py:26
  41.2 2.6 %shard_map.78.so_far_ref = bf16[128,4096]{1,0:T(8,128)(2,1)} custom-call(s32[1,128]{1,0:T(1,128)S(1)} %copy-done.3, bf16[512,4096]{1,0:T(8,128)(2,1)S(1)} %copy-done.1), custom_call_target="tpu_custom_call" | custom-call | flops 400000000 | tf_op jit(solution)/shard_map/pallas_call | solution.py:284
  45.9 1.6 %collective-permute-start.16 = (bf16[2,4,128,256]{3,2,1,0:T(8,128)(2,1)S(1)}, bf16[2,4,128,256]{3,2,1,0:T(8,128)(2,1)S(1)}, u32[]{:S(2)}, u32[]{:S(2)}) collective-permute-start(bf16[2,4,128,256]{3,2,1,0:T(8,128)(2,1)S(1)} %shard_map.79), channel_id=1, source_target_pairs={{0,4},{4,0},{8,12},{12,8},{16,20},{20,16},{24,28},{28,24},{1,5},{5... | collective-permute-start | bytes 1572872 | tf_op jit(solution)/shard_map/ppermute | solution.py:26
  50.4 1.5 %collective-permute-start.15 = (bf16[2,1,4,128,128]{4,3,2,1,0:T(8,128)(2,1)S(1)}, bf16[2,1,4,128,128]{4,3,2,1,0:T(8,128)(2,1)S(1)}, u32[]{:S(2)}, u32[]{:S(2)}) collective-permute-start(bf16[2,1,4,128,128]{4,3,2,1,0:T(8,128)(2,1)S(1)} %slice.129), channel_id=1, source_target_pairs={{0,16},{4,20},{8,24},{12,28},{16,0},{20,4},{24,8},{28,12},{1,17},{... | collective-permute-start | bytes 786440 | tf_op jit(solution)/shard_map/ppermute | solution.py:26
  53.4 5.8 %collective-permute-done.19.refs_5_ = bf16[2,512,256]{2,1,0:T(8,128)(2,1)S(1)} collective-permute-done((bf16[2,512,256]{2,1,0:T(8,128)(2,1)S(1)}, bf16[2,512,256]{2,1,0:T(8,128)(2,1)S(1)}, u32[]{:S(2)}, u32[]{:S(2)}) %collective-permute-start.19) | collective-permute-done | bytes 524320 | tf_op jit(solution)/shard_map/ppermute | solution.py:26
  60.1 1.5 %collective-permute-start.18 = (bf16[1,4,128,256]{3,2,1,0:T(8,128)(2,1)S(1)}, bf16[1,4,128,256]{3,2,1,0:T(8,128)(2,1)S(1)}, u32[]{:S(2)}, u32[]{:S(2)}) collective-permute-start(bf16[1,4,128,256]{3,2,1,0:T(8,128)(2,1)S(1)} %get-tuple-element.76), channel_id=1, source_target_pairs={{0,16},{4,20},{8,24},{12,28},{16,0},{20,4},{24,8},{28,12},{1,17},{... | collective-permute-start | bytes 786440 | tf_op jit(solution)/shard_map/ppermute | solution.py:26
  62.3 1.6 %collective-permute-start.20 = (bf16[2,4,128,256]{3,2,1,0:T(8,128)(2,1)S(1)}, bf16[2,4,128,256]{3,2,1,0:T(8,128)(2,1)S(1)}, u32[]{:S(2)}, u32[]{:S(2)}) collective-permute-start(bf16[2,4,128,256]{3,2,1,0:T(8,128)(2,1)S(1)} %shard_map.85), channel_id=1, source_target_pairs={{0,4},{4,0},{8,12},{12,8},{16,20},{20,16},{24,28},{28,24},{1,5},{5... | collective-permute-start | bytes 1572872 | tf_op jit(solution)/shard_map/ppermute | solution.py:26
  63.9 5.8 %collective-permute-done.22.refs_5_ = bf16[2,512,256]{2,1,0:T(8,128)(2,1)S(1)} collective-permute-done((bf16[2,512,256]{2,1,0:T(8,128)(2,1)S(1)}, bf16[2,512,256]{2,1,0:T(8,128)(2,1)S(1)}, u32[]{:S(2)}, u32[]{:S(2)}) %collective-permute-start.22) | collective-permute-done | bytes 524320 | tf_op jit(solution)/shard_map/ppermute | solution.py:26
  70.5 1.6 %collective-permute-start.23 = (bf16[2,4,128,256]{3,2,1,0:T(8,128)(2,1)S(1)}, bf16[2,4,128,256]{3,2,1,0:T(8,128)(2,1)S(1)}, u32[]{:S(2)}, u32[]{:S(2)}) collective-permute-start(bf16[2,4,128,256]{3,2,1,0:T(8,128)(2,1)S(1)} %shard_map.88), channel_id=1, source_target_pairs={{0,4},{4,0},{8,12},{12,8},{16,20},{20,16},{24,28},{28,24},{1,5},{5... | collective-permute-start | bytes 1572872 | tf_op jit(solution)/shard_map/ppermute | solution.py:26
  74.3 1.6 %collective-permute-start.17 = (bf16[1,4,128,128]{3,2,1,0:T(8,128)(2,1)S(1)}, bf16[1,4,128,128]{3,2,1,0:T(8,128)(2,1)S(1)}, u32[]{:S(2)}, u32[]{:S(2)}) collective-permute-start(bf16[1,4,128,128]{3,2,1,0:T(8,128)(2,1)S(1)} %get-tuple-element.85), channel_id=1, source_target_pairs={{0,4},{4,0},{8,12},{12,8},{16,20},{20,16},{24,28},{28,24},{1,5},{5... | collective-permute-start | bytes 393224 | tf_op jit(solution)/shard_map/ppermute | solution.py:26
  77.3 1.7 %collective-permute-start.21 = (bf16[1,4,128,256]{3,2,1,0:T(8,128)(2,1)S(1)}, bf16[1,4,128,256]{3,2,1,0:T(8,128)(2,1)S(1)}, u32[]{:S(2)}, u32[]{:S(2)}) collective-permute-start(bf16[1,4,128,256]{3,2,1,0:T(8,128)(2,1)S(1)} %get-tuple-element.71), channel_id=1, source_target_pairs={{0,16},{4,20},{8,24},{12,28},{16,0},{20,4},{24,8},{28,12},{1,17},{... | collective-permute-start | bytes 786440 | tf_op jit(solution)/shard_map/ppermute | solution.py:26
  79.0 9.4 %collective-permute-done.23 = bf16[2,4,128,256]{3,2,1,0:T(8,128)(2,1)S(1)} collective-permute-done((bf16[2,4,128,256]{3,2,1,0:T(8,128)(2,1)S(1)}, bf16[2,4,128,256]{3,2,1,0:T(8,128)(2,1)S(1)}, u32[]{:S(2)}, u32[]{:S(2)}) %collective-permute-start.23) | collective-permute-done | bytes 524320 | tf_op jit(solution)/shard_map/ppermute | solution.py:26
  88.5 1.7 %collective-permute-start.24 = (bf16[1,4,128,256]{3,2,1,0:T(8,128)(2,1)S(1)}, bf16[1,4,128,256]{3,2,1,0:T(8,128)(2,1)S(1)}, u32[]{:S(2)}, u32[]{:S(2)}) collective-permute-start(bf16[1,4,128,256]{3,2,1,0:T(8,128)(2,1)S(1)} %get-tuple-element.69), channel_id=1, source_target_pairs={{0,16},{4,20},{8,24},{12,28},{16,0},{20,4},{24,8},{28,12},{1,17},{... | collective-permute-start | bytes 786440 | tf_op jit(solution)/shard_map/ppermute | solution.py:26
  90.2 2.9 %collective-permute-done.25 = bf16[2,4,128,128]{3,2,1,0:T(8,128)(2,1)S(1)} collective-permute-done((bf16[2,4,128,128]{3,2,1,0:T(8,128)(2,1)S(1)}, bf16[2,4,128,128]{3,2,1,0:T(8,128)(2,1)S(1)}, u32[]{:S(2)}, u32[]{:S(2)}) %collective-permute-start.25) | collective-permute-done | bytes 262176 | tf_op jit(solution)/shard_map/ppermute | solution.py:26
  93.2 1.6 %collective-permute-start.26 = (bf16[1,4,128,128]{3,2,1,0:T(8,128)(2,1)S(1)}, bf16[1,4,128,128]{3,2,1,0:T(8,128)(2,1)S(1)}, u32[]{:S(2)}, u32[]{:S(2)}) collective-permute-start(bf16[1,4,128,128]{3,2,1,0:T(8,128)(2,1)S(1)} %get-tuple-element.80), channel_id=1, source_target_pairs={{0,16},{4,20},{8,24},{12,28},{16,0},{20,4},{24,8},{28,12},{1,17},{... | collective-permute-start | bytes 393224 | tf_op jit(solution)/shard_map/ppermute | solution.py:26
  94.8 1.9 %shard_map.82.so_far_ref = bf16[128,4096]{1,0:T(8,128)(2,1)} custom-call(s32[1]{0:T(128)} %bitcast.place_ref, bf16[128,4096]{1,0:T(8,128)(2,1)} %shard_map.78.so_far_ref, bf16[1,4,128,128]{3,2,1,0:T(8,128)(2,1)S(1)} %get-tuple-element.86.near_ref, bf16[1,4,128,128]{3,2,1,0:T(8,128)(2,1)S(1)} %collective-permute-done.17.far_ref), custom_call_target="tpu_custom_call", output_to_operand_aliasing={{}: (1, {})} | custom-call | bytes 1000000 | tf_op jit(solution)/shard_map/pallas_call | solution.py:312
  96.7 2.0 %shard_map.83.so_far_ref = bf16[128,4096]{1,0:T(8,128)(2,1)} custom-call(s32[1]{0:T(128)} %bitcast.place_ref, bf16[128,4096]{1,0:T(8,128)(2,1)} %shard_map.82.so_far_ref, bf16[1,4,128,256]{3,2,1,0:T(8,128)(2,1)S(1)} %get-tuple-element.75.near_ref, bf16[1,4,128,256]{3,2,1,0:T(8,128)(2,1)S(1)} %collective-permute-done.18.far_ref), custom_call_target="tpu_custom_call", output_to_operand_aliasing={{}: (1, {})} | custom-call | bytes 1000000 | tf_op jit(solution)/shard_map/pallas_call | solution.py:312
  98.7 2.0 %shard_map.86.so_far_ref = bf16[128,4096]{1,0:T(8,128)(2,1)} custom-call(s32[1]{0:T(128)} %bitcast.place_ref, bf16[128,4096]{1,0:T(8,128)(2,1)} %shard_map.83.so_far_ref, bf16[1,4,128,256]{3,2,1,0:T(8,128)(2,1)S(1)} %get-tuple-element.72.near_ref, bf16[1,4,128,256]{3,2,1,0:T(8,128)(2,1)S(1)} %collective-permute-done.21.far_ref), custom_call_target="tpu_custom_call", output_to_operand_aliasing={{}: (1, {})} | custom-call | bytes 1000000 | tf_op jit(solution)/shard_map/pallas_call | solution.py:312
  100.7 3.4 %collective-permute-done.24.far_ref = bf16[1,4,128,256]{3,2,1,0:T(8,128)(2,1)S(1)} collective-permute-done((bf16[1,4,128,256]{3,2,1,0:T(8,128)(2,1)S(1)}, bf16[1,4,128,256]{3,2,1,0:T(8,128)(2,1)S(1)}, u32[]{:S(2)}, u32[]{:S(2)}) %collective-permute-start.24) | collective-permute-done | bytes 262176 | tf_op jit(solution)/shard_map/ppermute | solution.py:26
  104.0 2.0 %shard_map.89.so_far_ref = bf16[128,4096]{1,0:T(8,128)(2,1)} custom-call(s32[1]{0:T(128)} %bitcast.place_ref, bf16[128,4096]{1,0:T(8,128)(2,1)} %shard_map.86.so_far_ref, bf16[1,4,128,256]{3,2,1,0:T(8,128)(2,1)S(1)} %get-tuple-element.70.near_ref, bf16[1,4,128,256]{3,2,1,0:T(8,128)(2,1)S(1)} %collective-permute-done.24.far_ref), custom_call_target="tpu_custom_call", output_to_operand_aliasing={{}: (1, {})} | custom-call | bytes 1000000 | tf_op jit(solution)/shard_map/pallas_call | solution.py:312
  106.2 1.9 %shard_map.92 = bf16[128,4096]{1,0:T(8,128)(2,1)} custom-call(s32[1]{0:T(128)} %bitcast.place_ref, bf16[128,4096]{1,0:T(8,128)(2,1)} %shard_map.89.so_far_ref, bf16[1,4,128,128]{3,2,1,0:T(8,128)(2,1)S(1)} %get-tuple-element.81.near_ref, bf16[1,4,128,128]{3,2,1,0:T(8,128)(2,1)S(1)} %collective-permute-done.26.far_ref), custom_call_target="tpu_custom_call", output_to_operand_aliasing={{}: (1, {})} | custom-call | bytes 1000000 | tf_op jit(solution)/shard_map/pallas_call | solution.py:312
  (82 shorter events, 16.7 us)
Async XLA Ops:
  0.0 8.6 %collective-permute-start.2 = (s32[1,128]{1,0:T(1,128)}, s32[1,128]{1,0:T(1,128)S(1)}, u32[]{:S(2)}, u32[]{:S(2)}) collective-permute-start(s32[1,128]{1,0:T(1,128)} %ids_ref), channel_id=1, source_target_pairs={{0,24},{4,28},{8,16},{12,20},{16,8},{20,12},{24,0},{28,4},{1,25},{... | collective-permute-start | bytes 1544 | tf_op jit(solution)/shard_map/ppermute | solution.py:26
  5.0 3.7 %collective-permute-start.1 = (s32[1,128]{1,0:T(1,128)}, s32[1,128]{1,0:T(1,128)S(1)}, u32[]{:S(2)}, u32[]{:S(2)}) collective-permute-start(s32[1,128]{1,0:T(1,128)} %ids_ref), channel_id=1, source_target_pairs={{0,8},{4,12},{8,0},{12,4},{16,24},{20,28},{24,16},{28,20},{1,9},{5... | collective-permute-start | bytes 1544 | tf_op jit(solution)/shard_map/ppermute | solution.py:26
  5.1 4.6 %collective-permute-start = (s32[1,128]{1,0:T(1,128)}, s32[1,128]{1,0:T(1,128)S(1)}, u32[]{:S(2)}, u32[]{:S(2)}) collective-permute-start(s32[1,128]{1,0:T(1,128)} %ids_ref), channel_id=1, source_target_pairs={{0,16},{4,20},{8,24},{12,28},{16,0},{20,4},{24,8},{28,12},{1,17},{... | collective-permute-start | bytes 1544 | tf_op jit(solution)/shard_map/ppermute | solution.py:26
  5.6 2.2 %copy-start.5 = (bf16[32,128]{1,0:T(8,128)(2,1)S(1)}, bf16[32,128]{1,0:T(8,128)(2,1)}, u32[]{:S(2)}) copy-start(bf16[32,128]{1,0:T(8,128)(2,1)} %param.12) | copy-start | bytes 24580
  5.6 4.0 %copy-start.3 = (s32[1,128]{1,0:T(1,128)S(1)}, s32[1,128]{1,0:T(1,128)}, u32[]{:S(2)}) copy-start(s32[1,128]{1,0:T(1,128)} %ids_ref) | copy-start | bytes 1540
  5.6 11.3 %copy-start.2 = (f32[4096]{0:T(1024)S(1)}, f32[4096]{0:T(1024)}, u32[]{:S(2)}) copy-start(f32[4096]{0:T(1024)} %param.9) | copy-start | bytes 49156
  9.6 3.7 %collective-permute-start.3 = (s32[4,128]{1,0:T(4,128)S(1)}, s32[4,128]{1,0:T(4,128)S(1)}, u32[]{:S(2)}, u32[]{:S(2)}) collective-permute-start(s32[4,128]{1,0:T(4,128)S(1)} %pad_add_fusion.4), channel_id=1, source_target_pairs={{0,4},{4,0},{8,12},{12,8},{16,20},{20,16},{24,28},{28,24},{1,5},{5... | collective-permute-start | bytes 6152 | tf_op jit(solution)/shard_map/ppermute | solution.py:26
  11.2 17.9 %collective-permute-start.6 = (bf16[512,512]{1,0:T(8,128)(2,1)}, bf16[512,512]{1,0:T(8,128)(2,1)S(1)}, u32[]{:S(2)}, u32[]{:S(2)}) collective-permute-start(bf16[512,512]{1,0:T(8,128)(2,1)} %get-tuple-element.44), channel_id=1, source_target_pairs={{0,8},{4,12},{8,0},{12,4},{16,24},{20,28},{24,16},{28,20},{1,9},{5... | collective-permute-start | bytes 1572872 | tf_op jit(solution)/shard_map/ppermute | solution.py:26
  13.3 15.6 %collective-permute-start.8 = (s32[8,128]{1,0:T(8,128)S(1)}, s32[8,128]{1,0:T(8,128)S(1)}, u32[]{:S(2)}, u32[]{:S(2)}) collective-permute-start(s32[8,128]{1,0:T(8,128)S(1)} %pad_add_fusion.2), channel_id=1, source_target_pairs={{0,1},{1,2},{2,3},{3,0},{4,5},{5,6},{6,7},{7,4},{8,9},{9,10},{10,1... | collective-permute-start | bytes 12296 | tf_op jit(solution)/shard_map/ppermute | solution.py:21
  13.3 15.4 %collective-permute-start.7 = (s32[8,128]{1,0:T(8,128)S(1)}, s32[8,128]{1,0:T(8,128)S(1)}, u32[]{:S(2)}, u32[]{:S(2)}) collective-permute-start(s32[8,128]{1,0:T(8,128)S(1)} %pad_add_fusion.2), channel_id=1, source_target_pairs={{0,2},{1,3},{2,0},{3,1},{4,6},{5,7},{6,4},{7,5},{8,10},{9,11},{10,... | collective-permute-start | bytes 12296 | tf_op jit(solution)/shard_map/ppermute | solution.py:21
  14.9 23.8 %collective-permute-start.4 = (bf16[512,512]{1,0:T(8,128)(2,1)}, bf16[512,512]{1,0:T(8,128)(2,1)S(1)}, u32[]{:S(2)}, u32[]{:S(2)}) collective-permute-start(bf16[512,512]{1,0:T(8,128)(2,1)} %get-tuple-element.42), channel_id=1, source_target_pairs={{0,8},{4,12},{8,0},{12,4},{16,24},{20,28},{24,16},{28,20},{1,9},{5... | collective-permute-start | bytes 1572872 | tf_op jit(solution)/shard_map/ppermute | solution.py:26
  19.1 10.7 %copy-start.4 = (f32[3,3,512]{2,1,0:T(4,128)S(1)}, f32[3,3,512]{2,1,0:T(4,128)}, u32[]{:S(2)}) copy-start(f32[3,3,512]{2,1,0:T(4,128)} %short_ref.3) | copy-start | bytes 55300
  29.1 9.6 %collective-permute-start.10 = (bf16[512,256]{1,0:T(8,128)(2,1)S(1)}, bf16[512,256]{1,0:T(8,128)(2,1)S(1)}, u32[]{:S(2)}, u32[]{:S(2)}) collective-permute-start(bf16[512,256]{1,0:T(8,128)(2,1)S(1)} %get-tuple-element.83), channel_id=1, source_target_pairs={{0,2},{1,3},{2,0},{3,1},{4,6},{5,7},{6,4},{7,5},{8,10},{9,11},{10,... | collective-permute-start | bytes 786440 | tf_op jit(solution)/shard_map/ppermute | solution.py:26
  31.6 13.6 %collective-permute-start.12 = (bf16[2,128,512]{2,1,0:T(8,128)(2,1)S(1)}, bf16[2,128,512]{2,1,0:T(8,128)(2,1)S(1)}, u32[]{:S(2)}, u32[]{:S(2)}) collective-permute-start(bf16[2,128,512]{2,1,0:T(8,128)(2,1)S(1)} %shard_map.76), channel_id=1, source_target_pairs={{0,8},{4,12},{8,0},{12,4},{16,24},{20,28},{24,16},{28,20},{1,9},{5... | collective-permute-start | bytes 786440 | tf_op jit(solution)/shard_map/ppermute | solution.py:26
  31.8 12.0 %collective-permute-start.9 = (bf16[512,256]{1,0:T(8,128)(2,1)S(1)}, bf16[512,256]{1,0:T(8,128)(2,1)S(1)}, u32[]{:S(2)}, u32[]{:S(2)}) collective-permute-start(bf16[512,256]{1,0:T(8,128)(2,1)S(1)} %get-tuple-element.50), channel_id=1, source_target_pairs={{0,2},{1,3},{2,0},{3,1},{4,6},{5,7},{6,4},{7,5},{8,10},{9,11},{10,... | collective-permute-start | bytes 786440 | tf_op jit(solution)/shard_map/ppermute | solution.py:26
  38.7 5.2 %collective-permute-start.5 = (bf16[512,512]{1,0:T(8,128)(2,1)S(1)}, bf16[512,512]{1,0:T(8,128)(2,1)S(1)}, u32[]{:S(2)}, u32[]{:S(2)}) collective-permute-start(bf16[512,512]{1,0:T(8,128)(2,1)S(1)} %collective-permute-done.4), channel_id=1, source_target_pairs={{0,1},{1,0},{2,3},{3,2},{4,5},{5,4},{6,7},{7,6},{8,9},{9,8},{10,11... | collective-permute-start | bytes 1572872 | tf_op jit(solution)/shard_map/ppermute | solution.py:26
  38.9 6.2 %copy-start = (bf16[512,4096]{1,0:T(8,128)(2,1)S(1)}, bf16[512,4096]{1,0:T(8,128)(2,1)}, u32[]{:S(2)}) copy-start(bf16[512,4096]{1,0:T(8,128)(2,1)} %refs_3_.17) | copy-start | bytes 12582916
  38.9 9.0 %collective-permute-start.11 = (bf16[2,128,512]{2,1,0:T(8,128)(2,1)S(1)}, bf16[2,128,512]{2,1,0:T(8,128)(2,1)S(1)}, u32[]{:S(2)}, u32[]{:S(2)}) collective-permute-start(bf16[2,128,512]{2,1,0:T(8,128)(2,1)S(1)} %get-tuple-element.79), channel_id=1, source_target_pairs={{0,8},{4,12},{8,0},{12,4},{16,24},{20,28},{24,16},{28,20},{1,9},{5... | collective-permute-start | bytes 786440 | tf_op jit(solution)/shard_map/ppermute | solution.py:26
  41.0 4.2 %collective-permute-start.13 = (bf16[2,512,256]{2,1,0:T(8,128)(2,1)S(1)}, bf16[2,512,256]{2,1,0:T(8,128)(2,1)S(1)}, u32[]{:S(2)}, u32[]{:S(2)}) collective-permute-start(bf16[2,512,256]{2,1,0:T(8,128)(2,1)S(1)} %pad_maximum_fusion.2.refs_4_), channel_id=1, source_target_pairs={{0,1},{1,0},{2,3},{3,2},{4,5},{5,4},{6,7},{7,6},{8,9},{9,8},{10,11... | collective-permute-start | bytes 1572872 | tf_op jit(solution)/shard_map/ppermute | solution.py:26
  44.0 5.0 %collective-permute-start.14 = (bf16[2,512,256]{2,1,0:T(8,128)(2,1)S(1)}, bf16[2,512,256]{2,1,0:T(8,128)(2,1)S(1)}, u32[]{:S(2)}, u32[]{:S(2)}) collective-permute-start(bf16[2,512,256]{2,1,0:T(8,128)(2,1)S(1)} %pad_maximum_fusion.1.refs_4_), channel_id=1, source_target_pairs={{0,1},{1,0},{2,3},{3,2},{4,5},{5,4},{6,7},{7,6},{8,9},{9,8},{10,11... | collective-permute-start | bytes 1572872 | tf_op jit(solution)/shard_map/ppermute | solution.py:26
  44.4 14.8 %collective-permute-start.19 = (bf16[2,512,256]{2,1,0:T(8,128)(2,1)S(1)}, bf16[2,512,256]{2,1,0:T(8,128)(2,1)S(1)}, u32[]{:S(2)}, u32[]{:S(2)}) collective-permute-start(bf16[2,512,256]{2,1,0:T(8,128)(2,1)S(1)} %get-tuple-element.73.refs_4_), channel_id=1, source_target_pairs={{0,2},{1,3},{2,0},{3,1},{4,6},{5,7},{6,4},{7,5},{8,10},{9,11},{10,... | collective-permute-start | bytes 1572872 | tf_op jit(solution)/shard_map/ppermute | solution.py:26
  45.9 14.1 %collective-permute-start.16 = (bf16[2,4,128,256]{3,2,1,0:T(8,128)(2,1)S(1)}, bf16[2,4,128,256]{3,2,1,0:T(8,128)(2,1)S(1)}, u32[]{:S(2)}, u32[]{:S(2)}) collective-permute-start(bf16[2,4,128,256]{3,2,1,0:T(8,128)(2,1)S(1)} %shard_map.79), channel_id=1, source_target_pairs={{0,4},{4,0},{8,12},{12,8},{16,20},{20,16},{24,28},{28,24},{1,5},{5... | collective-permute-start | bytes 1572872 | tf_op jit(solution)/shard_map/ppermute | solution.py:26
  47.9 21.8 %collective-permute-start.22 = (bf16[2,512,256]{2,1,0:T(8,128)(2,1)S(1)}, bf16[2,512,256]{2,1,0:T(8,128)(2,1)S(1)}, u32[]{:S(2)}, u32[]{:S(2)}) collective-permute-start(bf16[2,512,256]{2,1,0:T(8,128)(2,1)S(1)} %get-tuple-element.64.refs_4_), channel_id=1, source_target_pairs={{0,2},{1,3},{2,0},{3,1},{4,6},{5,7},{6,4},{7,5},{8,10},{9,11},{10,... | collective-permute-start | bytes 1572872 | tf_op jit(solution)/shard_map/ppermute | solution.py:26
  50.4 23.7 %collective-permute-start.15 = (bf16[2,1,4,128,128]{4,3,2,1,0:T(8,128)(2,1)S(1)}, bf16[2,1,4,128,128]{4,3,2,1,0:T(8,128)(2,1)S(1)}, u32[]{:S(2)}, u32[]{:S(2)}) collective-permute-start(bf16[2,1,4,128,128]{4,3,2,1,0:T(8,128)(2,1)S(1)} %slice.129), channel_id=1, source_target_pairs={{0,16},{4,20},{8,24},{12,28},{16,0},{20,4},{24,8},{28,12},{1,17},{... | collective-permute-start | bytes 786440 | tf_op jit(solution)/shard_map/ppermute | solution.py:26
  60.1 36.6 %collective-permute-start.18 = (bf16[1,4,128,256]{3,2,1,0:T(8,128)(2,1)S(1)}, bf16[1,4,128,256]{3,2,1,0:T(8,128)(2,1)S(1)}, u32[]{:S(2)}, u32[]{:S(2)}) collective-permute-start(bf16[1,4,128,256]{3,2,1,0:T(8,128)(2,1)S(1)} %get-tuple-element.76), channel_id=1, source_target_pairs={{0,16},{4,20},{8,24},{12,28},{16,0},{20,4},{24,8},{28,12},{1,17},{... | collective-permute-start | bytes 786440 | tf_op jit(solution)/shard_map/ppermute | solution.py:26
  62.3 14.8 %collective-permute-start.20 = (bf16[2,4,128,256]{3,2,1,0:T(8,128)(2,1)S(1)}, bf16[2,4,128,256]{3,2,1,0:T(8,128)(2,1)S(1)}, u32[]{:S(2)}, u32[]{:S(2)}) collective-permute-start(bf16[2,4,128,256]{3,2,1,0:T(8,128)(2,1)S(1)} %shard_map.85), channel_id=1, source_target_pairs={{0,4},{4,0},{8,12},{12,8},{16,20},{20,16},{24,28},{28,24},{1,5},{5... | collective-permute-start | bytes 1572872 | tf_op jit(solution)/shard_map/ppermute | solution.py:26
  70.5 17.9 %collective-permute-start.23 = (bf16[2,4,128,256]{3,2,1,0:T(8,128)(2,1)S(1)}, bf16[2,4,128,256]{3,2,1,0:T(8,128)(2,1)S(1)}, u32[]{:S(2)}, u32[]{:S(2)}) collective-permute-start(bf16[2,4,128,256]{3,2,1,0:T(8,128)(2,1)S(1)} %shard_map.88), channel_id=1, source_target_pairs={{0,4},{4,0},{8,12},{12,8},{16,20},{20,16},{24,28},{28,24},{1,5},{5... | collective-permute-start | bytes 1572872 | tf_op jit(solution)/shard_map/ppermute | solution.py:26
  72.8 20.3 %collective-permute-start.25 = (bf16[2,4,128,128]{3,2,1,0:T(8,128)(2,1)S(1)}, bf16[2,4,128,128]{3,2,1,0:T(8,128)(2,1)S(1)}, u32[]{:S(2)}, u32[]{:S(2)}) collective-permute-start(bf16[2,4,128,128]{3,2,1,0:T(8,128)(2,1)S(1)} %shard_map.91), channel_id=1, source_target_pairs={{0,4},{4,0},{8,12},{12,8},{16,20},{20,16},{24,28},{28,24},{1,5},{5... | collective-permute-start | bytes 786440 | tf_op jit(solution)/shard_map/ppermute | solution.py:26
  74.3 20.5 %collective-permute-start.17 = (bf16[1,4,128,128]{3,2,1,0:T(8,128)(2,1)S(1)}, bf16[1,4,128,128]{3,2,1,0:T(8,128)(2,1)S(1)}, u32[]{:S(2)}, u32[]{:S(2)}) collective-permute-start(bf16[1,4,128,128]{3,2,1,0:T(8,128)(2,1)S(1)} %get-tuple-element.85), channel_id=1, source_target_pairs={{0,4},{4,0},{8,12},{12,8},{16,20},{20,16},{24,28},{28,24},{1,5},{5... | collective-permute-start | bytes 393224 | tf_op jit(solution)/shard_map/ppermute | solution.py:26
  77.3 21.4 %collective-permute-start.21 = (bf16[1,4,128,256]{3,2,1,0:T(8,128)(2,1)S(1)}, bf16[1,4,128,256]{3,2,1,0:T(8,128)(2,1)S(1)}, u32[]{:S(2)}, u32[]{:S(2)}) collective-permute-start(bf16[1,4,128,256]{3,2,1,0:T(8,128)(2,1)S(1)} %get-tuple-element.71), channel_id=1, source_target_pairs={{0,16},{4,20},{8,24},{12,28},{16,0},{20,4},{24,8},{28,12},{1,17},{... | collective-permute-start | bytes 786440 | tf_op jit(solution)/shard_map/ppermute | solution.py:26
  88.5 15.5 %collective-permute-start.24 = (bf16[1,4,128,256]{3,2,1,0:T(8,128)(2,1)S(1)}, bf16[1,4,128,256]{3,2,1,0:T(8,128)(2,1)S(1)}, u32[]{:S(2)}, u32[]{:S(2)}) collective-permute-start(bf16[1,4,128,256]{3,2,1,0:T(8,128)(2,1)S(1)} %get-tuple-element.69), channel_id=1, source_target_pairs={{0,16},{4,20},{8,24},{12,28},{16,0},{20,4},{24,8},{28,12},{1,17},{... | collective-permute-start | bytes 786440 | tf_op jit(solution)/shard_map/ppermute | solution.py:26
  93.2 13.0 %collective-permute-start.26 = (bf16[1,4,128,128]{3,2,1,0:T(8,128)(2,1)S(1)}, bf16[1,4,128,128]{3,2,1,0:T(8,128)(2,1)S(1)}, u32[]{:S(2)}, u32[]{:S(2)}) collective-permute-start(bf16[1,4,128,128]{3,2,1,0:T(8,128)(2,1)S(1)} %get-tuple-element.80), channel_id=1, source_target_pairs={{0,16},{4,20},{8,24},{12,28},{16,0},{20,4},{24,8},{28,12},{1,17},{... | collective-permute-start | bytes 393224 | tf_op jit(solution)/shard_map/ppermute | solution.py:26
  (1 other events, 2.2 us)
